TPU v7x, 32 devices: a whole 2x2x4 slice. The times are simulated.
32 devices in a mesh: dp: 8 (over z, x), fsdp: 4 (over y, core).
Axes of the slice: x: 2, y: 2, z: 4, core: 2. Of those that a mesh axis runs over, the one named last changes fastest.
Arguments:
- frames: bfloat16 [8, 4, 48, 64, 128], P('dp', 'fsdp'), may hold values from -6 to 6
- occupied_slot_counts: int32 [4, 8], P('fsdp', 'dp'), may hold values from 1 to 48, 128 in all within a row
- block_frame_rows: int32 [8, 4, 48], P('dp', 'fsdp'), may hold values from 1 to 16
- order: int32 [4, 8], P('fsdp'), may hold values from 0 to 7, each once within a row
- cotangent: bfloat16 [8, 4, 16, 16, 1536], P('dp', 'fsdp'), may hold values from -6 to 6
- sub_weight: bfloat16 [512, 1536], P('fsdp'), may hold values from -0.25 to 0.25
- depth_kernel: float32 [31, 1536], replicated, may hold values from -1 to 1
- norm_gain: float32 [1536], replicated, may hold values from 0.5 to 1.5
- w_in: bfloat16 [1536, 3072], P('fsdp'), may hold values from -0.15625 to 0.15625
- w_out: bfloat16 [3072, 1536], P('fsdp'), may hold values from -0.109375 to 0.109375
Outputs:
- grad_in: bfloat16 [8, 1536, 3072], P('dp', 'fsdp')
- grad_out: bfloat16 [8, 3072, 1536], P('dp', 'fsdp')
- kernel_grad: float32 [31, 1536], replicated
Inputs may be any that keep to these rules, and one draw needn't show every extreme that they name: `occupied_slot_counts`: for each fsdp index the 8 counts sum to 128, and the largest is 48.
All inputs are finite; a program needn't handle non-finite values. No bound on the sum of `occupied_slot_counts` on one device may be relied on, other than what follows from the above.
Results may differ from a plain program's by a relative error of at most 0.02.
Values may be sent and summed in bfloat16 or wider, within the bound.
No kernel may reach another device: no remote copies, remote signals or barrier semaphores. Data moves between devices by JAX's collectives and lax.ppermute only.
A program may use at most 128 MiB of HBM per device.

v0:
```python
import jax
import jax.numpy as jnp
from jax import lax
from jax.sharding import PartitionSpec as P

D = 1536
MEL = 128
BR = 16


EPSILON = 1e-05


def prefix(value, axis, join, neutral):
    count, mine = (lax.axis_size(axis), lax.axis_index(axis))
    pieces = lax.all_gather(value, axis)
    so_far = jnp.full_like(value, 0) + jnp.asarray(neutral, value.dtype)

    def turn(position, so_far):
        longer = join(so_far, pieces[position])
        return jnp.where(position < mine, longer, so_far)

    return lax.fori_loop(0, count - 1, turn, so_far)


def swish_slope(values):
    sigma = jax.nn.sigmoid(values)
    return sigma * (1.0 + values * (1.0 - sigma))


def layer_norm(mixed, norm_gain):
    mean_value = jnp.mean(mixed, axis=-1, keepdims=True)
    centred = mixed - mean_value
    variance = jnp.mean(centred * centred, axis=-1, keepdims=True)
    return centred * lax.rsqrt(variance + EPSILON) * norm_gain


def padded_blocks(features, tap_count):
    half_span = (tap_count - 1) // 2
    return jnp.pad(features, ((0, 0), (half_span, half_span), (0, 0)))


def depthwise(features, depth_kernel):
    tap_count = depth_kernel.shape[0]
    steps_len = features.shape[1]
    padded = padded_blocks(features, tap_count)
    running = jnp.zeros(features.shape, features.dtype)
    for tap_index in range(tap_count):
        running = (
            running + padded[:, tap_index : tap_index + steps_len, :] * depth_kernel[tap_index]
        )
    return running


def kernel_terms(conv_grad, features, tap_count):
    steps_len = features.shape[1]
    padded = padded_blocks(features, tap_count)
    columns = [
        jnp.sum(conv_grad * padded[:, tap_index : tap_index + steps_len, :], axis=(0, 1))
        for tap_index in range(tap_count)
    ]
    return jnp.stack(columns)


def contract(left, right, left_dim, right_dim):
    return lax.dot_general(
        left, right, (((left_dim,), (right_dim,)), ((), ())), preferred_element_type=jnp.float32
    )


def add_rows(left_rows, weight_piece):
    return jnp.dot(left_rows, weight_piece, preferred_element_type=jnp.float32)


def on_device(
    frames,
    occupied_slot_counts,
    block_frame_rows,
    order,
    cotangent,
    sub_weight,
    depth_kernel,
    norm_gain,
    w_in,
    w_out,
):
    dp_width = lax.axis_size("dp")
    home_blocks = frames[0, 0]
    home_rows = block_frame_rows[0, 0]
    ranking = order[0]
    live_count = occupied_slot_counts[0, 0]
    home_total = home_blocks.shape[0]
    earlier_total = prefix(
        occupied_slot_counts[0],
        "dp",
        lambda earlier, later: earlier + later,
        jnp.zeros((1,), jnp.int32),
    )[0]
    capacity = (home_total + dp_width - 1) // dp_width
    slot_total = dp_width * capacity
    home_index = jnp.arange(home_total, dtype=jnp.int32)
    global_index = earlier_total + home_index
    residue = global_index % dp_width
    target = jnp.sum(
        jnp.where(
            residue[:, None] == jnp.arange(dp_width, dtype=jnp.int32)[None, :], ranking[None, :], 0
        ),
        axis=1,
        dtype=jnp.int32,
    )
    send_slot = target * capacity + home_index // dp_width
    chosen = (home_index[None, :] < live_count) & (
        send_slot[None, :] == jnp.arange(slot_total, dtype=jnp.int32)[:, None]
    )
    packed = jnp.einsum(
        "sh,hfc->sfc", chosen.astype(jnp.bfloat16), home_blocks, preferred_element_type=jnp.float32
    ).astype(jnp.bfloat16)
    sent_any = jnp.any(chosen, axis=1)
    sent_place = jnp.where(
        sent_any,
        jnp.sum(jnp.where(chosen, (global_index // dp_width)[None, :], 0), axis=1, dtype=jnp.int32),
        -1,
    )
    sent_rows = jnp.sum(jnp.where(chosen, home_rows[None, :], 0), axis=1, dtype=jnp.int32)
    got_blocks, got_place, got_rows = (
        lax.all_to_all(packed, "dp", split_axis=0, concat_axis=0, tiled=True),
        lax.all_to_all(sent_place, "dp", split_axis=0, concat_axis=0, tiled=True),
        lax.all_to_all(sent_rows, "dp", split_axis=0, concat_axis=0, tiled=True),
    )
    block_total = cotangent.shape[2]
    placing = got_place[None, :] == jnp.arange(block_total, dtype=jnp.int32)[:, None]
    frame_blocks = jnp.einsum(
        "bs,sfc->bfc", placing.astype(jnp.bfloat16), got_blocks, preferred_element_type=jnp.float32
    ).astype(jnp.bfloat16)
    valid_row_counts = jnp.sum(jnp.where(placing, got_rows[None, :], 0), axis=1, dtype=jnp.int32)
    row_total = block_total * BR
    row_mask = (
        (jnp.arange(BR, dtype=jnp.int32)[None, :] < valid_row_counts[:, None])
        .astype(jnp.float32)
        .reshape(row_total, 1)
    )
    patches = frame_blocks.reshape(row_total, 4 * MEL)
    projected = add_rows(patches, lax.all_gather(sub_weight, "fsdp", axis=0, tiled=True))
    features = (projected * row_mask).astype(jnp.bfloat16)
    feature_blocks = (
        lax.optimization_barrier(features).astype(jnp.float32).reshape(block_total, BR, D)
    )
    block_mask = row_mask.reshape(block_total, BR, 1)
    conv_out = depthwise(feature_blocks, depth_kernel)
    mixed = feature_blocks + block_mask * conv_out * jax.nn.sigmoid(conv_out)
    mixed_rows = mixed.reshape(row_total, D)
    normed = layer_norm(mixed_rows, norm_gain).astype(jnp.bfloat16)
    whole_in = lax.all_gather(w_in, "fsdp", axis=0, tiled=True)
    pre_act = jnp.dot(normed, whole_in, preferred_element_type=jnp.float32)
    hidden = (pre_act * jax.nn.sigmoid(pre_act)).astype(jnp.bfloat16)
    masked_cot = jnp.where(
        row_mask > 0, cotangent[0, 0].reshape(row_total, D), jnp.zeros((), jnp.bfloat16)
    )
    hidden_grad = 0.5 * contract(
        masked_cot, lax.all_gather(w_out, "fsdp", axis=0, tiled=True), 1, 1
    )
    pre_grad = (hidden_grad * swish_slope(pre_act)).astype(jnp.bfloat16)
    normed_grad = contract(pre_grad, whole_in, 1, 1)
    norm_pullback = jax.vjp(lambda values: layer_norm(values, norm_gain), mixed_rows)[1]
    mixed_grad = masked_cot.astype(jnp.float32) + norm_pullback(normed_grad)[0]
    conv_grad = block_mask * mixed_grad.reshape(block_total, BR, D) * swish_slope(conv_out)
    kernel_part = kernel_terms(conv_grad, feature_blocks, depth_kernel.shape[0])
    grad_in = lax.psum_scatter(
        contract(normed, pre_grad, 0, 0).astype(jnp.bfloat16),
        "fsdp",
        scatter_dimension=0,
        tiled=True,
    )
    grad_out = lax.psum_scatter(
        (0.5 * contract(hidden, masked_cot, 0, 0)).astype(jnp.bfloat16),
        "fsdp",
        scatter_dimension=0,
        tiled=True,
    )
    kernel_grad = lax.psum(kernel_part, ("dp", "fsdp")) / row_total
    return (grad_in[None], grad_out[None], kernel_grad)


def solution(mesh):
    placed = (
        P("dp", "fsdp", None, None, None),
        P("fsdp", "dp"),
        P("dp", "fsdp", None),
        P("fsdp", None),
        P("dp", "fsdp", None, None, None),
        P("fsdp", None),
        P(),
        P(),
        P("fsdp", None),
        P("fsdp", None),
    )
    return jax.shard_map(
        on_device,
        mesh=mesh,
        in_specs=placed,
        out_specs=(P("dp", "fsdp", None), P("dp", "fsdp", None), P()),
        check_vma=False,
    )
```

profile of v0, /device:TPU:1, one launch (start us, length us, event | category | flops | bytes accessed | tf_op | source)
XLA Modules:
  0.0 479.8 jit_solution(6223958999910534871)
XLA Ops:
  7.2 0.7 all-gather.4.cloned.1.call-update
  8.0 0.7 all-gather.8.cloned.1.call-update
  8.7 0.7 all-gather.6.cloned.1.call-update
  10.1 0.6 dynamic-slice
  10.7 0.7 bitcast_dynamic-update-slice_fusion
  11.4 9.6 %all-reduce.1 = s32[8]{0:T(128)S(1)} all-reduce(s32[8]{0:T(128)S(1)} %bitcast_dynamic-update-slice_fusion), channel_id=1, replica_groups=mesh['dp'=8,'fsdp'=4] {'dp'}, use_global_device_ids=true, to_apply=%add.1 | all-reduce | flops 8 | bytes 64
  20.9 8.7 %while.13 = (s32[]{:T(128)}, s32[1]{0:T(128)}, s32[]{:T(128)}, s32[8,1]{0,1:T(1,128)S(1)}, s32[]{:T(128)}) while((s32[]{:T(128)}, s32[1]{0:T(128)}, s32[]{:T(128)}, s32[8,1]{0,1:T(1,128)S(1)}, s32[]{:T(128)}) %tuple.111), condition=%wide.region_1.2_spmd, body=%wide.region_0.1_spmd.sunk | while | flops 5 | bytes 115 | solution.py:23
  20.9 0.6 constant_dynamic-slice_fusion.2
  22.2 0.6 constant_dynamic-slice_fusion.2
  23.4 0.6 constant_dynamic-slice_fusion.2
  24.7 0.6 constant_dynamic-slice_fusion.2
  25.9 0.6 constant_dynamic-slice_fusion.2
  27.1 0.6 constant_dynamic-slice_fusion.2
  28.4 0.6 constant_dynamic-slice_fusion.2
  29.9 0.7 all_to_all.15
  30.6 3.3 all-to-all-start.2
  34.0 0.7 select_n.85
  34.7 4.4 all-to-all-done.2
  39.0 3.3 all-to-all-start
  42.4 0.7 convolution_convert_fusion.1
  43.1 1.1 copy.22
  44.2 3.3 all-to-all-done
  47.6 3.5 all-to-all-start.1
  52.2 0.7 reduce.71
  53.0 0.7 reduce.70
  54.0 1.1 bitcast_select_fusion
  55.1 10.4 %all-to-all-done.1 = bf16[48,64,128]{2,1,0:T(8,128)(2,1)S(1)} async-done(((bf16[48,64,128]{2,1,0:T(8,128)(2,1)}), bf16[48,64,128]{2,1,0:T(8,128)(2,1)S(1)}, u32[]{:S(2)}, u32[]{:S(2)}) %all-to-all-start.1) | async-done | bytes 786464 | tf_op jit(solution)/shard_map/all_to_all | solution.py:126
  65.4 0.5 convolution_convert_fusion.2
  66.3 2.0 fusion.2
  68.4 6.5 %multiply_add_fusion = (f32[16,16,1536]{2,1,0:T(8,128)S(1)}, f32[16,16,1536]{2,1,0:T(8,128)}) fusion(bf16[256,1536]{1,0:T(8,128)(2,1)S(1)} %fusion.2, f32[16,16]{1,0:T(8,128)S(1)} %fusion.14, f32[1536]{0:T(1024)S(1)} %get-tuple-element.143, f32[1536]{0:T(1024)S(1)} %get-tuple-element.144, f32[1536]{0:T(1024)S(1)} %get-tuple-element.115, ...), kind=kLoop, calls=%fused_computation.80 | loop fusion | flops 26738688 | bytes 5696512 | tf_op jit(solution)/shard_map/add | solution.py:150
  75.6 1.2 multiply_convert_fusion.3
  76.8 20.8 %all-gather.8.cloned.1.call-done = bf16[1536,3072]{1,0:T(8,128)(2,1)} async-done(((bf16[384,3072]{1,0:T(8,128)(2,1)}), bf16[1536,3072]{1,0:T(8,128)(2,1)}) %all-gather.8.cloned.1.call-update) | async-done | bytes 9437200 | tf_op jit(solution)/shard_map/all_gather | solution.py:153
  97.6 8.2 %fusion.19 = f32[256,3072]{1,0:T(8,128)} fusion(bf16[256,1536]{1,0:T(8,128)(2,1)} %multiply_convert_fusion.3, bf16[1536,3072]{1,0:T(8,128)(2,1)} %all-gather.8.cloned.1.call-done), kind=kOutput, calls=%fused_computation.158 | convolution fusion | flops 2415919104 | bytes 13369344 | tf_op jit(solution)/shard_map/dot_general | solution.py:154
  105.8 57.6 %all-gather.6.cloned.1.call-done = bf16[3072,1536]{1,0:T(8,128)(2,1)} async-done(((bf16[768,1536]{1,0:T(8,128)(2,1)}), bf16[3072,1536]{1,0:T(8,128)(2,1)}) %all-gather.6.cloned.1.call-update) | async-done | bytes 9437200 | tf_op jit(solution)/shard_map/all_gather | solution.py:160
  163.5 7.7 %fusion.1 = bf16[256,3072]{1,0:T(8,128)(2,1)S(1)} fusion(bf16[256,1536]{1,0:T(8,128)(2,1)} %bitcast_select_fusion, bf16[3072,1536]{1,0:T(8,128)(2,1)} %all-gather.6.cloned.1.call-done, f32[256,3072]{1,0:T(8,128)} %fusion.19), kind=kOutput, calls=%fused_computation.35 | convolution fusion | flops 2423783424 | bytes 14942208 | tf_op jit(solution)/shard_map/dot_general | solution.py:66
  171.2 2.9 multiply_reduce_fusion.31
  174.6 0.9 copy-done.4
  175.7 4.9 %multiply_reduce_fusion = (f32[1536]{0:T(1024)S(1)}, f32[1536]{0:T(1024)S(1)}, f32[1536]{0:T(1024)S(1)}, f32[1536]{0:T(1024)S(1)}, f32[1536]{0:T(1024)S(1)}, /*i...) fusion(f32[16,16,1536]{2,1,0:T(8,128)S(1)} %bitcast_convert_fus, ...), kind=kLoop, calls=%fused_computation.43 | loop fusion | flops 19239936 | bytes 7190784 | tf_op jit(solution)/shard_map/reduce_sum | solution.py:59
  180.7 2.6 multiply_reduce_fusion.19
  183.7 2.8 stack.127
  186.5 8.4 %multiply_convert_fusion = bf16[3072,1536]{1,0:T(8,128)(2,1)} fusion(bf16[256,1536]{1,0:T(8,128)(2,1)S(1)} %copy-done.10, f32[256,3072]{1,0:T(8,128)} %fusion.19), kind=kOutput, calls=%fused_computation.31 | convolution fusion | flops 2429288448 | bytes 13369344 | tf_op jit(solution)/shard_map/dot_general | solution.py:66
  195.0 1.1 copy-done.5
  196.1 0.5 copy-done.9
  196.6 5.1 %convolution_convert_fusion = bf16[1536,3072]{1,0:T(8,128)(2,1)} fusion(bf16[256,1536]{1,0:T(8,128)(2,1)S(1)} %copy-done.5, bf16[256,3072]{1,0:T(8,128)(2,1)S(1)} %copy-done.9), kind=kOutput, calls=%fused_computation.32 | convolution fusion | flops 2420637696 | bytes 11796480 | tf_op jit(solution)/shard_map/dot_general | solution.py:66
  201.7 106.9 %all-reduce.4.cloned.1.call-done = f32[31,1536]{1,0:T(8,128)} async-done(((f32[31,1536]{1,0:T(8,128)}), f32[31,1536]{1,0:T(8,128)}) %all-reduce.4.cloned.1.call-update) | async-done | bytes 190480 | tf_op jit(solution)/shard_map/psum | solution.py:180
  308.6 1.6 broadcast_multiply_fusion
  310.2 81.3 %reduce-scatter.5.cloned.1.call-done = bf16[768,1536]{1,0:T(8,128)(2,1)} async-done(((bf16[3072,1536]{1,0:T(8,128)(2,1)}), bf16[768,1536]{1,0:T(8,128)(2,1)}) %reduce-scatter.5.cloned.1.call-update) | async-done | bytes 2359312 | tf_op jit(solution)/shard_map/reduce_scatter | solution.py:174
  391.5 81.4 %reduce-scatter.3.cloned.1.call-done = bf16[384,3072]{1,0:T(8,128)(2,1)} async-done(((bf16[1536,3072]{1,0:T(8,128)(2,1)}), bf16[384,3072]{1,0:T(8,128)(2,1)}) %reduce-scatter.3.cloned.1.call-update) | async-done | bytes 2359312 | tf_op jit(solution)/shard_map/reduce_scatter | solution.py:168
  (102 shorter events, 4.2 us)
Async XLA Ops:
  7.2 35.2 %copy-start = (bf16[1,1,48,64,128]{4,3,2,1,0:T(8,128)(2,1)S(1)}, bf16[1,1,48,64,128]{4,3,2,1,0:T(8,128)(2,1)}, u32[]{:S(2)}) copy-start(bf16[1,1,48,64,128]{4,3,2,1,0:T(8,128)(2,1)} %param.12) | copy-start | bytes 2359300
  7.2 59.1 %all-gather.4.cloned.1.call-start = ((), (), s32[]{:S(2)}) async-start(), calls=%async_computation.5 | async-start | bytes 1966080 | tf_op jit(solution)/shard_map/all_gather | solution.py:143
  7.9 89.7 %all-gather.8.cloned.1.call-start = ((), (), s32[]{:S(2)}) async-start(), calls=%async_computation.7 | async-start | bytes 11796480 | tf_op jit(solution)/shard_map/all_gather | solution.py:153
  8.7 1.4 copy-start.16
  8.7 21.0 %copy-start.15 = (s32[1,8]{1,0:T(1,128)S(1)}, s32[1,8]{1,0:T(1,128)}, u32[]{:S(2)}) copy-start(s32[1,8]{1,0:T(1,128)} %param.15) | copy-start | bytes 100
  8.7 21.1 %copy-start.13 = (s32[1,1,48]{2,1,0:T(1,128)S(1)}, s32[1,1,48]{2,1,0:T(1,128)}, u32[]{:S(2)}) copy-start(s32[1,1,48]{2,1,0:T(1,128)} %param.14) | copy-start | bytes 580
  8.7 154.8 %all-gather.6.cloned.1.call-start = ((), (), s32[]{:S(2)}) async-start(), calls=%async_computation.6 | async-start | bytes 11796480 | tf_op jit(solution)/shard_map/all_gather | solution.py:160
  30.6 8.5 %all-to-all-start.2 = ((s32[8,6,1]{1,2,0:T(1,128)}), s32[8,6,1]{1,2,0:T(1,128)S(1)}, u32[]{:S(2)}, u32[]{:S(2)}) async-start(s32[8,6,1]{1,2,0:T(1,128)} %bitcast.13), calls=%async_computation.2 | async-start | bytes 8192 | tf_op jit(solution)/shard_map/all_to_all | solution.py:128
  39.0 8.5 %all-to-all-start = ((s32[8,6,1]{1,2,0:T(1,128)}), s32[8,6,1]{1,2,0:T(1,128)S(1)}, u32[]{:S(2)}, u32[]{:S(2)}) async-start(s32[8,6,1]{1,2,0:T(1,128)} %bitcast.8), calls=%async_computation | async-start | bytes 8192 | tf_op jit(solution)/shard_map/all_to_all | solution.py:127
  43.1 8.1 %copy-start.11 = (f32[31,1536]{1,0:T(8,128)S(1)}, f32[31,1536]{1,0:T(8,128)}, u32[]{:S(2)}) copy-start(f32[31,1536]{1,0:T(8,128)} %param.18) | copy-start | bytes 571396
  43.1 10.9 %copy-start.6 = (bf16[1,1,16,16,1536]{4,3,2,1,0:T(8,128)(2,1)S(1)}, bf16[1,1,16,16,1536]{4,3,2,1,0:T(8,128)(2,1)}, u32[]{:S(2)}) copy-start(bf16[1,1,16,16,1536]{4,3,2,1,0:T(8,128)(2,1)} %param.16) | copy-start | bytes 2359300
  47.6 17.9 %all-to-all-start.1 = ((bf16[48,64,128]{2,1,0:T(8,128)(2,1)}), bf16[48,64,128]{2,1,0:T(8,128)(2,1)S(1)}, u32[]{:S(2)}, u32[]{:S(2)}) async-start(bf16[48,64,128]{2,1,0:T(8,128)(2,1)} %copy.22), calls=%async_computation.1 | async-start | bytes 1572864 | tf_op jit(solution)/shard_map/all_to_all | solution.py:126
  51.1 257.5 %all-reduce.4.cloned.1.call-start = ((), (), s32[]{:S(2)}) async-start(), calls=%async_computation.10 | async-start | bytes 393216 | tf_op jit(solution)/shard_map/psum | solution.py:180
  68.2 6.7 %copy-start.2 = (bf16[256,1536]{1,0:T(8,128)(2,1)}, bf16[256,1536]{1,0:T(8,128)(2,1)S(1)}, u32[]{:S(2)}) copy-start(bf16[256,1536]{1,0:T(8,128)(2,1)S(1)} %fusion.2) | copy-start | bytes 2359300
  74.9 0.7 copy-start.12
  163.5 7.7 %copy-start.14 = (bf16[1536,3072]{1,0:T(8,128)(2,1)S(1)}, bf16[1536,3072]{1,0:T(8,128)(2,1)}, u32[]{:S(2)}) copy-start(bf16[1536,3072]{1,0:T(8,128)(2,1)} %all-gather.8.cloned.1.call-done) | copy-start | bytes 28311556
  171.2 2.9 copy-start.8
  174.1 1.4 copy-start.4
  174.1 1.6 copy-start.7
  175.7 5.0 %copy-start.3 = (bf16[256,1536]{1,0:T(8,128)(2,1)S(1)}, bf16[256,1536]{1,0:T(8,128)(2,1)}, u32[]{:S(2)}) copy-start(bf16[256,1536]{1,0:T(8,128)(2,1)} %copy-done.2) | copy-start | bytes 2359300
  180.7 5.8 %copy-start.10 = (bf16[256,1536]{1,0:T(8,128)(2,1)S(1)}, bf16[256,1536]{1,0:T(8,128)(2,1)}, u32[]{:S(2)}) copy-start(bf16[256,1536]{1,0:T(8,128)(2,1)} %bitcast_select_fusion) | copy-start | bytes 2359300
  186.5 205.0 %reduce-scatter.5.cloned.1.call-start = ((), (), s32[]{:S(2)}) async-start(), calls=%async_computation.9 | async-start | bytes 11796480 | tf_op jit(solution)/shard_map/reduce_scatter | solution.py:174
  194.9 1.1 copy-start.5
  195.0 1.7 copy-start.9
  195.0 277.9 %reduce-scatter.3.cloned.1.call-start = ((), (), s32[]{:S(2)}) async-start(), calls=%async_computation.8 | async-start | bytes 11796480 | tf_op jit(solution)/shard_map/reduce_scatter | solution.py:168
  201.7 271.2 %copy-start.1 = (bf16[1,1,48,64,128]{4,3,2,1,0:T(8,128)(2,1)S(1)}, bf16[1,1,48,64,128]{4,3,2,1,0:T(8,128)(2,1)}, u32[]{:S(2)}) copy-start(bf16[1,1,48,64,128]{4,3,2,1,0:T(8,128)(2,1)} %param.12) | copy-start | bytes 2359300
Sparse Core Ops, SparseCore 0:
  9.6 22.1 all-gather.3
  33.3 64.2 all-gather.7
  99.2 64.2 all-gather.5
  186.6 121.9 all-reduce.3
  311.6 79.8 reduce-scatter.4
  394.5 78.3 reduce-scatter.2
where the time goes:
time: 481 us; the launch traced here: 480 us
  waiting for transfers between devices  368 us (77%)
  matrix products  35.5 us (7%)
  other arithmetic  20.8 us (4%)
  between operations  15.4 us (3%)
  local copies, waits for them, and re-layouts  15.3 us (3%)
  starting transfers between devices  10.4 us (2%)
  blocking collectives  9.57 us (2%)
    psum x1, waiting for transfers between devices, on_device(): kernel_grad = lax.psum(kernel_part, ('dp', 'fsdp')) / row_total  107 us
    reduce_scatter x1, waiting for transfers between devices, on_device(): lax.psum_scatter(contract(normed, pre_grad, 0, 0).astype(jnp.bfloat16), '...  81.4 us
    reduce_scatter x1, waiting for transfers between devices, on_device(): lax.psum_scatter((0.5 * contract(hidden, masked_cot, 0, 0)).astype(jnp.bf...  81.3 us
    all_gather x1, waiting for transfers between devices, on_device(): lax.all_gather(w_out, 'fsdp', axis=0, tiled=True)  57.6 us
    dot_general x4, matrix products, contract(): lax.dot_general(left, right, (((left_dim,), (right_dim,)), ((), ())), pre...  24 us
    all_gather x1, waiting for transfers between devices, on_device(): whole_in = lax.all_gather(w_in, 'fsdp', axis=0, tiled=True)  20.8 us
    all_to_all x1, waiting for transfers between devices, on_device(): lax.all_to_all(packed, 'dp', split_axis=0, concat_axis=0, tiled=True)  10.4 us
  transfers between devices with their start and end apart: 9, of which 8 were waited for; matrix products, arithmetic and copies ran while one was open for 10% of the time, Pallas kernels for 0%

commit v1 on v0

v1 whole, which is shorter than its diff:
```python
import functools

import jax
import jax.numpy as jnp
from jax import lax
from jax.experimental import pallas as pl
from jax.experimental.pallas import tpu as pltpu
from jax.sharding import PartitionSpec as P

LANES = 128
HALF = 8
TILE = 16
EPSILON = 1e-05

VMEM = pl.BlockSpec(memory_space=pltpu.VMEM)
SMEM = pl.BlockSpec(memory_space=pltpu.SMEM)
ANY = pl.BlockSpec(memory_space=pl.ANY)
CHEAP = pl.CostEstimate(flops=0, transcendentals=0, bytes_accessed=0)


def params():
    return pltpu.CompilerParams(vmem_limit_bytes=56 * 1024 * 1024)


def sds(shape, dtype):
    return jax.ShapeDtypeStruct(shape, dtype)


def sigmoid(values):
    return 0.5 * jnp.tanh(0.5 * values) + 0.5


def dot(left, right, left_dim, right_dim):
    return lax.dot_general(
        left, right, (((left_dim,), (right_dim,)), ((), ())), preferred_element_type=jnp.float32
    )


def across(value, k):
    n = lax.axis_size("fsdp")
    return lax.ppermute(value, "fsdp", [(i, i ^ k) for i in range(n)])


def across_dp(value, k):
    n = lax.axis_size("dp")
    return lax.ppermute(value, "dp", [(i, i ^ k) for i in range(n)])


def columns_of(index, width):
    return pl.ds(pl.multiple_of(index * width, LANES), width)


def turn_kernel(blocks, steps, cot_ref, out_ref, scratch):
    rows = blocks * steps
    for c in range(cot_ref.shape[-1] // LANES):
        cols = slice(c * LANES, (c + 1) * LANES)
        scratch[c * rows : (c + 1) * rows, :] = (
            cot_ref[:, :, cols].reshape(rows, LANES).astype(jnp.float32)
        )
        for t in range(steps):
            out_ref[t * blocks : (t + 1) * blocks, cols] = scratch[
                pl.ds(c * rows + t, blocks, stride=steps), :
            ].astype(jnp.bfloat16)


def pack_kernel(n, split, order_ref, info_ref, frames_ref, out_ref, held, sems):
    me = lax.axis_index("dp")
    classes = held.shape[0]
    coming = []
    for c in range(classes):
        source = frames_ref.at[:, c] if split else frames_ref.at[pl.ds(c, 1)]
        coming.append(pltpu.make_async_copy(source, held.at[c], sems.at[c]))
        coming[c].start()
    start = jnp.int32(0)
    for i in range(n - 1):
        start = start + jnp.where(i < me, info_ref[i, 0], 0)
    leaving = []
    for c in range(classes):
        target = order_ref[0, lax.rem(start + c, n)]
        leaving.append(
            pltpu.make_async_copy(held.at[c], out_ref.at[target], sems.at[classes + c])
        )
        coming[c].wait()
        leaving[c].start()
    for copy in leaving:
        copy.wait()


def unpack_kernel(
    n, cap, blocks, steps, order_ref, info_ref, got_ref, out_ref, landed, scratch, sems
):
    me = lax.axis_index("dp")
    residue = jnp.int32(0)
    for r in range(n):
        residue = residue + jnp.where(order_ref[0, r] == me, r, 0)
    starts, so_far = [], jnp.int32(0)
    for i in range(n):
        starts.append(so_far)
        so_far = so_far + info_ref[i, 0]
    length = got_ref.shape[1]
    copies, rows = [], []
    for m in range(blocks):
        g = residue + m * n
        source, start = jnp.int32(0), jnp.int32(0)
        for i in range(1, n):
            later = starts[i] <= g
            source = jnp.where(later, i, source)
            start = jnp.where(later, starts[i], start)
        h = g - start
        copy = pltpu.make_async_copy(
            got_ref.at[source * cap + lax.div(h, n)], landed.at[m], sems.at[m]
        )
        copy.start()
        copies.append(copy)
        rows.append(info_ref[source, 1 + h])
    height = lax.broadcasted_iota(jnp.int32, (blocks, out_ref.shape[1]), 0)
    counts = jnp.zeros((blocks, out_ref.shape[1]), jnp.int32)
    for m in range(blocks):
        counts = jnp.where(height == m, rows[m], counts)
    out_ref[steps * blocks :, :] = counts.astype(jnp.float32).astype(jnp.bfloat16)
    for m in range(blocks):
        copies[m].wait()
        scratch[m * length : (m + 1) * length, :] = landed[m].astype(jnp.float32)
    group = length // steps
    for t in range(steps):
        for j in range(group):
            out_ref[t * blocks : (t + 1) * blocks, j * LANES : (j + 1) * LANES] = scratch[
                pl.ds(group * t + j, blocks, stride=length), :
            ].astype(jnp.bfloat16)


def cut_kernel(width, w_ref, p1, p2, p3, held, sems):
    me = lax.axis_index("fsdp")
    half = p2.shape[0]
    part = pl.ds(pl.multiple_of(lax.rem(lax.axis_index("dp"), 2) * half, TILE), half)
    stops = [
        (w_ref.at[part, columns_of(me ^ 2, width)], held.at[0, :half], p2),
        (w_ref.at[part, columns_of(me ^ 3, width)], held.at[1, :half], p3),
        (w_ref.at[:, columns_of(me ^ 1, width)], held.at[2], p1),
    ]
    coming = [
        pltpu.make_async_copy(source, place, sems.at[i])
        for i, (source, place, _) in enumerate(stops)
    ]
    leaving = [
        pltpu.make_async_copy(place, target, sems.at[3 + i])
        for i, (_, place, target) in enumerate(stops)
    ]
    for copy in coming:
        copy.start()
    for first, second in zip(coming, leaving):
        first.wait()
        second.start()
    for copy in leaving:
        copy.wait()


def tree(terms, low, high):
    if high - low == 1:
        left, right = terms[low]
        return left * right
    middle = (low + high) // 2
    return tree(terms, low, middle) + tree(terms, middle, high)


def project(patches_ref, subs, rows):
    me = lax.axis_index("fsdp")
    depth = subs[0].shape[0]
    left = jnp.concatenate(
        [patches_ref[:rows, columns_of(me ^ k, depth)] for k in range(4)], axis=1
    )
    right = jnp.concatenate([piece[...] for piece in subs], axis=0)
    return dot(left, right, 1, 0)


def forward(steps, blocks, patches, subs, depth_ref, gain_ref, work, mask, outs):
    rows = steps * blocks
    feat_ref, normed_ref, slope_ref, rstd_ref = outs
    width, taps = depth_ref.shape[1], depth_ref.shape[0]
    span = (taps - 1) // 2
    groups = range(len(patches))
    for g in groups:
        work[g * rows : (g + 1) * rows, :] = project(patches[g], subs, rows)
        counts = patches[g][rows:, :LANES].astype(jnp.float32)
        for t in range(steps):
            spot = g * rows + t * blocks
            mask[spot : spot + blocks, :] = jnp.where(counts > t, 1.0, 0.0)

    def column(c, _):
        cols = pl.ds(pl.multiple_of(c * LANES, LANES), LANES)
        weights = [
            jnp.broadcast_to(depth_ref[k : k + 1, cols], (blocks, LANES)).astype(jnp.bfloat16)
            for k in range(taps)
        ]
        for g in groups:
            spots = [
                slice(g * rows + t * blocks, g * rows + (t + 1) * blocks) for t in range(steps)
            ]
            values = []
            for t in range(steps):
                rounded = (work[spots[t], cols] * mask[spots[t], :]).astype(jnp.bfloat16)
                feat_ref[spots[t], cols] = rounded
                values.append(rounded)
            for t in range(steps):
                terms = [
                    (values[s], weights[s - t + span])
                    for s in range(steps)
                    if 0 <= s - t + span < taps
                ]
                conv = tree(terms, 0, len(terms)).astype(jnp.float32)
                keep = mask[spots[t], :]
                sigma = sigmoid(conv)
                swish = conv * sigma
                slope_ref[spots[t], cols] = (keep * (sigma + swish * (1.0 - sigma))).astype(
                    jnp.bfloat16
                )
                work[spots[t], cols] = values[t].astype(jnp.float32) + keep * swish
        return 0

    lax.fori_loop(0, width // LANES, column, 0)

    def norm(i, _):
        at = pl.ds(pl.multiple_of(i * 32, 32), 32)
        values = work[at, :]
        centred = values - jnp.mean(values, axis=-1, keepdims=True)
        rstd = lax.rsqrt(jnp.mean(centred * centred, axis=-1, keepdims=True) + EPSILON)
        normed_ref[at, :] = (centred * rstd * gain_ref[...]).astype(jnp.bfloat16)
        rstd_ref[at, :] = jnp.broadcast_to(rstd, (32, LANES))
        return 0

    lax.fori_loop(0, len(patches) * rows // 32, norm, 0)


def own_kernel(steps, blocks, patches, s0, s1, s2, s3, depth, gain, o0, o1, o2, o3, work, mask):
    forward(
        steps, blocks, [patches], [s0, s1, s2, s3], depth, gain, work, mask, (o0, o1, o2, o3)
    )


def middle_kernel(steps, blocks, *refs):
    patches, subs, depth, gain = refs[0:4], refs[4:8], refs[8], refs[9]
    rstd0, normed0, cots, w_own, w1, w2, w3, w2b, w3b, w_out_in = (
        refs[10], refs[11], refs[12:16], *refs[16:23]
    )
    grad_in, g1, g2, g3, pre_out, hidden_out, masked_out, w_slice_out = refs[23:31]
    feat_out, normed_out, slope_out, means_out = refs[31:35]
    work, mask, feat, normed, slope, rstd, means = refs[35:42]
    masked, w_in, w_out, pre_grad, scaled, hidden, grads, sems = refs[42:50]
    me = lax.axis_index("fsdp")
    parity = lax.rem(lax.axis_index("dp"), 2)
    rows = steps * blocks
    high, wide = w_own.shape[0], w1.shape[1]
    half = high // 2
    used = iter(range(sems.shape[0]))

    def move(source, place):
        copy = pltpu.make_async_copy(source, place, sems.at[next(used)])
        copy.start()
        return copy

    def rows_of(index, part=0, size=high):
        return pl.ds(pl.multiple_of(index * high + part * half, TILE), size)

    def group(k):
        return slice(k * rows, (k + 1) * rows)

    coming = [
        move(normed0, normed.at[group(0), :]),
        move(w_own.at[:, columns_of(me, wide)], w_in.at[rows_of(me), :]),
        move(w1, w_in.at[rows_of(me ^ 1), :]),
        move(w2, w_in.at[rows_of(me ^ 2, parity, half), :]),
        move(w3, w_in.at[rows_of(me ^ 3, parity, half), :]),
        move(w2b, w_in.at[rows_of(me ^ 2, 1 - parity, half), :]),
        move(w3b, w_in.at[rows_of(me ^ 3, 1 - parity, half), :]),
        move(w_out_in, w_out),
    ] + [move(cots[k], masked.at[group(k), :]) for k in range(4)]
    tail = slice(rows, 4 * rows)
    forward(
        steps, blocks, patches[1:], subs, depth, gain, work, mask,
        (feat, normed.at[tail, :], slope, rstd),
    )
    leaving = [
        move(feat, feat_out),
        move(normed.at[tail, :], normed_out),
        move(slope, slope_out),
    ]
    for copy in coming:
        copy.wait()
    leaving.append(move(w_in, w_slice_out))
    fine = jnp.broadcast_to(gain[...], (TILE, gain.shape[1]))
    coarse = fine.astype(jnp.bfloat16)
    small = (fine - coarse.astype(jnp.float32)).astype(jnp.bfloat16)
    pulled = (dot(coarse, w_in[...], 1, 0) + dot(small, w_in[...], 1, 0))[:1, :]
    share = 1.0 / gain.shape[1]
    for k in range(4):
        counts = patches[k][rows:, :LANES].astype(jnp.float32)[:, :1]
        keep = jnp.concatenate([counts > t for t in range(steps)], axis=0)
        at = group(k)
        kept = jnp.where(keep, masked[at, :], jnp.zeros((), jnp.bfloat16))
        masked[at, :] = kept
        pre = dot(normed[at, :], w_in[...], 1, 0)
        back = dot(kept, w_out[...], 1, 1)
        sigma = sigmoid(pre)
        swish = pre * sigma
        hidden[at, :] = swish.astype(jnp.bfloat16)
        grown = 0.5 * back * (sigma + swish * (1.0 - sigma))
        pre_grad[at, :] = grown.astype(jnp.bfloat16)
        grown = grown * (rstd0[:, :1] if k == 0 else rstd[(k - 1) * rows : k * rows, :1])
        scaled[at, :] = grown.astype(jnp.bfloat16)
        for i, other in enumerate((pulled, pre)):
            mean = jnp.sum(grown * other, axis=-1, keepdims=True) * share
            means[i, at, :] = jnp.broadcast_to(mean, (rows, LANES)).astype(jnp.bfloat16)
    leaving.append(move(scaled, pre_out))
    leaving.append(move(means, means_out))
    for slot, (k, place) in enumerate(((2, g2), (3, g3), (1, g1), (0, None))):
        part = dot(normed[:, columns_of(me ^ k, high)], pre_grad[...], 0, 0)
        grads[slot] = part.astype(jnp.bfloat16)
        leaving.append(
            move(grads.at[slot], grad_in.at[:, columns_of(me, wide)] if k == 0 else place)
        )
    leaving.append(move(hidden, hidden_out))
    leaving.append(move(masked, masked_out))
    for copy in leaving:
        copy.wait()


def backward_kernel(steps, blocks, *refs):
    gain, sources, taps_out = refs[0], refs[1:11], refs[11]
    scaled, w_in, masked, normed, slope, feat, means = refs[12:19]
    grad, sems = refs[19:21]
    rows = steps * blocks
    first, rest = slice(0, rows), slice(rows, 4 * rows)
    origins = list(sources)
    origins[2] = origins[2].at[first, :]
    places = [
        scaled, w_in, masked, normed.at[first, :], slope.at[first, :], feat.at[first, :], means,
        normed.at[rest, :], slope.at[rest, :], feat.at[rest, :],
    ]
    copies = [
        pltpu.make_async_copy(source, place, sems.at[i])
        for i, (source, place) in enumerate(zip(origins, places))
    ]
    for copy in copies:
        copy.start()
    for copy in copies[:3]:
        copy.wait()
    for k in range(4):
        at = slice(k * rows, (k + 1) * rows)
        pulled = dot(scaled[at, :], w_in[...], 1, 1) * gain[...]
        if k == 0:
            pulled = pulled + masked[...].astype(jnp.float32)
        grad[at, :] = pulled.astype(jnp.bfloat16)
    for copy in copies[3:]:
        copy.wait()
    taps = 2 * steps - 1

    def column(c, _):
        cols = pl.ds(pl.multiple_of(c * LANES, LANES), LANES)

        inverse = jnp.broadcast_to(1.0 / gain[:, cols], (blocks, LANES)).astype(jnp.bfloat16)

        def add(k, totals):
            spots = [
                pl.ds(pl.multiple_of(k * rows + t * blocks, TILE), blocks) for t in range(steps)
            ]
            left = [
                slope[spot, cols]
                * (
                    grad[spot, cols]
                    - means[0, spot, :]
                    - normed[spot, cols] * inverse * means[1, spot, :]
                )
                for spot in spots
            ]
            right = [feat[spot, cols] for spot in spots]
            new = []
            for tap in range(taps):
                shift = tap - (steps - 1)
                terms = [
                    (left[t], right[t + shift]) for t in range(steps) if 0 <= t + shift < steps
                ]
                part = tree(terms, 0, len(terms)).astype(jnp.float32)
                for half in range(0, blocks, HALF):
                    piece = part[half : half + HALF, :]
                    total = piece if half == 0 else total + piece
                new.append(totals[tap] + total)
            return tuple(new)

        zero = jnp.zeros((HALF, LANES), jnp.float32)
        totals = lax.fori_loop(0, 4, add, (zero,) * taps)
        for tap in range(taps):
            taps_out[tap, :, cols] = jnp.sum(totals[tap], axis=0, keepdims=True)
        taps_out[taps, :, cols] = jnp.zeros((1, LANES), jnp.float32)
        return 0

    lax.fori_loop(0, gain.shape[1] // LANES, column, 0)


def out_kernel(hidden, masked, out_ref, turned):
    turned[...] = hidden[...].T
    width = out_ref.shape[1]
    for c in range(0, width, 256):
        out_ref[:, c : c + 256] = (0.5 * dot(turned[...], masked[:, c : c + 256], 1, 0)).astype(
            jnp.bfloat16
        )


def join_kernel(width, start_ref, p1, p2, p3, out_ref, sems):
    me = lax.axis_index("fsdp")
    copies = [
        pltpu.make_async_copy(piece, out_ref.at[:, columns_of(me ^ k, width)], sems.at[k])
        for k, piece in enumerate((p1, p2, p3), 1)
    ]
    for copy in copies:
        copy.start()
    for copy in copies:
        copy.wait()


def on_device(
    frames,
    occupied_slot_counts,
    block_frame_rows,
    order,
    cotangent,
    sub_weight,
    depth_kernel,
    norm_gain,
    w_in,
    w_out,
):
    n = lax.axis_size("dp")
    home = frames.shape[2]
    cap = (home + n - 1) // n
    split = home % n == 0
    blocks, steps, width = cotangent.shape[2:]
    rows = blocks * steps
    deep, hidden_width = w_in.shape
    wide = hidden_width // 4
    bf16, f32 = jnp.bfloat16, jnp.float32
    dma = pltpu.SemaphoreType.DMA

    info = jnp.concatenate([occupied_slot_counts[0], block_frame_rows[0, 0]])
    infos = lax.all_to_all(
        jnp.broadcast_to(info[None], (n, home + 1)), "dp", split_axis=0, concat_axis=0, tiled=True
    )

    subs = [sub_weight, across(sub_weight, 1), across(sub_weight, 2)]
    w1, w2, w3 = pl.pallas_call(
        functools.partial(cut_kernel, wide),
        out_shape=(
            sds((deep, wide), bf16),
            sds((deep // 2, wide), bf16),
            sds((deep // 2, wide), bf16),
        ),
        in_specs=[ANY],
        out_specs=(ANY,) * 3,
        scratch_shapes=[pltpu.VMEM((3, deep, wide), bf16), dma((6,))],
        compiler_params=params(),
        cost_estimate=CHEAP,
    )(w_in)
    w1, w2, w3 = across(w1, 1), across(w2, 2), across(w3, 3)

    cot0 = pl.pallas_call(
        functools.partial(turn_kernel, blocks, steps),
        out_shape=sds((rows, width), bf16),
        in_specs=[VMEM],
        out_specs=VMEM,
        scratch_shapes=[pltpu.VMEM((rows * width // LANES, LANES), f32)],
        compiler_params=params(),
        cost_estimate=CHEAP,
    )(cotangent[0, 0])
    cots = [cot0, across(cot0, 1), across(cot0, 2)]

    block_shape = frames.shape[3:]
    held = frames[0, 0].reshape((cap, n) + block_shape) if split else frames[0, 0]
    packed = pl.pallas_call(
        functools.partial(pack_kernel, n, split),
        out_shape=sds((n, cap) + block_shape, bf16),
        in_specs=[SMEM, SMEM, ANY],
        out_specs=ANY,
        scratch_shapes=[
            pltpu.VMEM((n if split else home, cap) + block_shape, bf16),
            dma((2 * (n if split else home),)),
        ],
        compiler_params=params(),
        cost_estimate=CHEAP,
    )(order, infos, held)
    gain = norm_gain.reshape(1, width)
    packed, w2, w3, gain = lax.optimization_barrier((packed, w2, w3, gain))
    w2b, w3b = across_dp(w2, 1), across_dp(w3, 1)
    got = lax.all_to_all(packed, "dp", split_axis=0, concat_axis=0, tiled=True)
    subs.append(across(subs[2], 1))
    got, subs[1], subs[2], subs[3] = lax.optimization_barrier((got, subs[1], subs[2], subs[3]))
    patches0 = pl.pallas_call(
        functools.partial(unpack_kernel, n, cap, blocks, steps),
        out_shape=sds((rows + blocks, block_shape[0] // steps * LANES), bf16),
        in_specs=[SMEM, SMEM, ANY],
        out_specs=VMEM,
        scratch_shapes=[
            pltpu.VMEM((blocks,) + block_shape, bf16),
            pltpu.VMEM((blocks * block_shape[0], LANES), f32),
            dma((blocks,)),
        ],
        compiler_params=params(),
        cost_estimate=CHEAP,
    )(order, infos, got.reshape((n * cap,) + block_shape))
    patches = [patches0, across(patches0, 1), across(patches0, 2)]
    patches.append(across(patches[2], 1))
    cots.append(across(cots[2], 1))

    def kept(count):
        return (
            sds((count * rows, width), bf16),
            sds((count * rows, width), bf16),
            sds((count * rows, width), bf16),
            sds((count * rows, LANES), f32),
        )

    feat0, normed0, slope0, rstd0 = pl.pallas_call(
        functools.partial(own_kernel, steps, blocks),
        out_shape=kept(1),
        in_specs=[VMEM] * 7,
        out_specs=(VMEM,) * 4,
        scratch_shapes=[pltpu.VMEM((rows, width), f32), pltpu.VMEM((rows, LANES), f32)],
        compiler_params=params(),
        cost_estimate=CHEAP,
    )(patches0, *subs, depth_kernel, gain)
    (
        grad_in, g1, g2, g3, scaled, hidden, masked, w_slice, feat, normed, slope, means
    ) = pl.pallas_call(
        functools.partial(middle_kernel, steps, blocks),
        out_shape=(
            sds((deep, hidden_width), bf16),
            *[sds((deep, wide), bf16)] * 3,
            sds((4 * rows, wide), bf16),
            sds((4 * rows, wide), bf16),
            sds((4 * rows, width), bf16),
            sds((width, wide), bf16),
            *kept(3)[:3],
            sds((2, 4 * rows, LANES), bf16),
        ),
        in_specs=[VMEM] * 11 + [ANY] * 12,
        out_specs=(ANY,) * 12,
        scratch_shapes=[
            pltpu.VMEM((3 * rows, width), f32),
            pltpu.VMEM((3 * rows, LANES), f32),
            pltpu.VMEM((3 * rows, width), bf16),
            pltpu.VMEM((4 * rows, width), bf16),
            pltpu.VMEM((3 * rows, width), bf16),
            pltpu.VMEM((3 * rows, LANES), f32),
            pltpu.VMEM((2, 4 * rows, LANES), bf16),
            pltpu.VMEM((4 * rows, width), bf16),
            pltpu.VMEM((width, wide), bf16),
            pltpu.VMEM((wide, width), bf16),
            pltpu.VMEM((4 * rows, wide), bf16),
            pltpu.VMEM((4 * rows, wide), bf16),
            pltpu.VMEM((4 * rows, wide), bf16),
            pltpu.VMEM((4, deep, wide), bf16),
            dma((32,)),
        ],
        compiler_params=params(),
        cost_estimate=CHEAP,
    )(
        *patches, *subs, depth_kernel, gain, rstd0, normed0, *cots, w_in, w1, w2, w3, w2b, w3b, w_out
    )
    g1, g2, g3 = across(g1, 1), across(g2, 2), across(g3, 3)

    taps = pl.pallas_call(
        functools.partial(backward_kernel, steps, blocks),
        out_shape=sds((2 * steps, 1, width), f32),
        in_specs=[VMEM] + [ANY] * 10,
        out_specs=VMEM,
        scratch_shapes=[
            pltpu.VMEM((4 * rows, wide), bf16),
            pltpu.VMEM((width, wide), bf16),
            pltpu.VMEM((rows, width), bf16),
            pltpu.VMEM((4 * rows, width), bf16),
            pltpu.VMEM((4 * rows, width), bf16),
            pltpu.VMEM((4 * rows, width), bf16),
            pltpu.VMEM((2, 4 * rows, LANES), bf16),
            pltpu.VMEM((4 * rows, width), bf16),
            dma((10,)),
        ],
        compiler_params=params(),
        cost_estimate=CHEAP,
    )(gain, scaled, w_slice, masked, normed0, slope0, feat0, means, normed, slope, feat)

    every = ("dp", "fsdp")
    devices = n * lax.axis_size("fsdp")
    shares = lax.all_to_all(
        taps.reshape(devices, 1, -1), every, split_axis=0, concat_axis=0, tiled=True
    )
    share = jnp.sum(shares, axis=0, keepdims=True) / rows
    whole = lax.all_to_all(
        jnp.broadcast_to(share, shares.shape), every, split_axis=0, concat_axis=0, tiled=True
    )
    kernel_grad = whole.reshape(2 * steps, width)[: depth_kernel.shape[0]]

    grad_out = pl.pallas_call(
        out_kernel,
        out_shape=sds((wide, width), bf16),
        in_specs=[VMEM] * 2,
        out_specs=VMEM,
        scratch_shapes=[pltpu.VMEM((wide, 4 * rows), bf16)],
        compiler_params=params(),
        cost_estimate=CHEAP,
    )(hidden, masked)
    grad_in = pl.pallas_call(
        functools.partial(join_kernel, wide),
        out_shape=sds((deep, hidden_width), bf16),
        in_specs=[ANY] + [VMEM] * 3,
        out_specs=ANY,
        scratch_shapes=[dma((4,))],
        input_output_aliases={0: 0},
        compiler_params=params(),
        cost_estimate=CHEAP,
    )(grad_in, g1, g2, g3)
    return (grad_in[None], grad_out[None], kernel_grad)


def solution(mesh):
    placed = (
        P("dp", "fsdp", None, None, None),
        P("fsdp", "dp"),
        P("dp", "fsdp", None),
        P("fsdp", None),
        P("dp", "fsdp", None, None, None),
        P("fsdp", None),
        P(),
        P(),
        P("fsdp", None),
        P("fsdp", None),
    )
    return jax.shard_map(
        on_device,
        mesh=mesh,
        in_specs=placed,
        out_specs=(P("dp", "fsdp", None), P("dp", "fsdp", None), P()),
        check_vma=False,
    )
```

time: 481 us -> 167 us (0.35)
  waiting for transfers between devices: 368 us -> 55.2 us
  Pallas kernels: 0 us -> 68.6 us
  matrix products: 35.5 us -> 0 us
  starting transfers between devices: 10.4 us -> 34.8 us
  other arithmetic: 20.8 us -> 0.21 us
  between operations: 15.4 us -> 1.57 us
  blocking collectives: 9.57 us -> 0 us
  local copies, waits for them, and re-layouts: 15.3 us -> 5.83 us
    reduce_scatter x2 -> x0, waiting for transfers between devices: 163 us -> none  [the longest x1 81.4 us: on_device(): lax.psum_scatter(contract(normed, pre_grad, 0, 0).astype(jnp.bfloat16), '...]
    psum x1 -> x0, waiting for transfers between devices: 107 us -> none  [on_device(): kernel_grad = lax.psum(kernel_part, ('dp', 'fsdp')) / row_total]
    all_gather x3 -> x0, waiting for transfers between devices: 78.5 us -> none  [the longest x1 57.6 us: on_device(): lax.all_gather(w_out, 'fsdp', axis=0, tiled=True)]
    pallas_call x0 -> x9, Pallas kernels: none -> 68.6 us  [the longest x1 24.9 us: on_device(): pl.pallas_call(functools.partial(middle_kernel, steps, blocks), out_shape...]
    ppermute x0 -> x17, waiting for transfers between devices: none -> 43.4 us  [the longest x15 36.2 us: across(): return lax.ppermute(value, 'fsdp', [(i, i ^ k) for i in range(n)])]
    dot_general x8 -> x0, matrix products: 35.5 us -> none  [the longest x4 24 us: contract(): lax.dot_general(left, right, (((left_dim,), (right_dim,)), ((), ())), pre...]
    ppermute x0 -> x17, starting transfers between devices: none -> 17.4 us  [the longest x15 15.5 us: across(): return lax.ppermute(value, 'fsdp', [(i, i ^ k) for i in range(n)])]
    unnamed x1 -> x0, blocking collectives: 9.57 us -> none
  transfers between devices with their start and end apart: 9 -> 21, of which waited for: 8 -> 7; matrix products, arithmetic and copies ran while one was open for 10% -> 1% of each run, Pallas kernels for 0% -> 15%
where the time goes in v1:
time: 167 us; the launch traced here: 166 us
  Pallas kernels  68.6 us (41%)
  waiting for transfers between devices  55.2 us (33%)
  starting transfers between devices  34.8 us (21%)
  local copies, waits for them, and re-layouts  5.83 us (3%)
    ppermute x15, waiting for transfers between devices, across(): return lax.ppermute(value, 'fsdp', [(i, i ^ k) for i in range(n)])  36.2 us
    pallas_call x1, Pallas kernels, on_device(): pl.pallas_call(functools.partial(middle_kernel, steps, blocks), out_shape...  24.9 us
    pallas_call x1, Pallas kernels, on_device(): pl.pallas_call(functools.partial(backward_kernel, steps, blocks), out_sha...  17.1 us
    ppermute x15, starting transfers between devices, across(): return lax.ppermute(value, 'fsdp', [(i, i ^ k) for i in range(n)])  15.5 us
    ppermute x2, waiting for transfers between devices, across_dp(): return lax.ppermute(value, 'dp', [(i, i ^ k) for i in range(n)])  7.21 us
    all_to_all x1, waiting for transfers between devices, on_device(): lax.all_to_all(taps.reshape(devices, 1, -1), every, split_axis=0, concat_...  7.12 us
    pallas_call x1, Pallas kernels, on_device(): pl.pallas_call(functools.partial(own_kernel, steps, blocks), out_shape=ke...  6.96 us
    pallas_call x1, Pallas kernels, on_device(): pl.pallas_call(out_kernel, out_shape=sds((wide, width), bf16), in_specs=[...  6.4 us
  transfers between devices with their start and end apart: 21, of which 7 were waited for; matrix products, arithmetic and copies ran while one was open for 1% of the time, Pallas kernels for 15%

profile of v1, /device:TPU:1, one launch (start us, length us, event | category | flops | bytes accessed | tf_op | source)
XLA Modules:
  0.0 166.2 jit_solution(6725680917628642326)
XLA Ops:
  0.7 2.1 %shard_map.122 = (bf16[384,768]{1,0:T(8,128)(2,1)}, bf16[192,768]{1,0:T(8,128)(2,1)}, bf16[192,768]{1,0:T(8,128)(2,1)}) custom-call(bf16[384,3072]{1,0:T(8,128)(2,1)} %refs_16_.1), custom_call_target="tpu_custom_call" | custom-call | tf_op jit(solution)/shard_map/pallas_call | solution.py:449
  2.8 2.1 %collective-permute-start = (bf16[192,768]{1,0:T(8,128)(2,1)}, bf16[192,768]{1,0:T(8,128)(2,1)S(1)}, u32[]{:S(2)}, u32[]{:S(2)}) collective-permute-start(bf16[192,768]{1,0:T(8,128)(2,1)} %get-tuple-element.30), channel_id=1, source_target_pairs={{0,2},{1,3},{2,0},{3,1},{4,6},{5,7},{6,4},{7,5},{8,10},{9,11},{10,... | collective-permute-start | bytes 884744 | tf_op jit(solution)/shard_map/ppermute | solution.py:41
  4.9 0.6 collective-permute-start.1
  6.2 0.1 pad_add_fusion
  6.3 0.6 broadcast_in_dim.8
  6.9 6.0 %all-to-all-start = ((s32[8,1,49]{2,1,0:T(1,128)}), s32[8,1,49]{2,1,0:T(1,128)S(1)}, u32[]{:S(2)}, u32[]{:S(2)}) async-start(s32[8,1,49]{2,1,0:T(1,128)} %broadcast_in_dim.8), calls=%async_computation | async-start | bytes 8192 | tf_op jit(solution)/shard_map/all_to_all | solution.py:444
  12.9 0.6 reshape.29.gain.refs_9_.refs_0_
  13.5 4.6 %all-to-all-done = s32[8,1,49]{2,1,0:T(1,128)S(1)} async-done(((s32[8,1,49]{2,1,0:T(1,128)}), s32[8,1,49]{2,1,0:T(1,128)S(1)}, u32[]{:S(2)}, u32[]{:S(2)}) %all-to-all-start) | async-done | bytes 1600 | tf_op jit(solution)/shard_map/all_to_all | solution.py:444
  18.1 0.6 copy-done.15
  18.7 2.9 %shard_map.121 = bf16[8,6,64,128]{3,2,1,0:T(8,128)(2,1)} custom-call(s32[1,8]{1,0:T(1,128)} %order_ref.3, s32[8,49]{1,0:T(8,128)} %bitcast.18, bf16[6,8,64,128]{3,2,1,0:T(8,128)(2,1)} %bitcast.15), custom_call_target="tpu_custom_call" | custom-call | tf_op jit(solution)/shard_map/pallas_call | solution.py:477
  21.6 3.6 %all-to-all-start.1 = ((bf16[8,6,64,128]{3,2,1,0:T(8,128)(2,1)}), bf16[8,6,64,128]{3,2,1,0:T(8,128)(2,1)S(1)}, u32[]{:S(2)}, u32[]{:S(2)}) async-start(bf16[8,6,64,128]{3,2,1,0:T(8,128)(2,1)} %shard_map.121), calls=%async_computation.1 | async-start | bytes 1572864 | tf_op jit(solution)/shard_map/all_to_all | solution.py:492
  25.2 2.6 %shard_map.125.refs_12_ = bf16[256,1536]{1,0:T(8,128)(2,1)} custom-call(bf16[16,16,1536]{2,1,0:T(8,128)(2,1)} %bitcast.16), custom_call_target="tpu_custom_call" | custom-call | tf_op jit(solution)/shard_map/pallas_call | solution.py:464
  27.8 1.2 collective-permute-start.9
  29.0 0.2 collective-permute-start.3
  29.3 1.9 %collective-permute-start.2 = (bf16[128,1536]{1,0:T(8,128)(2,1)S(1)}, bf16[128,1536]{1,0:T(8,128)(2,1)S(1)}, u32[]{:S(2)}, u32[]{:S(2)}) collective-permute-start(bf16[128,1536]{1,0:T(8,128)(2,1)S(1)} %copy-done.1), channel_id=1, source_target_pairs={{0,1},{1,0},{2,3},{3,2},{4,5},{5,4},{6,7},{7,6},{8,9},{9,8},{10,11... | collective-permute-start | bytes 1179656 | tf_op jit(solution)/shard_map/ppermute | solution.py:41
  31.2 23.0 %collective-permute-done.3.s2.refs_6_ = bf16[128,1536]{1,0:T(8,128)(2,1)S(1)} collective-permute-done((bf16[128,1536]{1,0:T(8,128)(2,1)S(1)}, bf16[128,1536]{1,0:T(8,128)(2,1)S(1)}, u32[]{:S(2)}, u32[]{:S(2)}) %collective-permute-start.3) | collective-permute-done | bytes 393248 | tf_op jit(solution)/shard_map/ppermute | solution.py:41
  54.2 2.2 %collective-permute-start.4 = (bf16[128,1536]{1,0:T(8,128)(2,1)S(1)}, bf16[128,1536]{1,0:T(8,128)(2,1)S(1)}, u32[]{:S(2)}, u32[]{:S(2)}) collective-permute-start(bf16[128,1536]{1,0:T(8,128)(2,1)S(1)} %collective-permute-done.3.s2.refs_6_), channel_id=1, source_target_pairs={{0,1},{1,0},{2,3},{3,2},{4,5},{5,4},{6,7},{7,6},{8,9},{9,8},{10,11... | collective-permute-start | bytes 1179656 | tf_op jit(solution)/shard_map/ppermute | solution.py:41
  56.4 1.4 collective-permute-start.12
  57.7 0.3 collective-permute-start.8
  58.0 0.2 collective-permute-start.10
  58.3 0.3 collective-permute-start.11
  58.6 0.5 collective-permute-start.13
  59.1 0.9 copy-done
  60.0 2.9 %shard_map.123.patches.refs_0_ = bf16[272,512]{1,0:T(8,128)(2,1)} custom-call(s32[1,8]{1,0:T(1,128)} %order_ref.3, s32[8,49]{1,0:T(8,128)} %bitcast.19, bf16[48,64,128]{2,1,0:T(8,128)(2,1)} %bitcast.12), custom_call_target="tpu_custom_call" | custom-call | tf_op jit(solution)/shard_map/pallas_call | solution.py:495
  62.9 2.2 %collective-permute-done.12.refs_20_ = bf16[192,768]{1,0:T(8,128)(2,1)} collective-permute-done((bf16[192,768]{1,0:T(8,128)(2,1)S(1)}, bf16[192,768]{1,0:T(8,128)(2,1)}, u32[]{:S(2)}, u32[]{:S(2)}) %collective-permute-start.12) | collective-permute-done | bytes 294944 | tf_op jit(solution)/shard_map/ppermute | solution.py:46
  65.1 1.2 collective-permute-start.6
  66.4 5.0 %collective-permute-done.13.refs_21_ = bf16[192,768]{1,0:T(8,128)(2,1)S(1)} collective-permute-done((bf16[192,768]{1,0:T(8,128)(2,1)}, bf16[192,768]{1,0:T(8,128)(2,1)S(1)}, u32[]{:S(2)}, u32[]{:S(2)}) %collective-permute-start.13) | collective-permute-done | bytes 294944 | tf_op jit(solution)/shard_map/ppermute | solution.py:46
  71.4 0.8 collective-permute-start.5
  72.1 0.2 collective-permute-done.6.refs_2_
  72.3 2.1 %collective-permute-start.7 = (bf16[272,512]{1,0:T(8,128)(2,1)S(1)}, bf16[272,512]{1,0:T(8,128)(2,1)S(1)}, u32[]{:S(2)}, u32[]{:S(2)}) collective-permute-start(bf16[272,512]{1,0:T(8,128)(2,1)S(1)} %collective-permute-done.6.refs_2_), channel_id=1, source_target_pairs={{0,1},{1,0},{2,3},{3,2},{4,5},{5,4},{6,7},{7,6},{8,9},{9,8},{10,11... | collective-permute-start | bytes 835592 | tf_op jit(solution)/shard_map/ppermute | solution.py:41
  74.4 7.0 %shard_map.124 = (bf16[256,1536]{1,0:T(8,128)(2,1)}, bf16[256,1536]{1,0:T(8,128)(2,1)}, bf16[256,1536]{1,0:T(8,128)(2,1)}, f32[256,128]{1,0:T(8,128)}) custom-call(bf16[272,512]{1,0:T(8,128)(2,1)} %shard_map.123.patches.refs_0_, bf16[128,1536]{1,0:T(8,128)(2,1)} %refs_4_.1, bf16[128,1536]{1,0:T(8,128)(2,1)} %copy-done.3, bf16[128,1536]{1,0:T(8,128)(2,1)} %copy-done.2, ...), custom_call_target="tpu_custom_call" | custom-call | tf_op jit(solution)/shard_map/pallas_call | solution.py:520
  81.5 0.7 copy-done.13
  82.1 0.1 copy-done.14
  82.3 24.9 %shard_map.126 = (bf16[384,3072]{1,0:T(8,128)(2,1)}, bf16[384,768]{1,0:T(8,128)(2,1)}, bf16[384,768]{1,0:T(8,128)(2,1)}, bf16[384,768]{1,0:T(8,128)(2,1)}, bf16[...) custom-call(bf16[272,512]{1,0:T(8,128)(2,1)} %shard_map.123.patches., ...), custom_call_target="tpu_custom_call" | custom-call | tf_op jit(solution)/shard_map/pallas_call | solution.py:531
  107.2 17.1 %shard_map.129 = f32[32,1,1536]{2,1,0:T(1,128)} custom-call(f32[1,1536]{1,0:T(1,128)} %reshape.29.gain.refs_9_.refs_0_, bf16[1024,768]{1,0:T(8,128)(2,1)} %get-tuple-element.49.refs_1_, bf16[1536,768]{1,0:T(8,128)(2,1)} %get-tuple-element.50.refs_2_, bf16[1024,1536]{1,0:T(8,128)(2,1)} %get-tuple-element.48.masked.refs_3_, ...), custom_call_target="tpu_custom_call" | custom-call | tf_op jit(solution)/shard_map/pallas_call | solution.py:569
  124.4 5.6 %all-to-all-start.2 = ((f32[32,1,1536]{2,1,0:T(1,128)}), f32[32,1,1536]{2,1,0:T(1,128)S(1)}, u32[]{:S(2)}, u32[]{:S(2)}) async-start(f32[32,1,1536]{2,1,0:T(1,128)} %shard_map.129), calls=%async_computation.2 | async-start | bytes 393216 | tf_op jit(solution)/shard_map/all_to_all | solution.py:591
  130.0 0.3 collective-permute-start.14
  130.3 1.5 collective-permute-start.15
  131.8 0.4 collective-permute-start.16
  132.2 7.1 %all-to-all-done.2 = f32[32,1,1536]{2,1,0:T(1,128)S(1)} async-done(((f32[32,1,1536]{2,1,0:T(1,128)}), f32[32,1,1536]{2,1,0:T(1,128)S(1)}, u32[]{:S(2)}, u32[]{:S(2)}) %all-to-all-start.2) | async-done | bytes 196640 | tf_op jit(solution)/shard_map/all_to_all | solution.py:591
  139.3 0.1 reduce_sum.9
  139.4 0.8 broadcast_in_dim.21
  140.2 2.3 %all-to-all-start.3 = ((f32[32,1,1536]{2,1,0:T(1,128)}), f32[32,1,1536]{2,1,0:T(1,128)S(1)}, u32[]{:S(2)}, u32[]{:S(2)}) async-start(f32[32,1,1536]{2,1,0:T(1,128)} %broadcast_in_dim.21), calls=%async_computation.3 | async-start | bytes 393216 | tf_op jit(solution)/shard_map/all_to_all | solution.py:595
  142.5 6.4 %shard_map.128 = bf16[768,1536]{1,0:T(8,128)(2,1)} custom-call(bf16[1024,768]{1,0:T(8,128)(2,1)} %get-tuple-element.47.hidden, bf16[1024,1536]{1,0:T(8,128)(2,1)} %get-tuple-element.48.masked.refs_3_), custom_call_target="tpu_custom_call" | custom-call | tf_op jit(solution)/shard_map/pallas_call | solution.py:600
  149.0 13.0 %collective-permute-done.16.p3 = bf16[384,768]{1,0:T(8,128)(2,1)S(1)} collective-permute-done((bf16[384,768]{1,0:T(8,128)(2,1)S(1)}, bf16[384,768]{1,0:T(8,128)(2,1)S(1)}, u32[]{:S(2)}, u32[]{:S(2)}) %collective-permute-start.16) | collective-permute-done | bytes 589856 | tf_op jit(solution)/shard_map/ppermute | solution.py:41
  162.0 0.8 copy-done.8
  162.8 2.7 %shard_map.127 = bf16[384,3072]{1,0:T(8,128)(2,1)} custom-call(bf16[384,3072]{1,0:T(8,128)(2,1)} %get-tuple-element.43.start_ref, bf16[384,768]{1,0:T(8,128)(2,1)} %copy-done.6, bf16[384,768]{1,0:T(8,128)(2,1)} %copy-done.7, bf16[384,768]{1,0:T(8,128)(2,1)} %copy-done.8), custom_call_target="tpu_custom_call", output_to_operand_aliasing={{}: (0, {})} | custom-call | tf_op jit(solution)/shard_map/pallas_call | solution.py:609
  165.5 0.7 copy.16
  (51 shorter events, 0.1 us)
Async XLA Ops:
  0.6 5.6 %copy-start.19 = (s32[1,1,48]{2,1,0:T(1,128)S(1)}, s32[1,1,48]{2,1,0:T(1,128)}, u32[]{:S(2)}) copy-start(s32[1,1,48]{2,1,0:T(1,128)} %param.12) | copy-start | bytes 580
  0.6 12.2 %copy-start.16 = (f32[1536]{0:T(1024)S(1)}, f32[1536]{0:T(1024)}, u32[]{:S(2)}) copy-start(f32[1536]{0:T(1024)} %param.17) | copy-start | bytes 18436
  2.8 18.8 %collective-permute-start = (bf16[192,768]{1,0:T(8,128)(2,1)}, bf16[192,768]{1,0:T(8,128)(2,1)S(1)}, u32[]{:S(2)}, u32[]{:S(2)}) collective-permute-start(bf16[192,768]{1,0:T(8,128)(2,1)} %get-tuple-element.30), channel_id=1, source_target_pairs={{0,2},{1,3},{2,0},{3,1},{4,6},{5,7},{6,4},{7,5},{8,10},{9,11},{10,... | collective-permute-start | bytes 884744 | tf_op jit(solution)/shard_map/ppermute | solution.py:41
  4.9 16.7 %collective-permute-start.1 = (bf16[192,768]{1,0:T(8,128)(2,1)}, bf16[192,768]{1,0:T(8,128)(2,1)S(1)}, u32[]{:S(2)}, u32[]{:S(2)}) collective-permute-start(bf16[192,768]{1,0:T(8,128)(2,1)} %get-tuple-element.31), channel_id=1, source_target_pairs={{0,3},{1,2},{2,1},{3,0},{4,7},{5,6},{6,5},{7,4},{8,11},{9,10},{10,... | collective-permute-start | bytes 884744 | tf_op jit(solution)/shard_map/ppermute | solution.py:41
  6.9 11.2 %all-to-all-start = ((s32[8,1,49]{2,1,0:T(1,128)}), s32[8,1,49]{2,1,0:T(1,128)S(1)}, u32[]{:S(2)}, u32[]{:S(2)}) async-start(s32[8,1,49]{2,1,0:T(1,128)} %broadcast_in_dim.8), calls=%async_computation | async-start | bytes 8192 | tf_op jit(solution)/shard_map/all_to_all | solution.py:444
  18.1 0.6 copy-start.15
  18.7 10.4 %copy-start.1 = (bf16[128,1536]{1,0:T(8,128)(2,1)S(1)}, bf16[128,1536]{1,0:T(8,128)(2,1)}, u32[]{:S(2)}) copy-start(bf16[128,1536]{1,0:T(8,128)(2,1)} %refs_4_.1) | copy-start | bytes 1179652
  21.6 59.8 %copy-start.9 = (bf16[192,768]{1,0:T(8,128)(2,1)}, bf16[192,768]{1,0:T(8,128)(2,1)S(1)}, u32[]{:S(2)}) copy-start(bf16[192,768]{1,0:T(8,128)(2,1)S(1)} %collective-permute-done.refs_18_) | copy-start | bytes 884740
  21.6 3.6 %copy-start.10 = (bf16[192,768]{1,0:T(8,128)(2,1)}, bf16[192,768]{1,0:T(8,128)(2,1)S(1)}, u32[]{:S(2)}) copy-start(bf16[192,768]{1,0:T(8,128)(2,1)S(1)} %collective-permute-done.1.refs_19_) | copy-start | bytes 884740
  21.6 37.5 %all-to-all-start.1 = ((bf16[8,6,64,128]{3,2,1,0:T(8,128)(2,1)}), bf16[8,6,64,128]{3,2,1,0:T(8,128)(2,1)S(1)}, u32[]{:S(2)}, u32[]{:S(2)}) async-start(bf16[8,6,64,128]{3,2,1,0:T(8,128)(2,1)} %shard_map.121), calls=%async_computation.1 | async-start | bytes 1572864 | tf_op jit(solution)/shard_map/all_to_all | solution.py:492
  27.8 30.2 %collective-permute-start.9 = (bf16[256,1536]{1,0:T(8,128)(2,1)}, bf16[256,1536]{1,0:T(8,128)(2,1)S(1)}, u32[]{:S(2)}, u32[]{:S(2)}) collective-permute-start(bf16[256,1536]{1,0:T(8,128)(2,1)} %shard_map.125.refs_12_), channel_id=1, source_target_pairs={{0,2},{1,3},{2,0},{3,1},{4,6},{5,7},{6,4},{7,5},{8,10},{9,11},{10,... | collective-permute-start | bytes 2359304 | tf_op jit(solution)/shard_map/ppermute | solution.py:41
  29.0 25.1 %collective-permute-start.3 = (bf16[128,1536]{1,0:T(8,128)(2,1)S(1)}, bf16[128,1536]{1,0:T(8,128)(2,1)S(1)}, u32[]{:S(2)}, u32[]{:S(2)}) collective-permute-start(bf16[128,1536]{1,0:T(8,128)(2,1)S(1)} %copy-done.1), channel_id=1, source_target_pairs={{0,2},{1,3},{2,0},{3,1},{4,6},{5,7},{6,4},{7,5},{8,10},{9,11},{10,... | collective-permute-start | bytes 1179656 | tf_op jit(solution)/shard_map/ppermute | solution.py:41
  29.3 29.0 %collective-permute-start.2 = (bf16[128,1536]{1,0:T(8,128)(2,1)S(1)}, bf16[128,1536]{1,0:T(8,128)(2,1)S(1)}, u32[]{:S(2)}, u32[]{:S(2)}) collective-permute-start(bf16[128,1536]{1,0:T(8,128)(2,1)S(1)} %copy-done.1), channel_id=1, source_target_pairs={{0,1},{1,0},{2,3},{3,2},{4,5},{5,4},{6,7},{7,6},{8,9},{9,8},{10,11... | collective-permute-start | bytes 1179656 | tf_op jit(solution)/shard_map/ppermute | solution.py:41
  54.2 20.3 %copy-start.2 = (bf16[128,1536]{1,0:T(8,128)(2,1)}, bf16[128,1536]{1,0:T(8,128)(2,1)S(1)}, u32[]{:S(2)}) copy-start(bf16[128,1536]{1,0:T(8,128)(2,1)S(1)} %collective-permute-done.3.s2.refs_6_) | copy-start | bytes 1179652
  54.2 4.4 %collective-permute-start.4 = (bf16[128,1536]{1,0:T(8,128)(2,1)S(1)}, bf16[128,1536]{1,0:T(8,128)(2,1)S(1)}, u32[]{:S(2)}, u32[]{:S(2)}) collective-permute-start(bf16[128,1536]{1,0:T(8,128)(2,1)S(1)} %collective-permute-done.3.s2.refs_6_), channel_id=1, source_target_pairs={{0,1},{1,0},{2,3},{3,2},{4,5},{5,4},{6,7},{7,6},{8,9},{9,8},{10,11... | collective-permute-start | bytes 1179656 | tf_op jit(solution)/shard_map/ppermute | solution.py:41
  56.4 8.7 %collective-permute-start.12 = (bf16[192,768]{1,0:T(8,128)(2,1)S(1)}, bf16[192,768]{1,0:T(8,128)(2,1)}, u32[]{:S(2)}, u32[]{:S(2)}) collective-permute-start(bf16[192,768]{1,0:T(8,128)(2,1)S(1)} %collective-permute-done.refs_18_), channel_id=1, source_target_pairs={{0,4},{4,0},{8,12},{12,8},{16,20},{20,16},{24,28},{28,24},{1,5},{5... | collective-permute-start | bytes 884744 | tf_op jit(solution)/shard_map/ppermute | solution.py:46
  57.7 23.7 %collective-permute-start.8 = (bf16[256,1536]{1,0:T(8,128)(2,1)}, bf16[256,1536]{1,0:T(8,128)(2,1)}, u32[]{:S(2)}, u32[]{:S(2)}) collective-permute-start(bf16[256,1536]{1,0:T(8,128)(2,1)} %shard_map.125.refs_12_), channel_id=1, source_target_pairs={{0,1},{1,0},{2,3},{3,2},{4,5},{5,4},{6,7},{7,6},{8,9},{9,8},{10,11... | collective-permute-start | bytes 2359304 | tf_op jit(solution)/shard_map/ppermute | solution.py:41
  58.0 23.4 %copy-start.5 = (bf16[256,1536]{1,0:T(8,128)(2,1)}, bf16[256,1536]{1,0:T(8,128)(2,1)S(1)}, u32[]{:S(2)}) copy-start(bf16[256,1536]{1,0:T(8,128)(2,1)S(1)} %collective-permute-done.9.refs_14_) | copy-start | bytes 2359300
  58.0 23.4 %collective-permute-start.10 = (bf16[256,1536]{1,0:T(8,128)(2,1)S(1)}, bf16[256,1536]{1,0:T(8,128)(2,1)}, u32[]{:S(2)}, u32[]{:S(2)}) collective-permute-start(bf16[256,1536]{1,0:T(8,128)(2,1)S(1)} %collective-permute-done.9.refs_14_), channel_id=1, source_target_pairs={{0,1},{1,0},{2,3},{3,2},{4,5},{5,4},{6,7},{7,6},{8,9},{9,8},{10,11... | collective-permute-start | bytes 2359304 | tf_op jit(solution)/shard_map/ppermute | solution.py:41
  58.3 16.2 %copy-start.3 = (bf16[128,1536]{1,0:T(8,128)(2,1)}, bf16[128,1536]{1,0:T(8,128)(2,1)S(1)}, u32[]{:S(2)}) copy-start(bf16[128,1536]{1,0:T(8,128)(2,1)S(1)} %collective-permute-done.2.s1.refs_5_) | copy-start | bytes 1179652
  58.3 23.1 %collective-permute-start.11 = (bf16[384,768]{1,0:T(8,128)(2,1)}, bf16[384,768]{1,0:T(8,128)(2,1)}, u32[]{:S(2)}, u32[]{:S(2)}) collective-permute-start(bf16[384,768]{1,0:T(8,128)(2,1)} %get-tuple-element.40), channel_id=1, source_target_pairs={{0,1},{1,0},{2,3},{3,2},{4,5},{5,4},{6,7},{7,6},{8,9},{9,8},{10,11... | collective-permute-start | bytes 1769480 | tf_op jit(solution)/shard_map/ppermute | solution.py:41
  58.6 15.9 %copy-start.4 = (bf16[128,1536]{1,0:T(8,128)(2,1)}, bf16[128,1536]{1,0:T(8,128)(2,1)S(1)}, u32[]{:S(2)}) copy-start(bf16[128,1536]{1,0:T(8,128)(2,1)S(1)} %collective-permute-done.4.s3.refs_7_) | copy-start | bytes 1179652
  58.6 12.8 %collective-permute-start.13 = (bf16[192,768]{1,0:T(8,128)(2,1)}, bf16[192,768]{1,0:T(8,128)(2,1)S(1)}, u32[]{:S(2)}, u32[]{:S(2)}) collective-permute-start(bf16[192,768]{1,0:T(8,128)(2,1)} %copy-done.10), channel_id=1, source_target_pairs={{0,4},{4,0},{8,12},{12,8},{16,20},{20,16},{24,28},{28,24},{1,5},{5... | collective-permute-start | bytes 884744 | tf_op jit(solution)/shard_map/ppermute | solution.py:46
  59.1 0.9 copy-start
  65.1 7.2 %collective-permute-start.6 = (bf16[272,512]{1,0:T(8,128)(2,1)}, bf16[272,512]{1,0:T(8,128)(2,1)S(1)}, u32[]{:S(2)}, u32[]{:S(2)}) collective-permute-start(bf16[272,512]{1,0:T(8,128)(2,1)} %shard_map.123.patches.refs_0_), channel_id=1, source_target_pairs={{0,2},{1,3},{2,0},{3,1},{4,6},{5,7},{6,4},{7,5},{8,10},{9,11},{10,... | collective-permute-start | bytes 835592 | tf_op jit(solution)/shard_map/ppermute | solution.py:41
  71.4 10.1 %copy-start.11 = (bf16[192,768]{1,0:T(8,128)(2,1)}, bf16[192,768]{1,0:T(8,128)(2,1)S(1)}, u32[]{:S(2)}) copy-start(bf16[192,768]{1,0:T(8,128)(2,1)S(1)} %collective-permute-done.13.refs_21_) | copy-start | bytes 884740
  71.4 10.1 %collective-permute-start.5 = (bf16[272,512]{1,0:T(8,128)(2,1)}, bf16[272,512]{1,0:T(8,128)(2,1)S(1)}, u32[]{:S(2)}, u32[]{:S(2)}) collective-permute-start(bf16[272,512]{1,0:T(8,128)(2,1)} %shard_map.123.patches.refs_0_), channel_id=1, source_target_pairs={{0,1},{1,0},{2,3},{3,2},{4,5},{5,4},{6,7},{7,6},{8,9},{9,8},{10,11... | collective-permute-start | bytes 835592 | tf_op jit(solution)/shard_map/ppermute | solution.py:41
  72.3 9.2 %copy-start.12 = (bf16[272,512]{1,0:T(8,128)(2,1)}, bf16[272,512]{1,0:T(8,128)(2,1)S(1)}, u32[]{:S(2)}) copy-start(bf16[272,512]{1,0:T(8,128)(2,1)S(1)} %collective-permute-done.6.refs_2_) | copy-start | bytes 835588
  72.3 9.1 %collective-permute-start.7 = (bf16[272,512]{1,0:T(8,128)(2,1)S(1)}, bf16[272,512]{1,0:T(8,128)(2,1)S(1)}, u32[]{:S(2)}, u32[]{:S(2)}) collective-permute-start(bf16[272,512]{1,0:T(8,128)(2,1)S(1)} %collective-permute-done.6.refs_2_), channel_id=1, source_target_pairs={{0,1},{1,0},{2,3},{3,2},{4,5},{5,4},{6,7},{7,6},{8,9},{9,8},{10,11... | collective-permute-start | bytes 835592 | tf_op jit(solution)/shard_map/ppermute | solution.py:41
  81.4 0.7 copy-start.13
  81.5 0.8 copy-start.14
  107.2 23.1 %copy-start.18 = (bf16[384,768]{1,0:T(8,128)(2,1)S(1)}, bf16[384,768]{1,0:T(8,128)(2,1)}, u32[]{:S(2)}) copy-start(bf16[384,768]{1,0:T(8,128)(2,1)} %get-tuple-element.45) | copy-start | bytes 1769476
  107.2 24.5 %copy-start.17 = (bf16[384,768]{1,0:T(8,128)(2,1)S(1)}, bf16[384,768]{1,0:T(8,128)(2,1)}, u32[]{:S(2)}) copy-start(bf16[384,768]{1,0:T(8,128)(2,1)} %get-tuple-element.46) | copy-start | bytes 1769476
  124.4 14.9 %all-to-all-start.2 = ((f32[32,1,1536]{2,1,0:T(1,128)}), f32[32,1,1536]{2,1,0:T(1,128)S(1)}, u32[]{:S(2)}, u32[]{:S(2)}) async-start(f32[32,1,1536]{2,1,0:T(1,128)} %shard_map.129), calls=%async_computation.2 | async-start | bytes 393216 | tf_op jit(solution)/shard_map/all_to_all | solution.py:591
  130.0 19.0 %collective-permute-start.14 = (bf16[384,768]{1,0:T(8,128)(2,1)}, bf16[384,768]{1,0:T(8,128)(2,1)S(1)}, u32[]{:S(2)}, u32[]{:S(2)}) collective-permute-start(bf16[384,768]{1,0:T(8,128)(2,1)} %get-tuple-element.44), channel_id=1, source_target_pairs={{0,1},{1,0},{2,3},{3,2},{4,5},{5,4},{6,7},{7,6},{8,9},{9,8},{10,11... | collective-permute-start | bytes 1769480 | tf_op jit(solution)/shard_map/ppermute | solution.py:41
  130.3 18.7 %collective-permute-start.15 = (bf16[384,768]{1,0:T(8,128)(2,1)S(1)}, bf16[384,768]{1,0:T(8,128)(2,1)S(1)}, u32[]{:S(2)}, u32[]{:S(2)}) collective-permute-start(bf16[384,768]{1,0:T(8,128)(2,1)S(1)} %copy-done.18), channel_id=1, source_target_pairs={{0,2},{1,3},{2,0},{3,1},{4,6},{5,7},{6,4},{7,5},{8,10},{9,11},{10,... | collective-permute-start | bytes 1769480 | tf_op jit(solution)/shard_map/ppermute | solution.py:41
  131.8 30.2 %collective-permute-start.16 = (bf16[384,768]{1,0:T(8,128)(2,1)S(1)}, bf16[384,768]{1,0:T(8,128)(2,1)S(1)}, u32[]{:S(2)}, u32[]{:S(2)}) collective-permute-start(bf16[384,768]{1,0:T(8,128)(2,1)S(1)} %copy-done.17), channel_id=1, source_target_pairs={{0,3},{1,2},{2,1},{3,0},{4,7},{5,6},{6,5},{7,4},{8,11},{9,10},{10,... | collective-permute-start | bytes 1769480 | tf_op jit(solution)/shard_map/ppermute | solution.py:41
  140.2 25.2 %all-to-all-start.3 = ((f32[32,1,1536]{2,1,0:T(1,128)}), f32[32,1,1536]{2,1,0:T(1,128)S(1)}, u32[]{:S(2)}, u32[]{:S(2)}) async-start(f32[32,1,1536]{2,1,0:T(1,128)} %broadcast_in_dim.21), calls=%async_computation.3 | async-start | bytes 393216 | tf_op jit(solution)/shard_map/all_to_all | solution.py:595
  148.9 13.0 %copy-start.6 = (bf16[384,768]{1,0:T(8,128)(2,1)}, bf16[384,768]{1,0:T(8,128)(2,1)S(1)}, u32[]{:S(2)}) copy-start(bf16[384,768]{1,0:T(8,128)(2,1)S(1)} %collective-permute-done.14.p1) | copy-start | bytes 1769476
  149.0 13.0 %copy-start.7 = (bf16[384,768]{1,0:T(8,128)(2,1)}, bf16[384,768]{1,0:T(8,128)(2,1)S(1)}, u32[]{:S(2)}) copy-start(bf16[384,768]{1,0:T(8,128)(2,1)S(1)} %collective-permute-done.15.p2) | copy-start | bytes 1769476
  162.0 0.8 copy-start.8

commit v2 on v1

--- a/solution.py
+++ b/solution.py
@@ -18,8 +18,12 @@
 CHEAP = pl.CostEstimate(flops=0, transcendentals=0, bytes_accessed=0)
 
 
-def params():
-    return pltpu.CompilerParams(vmem_limit_bytes=56 * 1024 * 1024)
+def params(mebibytes=16):
+    return pltpu.CompilerParams(vmem_limit_bytes=mebibytes * 1024 * 1024)
+
+
+def near(*arrays):
+    return [pltpu.with_memory_space_constraint(array, pltpu.VMEM) for array in arrays]
 
 
 def sds(shape, dtype):
@@ -129,29 +133,19 @@
             ].astype(jnp.bfloat16)
 
 
-def cut_kernel(width, w_ref, p1, p2, p3, held, sems):
+def cut_kernel(width, w_ref, p0, p1, p2, p3, sems):
     me = lax.axis_index("fsdp")
     half = p2.shape[0]
     part = pl.ds(pl.multiple_of(lax.rem(lax.axis_index("dp"), 2) * half, TILE), half)
-    stops = [
-        (w_ref.at[part, columns_of(me ^ 2, width)], held.at[0, :half], p2),
-        (w_ref.at[part, columns_of(me ^ 3, width)], held.at[1, :half], p3),
-        (w_ref.at[:, columns_of(me ^ 1, width)], held.at[2], p1),
+    copies = [
+        pltpu.make_async_copy(w_ref.at[part, columns_of(me ^ 2, width)], p2, sems.at[2]),
+        pltpu.make_async_copy(w_ref.at[part, columns_of(me ^ 3, width)], p3, sems.at[3]),
+        pltpu.make_async_copy(w_ref.at[:, columns_of(me ^ 1, width)], p1, sems.at[1]),
+        pltpu.make_async_copy(w_ref.at[:, columns_of(me, width)], p0, sems.at[0]),
     ]
-    coming = [
-        pltpu.make_async_copy(source, place, sems.at[i])
-        for i, (source, place, _) in enumerate(stops)
-    ]
-    leaving = [
-        pltpu.make_async_copy(place, target, sems.at[3 + i])
-        for i, (_, place, target) in enumerate(stops)
-    ]
-    for copy in coming:
+    for copy in copies:
         copy.start()
-    for first, second in zip(coming, leaving):
-        first.wait()
-        second.start()
-    for copy in leaving:
+    for copy in copies:
         copy.wait()
 
 
@@ -238,120 +232,69 @@
 
 
 def middle_kernel(steps, blocks, *refs):
-    patches, subs, depth, gain = refs[0:4], refs[4:8], refs[8], refs[9]
-    rstd0, normed0, cots, w_own, w1, w2, w3, w2b, w3b, w_out_in = (
-        refs[10], refs[11], refs[12:16], *refs[16:23]
-    )
-    grad_in, g1, g2, g3, pre_out, hidden_out, masked_out, w_slice_out = refs[23:31]
-    feat_out, normed_out, slope_out, means_out = refs[31:35]
-    work, mask, feat, normed, slope, rstd, means = refs[35:42]
-    masked, w_in, w_out, pre_grad, scaled, hidden, grads, sems = refs[42:50]
+    patches, subs, depth, gain, rstd0, normed0 = refs[0:4], refs[4:8], *refs[8:12]
+    cots, w_own, w1, w2, w3, w2b, w3b, w_out = refs[12:16], *refs[16:23]
+    grads, scaled, hidden, masked, w_in = refs[23:27], *refs[27:31]
+    feat, normed, slope, means = refs[31:35]
+    work, mask, rstd, pre_grad = refs[35:39]
     me = lax.axis_index("fsdp")
     parity = lax.rem(lax.axis_index("dp"), 2)
     rows = steps * blocks
-    high, wide = w_own.shape[0], w1.shape[1]
+    high, wide = w1.shape
     half = high // 2
-    used = iter(range(sems.shape[0]))
-
-    def move(source, place):
-        copy = pltpu.make_async_copy(source, place, sems.at[next(used)])
-        copy.start()
-        return copy
 
     def rows_of(index, part=0, size=high):
         return pl.ds(pl.multiple_of(index * high + part * half, TILE), size)
 
-    def group(k):
-        return slice(k * rows, (k + 1) * rows)
-
-    coming = [
-        move(normed0, normed.at[group(0), :]),
-        move(w_own.at[:, columns_of(me, wide)], w_in.at[rows_of(me), :]),
-        move(w1, w_in.at[rows_of(me ^ 1), :]),
-        move(w2, w_in.at[rows_of(me ^ 2, parity, half), :]),
-        move(w3, w_in.at[rows_of(me ^ 3, parity, half), :]),
-        move(w2b, w_in.at[rows_of(me ^ 2, 1 - parity, half), :]),
-        move(w3b, w_in.at[rows_of(me ^ 3, 1 - parity, half), :]),
-        move(w_out_in, w_out),
-    ] + [move(cots[k], masked.at[group(k), :]) for k in range(4)]
-    tail = slice(rows, 4 * rows)
+    w_in[rows_of(me), :] = w_own[...]
+    w_in[rows_of(me ^ 1), :] = w1[...]
+    w_in[rows_of(me ^ 2, parity, half), :] = w2[...]
+    w_in[rows_of(me ^ 3, parity, half), :] = w3[...]
+    w_in[rows_of(me ^ 2, 1 - parity, half), :] = w2b[...]
+    w_in[rows_of(me ^ 3, 1 - parity, half), :] = w3b[...]
     forward(
-        steps, blocks, patches[1:], subs, depth, gain, work, mask,
-        (feat, normed.at[tail, :], slope, rstd),
-    )
-    leaving = [
-        move(feat, feat_out),
-        move(normed.at[tail, :], normed_out),
-        move(slope, slope_out),
-    ]
-    for copy in coming:
-        copy.wait()
-    leaving.append(move(w_in, w_slice_out))
+        steps, blocks, patches[1:], subs, depth, gain, work, mask, (feat, normed, slope, rstd)
+    )
     fine = jnp.broadcast_to(gain[...], (TILE, gain.shape[1]))
     coarse = fine.astype(jnp.bfloat16)
     small = (fine - coarse.astype(jnp.float32)).astype(jnp.bfloat16)
     pulled = (dot(coarse, w_in[...], 1, 0) + dot(small, w_in[...], 1, 0))[:1, :]
     share = 1.0 / gain.shape[1]
     for k in range(4):
+        at = slice(k * rows, (k + 1) * rows)
+        tail = slice((k - 1) * rows, k * rows)
         counts = patches[k][rows:, :LANES].astype(jnp.float32)[:, :1]
         keep = jnp.concatenate([counts > t for t in range(steps)], axis=0)
-        at = group(k)
-        kept = jnp.where(keep, masked[at, :], jnp.zeros((), jnp.bfloat16))
+        kept = jnp.where(keep, cots[k][...], jnp.zeros((), jnp.bfloat16))
         masked[at, :] = kept
-        pre = dot(normed[at, :], w_in[...], 1, 0)
+        pre = dot(normed0[...] if k == 0 else normed[tail, :], w_in[...], 1, 0)
         back = dot(kept, w_out[...], 1, 1)
         sigma = sigmoid(pre)
         swish = pre * sigma
         hidden[at, :] = swish.astype(jnp.bfloat16)
         grown = 0.5 * back * (sigma + swish * (1.0 - sigma))
         pre_grad[at, :] = grown.astype(jnp.bfloat16)
-        grown = grown * (rstd0[:, :1] if k == 0 else rstd[(k - 1) * rows : k * rows, :1])
+        grown = grown * (rstd0[:, :1] if k == 0 else rstd[tail, :1])
         scaled[at, :] = grown.astype(jnp.bfloat16)
         for i, other in enumerate((pulled, pre)):
             mean = jnp.sum(grown * other, axis=-1, keepdims=True) * share
             means[i, at, :] = jnp.broadcast_to(mean, (rows, LANES)).astype(jnp.bfloat16)
-    leaving.append(move(scaled, pre_out))
-    leaving.append(move(means, means_out))
-    for slot, (k, place) in enumerate(((2, g2), (3, g3), (1, g1), (0, None))):
-        part = dot(normed[:, columns_of(me ^ k, high)], pre_grad[...], 0, 0)
-        grads[slot] = part.astype(jnp.bfloat16)
-        leaving.append(
-            move(grads.at[slot], grad_in.at[:, columns_of(me, wide)] if k == 0 else place)
-        )
-    leaving.append(move(hidden, hidden_out))
-    leaving.append(move(masked, masked_out))
-    for copy in leaving:
-        copy.wait()
+    for k in (2, 3, 1, 0):
+        cols = columns_of(me ^ k, high)
+        left = jnp.concatenate([normed0[:, cols], normed[:, cols]], axis=0)
+        grads[k][...] = dot(left, pre_grad[...], 0, 0).astype(jnp.bfloat16)
 
 
 def backward_kernel(steps, blocks, *refs):
-    gain, sources, taps_out = refs[0], refs[1:11], refs[11]
-    scaled, w_in, masked, normed, slope, feat, means = refs[12:19]
-    grad, sems = refs[19:21]
+    gain, scaled, w_in, masked, means, normed0, slope0, feat0, normed, slope, feat = refs[0:11]
+    taps_out, grad = refs[11:13]
     rows = steps * blocks
-    first, rest = slice(0, rows), slice(rows, 4 * rows)
-    origins = list(sources)
-    origins[2] = origins[2].at[first, :]
-    places = [
-        scaled, w_in, masked, normed.at[first, :], slope.at[first, :], feat.at[first, :], means,
-        normed.at[rest, :], slope.at[rest, :], feat.at[rest, :],
-    ]
-    copies = [
-        pltpu.make_async_copy(source, place, sems.at[i])
-        for i, (source, place) in enumerate(zip(origins, places))
-    ]
-    for copy in copies:
-        copy.start()
-    for copy in copies[:3]:
-        copy.wait()
     for k in range(4):
         at = slice(k * rows, (k + 1) * rows)
         pulled = dot(scaled[at, :], w_in[...], 1, 1) * gain[...]
         if k == 0:
-            pulled = pulled + masked[...].astype(jnp.float32)
+            pulled = pulled + masked[at, :].astype(jnp.float32)
         grad[at, :] = pulled.astype(jnp.bfloat16)
-    for copy in copies[3:]:
-        copy.wait()
     taps = 2 * steps - 1
 
     def column(c, _):
@@ -359,20 +302,23 @@
 
         inverse = jnp.broadcast_to(1.0 / gain[:, cols], (blocks, LANES)).astype(jnp.bfloat16)
 
-        def add(k, totals):
-            spots = [
-                pl.ds(pl.multiple_of(k * rows + t * blocks, TILE), blocks) for t in range(steps)
-            ]
+        def add(k, totals, held, near_normed, near_slope, near_feat):
+            def spots(group):
+                return [
+                    pl.ds(pl.multiple_of(group * rows + t * blocks, TILE), blocks)
+                    for t in range(steps)
+                ]
+
             left = [
-                slope[spot, cols]
+                near_slope[here, cols]
                 * (
                     grad[spot, cols]
                     - means[0, spot, :]
-                    - normed[spot, cols] * inverse * means[1, spot, :]
+                    - near_normed[here, cols] * inverse * means[1, spot, :]
                 )
-                for spot in spots
+                for spot, here in zip(spots(k), spots(held))
             ]
-            right = [feat[spot, cols] for spot in spots]
+            right = [near_feat[here, cols] for here in spots(held)]
             new = []
             for tap in range(taps):
                 shift = tap - (steps - 1)
@@ -387,7 +333,10 @@
             return tuple(new)
 
         zero = jnp.zeros((HALF, LANES), jnp.float32)
-        totals = lax.fori_loop(0, 4, add, (zero,) * taps)
+        totals = add(0, (zero,) * taps, 0, normed0, slope0, feat0)
+        totals = lax.fori_loop(
+            1, 4, lambda k, totals: add(k, totals, k - 1, normed, slope, feat), totals
+        )
         for tap in range(taps):
             taps_out[tap, :, cols] = jnp.sum(totals[tap], axis=0, keepdims=True)
         taps_out[taps, :, cols] = jnp.zeros((1, LANES), jnp.float32)
@@ -405,11 +354,11 @@
         )
 
 
-def join_kernel(width, start_ref, p1, p2, p3, out_ref, sems):
+def join_kernel(width, p0, p1, p2, p3, out_ref, sems):
     me = lax.axis_index("fsdp")
     copies = [
         pltpu.make_async_copy(piece, out_ref.at[:, columns_of(me ^ k, width)], sems.at[k])
-        for k, piece in enumerate((p1, p2, p3), 1)
+        for k, piece in enumerate((p0, p1, p2, p3))
     ]
     for copy in copies:
         copy.start()
@@ -446,16 +395,17 @@
     )
 
     subs = [sub_weight, across(sub_weight, 1), across(sub_weight, 2)]
-    w1, w2, w3 = pl.pallas_call(
+    w0, w1, w2, w3 = pl.pallas_call(
         functools.partial(cut_kernel, wide),
         out_shape=(
-            sds((deep, wide), bf16),
-            sds((deep // 2, wide), bf16),
-            sds((deep // 2, wide), bf16),
+            pltpu.VMEM((deep, wide), bf16),
+            pltpu.VMEM((deep, wide), bf16),
+            pltpu.VMEM((deep // 2, wide), bf16),
+            pltpu.VMEM((deep // 2, wide), bf16),
         ),
         in_specs=[ANY],
-        out_specs=(ANY,) * 3,
-        scratch_shapes=[pltpu.VMEM((3, deep, wide), bf16), dma((6,))],
+        out_specs=(VMEM,) * 4,
+        scratch_shapes=[dma((4,))],
         compiler_params=params(),
         cost_estimate=CHEAP,
     )(w_in)
@@ -487,11 +437,11 @@
         cost_estimate=CHEAP,
     )(order, infos, held)
     gain = norm_gain.reshape(1, width)
-    packed, w2, w3, gain = lax.optimization_barrier((packed, w2, w3, gain))
+    packed, w2, w3, subs[2], gain = lax.optimization_barrier((packed, w2, w3, subs[2], gain))
     w2b, w3b = across_dp(w2, 1), across_dp(w3, 1)
     got = lax.all_to_all(packed, "dp", split_axis=0, concat_axis=0, tiled=True)
     subs.append(across(subs[2], 1))
-    got, subs[1], subs[2], subs[3] = lax.optimization_barrier((got, subs[1], subs[2], subs[3]))
+    got, subs[1], subs[3] = lax.optimization_barrier((got, subs[1], subs[3]))
     patches0 = pl.pallas_call(
         functools.partial(unpack_kernel, n, cap, blocks, steps),
         out_shape=sds((rows + blocks, block_shape[0] // steps * LANES), bf16),
@@ -511,10 +461,10 @@
 
     def kept(count):
         return (
-            sds((count * rows, width), bf16),
-            sds((count * rows, width), bf16),
-            sds((count * rows, width), bf16),
-            sds((count * rows, LANES), f32),
+            pltpu.VMEM((count * rows, width), bf16),
+            pltpu.VMEM((count * rows, width), bf16),
+            pltpu.VMEM((count * rows, width), bf16),
+            pltpu.VMEM((count * rows, LANES), f32),
         )
 
     feat0, normed0, slope0, rstd0 = pl.pallas_call(
@@ -525,66 +475,52 @@
         scratch_shapes=[pltpu.VMEM((rows, width), f32), pltpu.VMEM((rows, LANES), f32)],
         compiler_params=params(),
         cost_estimate=CHEAP,
-    )(patches0, *subs, depth_kernel, gain)
+    )(*near(patches0, *subs, depth_kernel, gain))
     (
-        grad_in, g1, g2, g3, scaled, hidden, masked, w_slice, feat, normed, slope, means
+        g0, g1, g2, g3, scaled, hidden, masked, w_slice, feat, normed, slope, means
     ) = pl.pallas_call(
         functools.partial(middle_kernel, steps, blocks),
         out_shape=(
-            sds((deep, hidden_width), bf16),
-            *[sds((deep, wide), bf16)] * 3,
-            sds((4 * rows, wide), bf16),
-            sds((4 * rows, wide), bf16),
-            sds((4 * rows, width), bf16),
-            sds((width, wide), bf16),
+            *[pltpu.VMEM((deep, wide), bf16)] * 4,
+            pltpu.VMEM((4 * rows, wide), bf16),
+            pltpu.VMEM((4 * rows, wide), bf16),
+            pltpu.VMEM((4 * rows, width), bf16),
+            pltpu.VMEM((width, wide), bf16),
             *kept(3)[:3],
-            sds((2, 4 * rows, LANES), bf16),
+            pltpu.VMEM((2, 4 * rows, LANES), bf16),
         ),
-        in_specs=[VMEM] * 11 + [ANY] * 12,
-        out_specs=(ANY,) * 12,
+        in_specs=[VMEM] * 23,
+        out_specs=(VMEM,) * 12,
         scratch_shapes=[
             pltpu.VMEM((3 * rows, width), f32),
             pltpu.VMEM((3 * rows, LANES), f32),
-            pltpu.VMEM((3 * rows, width), bf16),
-            pltpu.VMEM((4 * rows, width), bf16),
-            pltpu.VMEM((3 * rows, width), bf16),
             pltpu.VMEM((3 * rows, LANES), f32),
-            pltpu.VMEM((2, 4 * rows, LANES), bf16),
-            pltpu.VMEM((4 * rows, width), bf16),
-            pltpu.VMEM((width, wide), bf16),
-            pltpu.VMEM((wide, width), bf16),
             pltpu.VMEM((4 * rows, wide), bf16),
-            pltpu.VMEM((4 * rows, wide), bf16),
-            pltpu.VMEM((4 * rows, wide), bf16),
-            pltpu.VMEM((4, deep, wide), bf16),
-            dma((32,)),
         ],
-        compiler_params=params(),
+        compiler_params=params(24),
         cost_estimate=CHEAP,
     )(
-        *patches, *subs, depth_kernel, gain, rstd0, normed0, *cots, w_in, w1, w2, w3, w2b, w3b, w_out
+        *near(
+            *patches, *subs, depth_kernel, gain, rstd0, normed0, *cots,
+            w0, w1, w2, w3, w2b, w3b, w_out,
+        )
     )
     g1, g2, g3 = across(g1, 1), across(g2, 2), across(g3, 3)
 
     taps = pl.pallas_call(
         functools.partial(backward_kernel, steps, blocks),
         out_shape=sds((2 * steps, 1, width), f32),
-        in_specs=[VMEM] + [ANY] * 10,
+        in_specs=[VMEM] * 11,
         out_specs=VMEM,
-        scratch_shapes=[
-            pltpu.VMEM((4 * rows, wide), bf16),
-            pltpu.VMEM((width, wide), bf16),
-            pltpu.VMEM((rows, width), bf16),
-            pltpu.VMEM((4 * rows, width), bf16),
-            pltpu.VMEM((4 * rows, width), bf16),
-            pltpu.VMEM((4 * rows, width), bf16),
-            pltpu.VMEM((2, 4 * rows, LANES), bf16),
-            pltpu.VMEM((4 * rows, width), bf16),
-            dma((10,)),
-        ],
-        compiler_params=params(),
-        cost_estimate=CHEAP,
-    )(gain, scaled, w_slice, masked, normed0, slope0, feat0, means, normed, slope, feat)
+        scratch_shapes=[pltpu.VMEM((4 * rows, width), bf16)],
+        compiler_params=params(),
+        cost_estimate=CHEAP,
+    )(
+        *near(
+            gain, scaled, w_slice, masked, means, normed0, slope0, feat0, normed, slope, feat
+        )
+    )
+    taps, g2, hidden = lax.optimization_barrier((taps, g2, hidden))
 
     every = ("dp", "fsdp")
     devices = n * lax.axis_size("fsdp")
@@ -605,17 +541,16 @@
         scratch_shapes=[pltpu.VMEM((wide, 4 * rows), bf16)],
         compiler_params=params(),
         cost_estimate=CHEAP,
-    )(hidden, masked)
+    )(*near(hidden, masked))
     grad_in = pl.pallas_call(
         functools.partial(join_kernel, wide),
         out_shape=sds((deep, hidden_width), bf16),
-        in_specs=[ANY] + [VMEM] * 3,
+        in_specs=[VMEM] * 4,
         out_specs=ANY,
         scratch_shapes=[dma((4,))],
-        input_output_aliases={0: 0},
-        compiler_params=params(),
-        cost_estimate=CHEAP,
-    )(grad_in, g1, g2, g3)
+        compiler_params=params(),
+        cost_estimate=CHEAP,
+    )(*near(g0, g1, g2, g3))
     return (grad_in[None], grad_out[None], kernel_grad)
 
 

time: 167 us -> 144 us (0.86)
  Pallas kernels: 68.6 us -> 51.3 us
  waiting for transfers between devices: 55.2 us -> 39.7 us
  local copies, waits for them, and re-layouts: 5.83 us -> 16.6 us
    ppermute x15, waiting for transfers between devices: 36.2 us -> 22.7 us  [across(): return lax.ppermute(value, 'fsdp', [(i, i ^ k) for i in range(n)])]
    unnamed x41 -> x67, local copies, waits for them, and re-layouts: 3.83 us -> 15.2 us
    pallas_call x1, Pallas kernels: 17.1 us -> 13.3 us  [on_device(): pl.pallas_call(functools.partial(backward_kernel, steps, blocks), out_sha...]
    ppermute x2, waiting for transfers between devices: 7.21 us -> 4.29 us  [across_dp(): return lax.ppermute(value, 'dp', [(i, i ^ k) for i in range(n)])]
    pallas_call x1, Pallas kernels: 6.96 us -> 4.22 us  [on_device(): pl.pallas_call(functools.partial(own_kernel, steps, blocks), out_shape=ke...]
    pallas_call x1, Pallas kernels: 6.4 us -> 4.03 us  [on_device(): pl.pallas_call(out_kernel, out_shape=sds((wide, width), bf16), in_specs=[...]
    all_to_all x1, starting transfers between devices: 3.56 us -> 5.75 us  [on_device(): got = lax.all_to_all(packed, 'dp', split_axis=0, concat_axis=0, tiled=True)]
    pallas_call x1, Pallas kernels: 24.9 us -> 22.7 us  [on_device(): pl.pallas_call(functools.partial(middle_kernel, steps, blocks), out_shape...]
  transfers between devices with their start and end apart: 21 -> 21, of which waited for: 7 -> 8; matrix products, arithmetic and copies ran while one was open for 1% -> 1% of each run, Pallas kernels for 15% -> 20%
where the time goes in v2:
time: 144 us
  Pallas kernels  51.3 us (36%)
  waiting for transfers between devices  39.7 us (28%)
  starting transfers between devices  34.2 us (24%)
  local copies, waits for them, and re-layouts  16.6 us (12%)
  between operations  1.62 us (1%)
    pallas_call x1, Pallas kernels, on_device(): pl.pallas_call(functools.partial(middle_kernel, steps, blocks), out_shape...  22.7 us
    ppermute x15, waiting for transfers between devices, across(): return lax.ppermute(value, 'fsdp', [(i, i ^ k) for i in range(n)])  22.7 us
    unnamed x67, local copies, waits for them, and re-layouts  15.2 us
    ppermute x15, starting transfers between devices, across(): return lax.ppermute(value, 'fsdp', [(i, i ^ k) for i in range(n)])  14 us
    pallas_call x1, Pallas kernels, on_device(): pl.pallas_call(functools.partial(backward_kernel, steps, blocks), out_sha...  13.3 us
    all_to_all x1, waiting for transfers between devices, on_device(): lax.all_to_all(taps.reshape(devices, 1, -1), every, split_axis=0, concat_...  7.47 us
    all_to_all x1, starting transfers between devices, on_device(): got = lax.all_to_all(packed, 'dp', split_axis=0, concat_axis=0, tiled=True)  5.75 us
    all_to_all x1, starting transfers between devices, on_device(): lax.all_to_all(jnp.broadcast_to(info[None], (n, home + 1)), 'dp', split_a...  5.53 us
  transfers between devices with their start and end apart: 21, of which 8 were waited for; matrix products, arithmetic and copies ran while one was open for 1% of the time, Pallas kernels for 20%

profile of v2, /device:TPU:1, one launch (start us, length us, event | category | flops | bytes accessed | tf_op | source)
XLA Modules:
  0.0 143.7 jit_solution(8529151175603231964)
XLA Ops:
  0.6 2.1 %collective-permute-start.2 = (bf16[128,1536]{1,0:T(8,128)(2,1)}, bf16[128,1536]{1,0:T(8,128)(2,1)S(1)}, u32[]{:S(2)}, u32[]{:S(2)}) collective-permute-start(bf16[128,1536]{1,0:T(8,128)(2,1)} %refs_4_.1), channel_id=1, source_target_pairs={{0,2},{1,3},{2,0},{3,1},{4,6},{5,7},{6,4},{7,5},{8,10},{9,11},{10,... | collective-permute-start | bytes 1179656 | tf_op jit(solution)/shard_map/ppermute | solution.py:45
  2.8 1.7 %copy-done.2 = bf16[384,3072]{1,0:T(8,128)(2,1)S(1)} copy-done((bf16[384,3072]{1,0:T(8,128)(2,1)S(1)}, bf16[384,3072]{1,0:T(8,128)(2,1)}, u32[]{:S(2)}) %copy-start.2) | copy-done | bytes 2359320
  4.7 0.8 copy-done.17
  5.5 0.8 copy-done.28
  6.3 1.8 %collective-permute-start.1 = (bf16[192,768]{1,0:T(8,128)(2,1)S(1)}, bf16[192,768]{1,0:T(8,128)(2,1)S(1)}, u32[]{:S(2)}, u32[]{:S(2)}) collective-permute-start(bf16[192,768]{1,0:T(8,128)(2,1)S(1)} %get-tuple-element.35), channel_id=1, source_target_pairs={{0,3},{1,2},{2,1},{3,0},{4,7},{5,6},{6,5},{7,4},{8,11},{9,10},{10,... | collective-permute-start | bytes 884744 | tf_op jit(solution)/shard_map/ppermute | solution.py:45
  8.8 0.6 broadcast_in_dim.8
  9.4 5.5 %all-to-all-start = ((s32[8,1,49]{2,1,0:T(1,128)}), s32[8,1,49]{2,1,0:T(1,128)S(1)}, u32[]{:S(2)}, u32[]{:S(2)}) async-start(s32[8,1,49]{2,1,0:T(1,128)} %broadcast_in_dim.8), calls=%async_computation | async-start | bytes 8192 | tf_op jit(solution)/shard_map/all_to_all | solution.py:393
  15.0 5.2 %all-to-all-done = s32[8,1,49]{2,1,0:T(1,128)S(1)} async-done(((s32[8,1,49]{2,1,0:T(1,128)}), s32[8,1,49]{2,1,0:T(1,128)S(1)}, u32[]{:S(2)}, u32[]{:S(2)}) %all-to-all-start) | async-done | bytes 1600 | tf_op jit(solution)/shard_map/all_to_all | solution.py:393
  20.2 1.8 %shard_map.121 = bf16[8,6,64,128]{3,2,1,0:T(8,128)(2,1)} custom-call(s32[1,8]{1,0:T(1,128)S(1)} %copy-done.27, s32[8,49]{1,0:T(8,128)S(1)} %bitcast.15, bf16[6,8,64,128]{3,2,1,0:T(8,128)(2,1)S(1)} %bitcast.13), custom_call_target="tpu_custom_call" | custom-call | tf_op jit(solution)/shard_map/pallas_call | solution.py:427
  22.1 2.9 %collective-permute-done.1.refs_19_ = bf16[192,768]{1,0:T(8,128)(2,1)S(1)} collective-permute-done((bf16[192,768]{1,0:T(8,128)(2,1)S(1)}, bf16[192,768]{1,0:T(8,128)(2,1)S(1)}, u32[]{:S(2)}, u32[]{:S(2)}) %collective-permute-start.1) | collective-permute-done | bytes 294944 | tf_op jit(solution)/shard_map/ppermute | solution.py:45
  25.0 5.8 %all-to-all-start.1 = ((bf16[8,6,64,128]{3,2,1,0:T(8,128)(2,1)}), bf16[8,6,64,128]{3,2,1,0:T(8,128)(2,1)S(1)}, u32[]{:S(2)}, u32[]{:S(2)}) async-start(bf16[8,6,64,128]{3,2,1,0:T(8,128)(2,1)} %shard_map.121), calls=%async_computation.1 | async-start | bytes 1572864 | tf_op jit(solution)/shard_map/all_to_all | solution.py:442
  30.8 1.1 copy-done.14
  31.9 0.6 shard_map.125.refs_12_
  32.5 1.3 collective-permute-start.9
  33.9 0.4 collective-permute-start.4
  34.4 0.4 collective-permute-start.8
  34.8 17.0 %collective-permute-done.9.refs_14_ = bf16[256,1536]{1,0:T(8,128)(2,1)} collective-permute-done((bf16[256,1536]{1,0:T(8,128)(2,1)S(1)}, bf16[256,1536]{1,0:T(8,128)(2,1)}, u32[]{:S(2)}, u32[]{:S(2)}) %collective-permute-start.9) | collective-permute-done | bytes 786464 | tf_op jit(solution)/shard_map/ppermute | solution.py:45
  51.9 0.8 collective-permute-start.10
  52.6 1.5 %collective-permute-start.12 = (bf16[192,768]{1,0:T(8,128)(2,1)}, bf16[192,768]{1,0:T(8,128)(2,1)}, u32[]{:S(2)}, u32[]{:S(2)}) collective-permute-start(bf16[192,768]{1,0:T(8,128)(2,1)} %copy-done.23), channel_id=1, source_target_pairs={{0,4},{4,0},{8,12},{12,8},{16,20},{20,16},{24,28},{28,24},{1,5},{5... | collective-permute-start | bytes 884744 | tf_op jit(solution)/shard_map/ppermute | solution.py:50
  54.1 1.7 %shard_map.123.patches.refs_0_ = bf16[272,512]{1,0:T(8,128)(2,1)S(1)} custom-call(s32[1,8]{1,0:T(1,128)S(1)} %copy-done.27, s32[8,49]{1,0:T(8,128)S(1)} %bitcast.16, bf16[48,64,128]{2,1,0:T(8,128)(2,1)S(1)} %bitcast.12), custom_call_target="tpu_custom_call" | custom-call | tf_op jit(solution)/shard_map/pallas_call | solution.py:445
  55.9 1.3 collective-permute-start.6
  57.2 4.3 %collective-permute-done.12.refs_20_ = bf16[192,768]{1,0:T(8,128)(2,1)} collective-permute-done((bf16[192,768]{1,0:T(8,128)(2,1)}, bf16[192,768]{1,0:T(8,128)(2,1)}, u32[]{:S(2)}, u32[]{:S(2)}) %collective-permute-start.12) | collective-permute-done | bytes 294944 | tf_op jit(solution)/shard_map/ppermute | solution.py:50
  61.5 1.3 collective-permute-start.5
  62.9 1.0 collective-permute-done.6.refs_2_
  63.8 1.2 collective-permute-start.7
  65.0 4.2 %shard_map.124 = (bf16[256,1536]{1,0:T(8,128)(2,1)S(1)}, bf16[256,1536]{1,0:T(8,128)(2,1)S(1)}, bf16[256,1536]{1,0:T(8,128)(2,1)S(1)}, f32[256,128]{1,0:T(8,128)S(1)}) custom-call(bf16[272,512]{1,0:T(8,128)(2,1)S(1)} %shard_map.123.patches.refs_0_, bf16[128,1536]{1,0:T(8,128)(2,1)S(1)} %copy-done.4, bf16[128,1536]{1,0:T(8,128)(2,1)S(1)} %collective-permute-done.3.s1.refs_5_, ...), custom_call_target="tpu_custom_call" | custom-call | tf_op jit(solution)/shard_map/pallas_call | solution.py:470
  69.4 1.1 copy-done.1
  70.5 1.0 copy-done.6
  71.5 1.0 copy-done.8
  72.5 1.0 copy-done.10
  73.5 0.9 copy-done.16
  74.4 1.0 copy-done.24
  75.4 1.0 copy-done.26
  76.3 22.7 %shard_map.126 = (bf16[384,768]{1,0:T(8,128)(2,1)S(1)}, bf16[384,768]{1,0:T(8,128)(2,1)S(1)}, bf16[384,768]{1,0:T(8,128)(2,1)S(1)}, bf16[384,768]{1,0:T(8,128)(2...) custom-call(bf16[272,512]{1,0:T(8,128)(2,1)S(1)} %shard_map.123.patc, ...), custom_call_target="tpu_custom_call" | custom-call | tf_op jit(solution)/shard_map/pallas_call | solution.py:481
  99.1 0.8 copy-done.30
  99.9 1.3 collective-permute-start.15
  101.2 13.3 %shard_map.127 = f32[32,1,1536]{2,1,0:T(1,128)} custom-call(f32[1,1536]{1,0:T(1,128)S(1)} %reshape.29.gain.refs_9_.refs_0_, bf16[1024,768]{1,0:T(8,128)(2,1)S(1)} %get-tuple-element.50.refs_1_, bf16[1536,768]{1,0:T(8,128)(2,1)S(1)} %get-tuple-element.51.refs_2_, bf16[1024,1536]{1,0:T(8,128)(2,1)S(1)} %get-tuple-element.52.refs_3_.masked, ...), custom_call_target="tpu_custom_call" | custom-call | tf_op jit(solution)/shard_map/pallas_call | solution.py:510
  114.9 0.8 copy-done.21
  115.7 5.1 %all-to-all-start.2 = ((f32[32,1,1536]{2,1,0:T(1,128)}), f32[32,1,1536]{2,1,0:T(1,128)S(1)}, u32[]{:S(2)}, u32[]{:S(2)}) async-start(f32[32,1,1536]{2,1,0:T(1,128)} %shard_map.127), calls=%async_computation.2 | async-start | bytes 393216 | tf_op jit(solution)/shard_map/all_to_all | solution.py:527
  121.2 1.5 %collective-permute-start.16 = (bf16[384,768]{1,0:T(8,128)(2,1)}, bf16[384,768]{1,0:T(8,128)(2,1)}, u32[]{:S(2)}, u32[]{:S(2)}) collective-permute-start(bf16[384,768]{1,0:T(8,128)(2,1)} %copy-done.29), channel_id=1, source_target_pairs={{0,3},{1,2},{2,1},{3,0},{4,7},{5,6},{6,5},{7,4},{8,11},{9,10},{10,... | collective-permute-start | bytes 1769480 | tf_op jit(solution)/shard_map/ppermute | solution.py:45
  122.7 7.5 %all-to-all-done.2 = f32[32,1,1536]{2,1,0:T(1,128)S(1)} async-done(((f32[32,1,1536]{2,1,0:T(1,128)}), f32[32,1,1536]{2,1,0:T(1,128)S(1)}, u32[]{:S(2)}, u32[]{:S(2)}) %all-to-all-start.2) | async-done | bytes 196640 | tf_op jit(solution)/shard_map/all_to_all | solution.py:527
  130.3 0.8 broadcast_in_dim.21
  131.1 2.3 %all-to-all-start.3 = ((f32[32,1,1536]{2,1,0:T(1,128)}), f32[32,1,1536]{2,1,0:T(1,128)S(1)}, u32[]{:S(2)}, u32[]{:S(2)}) async-start(f32[32,1,1536]{2,1,0:T(1,128)} %broadcast_in_dim.21), calls=%async_computation.3 | async-start | bytes 393216 | tf_op jit(solution)/shard_map/all_to_all | solution.py:531
  133.4 1.4 copy-done.12
  134.8 4.0 %shard_map.129 = bf16[768,1536]{1,0:T(8,128)(2,1)} custom-call(bf16[1024,768]{1,0:T(8,128)(2,1)S(1)} %copy-done.12, bf16[1024,1536]{1,0:T(8,128)(2,1)S(1)} %get-tuple-element.52.refs_3_.masked), custom_call_target="tpu_custom_call" | custom-call | tf_op jit(solution)/shard_map/pallas_call | solution.py:536
  138.9 1.4 collective-permute-done.16.p3
  140.3 2.7 %shard_map.128 = bf16[384,3072]{1,0:T(8,128)(2,1)} custom-call(bf16[384,768]{1,0:T(8,128)(2,1)S(1)} %copy-done.20, bf16[384,768]{1,0:T(8,128)(2,1)} %collective-permute-done.14.p1, bf16[384,768]{1,0:T(8,128)(2,1)S(1)} %copy-done.22, bf16[384,768]{1,0:T(8,128)(2,1)} %collective-permute-done.16.p3), custom_call_target="tpu_custom_call" | custom-call | tf_op jit(solution)/shard_map/pallas_call | solution.py:545
  143.0 0.7 copy.15
  (77 shorter events, 1.5 us)
Async XLA Ops:
  0.6 24.4 %collective-permute-start.2 = (bf16[128,1536]{1,0:T(8,128)(2,1)}, bf16[128,1536]{1,0:T(8,128)(2,1)S(1)}, u32[]{:S(2)}, u32[]{:S(2)}) collective-permute-start(bf16[128,1536]{1,0:T(8,128)(2,1)} %refs_4_.1), channel_id=1, source_target_pairs={{0,2},{1,3},{2,0},{3,1},{4,6},{5,7},{6,4},{7,5},{8,10},{9,11},{10,... | collective-permute-start | bytes 1179656 | tf_op jit(solution)/shard_map/ppermute | solution.py:45
  2.8 1.7 %copy-start.2 = (bf16[384,3072]{1,0:T(8,128)(2,1)S(1)}, bf16[384,3072]{1,0:T(8,128)(2,1)}, u32[]{:S(2)}) copy-start(bf16[384,3072]{1,0:T(8,128)(2,1)} %w_ref.1) | copy-start | bytes 7077892
  4.4 4.3 %copy-start.32 = (s32[1,1,48]{2,1,0:T(1,128)S(1)}, s32[1,1,48]{2,1,0:T(1,128)}, u32[]{:S(2)}) copy-start(s32[1,1,48]{2,1,0:T(1,128)} %param.12) | copy-start | bytes 580
  4.4 10.5 %copy-start.31 = (f32[1536]{0:T(1024)S(1)}, f32[1536]{0:T(1024)}, u32[]{:S(2)}) copy-start(f32[1536]{0:T(1024)} %param.17) | copy-start | bytes 18436
  4.4 15.8 %copy-start.13 = (bf16[1,1,48,64,128]{4,3,2,1,0:T(8,128)(2,1)S(1)}, bf16[1,1,48,64,128]{4,3,2,1,0:T(8,128)(2,1)}, u32[]{:S(2)}) copy-start(bf16[1,1,48,64,128]{4,3,2,1,0:T(8,128)(2,1)} %param.10) | copy-start | bytes 2359300
  4.4 15.8 %copy-start.27 = (s32[1,8]{1,0:T(1,128)S(1)}, s32[1,8]{1,0:T(1,128)}, u32[]{:S(2)}) copy-start(s32[1,8]{1,0:T(1,128)} %order_ref.3) | copy-start | bytes 100
  5.5 16.6 %collective-permute-start = (bf16[192,768]{1,0:T(8,128)(2,1)S(1)}, bf16[192,768]{1,0:T(8,128)(2,1)S(1)}, u32[]{:S(2)}, u32[]{:S(2)}) collective-permute-start(bf16[192,768]{1,0:T(8,128)(2,1)S(1)} %get-tuple-element.34), channel_id=1, source_target_pairs={{0,2},{1,3},{2,0},{3,1},{4,6},{5,7},{6,4},{7,5},{8,10},{9,11},{10,... | collective-permute-start | bytes 884744 | tf_op jit(solution)/shard_map/ppermute | solution.py:45
  6.3 18.7 %collective-permute-start.1 = (bf16[192,768]{1,0:T(8,128)(2,1)S(1)}, bf16[192,768]{1,0:T(8,128)(2,1)S(1)}, u32[]{:S(2)}, u32[]{:S(2)}) collective-permute-start(bf16[192,768]{1,0:T(8,128)(2,1)S(1)} %get-tuple-element.35), channel_id=1, source_target_pairs={{0,3},{1,2},{2,1},{3,0},{4,7},{5,6},{6,5},{7,4},{8,11},{9,10},{10,... | collective-permute-start | bytes 884744 | tf_op jit(solution)/shard_map/ppermute | solution.py:45
  9.4 10.8 %all-to-all-start = ((s32[8,1,49]{2,1,0:T(1,128)}), s32[8,1,49]{2,1,0:T(1,128)S(1)}, u32[]{:S(2)}, u32[]{:S(2)}) async-start(s32[8,1,49]{2,1,0:T(1,128)} %broadcast_in_dim.8), calls=%async_computation | async-start | bytes 8192 | tf_op jit(solution)/shard_map/all_to_all | solution.py:393
  20.2 13.6 %copy-start.4 = (bf16[128,1536]{1,0:T(8,128)(2,1)S(1)}, bf16[128,1536]{1,0:T(8,128)(2,1)}, u32[]{:S(2)}) copy-start(bf16[128,1536]{1,0:T(8,128)(2,1)} %refs_4_.1) | copy-start | bytes 1179652
  22.0 43.0 %copy-start.15 = (f32[31,1536]{1,0:T(8,128)S(1)}, f32[31,1536]{1,0:T(8,128)}, u32[]{:S(2)}) copy-start(f32[31,1536]{1,0:T(8,128)} %refs_8_.1) | copy-start | bytes 571396
  22.1 8.7 %copy-start.23 = (bf16[192,768]{1,0:T(8,128)(2,1)}, bf16[192,768]{1,0:T(8,128)(2,1)S(1)}, u32[]{:S(2)}) copy-start(bf16[192,768]{1,0:T(8,128)(2,1)S(1)} %collective-permute-done.refs_18_) | copy-start | bytes 884740
  25.0 5.8 %copy-start.25 = (bf16[192,768]{1,0:T(8,128)(2,1)}, bf16[192,768]{1,0:T(8,128)(2,1)S(1)}, u32[]{:S(2)}) copy-start(bf16[192,768]{1,0:T(8,128)(2,1)S(1)} %collective-permute-done.1.refs_19_) | copy-start | bytes 884740
  25.0 44.2 %copy-start.5 = (bf16[128,1536]{1,0:T(8,128)(2,1)}, bf16[128,1536]{1,0:T(8,128)(2,1)S(1)}, u32[]{:S(2)}) copy-start(bf16[128,1536]{1,0:T(8,128)(2,1)S(1)} %collective-permute-done.2.s2.refs_6_) | copy-start | bytes 1179652
  25.0 29.1 %all-to-all-start.1 = ((bf16[8,6,64,128]{3,2,1,0:T(8,128)(2,1)}), bf16[8,6,64,128]{3,2,1,0:T(8,128)(2,1)S(1)}, u32[]{:S(2)}, u32[]{:S(2)}) async-start(bf16[8,6,64,128]{3,2,1,0:T(8,128)(2,1)} %shard_map.121), calls=%async_computation.1 | async-start | bytes 1572864 | tf_op jit(solution)/shard_map/all_to_all | solution.py:442
  30.8 1.1 copy-start.14
  32.5 36.8 %copy-start = (bf16[256,1536]{1,0:T(8,128)(2,1)}, bf16[256,1536]{1,0:T(8,128)(2,1)S(1)}, u32[]{:S(2)}) copy-start(bf16[256,1536]{1,0:T(8,128)(2,1)S(1)} %shard_map.125.refs_12_) | copy-start | bytes 2359300
  32.5 19.3 %collective-permute-start.9 = (bf16[256,1536]{1,0:T(8,128)(2,1)S(1)}, bf16[256,1536]{1,0:T(8,128)(2,1)}, u32[]{:S(2)}, u32[]{:S(2)}) collective-permute-start(bf16[256,1536]{1,0:T(8,128)(2,1)S(1)} %shard_map.125.refs_12_), channel_id=1, source_target_pairs={{0,2},{1,3},{2,0},{3,1},{4,6},{5,7},{6,4},{7,5},{8,10},{9,11},{10,... | collective-permute-start | bytes 2359304 | tf_op jit(solution)/shard_map/ppermute | solution.py:45
  33.8 18.8 %collective-permute-start.3 = (bf16[128,1536]{1,0:T(8,128)(2,1)S(1)}, bf16[128,1536]{1,0:T(8,128)(2,1)S(1)}, u32[]{:S(2)}, u32[]{:S(2)}) collective-permute-start(bf16[128,1536]{1,0:T(8,128)(2,1)S(1)} %copy-done.4), channel_id=1, source_target_pairs={{0,1},{1,0},{2,3},{3,2},{4,5},{5,4},{6,7},{7,6},{8,9},{9,8},{10,11... | collective-permute-start | bytes 1179656 | tf_op jit(solution)/shard_map/ppermute | solution.py:45
  33.9 20.2 %collective-permute-start.4 = (bf16[128,1536]{1,0:T(8,128)(2,1)S(1)}, bf16[128,1536]{1,0:T(8,128)(2,1)S(1)}, u32[]{:S(2)}, u32[]{:S(2)}) collective-permute-start(bf16[128,1536]{1,0:T(8,128)(2,1)S(1)} %collective-permute-done.2.s2.refs_6_), channel_id=1, source_target_pairs={{0,1},{1,0},{2,3},{3,2},{4,5},{5,4},{6,7},{7,6},{8,9},{9,8},{10,11... | collective-permute-start | bytes 1179656 | tf_op jit(solution)/shard_map/ppermute | solution.py:45
  34.3 22.9 %collective-permute-start.11 = (bf16[384,768]{1,0:T(8,128)(2,1)}, bf16[384,768]{1,0:T(8,128)(2,1)}, u32[]{:S(2)}, u32[]{:S(2)}) collective-permute-start(bf16[384,768]{1,0:T(8,128)(2,1)} %copy-done.28), channel_id=1, source_target_pairs={{0,1},{1,0},{2,3},{3,2},{4,5},{5,4},{6,7},{7,6},{8,9},{9,8},{10,11... | collective-permute-start | bytes 1769480 | tf_op jit(solution)/shard_map/ppermute | solution.py:45
  34.4 34.8 %collective-permute-start.8 = (bf16[256,1536]{1,0:T(8,128)(2,1)S(1)}, bf16[256,1536]{1,0:T(8,128)(2,1)}, u32[]{:S(2)}, u32[]{:S(2)}) collective-permute-start(bf16[256,1536]{1,0:T(8,128)(2,1)S(1)} %shard_map.125.refs_12_), channel_id=1, source_target_pairs={{0,1},{1,0},{2,3},{3,2},{4,5},{5,4},{6,7},{7,6},{8,9},{9,8},{10,11... | collective-permute-start | bytes 2359304 | tf_op jit(solution)/shard_map/ppermute | solution.py:45
  51.9 17.4 %collective-permute-start.10 = (bf16[256,1536]{1,0:T(8,128)(2,1)}, bf16[256,1536]{1,0:T(8,128)(2,1)}, u32[]{:S(2)}, u32[]{:S(2)}) collective-permute-start(bf16[256,1536]{1,0:T(8,128)(2,1)} %collective-permute-done.9.refs_14_), channel_id=1, source_target_pairs={{0,1},{1,0},{2,3},{3,2},{4,5},{5,4},{6,7},{7,6},{8,9},{9,8},{10,11... | collective-permute-start | bytes 2359304 | tf_op jit(solution)/shard_map/ppermute | solution.py:45
  52.6 16.7 %copy-start.7 = (bf16[128,1536]{1,0:T(8,128)(2,1)}, bf16[128,1536]{1,0:T(8,128)(2,1)S(1)}, u32[]{:S(2)}) copy-start(bf16[128,1536]{1,0:T(8,128)(2,1)S(1)} %collective-permute-done.3.s1.refs_5_) | copy-start | bytes 1179652
  52.6 8.9 %collective-permute-start.12 = (bf16[192,768]{1,0:T(8,128)(2,1)}, bf16[192,768]{1,0:T(8,128)(2,1)}, u32[]{:S(2)}, u32[]{:S(2)}) collective-permute-start(bf16[192,768]{1,0:T(8,128)(2,1)} %copy-done.23), channel_id=1, source_target_pairs={{0,4},{4,0},{8,12},{12,8},{16,20},{20,16},{24,28},{28,24},{1,5},{5... | collective-permute-start | bytes 884744 | tf_op jit(solution)/shard_map/ppermute | solution.py:50
  54.1 15.2 %copy-start.9 = (bf16[128,1536]{1,0:T(8,128)(2,1)}, bf16[128,1536]{1,0:T(8,128)(2,1)S(1)}, u32[]{:S(2)}) copy-start(bf16[128,1536]{1,0:T(8,128)(2,1)S(1)} %collective-permute-done.4.s3.refs_7_) | copy-start | bytes 1179652
  54.1 15.2 %copy-start.3 = (bf16[768,1536]{1,0:T(8,128)(2,1)S(1)}, bf16[768,1536]{1,0:T(8,128)(2,1)}, u32[]{:S(2)}) copy-start(bf16[768,1536]{1,0:T(8,128)(2,1)} %refs_22_.1) | copy-start | bytes 7077892
  54.1 15.2 %copy-start.18 = (bf16[384,768]{1,0:T(8,128)(2,1)S(1)}, bf16[384,768]{1,0:T(8,128)(2,1)}, u32[]{:S(2)}) copy-start(bf16[384,768]{1,0:T(8,128)(2,1)} %copy-done.17) | copy-start | bytes 1769476
  55.9 8.0 %collective-permute-start.6 = (bf16[272,512]{1,0:T(8,128)(2,1)S(1)}, bf16[272,512]{1,0:T(8,128)(2,1)S(1)}, u32[]{:S(2)}, u32[]{:S(2)}) collective-permute-start(bf16[272,512]{1,0:T(8,128)(2,1)S(1)} %shard_map.123.patches.refs_0_), channel_id=1, source_target_pairs={{0,2},{1,3},{2,0},{3,1},{4,6},{5,7},{6,4},{7,5},{8,10},{9,11},{10,... | collective-permute-start | bytes 835592 | tf_op jit(solution)/shard_map/ppermute | solution.py:45
  57.2 12.1 %collective-permute-start.13 = (bf16[192,768]{1,0:T(8,128)(2,1)}, bf16[192,768]{1,0:T(8,128)(2,1)S(1)}, u32[]{:S(2)}, u32[]{:S(2)}) collective-permute-start(bf16[192,768]{1,0:T(8,128)(2,1)} %copy-done.25), channel_id=1, source_target_pairs={{0,4},{4,0},{8,12},{12,8},{16,20},{20,16},{24,28},{28,24},{1,5},{5... | collective-permute-start | bytes 884744 | tf_op jit(solution)/shard_map/ppermute | solution.py:50
  61.5 7.8 %collective-permute-start.5 = (bf16[272,512]{1,0:T(8,128)(2,1)S(1)}, bf16[272,512]{1,0:T(8,128)(2,1)S(1)}, u32[]{:S(2)}, u32[]{:S(2)}) collective-permute-start(bf16[272,512]{1,0:T(8,128)(2,1)S(1)} %shard_map.123.patches.refs_0_), channel_id=1, source_target_pairs={{0,1},{1,0},{2,3},{3,2},{4,5},{5,4},{6,7},{7,6},{8,9},{9,8},{10,11... | collective-permute-start | bytes 835592 | tf_op jit(solution)/shard_map/ppermute | solution.py:45
  63.8 5.5 %collective-permute-start.7 = (bf16[272,512]{1,0:T(8,128)(2,1)S(1)}, bf16[272,512]{1,0:T(8,128)(2,1)S(1)}, u32[]{:S(2)}, u32[]{:S(2)}) collective-permute-start(bf16[272,512]{1,0:T(8,128)(2,1)S(1)} %collective-permute-done.6.refs_2_), channel_id=1, source_target_pairs={{0,1},{1,0},{2,3},{3,2},{4,5},{5,4},{6,7},{7,6},{8,9},{9,8},{10,11... | collective-permute-start | bytes 835592 | tf_op jit(solution)/shard_map/ppermute | solution.py:45
  69.4 1.1 copy-start.1
  70.5 1.0 copy-start.6
  71.5 1.0 copy-start.8
  72.5 1.0 copy-start.10
  74.4 1.0 copy-start.24
  99.9 14.6 %copy-start.11 = (bf16[1024,768]{1,0:T(8,128)(2,1)}, bf16[1024,768]{1,0:T(8,128)(2,1)S(1)}, u32[]{:S(2)}) copy-start(bf16[1024,768]{1,0:T(8,128)(2,1)S(1)} %get-tuple-element.63.hidden) | copy-start | bytes 4718596
  99.9 14.6 %copy-start.19 = (bf16[384,768]{1,0:T(8,128)(2,1)}, bf16[384,768]{1,0:T(8,128)(2,1)S(1)}, u32[]{:S(2)}) copy-start(bf16[384,768]{1,0:T(8,128)(2,1)S(1)} %get-tuple-element.48.p0) | copy-start | bytes 1769476
  99.9 14.6 %copy-start.29 = (bf16[384,768]{1,0:T(8,128)(2,1)}, bf16[384,768]{1,0:T(8,128)(2,1)S(1)}, u32[]{:S(2)}) copy-start(bf16[384,768]{1,0:T(8,128)(2,1)S(1)} %get-tuple-element.62) | copy-start | bytes 1769476
  99.9 15.0 %collective-permute-start.15 = (bf16[384,768]{1,0:T(8,128)(2,1)S(1)}, bf16[384,768]{1,0:T(8,128)(2,1)S(1)}, u32[]{:S(2)}, u32[]{:S(2)}) collective-permute-start(bf16[384,768]{1,0:T(8,128)(2,1)S(1)} %get-tuple-element.59), channel_id=1, source_target_pairs={{0,2},{1,3},{2,0},{3,1},{4,6},{5,7},{6,4},{7,5},{8,10},{9,11},{10,... | collective-permute-start | bytes 1769480 | tf_op jit(solution)/shard_map/ppermute | solution.py:45
  115.7 14.5 %all-to-all-start.2 = ((f32[32,1,1536]{2,1,0:T(1,128)}), f32[32,1,1536]{2,1,0:T(1,128)S(1)}, u32[]{:S(2)}, u32[]{:S(2)}) async-start(f32[32,1,1536]{2,1,0:T(1,128)} %shard_map.127), calls=%async_computation.2 | async-start | bytes 393216 | tf_op jit(solution)/shard_map/all_to_all | solution.py:527
  120.8 18.0 %collective-permute-start.14 = (bf16[384,768]{1,0:T(8,128)(2,1)}, bf16[384,768]{1,0:T(8,128)(2,1)}, u32[]{:S(2)}, u32[]{:S(2)}) collective-permute-start(bf16[384,768]{1,0:T(8,128)(2,1)} %copy-done.30), channel_id=1, source_target_pairs={{0,1},{1,0},{2,3},{3,2},{4,5},{5,4},{6,7},{7,6},{8,9},{9,8},{10,11... | collective-permute-start | bytes 1769480 | tf_op jit(solution)/shard_map/ppermute | solution.py:45
  121.2 19.1 %collective-permute-start.16 = (bf16[384,768]{1,0:T(8,128)(2,1)}, bf16[384,768]{1,0:T(8,128)(2,1)}, u32[]{:S(2)}, u32[]{:S(2)}) collective-permute-start(bf16[384,768]{1,0:T(8,128)(2,1)} %copy-done.29), channel_id=1, source_target_pairs={{0,3},{1,2},{2,1},{3,0},{4,7},{5,6},{6,5},{7,4},{8,11},{9,10},{10,... | collective-permute-start | bytes 1769480 | tf_op jit(solution)/shard_map/ppermute | solution.py:45
  131.1 11.8 %all-to-all-start.3 = ((f32[32,1,1536]{2,1,0:T(1,128)}), f32[32,1,1536]{2,1,0:T(1,128)S(1)}, u32[]{:S(2)}, u32[]{:S(2)}) async-start(f32[32,1,1536]{2,1,0:T(1,128)} %broadcast_in_dim.21), calls=%async_computation.3 | async-start | bytes 393216 | tf_op jit(solution)/shard_map/all_to_all | solution.py:531
  133.4 1.4 copy-start.12
  134.8 5.4 %copy-start.20 = (bf16[384,768]{1,0:T(8,128)(2,1)S(1)}, bf16[384,768]{1,0:T(8,128)(2,1)}, u32[]{:S(2)}) copy-start(bf16[384,768]{1,0:T(8,128)(2,1)} %copy-done.19) | copy-start | bytes 1769476
  134.8 5.4 %copy-start.22 = (bf16[384,768]{1,0:T(8,128)(2,1)S(1)}, bf16[384,768]{1,0:T(8,128)(2,1)}, u32[]{:S(2)}) copy-start(bf16[384,768]{1,0:T(8,128)(2,1)} %copy-done.21) | copy-start | bytes 1769476
  (6 other events, 5.2 us)

commit v3 on v2

--- a/solution.py
+++ b/solution.py
@@ -15,11 +15,16 @@
 VMEM = pl.BlockSpec(memory_space=pltpu.VMEM)
 SMEM = pl.BlockSpec(memory_space=pltpu.SMEM)
 ANY = pl.BlockSpec(memory_space=pl.ANY)
-CHEAP = pl.CostEstimate(flops=0, transcendentals=0, bytes_accessed=0)
 
 
 def params(mebibytes=16):
     return pltpu.CompilerParams(vmem_limit_bytes=mebibytes * 1024 * 1024)
+
+
+def cost(microseconds):
+    return pl.CostEstimate(
+        flops=0, transcendentals=0, bytes_accessed=int(microseconds * 3.6e6)
+    )
 
 
 def near(*arrays):
@@ -54,17 +59,32 @@
     return pl.ds(pl.multiple_of(index * width, LANES), width)
 
 
-def turn_kernel(blocks, steps, cot_ref, out_ref, scratch):
+def prepare_kernel(blocks, steps, width, cot_ref, w_ref, out_ref, pair_ref, scratch, sems):
     rows = blocks * steps
+    half = pair_ref.shape[0] - rows
+    cols = columns_of(lax.axis_index("fsdp") ^ 1, width)
+    copies = [
+        pltpu.make_async_copy(
+            w_ref.at[i * half : (i + 1) * half, cols],
+            pair_ref.at[rows:, i * width : (i + 1) * width],
+            sems.at[i],
+        )
+        for i in range(2)
+    ]
+    for copy in copies:
+        copy.start()
     for c in range(cot_ref.shape[-1] // LANES):
         cols = slice(c * LANES, (c + 1) * LANES)
         scratch[c * rows : (c + 1) * rows, :] = (
             cot_ref[:, :, cols].reshape(rows, LANES).astype(jnp.float32)
         )
         for t in range(steps):
-            out_ref[t * blocks : (t + 1) * blocks, cols] = scratch[
-                pl.ds(c * rows + t, blocks, stride=steps), :
-            ].astype(jnp.bfloat16)
+            at = slice(t * blocks, (t + 1) * blocks)
+            turned = scratch[pl.ds(c * rows + t, blocks, stride=steps), :].astype(jnp.bfloat16)
+            out_ref[at, cols] = turned
+            pair_ref[at, cols] = turned
+    for copy in copies:
+        copy.wait()
 
 
 def pack_kernel(n, split, order_ref, info_ref, frames_ref, out_ref, held, sems):
@@ -133,19 +153,24 @@
             ].astype(jnp.bfloat16)
 
 
-def cut_kernel(width, w_ref, p0, p1, p2, p3, sems):
+def cut_kernel(width, w_ref, p2, p3, held, sems):
     me = lax.axis_index("fsdp")
     half = p2.shape[0]
     part = pl.ds(pl.multiple_of(lax.rem(lax.axis_index("dp"), 2) * half, TILE), half)
-    copies = [
-        pltpu.make_async_copy(w_ref.at[part, columns_of(me ^ 2, width)], p2, sems.at[2]),
-        pltpu.make_async_copy(w_ref.at[part, columns_of(me ^ 3, width)], p3, sems.at[3]),
-        pltpu.make_async_copy(w_ref.at[:, columns_of(me ^ 1, width)], p1, sems.at[1]),
-        pltpu.make_async_copy(w_ref.at[:, columns_of(me, width)], p0, sems.at[0]),
+    coming = [
+        pltpu.make_async_copy(w_ref.at[part, columns_of(me ^ k, width)], held.at[i], sems.at[0, i])
+        for i, k in enumerate((2, 3))
     ]
-    for copy in copies:
+    leaving = [
+        pltpu.make_async_copy(held.at[i], target, sems.at[1, i])
+        for i, target in enumerate((p2, p3))
+    ]
+    for copy in coming:
         copy.start()
-    for copy in copies:
+    for first, second in zip(coming, leaving):
+        first.wait()
+        second.start()
+    for copy in leaving:
         copy.wait()
 
 
@@ -157,24 +182,14 @@
     return tree(terms, low, middle) + tree(terms, middle, high)
 
 
-def project(patches_ref, subs, rows):
-    me = lax.axis_index("fsdp")
-    depth = subs[0].shape[0]
-    left = jnp.concatenate(
-        [patches_ref[:rows, columns_of(me ^ k, depth)] for k in range(4)], axis=1
-    )
-    right = jnp.concatenate([piece[...] for piece in subs], axis=0)
-    return dot(left, right, 1, 0)
-
-
-def forward(steps, blocks, patches, subs, depth_ref, gain_ref, work, mask, outs):
+def forward(steps, blocks, patches, sub_ref, depth_ref, gain_ref, work, mask, outs):
     rows = steps * blocks
     feat_ref, normed_ref, slope_ref, rstd_ref = outs
     width, taps = depth_ref.shape[1], depth_ref.shape[0]
     span = (taps - 1) // 2
     groups = range(len(patches))
     for g in groups:
-        work[g * rows : (g + 1) * rows, :] = project(patches[g], subs, rows)
+        work[g * rows : (g + 1) * rows, :] = dot(patches[g][:rows, :], sub_ref[...], 1, 0)
         counts = patches[g][rows:, :LANES].astype(jnp.float32)
         for t in range(steps):
             spot = g * rows + t * blocks
@@ -225,36 +240,50 @@
     lax.fori_loop(0, len(patches) * rows // 32, norm, 0)
 
 
-def own_kernel(steps, blocks, patches, s0, s1, s2, s3, depth, gain, o0, o1, o2, o3, work, mask):
-    forward(
-        steps, blocks, [patches], [s0, s1, s2, s3], depth, gain, work, mask, (o0, o1, o2, o3)
-    )
+def own_kernel(steps, blocks, patches, weight, depth, gain, o0, o1, o2, o3, work, mask):
+    forward(steps, blocks, [patches], weight, depth, gain, work, mask, (o0, o1, o2, o3))
 
 
 def middle_kernel(steps, blocks, *refs):
-    patches, subs, depth, gain, rstd0, normed0 = refs[0:4], refs[4:8], *refs[8:12]
-    cots, w_own, w1, w2, w3, w2b, w3b, w_out = refs[12:16], *refs[16:23]
-    grads, scaled, hidden, masked, w_in = refs[23:27], *refs[27:31]
-    feat, normed, slope, means = refs[31:35]
-    work, mask, rstd, pre_grad = refs[35:39]
+    patches, weight, depth, gain, rstd0, normed0 = refs[0:4], *refs[4:9]
+    cot0, pair, cot2, cot3, w_own, w2, w3, w2b, w3b, w_out_in = refs[9:19]
+    grads, scaled, hidden, masked, w_in = refs[19:23], *refs[23:27]
+    feat, normed, slope, means = refs[27:31]
+    work, mask, rstd, pre_grad, w_out, held, sems = refs[31:38]
     me = lax.axis_index("fsdp")
     parity = lax.rem(lax.axis_index("dp"), 2)
     rows = steps * blocks
-    high, wide = w1.shape
-    half = high // 2
+    half, wide = w2.shape
+    high = 2 * half
+    used = iter(range(sems.shape[0]))
+
+    def move(source, place):
+        copy = pltpu.make_async_copy(source, place, sems.at[next(used)])
+        copy.start()
+        return copy
 
     def rows_of(index, part=0, size=high):
         return pl.ds(pl.multiple_of(index * high + part * half, TILE), size)
 
-    w_in[rows_of(me), :] = w_own[...]
-    w_in[rows_of(me ^ 1), :] = w1[...]
-    w_in[rows_of(me ^ 2, parity, half), :] = w2[...]
-    w_in[rows_of(me ^ 3, parity, half), :] = w3[...]
-    w_in[rows_of(me ^ 2, 1 - parity, half), :] = w2b[...]
-    w_in[rows_of(me ^ 3, 1 - parity, half), :] = w3b[...]
+    coming = [
+        move(w_own.at[:, columns_of(me, wide)], w_in.at[rows_of(me), :]),
+        move(pair.at[rows:, :wide], w_in.at[rows_of(me ^ 1, 0, half), :]),
+        move(pair.at[rows:, wide:], w_in.at[rows_of(me ^ 1, 1, half), :]),
+        move(w2, w_in.at[rows_of(me ^ 2, parity, half), :]),
+        move(w3, w_in.at[rows_of(me ^ 3, parity, half), :]),
+        move(w2b, w_in.at[rows_of(me ^ 2, 1 - parity, half), :]),
+        move(w3b, w_in.at[rows_of(me ^ 3, 1 - parity, half), :]),
+        move(w_out_in, w_out),
+        move(cot0, masked.at[:rows, :]),
+        move(pair.at[:rows, :], masked.at[rows : 2 * rows, :]),
+        move(cot2, masked.at[2 * rows : 3 * rows, :]),
+        move(cot3, masked.at[3 * rows :, :]),
+    ]
     forward(
-        steps, blocks, patches[1:], subs, depth, gain, work, mask, (feat, normed, slope, rstd)
-    )
+        steps, blocks, patches[1:], weight, depth, gain, work, mask, (feat, normed, slope, rstd)
+    )
+    for copy in coming:
+        copy.wait()
     fine = jnp.broadcast_to(gain[...], (TILE, gain.shape[1]))
     coarse = fine.astype(jnp.bfloat16)
     small = (fine - coarse.astype(jnp.float32)).astype(jnp.bfloat16)
@@ -265,7 +294,7 @@
         tail = slice((k - 1) * rows, k * rows)
         counts = patches[k][rows:, :LANES].astype(jnp.float32)[:, :1]
         keep = jnp.concatenate([counts > t for t in range(steps)], axis=0)
-        kept = jnp.where(keep, cots[k][...], jnp.zeros((), jnp.bfloat16))
+        kept = jnp.where(keep, masked[at, :], jnp.zeros((), jnp.bfloat16))
         masked[at, :] = kept
         pre = dot(normed0[...] if k == 0 else normed[tail, :], w_in[...], 1, 0)
         back = dot(kept, w_out[...], 1, 1)
@@ -279,10 +308,14 @@
         for i, other in enumerate((pulled, pre)):
             mean = jnp.sum(grown * other, axis=-1, keepdims=True) * share
             means[i, at, :] = jnp.broadcast_to(mean, (rows, LANES)).astype(jnp.bfloat16)
+    leaving = []
     for k in (2, 3, 1, 0):
         cols = columns_of(me ^ k, high)
         left = jnp.concatenate([normed0[:, cols], normed[:, cols]], axis=0)
-        grads[k][...] = dot(left, pre_grad[...], 0, 0).astype(jnp.bfloat16)
+        held[k] = dot(left, pre_grad[...], 0, 0).astype(jnp.bfloat16)
+        leaving.append(move(held.at[k], grads[k]))
+    for copy in leaving:
+        copy.wait()
 
 
 def backward_kernel(steps, blocks, *refs):
@@ -354,15 +387,22 @@
         )
 
 
-def join_kernel(width, p0, p1, p2, p3, out_ref, sems):
+def join_kernel(width, *refs):
+    pieces, out_ref, held, sems = refs[0:4], refs[4], refs[5], refs[6]
     me = lax.axis_index("fsdp")
-    copies = [
-        pltpu.make_async_copy(piece, out_ref.at[:, columns_of(me ^ k, width)], sems.at[k])
-        for k, piece in enumerate((p0, p1, p2, p3))
+    coming = [
+        pltpu.make_async_copy(piece, held.at[k], sems.at[0, k]) for k, piece in enumerate(pieces)
     ]
-    for copy in copies:
+    leaving = [
+        pltpu.make_async_copy(held.at[k], out_ref.at[:, columns_of(me ^ k, width)], sems.at[1, k])
+        for k in range(4)
+    ]
+    for copy in coming:
         copy.start()
-    for copy in copies:
+    for first, second in zip(coming, leaving):
+        first.wait()
+        second.start()
+    for copy in leaving:
         copy.wait()
 
 
@@ -394,33 +434,18 @@
         jnp.broadcast_to(info[None], (n, home + 1)), "dp", split_axis=0, concat_axis=0, tiled=True
     )
 
-    subs = [sub_weight, across(sub_weight, 1), across(sub_weight, 2)]
-    w0, w1, w2, w3 = pl.pallas_call(
+    weight = lax.all_gather(sub_weight, "fsdp", axis=0, tiled=True)
+    w_far = pltpu.with_memory_space_constraint(w_in, pltpu.HBM)
+    w2, w3 = pl.pallas_call(
         functools.partial(cut_kernel, wide),
-        out_shape=(
-            pltpu.VMEM((deep, wide), bf16),
-            pltpu.VMEM((deep, wide), bf16),
-            pltpu.VMEM((deep // 2, wide), bf16),
-            pltpu.VMEM((deep // 2, wide), bf16),
-        ),
+        out_shape=(sds((deep // 2, wide), bf16),) * 2,
         in_specs=[ANY],
-        out_specs=(VMEM,) * 4,
-        scratch_shapes=[dma((4,))],
-        compiler_params=params(),
-        cost_estimate=CHEAP,
-    )(w_in)
-    w1, w2, w3 = across(w1, 1), across(w2, 2), across(w3, 3)
-
-    cot0 = pl.pallas_call(
-        functools.partial(turn_kernel, blocks, steps),
-        out_shape=sds((rows, width), bf16),
-        in_specs=[VMEM],
-        out_specs=VMEM,
-        scratch_shapes=[pltpu.VMEM((rows * width // LANES, LANES), f32)],
-        compiler_params=params(),
-        cost_estimate=CHEAP,
-    )(cotangent[0, 0])
-    cots = [cot0, across(cot0, 1), across(cot0, 2)]
+        out_specs=(ANY,) * 2,
+        scratch_shapes=[pltpu.VMEM((2, deep // 2, wide), bf16), dma((2, 2))],
+        compiler_params=params(),
+        cost_estimate=cost(1),
+    )(w_far)
+    w2, w3 = across(w2, 2), across(w3, 3)
 
     block_shape = frames.shape[3:]
     held = frames[0, 0].reshape((cap, n) + block_shape) if split else frames[0, 0]
@@ -434,14 +459,25 @@
             dma((2 * (n if split else home),)),
         ],
         compiler_params=params(),
-        cost_estimate=CHEAP,
+        cost_estimate=cost(2),
     )(order, infos, held)
     gain = norm_gain.reshape(1, width)
-    packed, w2, w3, subs[2], gain = lax.optimization_barrier((packed, w2, w3, subs[2], gain))
+    packed, w2, w3, gain, cot = lax.optimization_barrier(
+        (packed, w2, w3, gain, cotangent[0, 0])
+    )
+    got = lax.all_to_all(packed, "dp", split_axis=0, concat_axis=0, tiled=True)
+    cot0, pair = pl.pallas_call(
+        functools.partial(prepare_kernel, blocks, steps, wide),
+        out_shape=(sds((rows, width), bf16), sds((rows + deep // 2, width), bf16)),
+        in_specs=[VMEM, ANY],
+        out_specs=(VMEM,) * 2,
+        scratch_shapes=[pltpu.VMEM((rows * width // LANES, LANES), f32), dma((2,))],
+        compiler_params=params(),
+        cost_estimate=cost(2),
+    )(cot, w_far)
+    cot2, pair = across(cot0, 2), across(pair, 1)
     w2b, w3b = across_dp(w2, 1), across_dp(w3, 1)
-    got = lax.all_to_all(packed, "dp", split_axis=0, concat_axis=0, tiled=True)
-    subs.append(across(subs[2], 1))
-    got, subs[1], subs[3] = lax.optimization_barrier((got, subs[1], subs[3]))
+    got, w2b = lax.optimization_barrier((got, w2b))
     patches0 = pl.pallas_call(
         functools.partial(unpack_kernel, n, cap, blocks, steps),
         out_shape=sds((rows + blocks, block_shape[0] // steps * LANES), bf16),
@@ -453,11 +489,9 @@
             dma((blocks,)),
         ],
         compiler_params=params(),
-        cost_estimate=CHEAP,
+        cost_estimate=cost(2),
     )(order, infos, got.reshape((n * cap,) + block_shape))
     patches = [patches0, across(patches0, 1), across(patches0, 2)]
-    patches.append(across(patches[2], 1))
-    cots.append(across(cots[2], 1))
 
     def kept(count):
         return (
@@ -470,18 +504,23 @@
     feat0, normed0, slope0, rstd0 = pl.pallas_call(
         functools.partial(own_kernel, steps, blocks),
         out_shape=kept(1),
-        in_specs=[VMEM] * 7,
+        in_specs=[VMEM] * 4,
         out_specs=(VMEM,) * 4,
         scratch_shapes=[pltpu.VMEM((rows, width), f32), pltpu.VMEM((rows, LANES), f32)],
         compiler_params=params(),
-        cost_estimate=CHEAP,
-    )(*near(patches0, *subs, depth_kernel, gain))
+        cost_estimate=cost(4),
+    )(*near(patches0), weight, depth_kernel, gain)
+    feat0, cot_relay, patch_relay, w3b = lax.optimization_barrier(
+        (feat0, cot2, patches[2], w3b)
+    )
+    cot3 = across(cot_relay, 1)
+    patches.append(across(patch_relay, 1))
     (
         g0, g1, g2, g3, scaled, hidden, masked, w_slice, feat, normed, slope, means
     ) = pl.pallas_call(
         functools.partial(middle_kernel, steps, blocks),
         out_shape=(
-            *[pltpu.VMEM((deep, wide), bf16)] * 4,
+            *[sds((deep, wide), bf16)] * 4,
             pltpu.VMEM((4 * rows, wide), bf16),
             pltpu.VMEM((4 * rows, wide), bf16),
             pltpu.VMEM((4 * rows, width), bf16),
@@ -489,21 +528,22 @@
             *kept(3)[:3],
             pltpu.VMEM((2, 4 * rows, LANES), bf16),
         ),
-        in_specs=[VMEM] * 23,
-        out_specs=(VMEM,) * 12,
+        in_specs=[VMEM] * 9 + [ANY] * 10,
+        out_specs=(ANY,) * 4 + (VMEM,) * 8,
         scratch_shapes=[
             pltpu.VMEM((3 * rows, width), f32),
             pltpu.VMEM((3 * rows, LANES), f32),
             pltpu.VMEM((3 * rows, LANES), f32),
             pltpu.VMEM((4 * rows, wide), bf16),
+            pltpu.VMEM((wide, width), bf16),
+            pltpu.VMEM((4, deep, wide), bf16),
+            dma((16,)),
         ],
-        compiler_params=params(24),
-        cost_estimate=CHEAP,
+        compiler_params=params(28),
+        cost_estimate=cost(20),
     )(
-        *near(
-            *patches, *subs, depth_kernel, gain, rstd0, normed0, *cots,
-            w0, w1, w2, w3, w2b, w3b, w_out,
-        )
+        *near(*patches), weight, depth_kernel, gain, *near(rstd0, normed0),
+        cot0, pair, cot2, cot3, w_far, w2, w3, w2b, w3b, w_out,
     )
     g1, g2, g3 = across(g1, 1), across(g2, 2), across(g3, 3)
 
@@ -514,7 +554,7 @@
         out_specs=VMEM,
         scratch_shapes=[pltpu.VMEM((4 * rows, width), bf16)],
         compiler_params=params(),
-        cost_estimate=CHEAP,
+        cost_estimate=cost(13),
     )(
         *near(
             gain, scaled, w_slice, masked, means, normed0, slope0, feat0, normed, slope, feat
@@ -528,11 +568,6 @@
         taps.reshape(devices, 1, -1), every, split_axis=0, concat_axis=0, tiled=True
     )
     share = jnp.sum(shares, axis=0, keepdims=True) / rows
-    whole = lax.all_to_all(
-        jnp.broadcast_to(share, shares.shape), every, split_axis=0, concat_axis=0, tiled=True
-    )
-    kernel_grad = whole.reshape(2 * steps, width)[: depth_kernel.shape[0]]
-
     grad_out = pl.pallas_call(
         out_kernel,
         out_shape=sds((wide, width), bf16),
@@ -540,17 +575,23 @@
         out_specs=VMEM,
         scratch_shapes=[pltpu.VMEM((wide, 4 * rows), bf16)],
         compiler_params=params(),
-        cost_estimate=CHEAP,
+        cost_estimate=cost(4),
     )(*near(hidden, masked))
+    share, grad_out = lax.optimization_barrier((share, grad_out))
+    whole = lax.all_to_all(
+        jnp.broadcast_to(share, shares.shape), every, split_axis=0, concat_axis=0, tiled=True
+    )
+    kernel_grad = whole.reshape(2 * steps, width)[: depth_kernel.shape[0]]
+
     grad_in = pl.pallas_call(
         functools.partial(join_kernel, wide),
         out_shape=sds((deep, hidden_width), bf16),
-        in_specs=[VMEM] * 4,
+        in_specs=[ANY] * 4,
         out_specs=ANY,
-        scratch_shapes=[dma((4,))],
-        compiler_params=params(),
-        cost_estimate=CHEAP,
-    )(*near(g0, g1, g2, g3))
+        scratch_shapes=[pltpu.VMEM((4, deep, wide), bf16), dma((2, 4))],
+        compiler_params=params(),
+        cost_estimate=cost(2),
+    )(g0, g1, g2, g3)
     return (grad_in[None], grad_out[None], kernel_grad)
 
 

time: 144 us -> 154 us (1.069)
  between operations: 1.62 us -> 14.9 us
  waiting for transfers between devices: 39.7 us -> 31.3 us
  Pallas kernels: 51.3 us -> 55.5 us
  local copies, waits for them, and re-layouts: 16.6 us -> 18.5 us
    ppermute x15 -> x11, waiting for transfers between devices: 22.7 us -> 10.5 us  [across(): return lax.ppermute(value, 'fsdp', [(i, i ^ k) for i in range(n)])]
    ppermute x2, waiting for transfers between devices: 4.29 us -> 11.8 us  [across_dp(): return lax.ppermute(value, 'dp', [(i, i ^ k) for i in range(n)])]
    all_to_all x1, waiting for transfers between devices: 7.47 us -> 2.03 us  [on_device(): lax.all_to_all(taps.reshape(devices, 1, -1), every, split_axis=0, concat_...]
    pallas_call x2, Pallas kernels: 0.8 us -> 3.43 us  [the longest x1 2.2 us: on_device(): pl.pallas_call(functools.partial(prepare_kernel, blocks, steps, wide), ou...]
    ppermute x15 -> x11, starting transfers between devices: 14 us -> 11.6 us  [across(): return lax.ppermute(value, 'fsdp', [(i, i ^ k) for i in range(n)])]
    unnamed x67 -> x57, local copies, waits for them, and re-layouts: 15.2 us -> 17.1 us
    pallas_call x1, Pallas kernels: 22.7 us -> 24.5 us  [on_device(): pl.pallas_call(functools.partial(middle_kernel, steps, blocks), out_shape...]
  transfers between devices with their start and end apart: 21 -> 18, of which waited for: 8 -> 10; matrix products, arithmetic and copies ran while one was open for 1% -> 1% of each run, Pallas kernels for 20% -> 20%
where the time goes in v3:
time: 154 us
  Pallas kernels  55.5 us (36%)
  starting transfers between devices  33.1 us (21%)
  waiting for transfers between devices  31.3 us (20%)
  local copies, waits for them, and re-layouts  18.5 us (12%)
  between operations  14.9 us (10%)
    pallas_call x1, Pallas kernels, on_device(): pl.pallas_call(functools.partial(middle_kernel, steps, blocks), out_shape...  24.5 us
    unnamed x57, local copies, waits for them, and re-layouts  17.1 us
    pallas_call x1, Pallas kernels, on_device(): pl.pallas_call(functools.partial(backward_kernel, steps, blocks), out_sha...  13.3 us
    ppermute x2, waiting for transfers between devices, across_dp(): return lax.ppermute(value, 'dp', [(i, i ^ k) for i in range(n)])  11.8 us
    ppermute x11, starting transfers between devices, across(): return lax.ppermute(value, 'fsdp', [(i, i ^ k) for i in range(n)])  11.6 us
    ppermute x11, waiting for transfers between devices, across(): return lax.ppermute(value, 'fsdp', [(i, i ^ k) for i in range(n)])  10.5 us
    all_to_all x1, starting transfers between devices, on_device(): got = lax.all_to_all(packed, 'dp', split_axis=0, concat_axis=0, tiled=True)  6.58 us
    all_to_all x1, starting transfers between devices, on_device(): lax.all_to_all(jnp.broadcast_to(info[None], (n, home + 1)), 'dp', split_a...  5.95 us
  transfers between devices with their start and end apart: 18, of which 10 were waited for; matrix products, arithmetic and copies ran while one was open for 1% of the time, Pallas kernels for 20%

profile of v3, /device:TPU:1, one launch (start us, length us, event | category | flops | bytes accessed | tf_op | source)
XLA Modules:
  0.0 153.6 jit_solution(736571475952029064)
XLA Ops:
  7.3 0.7 all-gather.2.cloned.1.call-update
  7.9 1.2 shard_map.122
  9.2 2.1 %collective-permute-start = (bf16[192,768]{1,0:T(8,128)(2,1)S(1)}, bf16[192,768]{1,0:T(8,128)(2,1)S(1)}, u32[]{:S(2)}, u32[]{:S(2)}) collective-permute-start(bf16[192,768]{1,0:T(8,128)(2,1)S(1)} %get-tuple-element.39), channel_id=1, source_target_pairs={{0,2},{1,3},{2,0},{3,1},{4,6},{5,7},{6,4},{7,5},{8,10},{9,11},{10,... | collective-permute-start | bytes 884744 | tf_op jit(solution)/shard_map/ppermute | solution.py:50
  11.3 0.6 collective-permute-start.1
  12.7 0.6 broadcast_in_dim.20
  13.3 6.0 %all-to-all-start = ((s32[8,1,49]{2,1,0:T(1,128)}), s32[8,1,49]{2,1,0:T(1,128)S(1)}, u32[]{:S(2)}, u32[]{:S(2)}) async-start(s32[8,1,49]{2,1,0:T(1,128)} %broadcast_in_dim.20), calls=%async_computation | async-start | bytes 8192 | tf_op jit(solution)/shard_map/all_to_all | solution.py:433
  19.3 5.2 %all-to-all-done = s32[8,1,49]{2,1,0:T(1,128)S(1)} async-done(((s32[8,1,49]{2,1,0:T(1,128)}), s32[8,1,49]{2,1,0:T(1,128)S(1)}, u32[]{:S(2)}, u32[]{:S(2)}) %all-to-all-start) | async-done | bytes 1600 | tf_op jit(solution)/shard_map/all_to_all | solution.py:433
  24.5 1.8 %shard_map.121 = bf16[8,6,64,128]{3,2,1,0:T(8,128)(2,1)} custom-call(s32[1,8]{1,0:T(1,128)S(1)} %copy-done.23, s32[8,49]{1,0:T(8,128)S(1)} %bitcast.15, bf16[6,8,64,128]{3,2,1,0:T(8,128)(2,1)S(1)} %bitcast.13), custom_call_target="tpu_custom_call" | custom-call | bytes 7200000 | tf_op jit(solution)/shard_map/pallas_call | solution.py:452
  26.3 3.2 %collective-permute-done.1.refs_15_ = bf16[192,768]{1,0:T(8,128)(2,1)S(1)} collective-permute-done((bf16[192,768]{1,0:T(8,128)(2,1)S(1)}, bf16[192,768]{1,0:T(8,128)(2,1)S(1)}, u32[]{:S(2)}, u32[]{:S(2)}) %collective-permute-start.1) | collective-permute-done | bytes 294944 | tf_op jit(solution)/shard_map/ppermute | solution.py:50
  29.5 6.6 %all-to-all-start.1 = ((bf16[8,6,64,128]{3,2,1,0:T(8,128)(2,1)}), bf16[8,6,64,128]{3,2,1,0:T(8,128)(2,1)S(1)}, u32[]{:S(2)}, u32[]{:S(2)}) async-start(bf16[8,6,64,128]{3,2,1,0:T(8,128)(2,1)} %shard_map.121), calls=%async_computation.1 | async-start | bytes 1572864 | tf_op jit(solution)/shard_map/all_to_all | solution.py:468
  36.1 2.2 %shard_map.125 = (bf16[256,1536]{1,0:T(8,128)(2,1)S(1)}, bf16[448,1536]{1,0:T(8,128)(2,1)}) custom-call(bf16[16,16,1536]{2,1,0:T(8,128)(2,1)S(1)} %bitcast.14, bf16[384,3072]{1,0:T(8,128)(2,1)} %refs_13_.1), custom_call_target="tpu_custom_call" | custom-call | bytes 7200000 | tf_op jit(solution)/shard_map/pallas_call | solution.py:469
  38.3 2.3 %collective-permute-start.5 = (bf16[256,1536]{1,0:T(8,128)(2,1)S(1)}, bf16[256,1536]{1,0:T(8,128)(2,1)}, u32[]{:S(2)}, u32[]{:S(2)}) collective-permute-start(bf16[256,1536]{1,0:T(8,128)(2,1)S(1)} %get-tuple-element.47.refs_9_), channel_id=1, source_target_pairs={{0,2},{1,3},{2,0},{3,1},{4,6},{5,7},{6,4},{7,5},{8,10},{9,11},{10,... | collective-permute-start | bytes 2359304 | tf_op jit(solution)/shard_map/ppermute | solution.py:50
  40.6 1.5 collective-permute-start.2
  42.2 11.8 %collective-permute-done.2.refs_16_ = bf16[192,768]{1,0:T(8,128)(2,1)S(1)} collective-permute-done((bf16[192,768]{1,0:T(8,128)(2,1)S(1)}, bf16[192,768]{1,0:T(8,128)(2,1)S(1)}, u32[]{:S(2)}, u32[]{:S(2)}) %collective-permute-start.2) | collective-permute-done | bytes 294944 | tf_op jit(solution)/shard_map/ppermute | solution.py:55
  54.0 0.7 copy-done.19
  54.7 1.0 all-to-all-done.1
  55.8 1.7 %shard_map.123.patches.refs_0_ = bf16[272,512]{1,0:T(8,128)(2,1)S(1)} custom-call(s32[1,8]{1,0:T(1,128)S(1)} %copy-done.23, s32[8,49]{1,0:T(8,128)S(1)} %bitcast.16, bf16[48,64,128]{2,1,0:T(8,128)(2,1)S(1)} %bitcast.12), custom_call_target="tpu_custom_call" | custom-call | bytes 7200000 | tf_op jit(solution)/shard_map/pallas_call | solution.py:481
  57.5 1.2 collective-permute-start.4
  58.7 1.4 copy-done
  60.1 4.2 %shard_map.124 = (bf16[256,1536]{1,0:T(8,128)(2,1)S(1)}, bf16[256,1536]{1,0:T(8,128)(2,1)S(1)}, bf16[256,1536]{1,0:T(8,128)(2,1)S(1)}, f32[256,128]{1,0:T(8,128)S(1)}) custom-call(bf16[272,512]{1,0:T(8,128)(2,1)S(1)} %shard_map.123.patches.refs_0_, bf16[512,1536]{1,0:T(8,128)(2,1)S(1)} %copy-done, f32[31,1536]{1,0:T(8,128)S(1)} %copy-done.7, ...), custom_call_target="tpu_custom_call" | custom-call | bytes 14400000 | tf_op jit(solution)/shard_map/pallas_call | solution.py:504
  64.7 1.9 %collective-permute-start.9 = (bf16[256,1536]{1,0:T(8,128)(2,1)}, bf16[256,1536]{1,0:T(8,128)(2,1)S(1)}, u32[]{:S(2)}, u32[]{:S(2)}) collective-permute-start(bf16[256,1536]{1,0:T(8,128)(2,1)} %collective-permute-done.5.refs_11_), channel_id=1, source_target_pairs={{0,1},{1,0},{2,3},{3,2},{4,5},{5,4},{6,7},{7,6},{8,9},{9,8},{10,11... | collective-permute-start | bytes 2359304 | tf_op jit(solution)/shard_map/ppermute | solution.py:50
  66.7 0.5 collective-permute-start.7
  67.2 0.7 copy-done.21
  67.9 1.1 copy-done.3
  69.6 1.3 copy-done.4
  70.9 0.9 copy-done.8
  71.9 1.1 copy-done.10
  73.0 1.0 copy-done.16
  74.0 1.0 copy-done.18
  74.9 1.0 copy-done.20
  75.9 1.0 copy-done.22
  76.8 24.5 %shard_map.126 = (bf16[384,768]{1,0:T(8,128)(2,1)S(1)}, bf16[384,768]{1,0:T(8,128)(2,1)S(1)}, bf16[384,768]{1,0:T(8,128)(2,1)S(1)}, bf16[384,768]{1,0:T(8,128)(2...) custom-call(bf16[272,512]{1,0:T(8,128)(2,1)S(1)} %shard_map.123.patc, ...), custom_call_target="tpu_custom_call" | custom-call | bytes 72000000 | tf_op jit(solution)/shard_map/pallas_call | solution.py:520
  101.3 0.8 copy-done.25
  102.1 1.1 collective-permute-start.11
  103.2 13.3 %shard_map.127 = f32[32,1,1536]{2,1,0:T(1,128)} custom-call(f32[1,1536]{1,0:T(1,128)S(1)} %reshape.35.gain.refs_6_.refs_0_, bf16[1024,768]{1,0:T(8,128)(2,1)S(1)} %get-tuple-element.58.refs_1_, bf16[1536,768]{1,0:T(8,128)(2,1)S(1)} %get-tuple-element.59.refs_2_, bf16[1024,1536]{1,0:T(8,128)(2,1)S(1)} %get-tuple-element.60.refs_3_.masked, ...), custom_call_target="tpu_custom_call" | custom-call | bytes 46800000 | tf_op jit(solution)/shard_map/pallas_call | solution.py:550
  116.7 0.8 copy-done.13
  117.5 4.6 %all-to-all-start.2 = ((f32[32,1,1536]{2,1,0:T(1,128)}), f32[32,1,1536]{2,1,0:T(1,128)S(1)}, u32[]{:S(2)}, u32[]{:S(2)}) async-start(f32[32,1,1536]{2,1,0:T(1,128)} %shard_map.127), calls=%async_computation.2 | async-start | bytes 393216 | tf_op jit(solution)/shard_map/all_to_all | solution.py:567
  122.5 1.5 %collective-permute-start.12 = (bf16[384,768]{1,0:T(8,128)(2,1)}, bf16[384,768]{1,0:T(8,128)(2,1)}, u32[]{:S(2)}, u32[]{:S(2)}) collective-permute-start(bf16[384,768]{1,0:T(8,128)(2,1)} %copy-done.24), channel_id=1, source_target_pairs={{0,3},{1,2},{2,1},{3,0},{4,7},{5,6},{6,5},{7,4},{8,11},{9,10},{10,... | collective-permute-start | bytes 1769480 | tf_op jit(solution)/shard_map/ppermute | solution.py:50
  124.0 1.4 copy-done.2
  125.4 4.0 %shard_map.129 = bf16[768,1536]{1,0:T(8,128)(2,1)} custom-call(bf16[1024,768]{1,0:T(8,128)(2,1)S(1)} %copy-done.2, bf16[1024,1536]{1,0:T(8,128)(2,1)S(1)} %get-tuple-element.60.refs_3_.masked), custom_call_target="tpu_custom_call" | custom-call | bytes 14400000 | tf_op jit(solution)/shard_map/pallas_call | solution.py:571
  129.5 2.0 %all-to-all-done.2 = f32[32,1,1536]{2,1,0:T(1,128)S(1)} async-done(((f32[32,1,1536]{2,1,0:T(1,128)}), f32[32,1,1536]{2,1,0:T(1,128)S(1)}, u32[]{:S(2)}, u32[]{:S(2)}) %all-to-all-start.2) | async-done | bytes 196640 | tf_op jit(solution)/shard_map/all_to_all | solution.py:567
  131.7 0.8 broadcast_in_dim.24
  132.4 2.7 %all-to-all-start.3 = ((f32[32,1,1536]{2,1,0:T(1,128)}), f32[32,1,1536]{2,1,0:T(1,128)S(1)}, u32[]{:S(2)}, u32[]{:S(2)}) async-start(f32[32,1,1536]{2,1,0:T(1,128)} %broadcast_in_dim.24), calls=%async_computation.3 | async-start | bytes 393216 | tf_op jit(solution)/shard_map/all_to_all | solution.py:581
  135.1 6.2 %collective-permute-done.12.refs_3_ = bf16[384,768]{1,0:T(8,128)(2,1)} collective-permute-done((bf16[384,768]{1,0:T(8,128)(2,1)}, bf16[384,768]{1,0:T(8,128)(2,1)}, u32[]{:S(2)}, u32[]{:S(2)}) %collective-permute-start.12) | collective-permute-done | bytes 589856 | tf_op jit(solution)/shard_map/ppermute | solution.py:50
  141.4 1.1 copy-done.12
  142.4 1.1 copy-done.14
  143.5 2.5 %shard_map.128 = bf16[384,3072]{1,0:T(8,128)(2,1)} custom-call(bf16[384,768]{1,0:T(8,128)(2,1)S(1)} %copy-done.12, bf16[384,768]{1,0:T(8,128)(2,1)} %collective-permute-done.10.refs_1_, bf16[384,768]{1,0:T(8,128)(2,1)S(1)} %copy-done.14, bf16[384,768]{1,0:T(8,128)(2,1)} %collective-permute-done.12.refs_3_), custom_call_target="tpu_custom_call" | custom-call | bytes 7200000 | tf_op jit(solution)/shard_map/pallas_call | solution.py:586
  146.1 0.7 copy.15
  (64 shorter events, 2.0 us)
Async XLA Ops:
  7.2 5.5 %copy-start.27 = (s32[1,1,48]{2,1,0:T(1,128)S(1)}, s32[1,1,48]{2,1,0:T(1,128)}, u32[]{:S(2)}) copy-start(s32[1,1,48]{2,1,0:T(1,128)} %param.12) | copy-start | bytes 580
  7.2 12.1 %copy-start.26 = (f32[1536]{0:T(1024)S(1)}, f32[1536]{0:T(1024)}, u32[]{:S(2)}) copy-start(f32[1536]{0:T(1024)} %param.17) | copy-start | bytes 18436
  7.2 17.3 %copy-start.23 = (s32[1,8]{1,0:T(1,128)S(1)}, s32[1,8]{1,0:T(1,128)}, u32[]{:S(2)}) copy-start(s32[1,8]{1,0:T(1,128)} %order_ref.3) | copy-start | bytes 100
  7.2 17.3 %copy-start.5 = (bf16[1,1,48,64,128]{4,3,2,1,0:T(8,128)(2,1)S(1)}, bf16[1,1,48,64,128]{4,3,2,1,0:T(8,128)(2,1)}, u32[]{:S(2)}) copy-start(bf16[1,1,48,64,128]{4,3,2,1,0:T(8,128)(2,1)} %param.10) | copy-start | bytes 2359300
  7.2 51.5 %all-gather.2.cloned.1.call-start = ((), (), s32[]{:S(2)}) async-start(), calls=%async_computation.4 | async-start | bytes 1966080 | tf_op jit(solution)/shard_map/all_gather | solution.py:437
  7.9 28.1 %copy-start.6 = (bf16[1,1,16,16,1536]{4,3,2,1,0:T(8,128)(2,1)S(1)}, bf16[1,1,16,16,1536]{4,3,2,1,0:T(8,128)(2,1)}, u32[]{:S(2)}) copy-start(bf16[1,1,16,16,1536]{4,3,2,1,0:T(8,128)(2,1)} %param.14) | copy-start | bytes 2359300
  9.2 17.1 %collective-permute-start = (bf16[192,768]{1,0:T(8,128)(2,1)S(1)}, bf16[192,768]{1,0:T(8,128)(2,1)S(1)}, u32[]{:S(2)}, u32[]{:S(2)}) collective-permute-start(bf16[192,768]{1,0:T(8,128)(2,1)S(1)} %get-tuple-element.39), channel_id=1, source_target_pairs={{0,2},{1,3},{2,0},{3,1},{4,6},{5,7},{6,4},{7,5},{8,10},{9,11},{10,... | collective-permute-start | bytes 884744 | tf_op jit(solution)/shard_map/ppermute | solution.py:50
  11.3 18.2 %collective-permute-start.1 = (bf16[192,768]{1,0:T(8,128)(2,1)S(1)}, bf16[192,768]{1,0:T(8,128)(2,1)S(1)}, u32[]{:S(2)}, u32[]{:S(2)}) collective-permute-start(bf16[192,768]{1,0:T(8,128)(2,1)S(1)} %get-tuple-element.40), channel_id=1, source_target_pairs={{0,3},{1,2},{2,1},{3,0},{4,7},{5,6},{6,5},{7,4},{8,11},{9,10},{10,... | collective-permute-start | bytes 884744 | tf_op jit(solution)/shard_map/ppermute | solution.py:50
  13.3 11.2 %all-to-all-start = ((s32[8,1,49]{2,1,0:T(1,128)}), s32[8,1,49]{2,1,0:T(1,128)S(1)}, u32[]{:S(2)}, u32[]{:S(2)}) async-start(s32[8,1,49]{2,1,0:T(1,128)} %broadcast_in_dim.20), calls=%async_computation | async-start | bytes 8192 | tf_op jit(solution)/shard_map/all_to_all | solution.py:433
  26.3 14.3 %copy-start.15 = (bf16[192,768]{1,0:T(8,128)(2,1)}, bf16[192,768]{1,0:T(8,128)(2,1)S(1)}, u32[]{:S(2)}) copy-start(bf16[192,768]{1,0:T(8,128)(2,1)S(1)} %collective-permute-done.refs_14_) | copy-start | bytes 884740
  29.5 11.1 %copy-start.17 = (bf16[192,768]{1,0:T(8,128)(2,1)}, bf16[192,768]{1,0:T(8,128)(2,1)S(1)}, u32[]{:S(2)}) copy-start(bf16[192,768]{1,0:T(8,128)(2,1)S(1)} %collective-permute-done.1.refs_15_) | copy-start | bytes 884740
  29.5 26.3 %all-to-all-start.1 = ((bf16[8,6,64,128]{3,2,1,0:T(8,128)(2,1)}), bf16[8,6,64,128]{3,2,1,0:T(8,128)(2,1)S(1)}, u32[]{:S(2)}, u32[]{:S(2)}) async-start(bf16[8,6,64,128]{3,2,1,0:T(8,128)(2,1)} %shard_map.121), calls=%async_computation.1 | async-start | bytes 1572864 | tf_op jit(solution)/shard_map/all_to_all | solution.py:468
  36.1 22.6 %copy-start.7 = (f32[31,1536]{1,0:T(8,128)S(1)}, f32[31,1536]{1,0:T(8,128)}, u32[]{:S(2)}) copy-start(f32[31,1536]{1,0:T(8,128)} %refs_5_.1) | copy-start | bytes 571396
  38.3 31.3 %copy-start.9 = (bf16[256,1536]{1,0:T(8,128)(2,1)}, bf16[256,1536]{1,0:T(8,128)(2,1)S(1)}, u32[]{:S(2)}) copy-start(bf16[256,1536]{1,0:T(8,128)(2,1)S(1)} %get-tuple-element.47.refs_9_) | copy-start | bytes 2359300
  38.3 26.0 %collective-permute-start.5 = (bf16[256,1536]{1,0:T(8,128)(2,1)S(1)}, bf16[256,1536]{1,0:T(8,128)(2,1)}, u32[]{:S(2)}, u32[]{:S(2)}) collective-permute-start(bf16[256,1536]{1,0:T(8,128)(2,1)S(1)} %get-tuple-element.47.refs_9_), channel_id=1, source_target_pairs={{0,2},{1,3},{2,0},{3,1},{4,6},{5,7},{6,4},{7,5},{8,10},{9,11},{10,... | collective-permute-start | bytes 2359304 | tf_op jit(solution)/shard_map/ppermute | solution.py:50
  40.6 27.3 %collective-permute-start.8 = (bf16[448,1536]{1,0:T(8,128)(2,1)}, bf16[448,1536]{1,0:T(8,128)(2,1)S(1)}, u32[]{:S(2)}, u32[]{:S(2)}) collective-permute-start(bf16[448,1536]{1,0:T(8,128)(2,1)} %get-tuple-element.52), channel_id=1, source_target_pairs={{0,1},{1,0},{2,3},{3,2},{4,5},{5,4},{6,7},{7,6},{8,9},{9,8},{10,11... | collective-permute-start | bytes 4128776 | tf_op jit(solution)/shard_map/ppermute | solution.py:50
  40.6 13.4 %collective-permute-start.2 = (bf16[192,768]{1,0:T(8,128)(2,1)S(1)}, bf16[192,768]{1,0:T(8,128)(2,1)S(1)}, u32[]{:S(2)}, u32[]{:S(2)}) collective-permute-start(bf16[192,768]{1,0:T(8,128)(2,1)S(1)} %collective-permute-done.refs_14_), channel_id=1, source_target_pairs={{0,4},{4,0},{8,12},{12,8},{16,20},{20,16},{24,28},{28,24},{1,5},{5... | collective-permute-start | bytes 884744 | tf_op jit(solution)/shard_map/ppermute | solution.py:55
  42.1 22.2 %collective-permute-start.6 = (bf16[192,768]{1,0:T(8,128)(2,1)}, bf16[192,768]{1,0:T(8,128)(2,1)}, u32[]{:S(2)}, u32[]{:S(2)}) collective-permute-start(bf16[192,768]{1,0:T(8,128)(2,1)} %copy-done.17), channel_id=1, source_target_pairs={{0,4},{4,0},{8,12},{12,8},{16,20},{20,16},{24,28},{28,24},{1,5},{5... | collective-permute-start | bytes 884744 | tf_op jit(solution)/shard_map/ppermute | solution.py:55
  54.0 0.7 copy-start.19
  57.5 7.2 %collective-permute-start.4 = (bf16[272,512]{1,0:T(8,128)(2,1)S(1)}, bf16[272,512]{1,0:T(8,128)(2,1)S(1)}, u32[]{:S(2)}, u32[]{:S(2)}) collective-permute-start(bf16[272,512]{1,0:T(8,128)(2,1)S(1)} %shard_map.123.patches.refs_0_), channel_id=1, source_target_pairs={{0,2},{1,3},{2,0},{3,1},{4,6},{5,7},{6,4},{7,5},{8,10},{9,11},{10,... | collective-permute-start | bytes 835592 | tf_op jit(solution)/shard_map/ppermute | solution.py:50
  58.7 1.4 copy-start
  64.7 4.8 %collective-permute-start.9 = (bf16[256,1536]{1,0:T(8,128)(2,1)}, bf16[256,1536]{1,0:T(8,128)(2,1)S(1)}, u32[]{:S(2)}, u32[]{:S(2)}) collective-permute-start(bf16[256,1536]{1,0:T(8,128)(2,1)} %collective-permute-done.5.refs_11_), channel_id=1, source_target_pairs={{0,1},{1,0},{2,3},{3,2},{4,5},{5,4},{6,7},{7,6},{8,9},{9,8},{10,11... | collective-permute-start | bytes 2359304 | tf_op jit(solution)/shard_map/ppermute | solution.py:50
  66.7 2.3 %collective-permute-start.3 = (bf16[272,512]{1,0:T(8,128)(2,1)S(1)}, bf16[272,512]{1,0:T(8,128)(2,1)S(1)}, u32[]{:S(2)}, u32[]{:S(2)}) collective-permute-start(bf16[272,512]{1,0:T(8,128)(2,1)S(1)} %shard_map.123.patches.refs_0_), channel_id=1, source_target_pairs={{0,1},{1,0},{2,3},{3,2},{4,5},{5,4},{6,7},{7,6},{8,9},{9,8},{10,11... | collective-permute-start | bytes 835592 | tf_op jit(solution)/shard_map/ppermute | solution.py:50
  66.7 2.6 %collective-permute-start.7 = (bf16[272,512]{1,0:T(8,128)(2,1)S(1)}, bf16[272,512]{1,0:T(8,128)(2,1)S(1)}, u32[]{:S(2)}, u32[]{:S(2)}) collective-permute-start(bf16[272,512]{1,0:T(8,128)(2,1)S(1)} %collective-permute-done.4.refs_2_), channel_id=1, source_target_pairs={{0,1},{1,0},{2,3},{3,2},{4,5},{5,4},{6,7},{7,6},{8,9},{9,8},{10,11... | collective-permute-start | bytes 835592 | tf_op jit(solution)/shard_map/ppermute | solution.py:50
  67.2 0.7 copy-start.21
  67.9 1.1 copy-start.3
  69.6 1.3 copy-start.4
  70.9 0.9 copy-start.8
  71.9 1.1 copy-start.10
  73.0 1.0 copy-start.16
  74.0 1.0 copy-start.18
  74.9 1.0 copy-start.20
  75.9 1.0 copy-start.22
  101.3 0.8 copy-start.25
  102.1 14.4 %copy-start.1 = (bf16[1024,768]{1,0:T(8,128)(2,1)}, bf16[1024,768]{1,0:T(8,128)(2,1)S(1)}, u32[]{:S(2)}) copy-start(bf16[1024,768]{1,0:T(8,128)(2,1)S(1)} %get-tuple-element.72.hidden) | copy-start | bytes 4718596
  102.1 14.4 %copy-start.11 = (bf16[384,768]{1,0:T(8,128)(2,1)}, bf16[384,768]{1,0:T(8,128)(2,1)S(1)}, u32[]{:S(2)}) copy-start(bf16[384,768]{1,0:T(8,128)(2,1)S(1)} %get-tuple-element.56.refs_0_) | copy-start | bytes 1769476
  102.1 14.4 %copy-start.24 = (bf16[384,768]{1,0:T(8,128)(2,1)}, bf16[384,768]{1,0:T(8,128)(2,1)S(1)}, u32[]{:S(2)}) copy-start(bf16[384,768]{1,0:T(8,128)(2,1)S(1)} %get-tuple-element.70) | copy-start | bytes 1769476
  102.1 14.6 %collective-permute-start.11 = (bf16[384,768]{1,0:T(8,128)(2,1)S(1)}, bf16[384,768]{1,0:T(8,128)(2,1)S(1)}, u32[]{:S(2)}, u32[]{:S(2)}) collective-permute-start(bf16[384,768]{1,0:T(8,128)(2,1)S(1)} %get-tuple-element.67), channel_id=1, source_target_pairs={{0,2},{1,3},{2,0},{3,1},{4,6},{5,7},{6,4},{7,5},{8,10},{9,11},{10,... | collective-permute-start | bytes 1769480 | tf_op jit(solution)/shard_map/ppermute | solution.py:50
  116.7 0.8 copy-start.13
  117.5 14.0 %all-to-all-start.2 = ((f32[32,1,1536]{2,1,0:T(1,128)}), f32[32,1,1536]{2,1,0:T(1,128)S(1)}, u32[]{:S(2)}, u32[]{:S(2)}) async-start(f32[32,1,1536]{2,1,0:T(1,128)} %shard_map.127), calls=%async_computation.2 | async-start | bytes 393216 | tf_op jit(solution)/shard_map/all_to_all | solution.py:567
  122.1 13.0 %collective-permute-start.10 = (bf16[384,768]{1,0:T(8,128)(2,1)}, bf16[384,768]{1,0:T(8,128)(2,1)}, u32[]{:S(2)}, u32[]{:S(2)}) collective-permute-start(bf16[384,768]{1,0:T(8,128)(2,1)} %copy-done.25), channel_id=1, source_target_pairs={{0,1},{1,0},{2,3},{3,2},{4,5},{5,4},{6,7},{7,6},{8,9},{9,8},{10,11... | collective-permute-start | bytes 1769480 | tf_op jit(solution)/shard_map/ppermute | solution.py:50
  122.5 18.9 %collective-permute-start.12 = (bf16[384,768]{1,0:T(8,128)(2,1)}, bf16[384,768]{1,0:T(8,128)(2,1)}, u32[]{:S(2)}, u32[]{:S(2)}) collective-permute-start(bf16[384,768]{1,0:T(8,128)(2,1)} %copy-done.24), channel_id=1, source_target_pairs={{0,3},{1,2},{2,1},{3,0},{4,7},{5,6},{6,5},{7,4},{8,11},{9,10},{10,... | collective-permute-start | bytes 1769480 | tf_op jit(solution)/shard_map/ppermute | solution.py:50
  124.0 1.4 copy-start.2
  132.4 13.6 %all-to-all-start.3 = ((f32[32,1,1536]{2,1,0:T(1,128)}), f32[32,1,1536]{2,1,0:T(1,128)S(1)}, u32[]{:S(2)}, u32[]{:S(2)}) async-start(f32[32,1,1536]{2,1,0:T(1,128)} %broadcast_in_dim.24), calls=%async_computation.3 | async-start | bytes 393216 | tf_op jit(solution)/shard_map/all_to_all | solution.py:581
  141.4 1.1 copy-start.12
  142.4 1.1 copy-start.14
Sparse Core Ops, SparseCore 0:
  9.6 25.6 all-gather.1

commit v4 on v3

--- a/solution.py
+++ b/solution.py
@@ -31,6 +31,10 @@
     return [pltpu.with_memory_space_constraint(array, pltpu.VMEM) for array in arrays]
 
 
+def far(*arrays):
+    return [pltpu.with_memory_space_constraint(array, pltpu.HBM) for array in arrays]
+
+
 def sds(shape, dtype):
     return jax.ShapeDtypeStruct(shape, dtype)
 
@@ -59,14 +63,16 @@
     return pl.ds(pl.multiple_of(index * width, LANES), width)
 
 
-def prepare_kernel(blocks, steps, width, cot_ref, w_ref, out_ref, pair_ref, scratch, sems):
+def prepare_kernel(
+    blocks, steps, width, cot_ref, w_ref, cot_out, pair_out, cot, pair, scratch, sems
+):
     rows = blocks * steps
-    half = pair_ref.shape[0] - rows
+    half = w_ref.shape[0] // 2
     cols = columns_of(lax.axis_index("fsdp") ^ 1, width)
     copies = [
         pltpu.make_async_copy(
             w_ref.at[i * half : (i + 1) * half, cols],
-            pair_ref.at[rows:, i * width : (i + 1) * width],
+            pair.at[rows:, i * width : (i + 1) * width],
             sems.at[i],
         )
         for i in range(2)
@@ -81,9 +87,17 @@
         for t in range(steps):
             at = slice(t * blocks, (t + 1) * blocks)
             turned = scratch[pl.ds(c * rows + t, blocks, stride=steps), :].astype(jnp.bfloat16)
-            out_ref[at, cols] = turned
-            pair_ref[at, cols] = turned
+            cot[at, cols] = turned
+            pair[at, cols] = turned
     for copy in copies:
+        copy.wait()
+    leaving = [
+        pltpu.make_async_copy(cot, cot_out, sems.at[3]),
+        pltpu.make_async_copy(pair, pair_out, sems.at[4]),
+    ]
+    for copy in leaving:
+        copy.start()
+    for copy in leaving:
         copy.wait()
 
 
@@ -182,10 +196,10 @@
     return tree(terms, low, middle) + tree(terms, middle, high)
 
 
-def forward(steps, blocks, patches, sub_ref, depth_ref, gain_ref, work, mask, outs):
+def forward(steps, blocks, patches, sub_ref, scales, work, mask, outs):
     rows = steps * blocks
     feat_ref, normed_ref, slope_ref, rstd_ref = outs
-    width, taps = depth_ref.shape[1], depth_ref.shape[0]
+    width, taps = scales.shape[1], scales.shape[0] - 1
     span = (taps - 1) // 2
     groups = range(len(patches))
     for g in groups:
@@ -198,7 +212,7 @@
     def column(c, _):
         cols = pl.ds(pl.multiple_of(c * LANES, LANES), LANES)
         weights = [
-            jnp.broadcast_to(depth_ref[k : k + 1, cols], (blocks, LANES)).astype(jnp.bfloat16)
+            jnp.broadcast_to(scales[k : k + 1, cols], (blocks, LANES)).astype(jnp.bfloat16)
             for k in range(taps)
         ]
         for g in groups:
@@ -233,23 +247,43 @@
         values = work[at, :]
         centred = values - jnp.mean(values, axis=-1, keepdims=True)
         rstd = lax.rsqrt(jnp.mean(centred * centred, axis=-1, keepdims=True) + EPSILON)
-        normed_ref[at, :] = (centred * rstd * gain_ref[...]).astype(jnp.bfloat16)
+        normed_ref[at, :] = (centred * rstd * scales[taps:, :]).astype(jnp.bfloat16)
         rstd_ref[at, :] = jnp.broadcast_to(rstd, (32, LANES))
         return 0
 
     lax.fori_loop(0, len(patches) * rows // 32, norm, 0)
 
 
-def own_kernel(steps, blocks, patches, weight, depth, gain, o0, o1, o2, o3, work, mask):
-    forward(steps, blocks, [patches], weight, depth, gain, work, mask, (o0, o1, o2, o3))
+def next_kernel(steps, blocks, patches, weight, scales, o0, o1, o2, o3, work, mask):
+    forward(steps, blocks, [patches], weight, scales, work, mask, (o0, o1, o2, o3))
+
+
+def first_kernel(
+    steps, blocks, patches, sub0, sub1, sub2, sub3, depth, gain,
+    o0, o1, o2, o3, weight, scales, work, mask, sems,
+):
+    me = lax.axis_index("fsdp")
+    deep = sub0.shape[0]
+    copies = [
+        pltpu.make_async_copy(
+            piece, weight.at[pl.ds(pl.multiple_of((me ^ k) * deep, TILE), deep), :], sems.at[k]
+        )
+        for k, piece in enumerate((sub0, sub1, sub2, sub3))
+    ]
+    for copy in copies:
+        copy.start()
+    scales[: depth.shape[0], :] = depth[...]
+    scales[depth.shape[0] :, :] = gain[...]
+    for copy in copies:
+        copy.wait()
+    forward(steps, blocks, [patches], weight, scales, work, mask, (o0, o1, o2, o3))
 
 
 def middle_kernel(steps, blocks, *refs):
-    patches, weight, depth, gain, rstd0, normed0 = refs[0:4], *refs[4:9]
-    cot0, pair, cot2, cot3, w_own, w2, w3, w2b, w3b, w_out_in = refs[9:19]
-    grads, scaled, hidden, masked, w_in = refs[19:23], *refs[23:27]
-    feat, normed, slope, means = refs[27:31]
-    work, mask, rstd, pre_grad, w_out, held, sems = refs[31:38]
+    patches, normed, rstds, gain = refs[0:4], refs[4:8], refs[8:12], refs[12]
+    cot0, pair, cot2, cot3, w_own, w2, w3, w2b, w3b, w_out_in = refs[13:23]
+    grads, scaled, hidden, masked, w_in, means = refs[23:27], *refs[27:32]
+    pre_grad, w_out, held, sems = refs[32:36]
     me = lax.axis_index("fsdp")
     parity = lax.rem(lax.axis_index("dp"), 2)
     rows = steps * blocks
@@ -273,15 +307,14 @@
         move(w3, w_in.at[rows_of(me ^ 3, parity, half), :]),
         move(w2b, w_in.at[rows_of(me ^ 2, 1 - parity, half), :]),
         move(w3b, w_in.at[rows_of(me ^ 3, 1 - parity, half), :]),
+    ]
+    later = [
         move(w_out_in, w_out),
         move(cot0, masked.at[:rows, :]),
         move(pair.at[:rows, :], masked.at[rows : 2 * rows, :]),
         move(cot2, masked.at[2 * rows : 3 * rows, :]),
         move(cot3, masked.at[3 * rows :, :]),
     ]
-    forward(
-        steps, blocks, patches[1:], weight, depth, gain, work, mask, (feat, normed, slope, rstd)
-    )
     for copy in coming:
         copy.wait()
     fine = jnp.broadcast_to(gain[...], (TILE, gain.shape[1]))
@@ -291,19 +324,20 @@
     share = 1.0 / gain.shape[1]
     for k in range(4):
         at = slice(k * rows, (k + 1) * rows)
-        tail = slice((k - 1) * rows, k * rows)
         counts = patches[k][rows:, :LANES].astype(jnp.float32)[:, :1]
         keep = jnp.concatenate([counts > t for t in range(steps)], axis=0)
+        pre = dot(normed[k][...], w_in[...], 1, 0)
+        for copy in later[:2] if k == 0 else later[k + 1 : k + 2]:
+            copy.wait()
         kept = jnp.where(keep, masked[at, :], jnp.zeros((), jnp.bfloat16))
         masked[at, :] = kept
-        pre = dot(normed0[...] if k == 0 else normed[tail, :], w_in[...], 1, 0)
         back = dot(kept, w_out[...], 1, 1)
         sigma = sigmoid(pre)
         swish = pre * sigma
         hidden[at, :] = swish.astype(jnp.bfloat16)
         grown = 0.5 * back * (sigma + swish * (1.0 - sigma))
         pre_grad[at, :] = grown.astype(jnp.bfloat16)
-        grown = grown * (rstd0[:, :1] if k == 0 else rstd[tail, :1])
+        grown = grown * rstds[k][:, :1]
         scaled[at, :] = grown.astype(jnp.bfloat16)
         for i, other in enumerate((pulled, pre)):
             mean = jnp.sum(grown * other, axis=-1, keepdims=True) * share
@@ -311,7 +345,7 @@
     leaving = []
     for k in (2, 3, 1, 0):
         cols = columns_of(me ^ k, high)
-        left = jnp.concatenate([normed0[:, cols], normed[:, cols]], axis=0)
+        left = jnp.concatenate([normed[j][:, cols] for j in range(4)], axis=0)
         held[k] = dot(left, pre_grad[...], 0, 0).astype(jnp.bfloat16)
         leaving.append(move(held.at[k], grads[k]))
     for copy in leaving:
@@ -319,8 +353,9 @@
 
 
 def backward_kernel(steps, blocks, *refs):
-    gain, scaled, w_in, masked, means, normed0, slope0, feat0, normed, slope, feat = refs[0:11]
-    taps_out, grad = refs[11:13]
+    gain, scaled, w_in, masked, means = refs[0:5]
+    normed, slope, feat = refs[5:9], refs[9:13], refs[13:17]
+    taps_out, grad, totals = refs[17:20]
     rows = steps * blocks
     for k in range(4):
         at = slice(k * rows, (k + 1) * rows)
@@ -330,52 +365,40 @@
         grad[at, :] = pulled.astype(jnp.bfloat16)
     taps = 2 * steps - 1
 
-    def column(c, _):
+    def column(k, c):
         cols = pl.ds(pl.multiple_of(c * LANES, LANES), LANES)
-
         inverse = jnp.broadcast_to(1.0 / gain[:, cols], (blocks, LANES)).astype(jnp.bfloat16)
-
-        def add(k, totals, held, near_normed, near_slope, near_feat):
-            def spots(group):
-                return [
-                    pl.ds(pl.multiple_of(group * rows + t * blocks, TILE), blocks)
-                    for t in range(steps)
-                ]
-
-            left = [
-                near_slope[here, cols]
-                * (
-                    grad[spot, cols]
-                    - means[0, spot, :]
-                    - near_normed[here, cols] * inverse * means[1, spot, :]
-                )
-                for spot, here in zip(spots(k), spots(held))
-            ]
-            right = [near_feat[here, cols] for here in spots(held)]
-            new = []
-            for tap in range(taps):
-                shift = tap - (steps - 1)
-                terms = [
-                    (left[t], right[t + shift]) for t in range(steps) if 0 <= t + shift < steps
-                ]
-                part = tree(terms, 0, len(terms)).astype(jnp.float32)
-                for half in range(0, blocks, HALF):
-                    piece = part[half : half + HALF, :]
-                    total = piece if half == 0 else total + piece
-                new.append(totals[tap] + total)
-            return tuple(new)
-
-        zero = jnp.zeros((HALF, LANES), jnp.float32)
-        totals = add(0, (zero,) * taps, 0, normed0, slope0, feat0)
-        totals = lax.fori_loop(
-            1, 4, lambda k, totals: add(k, totals, k - 1, normed, slope, feat), totals
-        )
+        here = [slice(t * blocks, (t + 1) * blocks) for t in range(steps)]
+        spots = [slice(k * rows + t * blocks, k * rows + (t + 1) * blocks) for t in range(steps)]
+        left = [
+            slope[k][at, cols]
+            * (
+                grad[spot, cols]
+                - means[0, spot, :]
+                - normed[k][at, cols] * inverse * means[1, spot, :]
+            )
+            for spot, at in zip(spots, here)
+        ]
+        right = [feat[k][at, cols] for at in here]
         for tap in range(taps):
-            taps_out[tap, :, cols] = jnp.sum(totals[tap], axis=0, keepdims=True)
-        taps_out[taps, :, cols] = jnp.zeros((1, LANES), jnp.float32)
+            shift = tap - (steps - 1)
+            terms = [(left[t], right[t + shift]) for t in range(steps) if 0 <= t + shift < steps]
+            part = tree(terms, 0, len(terms))
+            if k > 0:
+                part = part + totals[tap, :, cols]
+            if k < 3:
+                totals[tap, :, cols] = part
+            else:
+                taps_out[tap, :, cols] = jnp.sum(part.astype(jnp.float32), axis=0, keepdims=True)
+        if k == 3:
+            taps_out[taps, :, cols] = jnp.zeros((1, LANES), jnp.float32)
+
+    def step(c, _, k):
+        column(k, c)
         return 0
 
-    lax.fori_loop(0, gain.shape[1] // LANES, column, 0)
+    for k in range(4):
+        lax.fori_loop(0, gain.shape[1] // LANES, functools.partial(step, k=k), 0)
 
 
 def out_kernel(hidden, masked, out_ref, turned):
@@ -434,18 +457,8 @@
         jnp.broadcast_to(info[None], (n, home + 1)), "dp", split_axis=0, concat_axis=0, tiled=True
     )
 
-    weight = lax.all_gather(sub_weight, "fsdp", axis=0, tiled=True)
-    w_far = pltpu.with_memory_space_constraint(w_in, pltpu.HBM)
-    w2, w3 = pl.pallas_call(
-        functools.partial(cut_kernel, wide),
-        out_shape=(sds((deep // 2, wide), bf16),) * 2,
-        in_specs=[ANY],
-        out_specs=(ANY,) * 2,
-        scratch_shapes=[pltpu.VMEM((2, deep // 2, wide), bf16), dma((2, 2))],
-        compiler_params=params(),
-        cost_estimate=cost(1),
-    )(w_far)
-    w2, w3 = across(w2, 2), across(w3, 3)
+    w_far, w_out, sub_weight, depth_kernel = far(w_in, w_out, sub_weight, depth_kernel)
+    sub1, sub2 = across(sub_weight, 1), across(sub_weight, 2)
 
     block_shape = frames.shape[3:]
     held = frames[0, 0].reshape((cap, n) + block_shape) if split else frames[0, 0]
@@ -462,22 +475,43 @@
         cost_estimate=cost(2),
     )(order, infos, held)
     gain = norm_gain.reshape(1, width)
-    packed, w2, w3, gain, cot = lax.optimization_barrier(
-        (packed, w2, w3, gain, cotangent[0, 0])
+    packed, sub1, sub2, gain, cot, w_late = lax.optimization_barrier(
+        (packed, sub1, sub2, gain, cotangent[0, 0], w_far)
     )
     got = lax.all_to_all(packed, "dp", split_axis=0, concat_axis=0, tiled=True)
+    w_late = far(w_late)[0]
+    w2, w3 = pl.pallas_call(
+        functools.partial(cut_kernel, wide),
+        out_shape=(pltpu.HBM((deep // 2, wide), bf16),) * 2,
+        in_specs=[ANY],
+        out_specs=(ANY,) * 2,
+        scratch_shapes=[pltpu.VMEM((2, deep // 2, wide), bf16), dma((2, 2))],
+        compiler_params=params(),
+        cost_estimate=cost(1),
+    )(w_late)
+    w2, w3 = across(w2, 2), across(w3, 3)
+    sub_rows = sub_weight.shape[0]
     cot0, pair = pl.pallas_call(
         functools.partial(prepare_kernel, blocks, steps, wide),
-        out_shape=(sds((rows, width), bf16), sds((rows + deep // 2, width), bf16)),
+        out_shape=(
+            pltpu.HBM((rows, width), bf16),
+            pltpu.HBM((rows + deep // 2, width), bf16),
+        ),
         in_specs=[VMEM, ANY],
-        out_specs=(VMEM,) * 2,
-        scratch_shapes=[pltpu.VMEM((rows * width // LANES, LANES), f32), dma((2,))],
+        out_specs=(ANY,) * 2,
+        scratch_shapes=[
+            pltpu.VMEM((rows, width), bf16),
+            pltpu.VMEM((rows + deep // 2, width), bf16),
+            pltpu.VMEM((rows * width // LANES, LANES), f32),
+            dma((5,)),
+        ],
         compiler_params=params(),
         cost_estimate=cost(2),
-    )(cot, w_far)
+    )(cot, w_late)
+    sub3 = across(sub2, 1)
     cot2, pair = across(cot0, 2), across(pair, 1)
+    got, sub3, w2, w3 = lax.optimization_barrier((got, sub3, w2, w3))
     w2b, w3b = across_dp(w2, 1), across_dp(w3, 1)
-    got, w2b = lax.optimization_barrier((got, w2b))
     patches0 = pl.pallas_call(
         functools.partial(unpack_kernel, n, cap, blocks, steps),
         out_shape=sds((rows + blocks, block_shape[0] // steps * LANES), bf16),
@@ -493,73 +527,80 @@
     )(order, infos, got.reshape((n * cap,) + block_shape))
     patches = [patches0, across(patches0, 1), across(patches0, 2)]
 
-    def kept(count):
-        return (
-            pltpu.VMEM((count * rows, width), bf16),
-            pltpu.VMEM((count * rows, width), bf16),
-            pltpu.VMEM((count * rows, width), bf16),
-            pltpu.VMEM((count * rows, LANES), f32),
-        )
-
-    feat0, normed0, slope0, rstd0 = pl.pallas_call(
-        functools.partial(own_kernel, steps, blocks),
-        out_shape=kept(1),
-        in_specs=[VMEM] * 4,
-        out_specs=(VMEM,) * 4,
-        scratch_shapes=[pltpu.VMEM((rows, width), f32), pltpu.VMEM((rows, LANES), f32)],
+    kept = (
+        pltpu.VMEM((rows, width), bf16),
+        pltpu.VMEM((rows, width), bf16),
+        pltpu.VMEM((rows, width), bf16),
+        pltpu.VMEM((rows, LANES), f32),
+    )
+    work = [pltpu.VMEM((rows, width), f32), pltpu.VMEM((rows, LANES), f32)]
+    *first, weight, scales = pl.pallas_call(
+        functools.partial(first_kernel, steps, blocks),
+        out_shape=(
+            *kept,
+            pltpu.VMEM((4 * sub_rows, width), bf16),
+            pltpu.VMEM((2 * steps, width), f32),
+        ),
+        in_specs=[VMEM] + [ANY] * 4 + [VMEM] * 2,
+        out_specs=(VMEM,) * 6,
+        scratch_shapes=[*work, dma((4,))],
         compiler_params=params(),
         cost_estimate=cost(4),
-    )(*near(patches0), weight, depth_kernel, gain)
-    feat0, cot_relay, patch_relay, w3b = lax.optimization_barrier(
-        (feat0, cot2, patches[2], w3b)
-    )
+    )(*near(patches0), sub_weight, *far(sub1, sub2, sub3), depth_kernel, gain)
+    first[0], cot_relay, patch_relay = lax.optimization_barrier((first[0], cot2, patches[2]))
     cot3 = across(cot_relay, 1)
     patches.append(across(patch_relay, 1))
-    (
-        g0, g1, g2, g3, scaled, hidden, masked, w_slice, feat, normed, slope, means
-    ) = pl.pallas_call(
+    following = pl.pallas_call(
+        functools.partial(next_kernel, steps, blocks),
+        out_shape=kept,
+        in_specs=[VMEM] * 3,
+        out_specs=(VMEM,) * 4,
+        scratch_shapes=work,
+        compiler_params=params(),
+        cost_estimate=cost(4),
+    )
+    groups = [first]
+    for k in (1, 2, 3):
+        groups.append(following(*near(patches[k], weight, scales)))
+    feats, normeds, slopes, rstds = [near(*arrays) for arrays in zip(*groups)]
+    g0, g1, g2, g3, scaled, hidden, masked, w_slice, means = pl.pallas_call(
         functools.partial(middle_kernel, steps, blocks),
         out_shape=(
-            *[sds((deep, wide), bf16)] * 4,
+            *[pltpu.HBM((deep, wide), bf16)] * 4,
             pltpu.VMEM((4 * rows, wide), bf16),
             pltpu.VMEM((4 * rows, wide), bf16),
             pltpu.VMEM((4 * rows, width), bf16),
             pltpu.VMEM((width, wide), bf16),
-            *kept(3)[:3],
             pltpu.VMEM((2, 4 * rows, LANES), bf16),
         ),
-        in_specs=[VMEM] * 9 + [ANY] * 10,
-        out_specs=(ANY,) * 4 + (VMEM,) * 8,
+        in_specs=[VMEM] * 13 + [ANY] * 10,
+        out_specs=(ANY,) * 4 + (VMEM,) * 5,
         scratch_shapes=[
-            pltpu.VMEM((3 * rows, width), f32),
-            pltpu.VMEM((3 * rows, LANES), f32),
-            pltpu.VMEM((3 * rows, LANES), f32),
             pltpu.VMEM((4 * rows, wide), bf16),
             pltpu.VMEM((wide, width), bf16),
             pltpu.VMEM((4, deep, wide), bf16),
             dma((16,)),
         ],
-        compiler_params=params(28),
-        cost_estimate=cost(20),
+        compiler_params=params(24),
+        cost_estimate=cost(12),
     )(
-        *near(*patches), weight, depth_kernel, gain, *near(rstd0, normed0),
-        cot0, pair, cot2, cot3, w_far, w2, w3, w2b, w3b, w_out,
-    )
-    g1, g2, g3 = across(g1, 1), across(g2, 2), across(g3, 3)
+        *patches, *normeds, *rstds, gain,
+        *far(cot0, pair, cot2, cot3), w_far, *far(w2, w3, w2b, w3b), w_out,
+    )
+    g3, g2, g1 = across(g3, 3), across(g2, 2), across(g1, 1)
 
     taps = pl.pallas_call(
         functools.partial(backward_kernel, steps, blocks),
         out_shape=sds((2 * steps, 1, width), f32),
-        in_specs=[VMEM] * 11,
+        in_specs=[VMEM] * 17,
         out_specs=VMEM,
-        scratch_shapes=[pltpu.VMEM((4 * rows, width), bf16)],
+        scratch_shapes=[
+            pltpu.VMEM((4 * rows, width), bf16),
+            pltpu.VMEM((2 * steps - 1, blocks, width), bf16),
+        ],
         compiler_params=params(),
         cost_estimate=cost(13),
-    )(
-        *near(
-            gain, scaled, w_slice, masked, means, normed0, slope0, feat0, normed, slope, feat
-        )
-    )
+    )(gain, *near(scaled, w_slice, masked, means), *normeds, *slopes, *feats)
     taps, g2, hidden = lax.optimization_barrier((taps, g2, hidden))
 
     every = ("dp", "fsdp")
@@ -591,7 +632,7 @@
         scratch_shapes=[pltpu.VMEM((4, deep, wide), bf16), dma((2, 4))],
         compiler_params=params(),
         cost_estimate=cost(2),
-    )(g0, g1, g2, g3)
+    )(*far(g0, g1, g2, g3))
     return (grad_in[None], grad_out[None], kernel_grad)
 
 

time: 154 us -> 144 us (0.935)
  between operations: 14.9 us -> 1.61 us
  waiting for transfers between devices: 31.3 us -> 41.8 us
  local copies, waits for them, and re-layouts: 18.5 us -> 9.08 us
  Pallas kernels: 55.5 us -> 58 us
    ppermute x11 -> x14, waiting for transfers between devices: 10.5 us -> 34.7 us  [across(): return lax.ppermute(value, 'fsdp', [(i, i ^ k) for i in range(n)])]
    pallas_call x2 -> x5, Pallas kernels: 5.44 us -> 21.2 us  [the longest x3 12.8 us: on_device(): groups.append(following(*near(patches[k], weight, scales)))]
    pallas_call x1, Pallas kernels: 24.5 us -> 12.1 us  [on_device(): pl.pallas_call(functools.partial(middle_kernel, steps, blocks), out_shape...]
    ppermute x2, waiting for transfers between devices: 11.8 us -> 0.01 us  [across_dp(): return lax.ppermute(value, 'dp', [(i, i ^ k) for i in range(n)])]
    unnamed x57 -> x37, local copies, waits for them, and re-layouts: 17.1 us -> 6.97 us
    all_to_all x1, starting transfers between devices: 6.58 us -> 3.56 us  [on_device(): got = lax.all_to_all(packed, 'dp', split_axis=0, concat_axis=0, tiled=True)]
    all_to_all x1, starting transfers between devices: 4.64 us -> 6.79 us  [on_device(): lax.all_to_all(taps.reshape(devices, 1, -1), every, split_axis=0, concat_...]
    ppermute x11 -> x14, starting transfers between devices: 11.6 us -> 11.7 us  [across(): return lax.ppermute(value, 'fsdp', [(i, i ^ k) for i in range(n)])]
  transfers between devices with their start and end apart: 18 -> 20, of which waited for: 10 -> 9; matrix products, arithmetic and copies ran while one was open for 1% -> 2% of each run, Pallas kernels for 20% -> 32%
where the time goes in v4:
time: 144 us; the launch traced here: 143 us
  Pallas kernels  58 us (40%)
  waiting for transfers between devices  41.8 us (29%)
  starting transfers between devices  31.8 us (22%)
  local copies, waits for them, and re-layouts  9.08 us (6%)
  between operations  1.61 us (1%)
    ppermute x14, waiting for transfers between devices, across(): return lax.ppermute(value, 'fsdp', [(i, i ^ k) for i in range(n)])  34.7 us
    pallas_call x3, Pallas kernels, on_device(): groups.append(following(*near(patches[k], weight, scales)))  12.8 us
    pallas_call x1, Pallas kernels, on_device(): pl.pallas_call(functools.partial(backward_kernel, steps, blocks), out_sha...  12.2 us
    pallas_call x1, Pallas kernels, on_device(): pl.pallas_call(functools.partial(middle_kernel, steps, blocks), out_shape...  12.1 us
    ppermute x14, starting transfers between devices, across(): return lax.ppermute(value, 'fsdp', [(i, i ^ k) for i in range(n)])  11.7 us
    unnamed x37, local copies, waits for them, and re-layouts  6.97 us
    all_to_all x1, starting transfers between devices, on_device(): lax.all_to_all(taps.reshape(devices, 1, -1), every, split_axis=0, concat_...  6.79 us
    pallas_call x1, Pallas kernels, on_device(): pl.pallas_call(functools.partial(first_kernel, steps, blocks), out_shape=...  6.54 us
  transfers between devices with their start and end apart: 20, of which 9 were waited for; matrix products, arithmetic and copies ran while one was open for 2% of the time, Pallas kernels for 32%

profile of v4, /device:TPU:1, one launch (start us, length us, event | category | flops | bytes accessed | tf_op | source)
XLA Modules:
  0.0 143.1 jit_solution(12442947106069803699)
XLA Ops:
  0.8 2.7 %collective-permute-start.1 = (bf16[128,1536]{1,0:T(8,128)(2,1)}, bf16[128,1536]{1,0:T(8,128)(2,1)}, u32[]{:S(2)}, u32[]{:S(2)}) collective-permute-start(bf16[128,1536]{1,0:T(8,128)(2,1)} %sub0.1), channel_id=1, source_target_pairs={{0,2},{1,3},{2,0},{3,1},{4,6},{5,7},{6,4},{7,5},{8,10},{9,11},{10,... | collective-permute-start | bytes 1179656 | tf_op jit(solution)/shard_map/ppermute | solution.py:54
  4.1 0.7 pad_add_fusion
  4.8 0.6 broadcast_in_dim.20
  5.4 5.5 %all-to-all-start = ((s32[8,1,49]{2,1,0:T(1,128)}), s32[8,1,49]{2,1,0:T(1,128)S(1)}, u32[]{:S(2)}, u32[]{:S(2)}) async-start(s32[8,1,49]{2,1,0:T(1,128)} %broadcast_in_dim.20), calls=%async_computation | async-start | bytes 8192 | tf_op jit(solution)/shard_map/all_to_all | solution.py:456
  11.0 0.7 reshape.35.gain.refs_12_.refs_0_
  11.7 4.5 %all-to-all-done = s32[8,1,49]{2,1,0:T(1,128)S(1)} async-done(((s32[8,1,49]{2,1,0:T(1,128)}), s32[8,1,49]{2,1,0:T(1,128)S(1)}, u32[]{:S(2)}, u32[]{:S(2)}) %all-to-all-start) | async-done | bytes 1600 | tf_op jit(solution)/shard_map/all_to_all | solution.py:456
  16.2 1.1 copy-done.2
  17.3 0.7 copy-done.4
  18.0 1.8 %shard_map.121 = bf16[8,6,64,128]{3,2,1,0:T(8,128)(2,1)} custom-call(s32[1,8]{1,0:T(1,128)S(1)} %copy-done.4, s32[8,49]{1,0:T(8,128)S(1)} %bitcast.15, bf16[6,8,64,128]{3,2,1,0:T(8,128)(2,1)S(1)} %bitcast.13), custom_call_target="tpu_custom_call" | custom-call | bytes 7200000 | tf_op jit(solution)/shard_map/pallas_call | solution.py:465
  19.8 3.6 %all-to-all-start.1 = ((bf16[8,6,64,128]{3,2,1,0:T(8,128)(2,1)}), bf16[8,6,64,128]{3,2,1,0:T(8,128)(2,1)S(1)}, u32[]{:S(2)}, u32[]{:S(2)}) async-start(bf16[8,6,64,128]{3,2,1,0:T(8,128)(2,1)} %shard_map.121), calls=%async_computation.1 | async-start | bytes 1572864 | tf_op jit(solution)/shard_map/all_to_all | solution.py:481
  23.4 2.4 %shard_map.125 = (bf16[256,1536]{1,0:T(8,128)(2,1)}, bf16[448,1536]{1,0:T(8,128)(2,1)}) custom-call(bf16[16,16,1536]{2,1,0:T(8,128)(2,1)S(1)} %bitcast.14, bf16[384,3072]{1,0:T(8,128)(2,1)} %refs_17_.1), custom_call_target="tpu_custom_call" | custom-call | bytes 7200000 | tf_op jit(solution)/shard_map/pallas_call | solution.py:494
  25.9 0.3 collective-permute-start.7
  26.2 2.1 %collective-permute-start.2 = (bf16[128,1536]{1,0:T(8,128)(2,1)}, bf16[128,1536]{1,0:T(8,128)(2,1)S(1)}, u32[]{:S(2)}, u32[]{:S(2)}) collective-permute-start(bf16[128,1536]{1,0:T(8,128)(2,1)} %collective-permute-done.1.sub2), channel_id=1, source_target_pairs={{0,1},{1,0},{2,3},{3,2},{4,5},{5,4},{6,7},{7,6},{8,9},{9,8},{10,11... | collective-permute-start | bytes 1179656 | tf_op jit(solution)/shard_map/ppermute | solution.py:54
  28.2 1.8 %shard_map.122 = (bf16[192,768]{1,0:T(8,128)(2,1)}, bf16[192,768]{1,0:T(8,128)(2,1)}) custom-call(bf16[384,3072]{1,0:T(8,128)(2,1)} %refs_17_.1), custom_call_target="tpu_custom_call" | custom-call | bytes 3600000 | tf_op jit(solution)/shard_map/pallas_call | solution.py:483
  30.1 1.3 collective-permute-start.3
  31.4 0.9 collective-permute-start.4
  32.3 17.5 %collective-permute-done.3.refs_18_ = bf16[192,768]{1,0:T(8,128)(2,1)S(1)} collective-permute-done((bf16[192,768]{1,0:T(8,128)(2,1)}, bf16[192,768]{1,0:T(8,128)(2,1)S(1)}, u32[]{:S(2)}, u32[]{:S(2)}) %collective-permute-start.3) | collective-permute-done | bytes 294944 | tf_op jit(solution)/shard_map/ppermute | solution.py:54
  49.7 8.3 %collective-permute-done.4.refs_19_ = bf16[192,768]{1,0:T(8,128)(2,1)S(1)} collective-permute-done((bf16[192,768]{1,0:T(8,128)(2,1)}, bf16[192,768]{1,0:T(8,128)(2,1)S(1)}, u32[]{:S(2)}, u32[]{:S(2)}) %collective-permute-start.4) | collective-permute-done | bytes 294944 | tf_op jit(solution)/shard_map/ppermute | solution.py:54
  58.1 0.7 copy-done.14
  58.8 1.7 %shard_map.123.patches.refs_0_ = bf16[272,512]{1,0:T(8,128)(2,1)S(1)} custom-call(s32[1,8]{1,0:T(1,128)S(1)} %copy-done.5, s32[8,49]{1,0:T(8,128)S(1)} %bitcast.16, bf16[48,64,128]{2,1,0:T(8,128)(2,1)S(1)} %bitcast.12), custom_call_target="tpu_custom_call" | custom-call | bytes 7200000 | tf_op jit(solution)/shard_map/pallas_call | solution.py:515
  60.6 0.3 collective-permute-start.6
  60.9 6.5 %shard_map.124 = (bf16[256,1536]{1,0:T(8,128)(2,1)S(1)}, bf16[256,1536]{1,0:T(8,128)(2,1)S(1)}, bf16[256,1536]{1,0:T(8,128)(2,1)S(1)}, f32[256,128]{1,0:T(8,128)...) custom-call(bf16[272,512]{1,0:T(8,128)(2,1)S(1)} %shard_map.123.patches.refs_0_, bf16[128,1536]{1,0:T(8,128)(2,1)} %sub0.1, ...), custom_call_target="tpu_custom_call" | custom-call | bytes 14400000 | tf_op jit(solution)/shard_map/pallas_call | solution.py:537
  67.5 0.9 collective-permute-done.6.patches.refs_2_
  68.3 0.5 collective-permute-start.5
  68.8 1.3 collective-permute-start.11
  70.3 0.7 collective-permute-done.5.patches.refs_1_
  71.1 4.2 %shard_map.127 = (bf16[256,1536]{1,0:T(8,128)(2,1)S(1)}, bf16[256,1536]{1,0:T(8,128)(2,1)S(1)}, bf16[256,1536]{1,0:T(8,128)(2,1)S(1)}, f32[256,128]{1,0:T(8,128)S(1)}) custom-call(bf16[272,512]{1,0:T(8,128)(2,1)S(1)} %collective-permute-done.6.patches.refs_2_, bf16[512,1536]{1,0:T(8,128)(2,1)S(1)} %get-tuple-element.66.weight, ...), custom_call_target="tpu_custom_call" | custom-call | bytes 14400000 | tf_op jit(solution)/shard_map/pallas_call | solution.py:564
  75.4 4.2 %shard_map.126 = (bf16[256,1536]{1,0:T(8,128)(2,1)S(1)}, bf16[256,1536]{1,0:T(8,128)(2,1)S(1)}, bf16[256,1536]{1,0:T(8,128)(2,1)S(1)}, f32[256,128]{1,0:T(8,128)S(1)}) custom-call(bf16[272,512]{1,0:T(8,128)(2,1)S(1)} %collective-permute-done.5.patches.refs_1_, bf16[512,1536]{1,0:T(8,128)(2,1)S(1)} %get-tuple-element.66.weight, ...), custom_call_target="tpu_custom_call" | custom-call | bytes 14400000 | tf_op jit(solution)/shard_map/pallas_call | solution.py:564
  79.6 4.4 %shard_map.128 = (bf16[256,1536]{1,0:T(8,128)(2,1)S(1)}, bf16[256,1536]{1,0:T(8,128)(2,1)S(1)}, bf16[256,1536]{1,0:T(8,128)(2,1)S(1)}, f32[256,128]{1,0:T(8,128)S(1)}) custom-call(bf16[272,512]{1,0:T(8,128)(2,1)S(1)} %collective-permute-done.8.patches.refs_3_, bf16[512,1536]{1,0:T(8,128)(2,1)S(1)} %get-tuple-element.66.weight, ...), custom_call_target="tpu_custom_call" | custom-call | bytes 14400000 | tf_op jit(solution)/shard_map/pallas_call | solution.py:564
  84.1 1.0 copy-done.6
  85.3 0.2 copy-done.8
  85.5 12.1 %shard_map.129 = (bf16[384,768]{1,0:T(8,128)(2,1)}, bf16[384,768]{1,0:T(8,128)(2,1)}, bf16[384,768]{1,0:T(8,128)(2,1)}, bf16[384,768]{1,0:T(8,128)(2,1)}, bf16[1...) custom-call(bf16[272,512]{1,0:T(8,128)(2,1)S(1)} %shard_map.123.patc, ...), custom_call_target="tpu_custom_call" | custom-call | bytes 43200000 | tf_op jit(solution)/shard_map/pallas_call | solution.py:566
  97.6 1.6 %collective-permute-start.14 = (bf16[384,768]{1,0:T(8,128)(2,1)}, bf16[384,768]{1,0:T(8,128)(2,1)S(1)}, u32[]{:S(2)}, u32[]{:S(2)}) collective-permute-start(bf16[384,768]{1,0:T(8,128)(2,1)} %get-tuple-element.93), channel_id=1, source_target_pairs={{0,2},{1,3},{2,0},{3,1},{4,6},{5,7},{6,4},{7,5},{8,10},{9,11},{10,... | collective-permute-start | bytes 1769480 | tf_op jit(solution)/shard_map/ppermute | solution.py:54
  99.2 12.2 %shard_map.130 = f32[32,1,1536]{2,1,0:T(1,128)} custom-call(f32[1,1536]{1,0:T(1,128)S(1)} %reshape.35.gain.refs_12_.refs_0_, bf16[1024,768]{1,0:T(8,128)(2,1)S(1)} %get-tuple-element.81.refs_1_, bf16[1536,768]{1,0:T(8,128)(2,1)S(1)} %get-tuple-element.82.refs_2_, bf16[1024,1536]{1,0:T(8,128)(2,1)S(1)} %get-tuple-element.83.refs_3_.masked, ...), custom_call_target="tpu_custom_call" | custom-call | bytes 46800000 | tf_op jit(solution)/shard_map/pallas_call | solution.py:592
  111.4 1.1 collective-permute-done.14.refs_2_
  112.6 0.8 copy-done.9
  113.4 6.8 %all-to-all-start.2 = ((f32[32,1,1536]{2,1,0:T(1,128)}), f32[32,1,1536]{2,1,0:T(1,128)S(1)}, u32[]{:S(2)}, u32[]{:S(2)}) async-start(f32[32,1,1536]{2,1,0:T(1,128)} %shard_map.130), calls=%async_computation.2 | async-start | bytes 393216 | tf_op jit(solution)/shard_map/all_to_all | solution.py:608
  120.2 0.3 collective-permute-start.13
  120.5 1.5 %collective-permute-start.15 = (bf16[384,768]{1,0:T(8,128)(2,1)}, bf16[384,768]{1,0:T(8,128)(2,1)}, u32[]{:S(2)}, u32[]{:S(2)}) collective-permute-start(bf16[384,768]{1,0:T(8,128)(2,1)} %get-tuple-element.96), channel_id=1, source_target_pairs={{0,3},{1,2},{2,1},{3,0},{4,7},{5,6},{6,5},{7,4},{8,11},{9,10},{10,... | collective-permute-start | bytes 1769480 | tf_op jit(solution)/shard_map/ppermute | solution.py:54
  122.1 1.4 copy-done.1
  123.5 4.0 %shard_map.132 = bf16[768,1536]{1,0:T(8,128)(2,1)} custom-call(bf16[1024,768]{1,0:T(8,128)(2,1)S(1)} %copy-done.1, bf16[1024,1536]{1,0:T(8,128)(2,1)S(1)} %get-tuple-element.83.refs_3_.masked), custom_call_target="tpu_custom_call" | custom-call | bytes 14400000 | tf_op jit(solution)/shard_map/pallas_call | solution.py:612
  127.5 2.0 %all-to-all-done.2 = f32[32,1,1536]{2,1,0:T(1,128)S(1)} async-done(((f32[32,1,1536]{2,1,0:T(1,128)}), f32[32,1,1536]{2,1,0:T(1,128)S(1)}, u32[]{:S(2)}, u32[]{:S(2)}) %all-to-all-start.2) | async-done | bytes 196640 | tf_op jit(solution)/shard_map/all_to_all | solution.py:608
  129.7 0.8 broadcast_in_dim.24
  130.5 2.7 %all-to-all-start.3 = ((f32[32,1,1536]{2,1,0:T(1,128)}), f32[32,1,1536]{2,1,0:T(1,128)S(1)}, u32[]{:S(2)}, u32[]{:S(2)}) async-start(f32[32,1,1536]{2,1,0:T(1,128)} %broadcast_in_dim.24), calls=%async_computation.3 | async-start | bytes 393216 | tf_op jit(solution)/shard_map/all_to_all | solution.py:622
  133.2 6.2 %collective-permute-done.15.refs_3_ = bf16[384,768]{1,0:T(8,128)(2,1)} collective-permute-done((bf16[384,768]{1,0:T(8,128)(2,1)}, bf16[384,768]{1,0:T(8,128)(2,1)}, u32[]{:S(2)}, u32[]{:S(2)}) %collective-permute-start.15) | collective-permute-done | bytes 589856 | tf_op jit(solution)/shard_map/ppermute | solution.py:54
  139.4 2.5 %shard_map.131 = bf16[384,3072]{1,0:T(8,128)(2,1)} custom-call(bf16[384,768]{1,0:T(8,128)(2,1)} %get-tuple-element.79.refs_0_, bf16[384,768]{1,0:T(8,128)(2,1)} %collective-permute-done.13.refs_1_, bf16[384,768]{1,0:T(8,128)(2,1)} %copy-done.9, bf16[384,768]{1,0:T(8,128)(2,1)} %collective-permute-done.15.refs_3_), custom_call_target="tpu_custom_call" | custom-call | bytes 7200000 | tf_op jit(solution)/shard_map/pallas_call | solution.py:627
  141.9 0.5 all-to-all-done.3
  142.4 0.7 copy.15
  (50 shorter events, 0.9 us)
Async XLA Ops:
  0.6 19.2 %collective-permute-start = (bf16[128,1536]{1,0:T(8,128)(2,1)}, bf16[128,1536]{1,0:T(8,128)(2,1)S(1)}, u32[]{:S(2)}, u32[]{:S(2)}) collective-permute-start(bf16[128,1536]{1,0:T(8,128)(2,1)} %sub0.1), channel_id=1, source_target_pairs={{0,1},{1,0},{2,3},{3,2},{4,5},{5,4},{6,7},{7,6},{8,9},{9,8},{10,11... | collective-permute-start | bytes 1179656 | tf_op jit(solution)/shard_map/ppermute | solution.py:54
  0.8 19.1 %collective-permute-start.1 = (bf16[128,1536]{1,0:T(8,128)(2,1)}, bf16[128,1536]{1,0:T(8,128)(2,1)}, u32[]{:S(2)}, u32[]{:S(2)}) collective-permute-start(bf16[128,1536]{1,0:T(8,128)(2,1)} %sub0.1), channel_id=1, source_target_pairs={{0,2},{1,3},{2,0},{3,1},{4,6},{5,7},{6,4},{7,5},{8,10},{9,11},{10,... | collective-permute-start | bytes 1179656 | tf_op jit(solution)/shard_map/ppermute | solution.py:54
  5.4 10.8 %all-to-all-start = ((s32[8,1,49]{2,1,0:T(1,128)}), s32[8,1,49]{2,1,0:T(1,128)S(1)}, u32[]{:S(2)}, u32[]{:S(2)}) async-start(s32[8,1,49]{2,1,0:T(1,128)} %broadcast_in_dim.20), calls=%async_computation | async-start | bytes 8192 | tf_op jit(solution)/shard_map/all_to_all | solution.py:456
  16.2 1.1 copy-start.2
  17.3 0.7 copy-start.4
  18.0 5.4 %copy-start.3 = (bf16[1,1,16,16,1536]{4,3,2,1,0:T(8,128)(2,1)S(1)}, bf16[1,1,16,16,1536]{4,3,2,1,0:T(8,128)(2,1)}, u32[]{:S(2)}) copy-start(bf16[1,1,16,16,1536]{4,3,2,1,0:T(8,128)(2,1)} %param.14) | copy-start | bytes 2359300
  19.8 6.1 %copy-start.10 = (bf16[128,1536]{1,0:T(8,128)(2,1)}, bf16[128,1536]{1,0:T(8,128)(2,1)S(1)}, u32[]{:S(2)}) copy-start(bf16[128,1536]{1,0:T(8,128)(2,1)S(1)} %collective-permute-done.sub1) | copy-start | bytes 1179652
  19.8 39.0 %all-to-all-start.1 = ((bf16[8,6,64,128]{3,2,1,0:T(8,128)(2,1)}), bf16[8,6,64,128]{3,2,1,0:T(8,128)(2,1)S(1)}, u32[]{:S(2)}, u32[]{:S(2)}) async-start(bf16[8,6,64,128]{3,2,1,0:T(8,128)(2,1)} %shard_map.121), calls=%async_computation.1 | async-start | bytes 1572864 | tf_op jit(solution)/shard_map/all_to_all | solution.py:481
  23.4 35.4 %copy-start.5 = (s32[1,8]{1,0:T(1,128)S(1)}, s32[1,8]{1,0:T(1,128)}, u32[]{:S(2)}) copy-start(s32[1,8]{1,0:T(1,128)} %order_ref.3) | copy-start | bytes 100
  25.9 41.6 %collective-permute-start.7 = (bf16[256,1536]{1,0:T(8,128)(2,1)}, bf16[256,1536]{1,0:T(8,128)(2,1)S(1)}, u32[]{:S(2)}, u32[]{:S(2)}) collective-permute-start(bf16[256,1536]{1,0:T(8,128)(2,1)} %get-tuple-element.63.refs_13_), channel_id=1, source_target_pairs={{0,2},{1,3},{2,0},{3,1},{4,6},{5,7},{6,4},{7,5},{8,10},{9,11},{10,... | collective-permute-start | bytes 2359304 | tf_op jit(solution)/shard_map/ppermute | solution.py:54
  26.2 32.6 %collective-permute-start.2 = (bf16[128,1536]{1,0:T(8,128)(2,1)}, bf16[128,1536]{1,0:T(8,128)(2,1)S(1)}, u32[]{:S(2)}, u32[]{:S(2)}) collective-permute-start(bf16[128,1536]{1,0:T(8,128)(2,1)} %collective-permute-done.1.sub2), channel_id=1, source_target_pairs={{0,1},{1,0},{2,3},{3,2},{4,5},{5,4},{6,7},{7,6},{8,9},{9,8},{10,11... | collective-permute-start | bytes 1179656 | tf_op jit(solution)/shard_map/ppermute | solution.py:54
  28.2 55.8 %collective-permute-start.9 = (bf16[448,1536]{1,0:T(8,128)(2,1)}, bf16[448,1536]{1,0:T(8,128)(2,1)S(1)}, u32[]{:S(2)}, u32[]{:S(2)}) collective-permute-start(bf16[448,1536]{1,0:T(8,128)(2,1)} %get-tuple-element.75), channel_id=1, source_target_pairs={{0,1},{1,0},{2,3},{3,2},{4,5},{5,4},{6,7},{7,6},{8,9},{9,8},{10,11... | collective-permute-start | bytes 4128776 | tf_op jit(solution)/shard_map/ppermute | solution.py:54
  30.1 19.7 %collective-permute-start.3 = (bf16[192,768]{1,0:T(8,128)(2,1)}, bf16[192,768]{1,0:T(8,128)(2,1)S(1)}, u32[]{:S(2)}, u32[]{:S(2)}) collective-permute-start(bf16[192,768]{1,0:T(8,128)(2,1)} %get-tuple-element.55), channel_id=1, source_target_pairs={{0,2},{1,3},{2,0},{3,1},{4,6},{5,7},{6,4},{7,5},{8,10},{9,11},{10,... | collective-permute-start | bytes 884744 | tf_op jit(solution)/shard_map/ppermute | solution.py:54
  31.4 26.7 %collective-permute-start.4 = (bf16[192,768]{1,0:T(8,128)(2,1)}, bf16[192,768]{1,0:T(8,128)(2,1)S(1)}, u32[]{:S(2)}, u32[]{:S(2)}) collective-permute-start(bf16[192,768]{1,0:T(8,128)(2,1)} %get-tuple-element.56), channel_id=1, source_target_pairs={{0,3},{1,2},{2,1},{3,0},{4,7},{5,6},{6,5},{7,4},{8,11},{9,10},{10,... | collective-permute-start | bytes 884744 | tf_op jit(solution)/shard_map/ppermute | solution.py:54
  49.7 8.3 %copy-start.12 = (bf16[192,768]{1,0:T(8,128)(2,1)}, bf16[192,768]{1,0:T(8,128)(2,1)S(1)}, u32[]{:S(2)}) copy-start(bf16[192,768]{1,0:T(8,128)(2,1)S(1)} %collective-permute-done.3.refs_18_) | copy-start | bytes 884740
  58.1 0.7 copy-start.14
  58.8 2.1 %copy-start.11 = (bf16[128,1536]{1,0:T(8,128)(2,1)}, bf16[128,1536]{1,0:T(8,128)(2,1)S(1)}, u32[]{:S(2)}) copy-start(bf16[128,1536]{1,0:T(8,128)(2,1)S(1)} %collective-permute-done.2.sub3) | copy-start | bytes 1179652
  58.8 10.0 %copy-start.13 = (bf16[192,768]{1,0:T(8,128)(2,1)S(1)}, bf16[192,768]{1,0:T(8,128)(2,1)}, u32[]{:S(2)}) copy-start(bf16[192,768]{1,0:T(8,128)(2,1)} %copy-done.12) | copy-start | bytes 884740
  58.8 11.4 %copy-start.15 = (bf16[192,768]{1,0:T(8,128)(2,1)S(1)}, bf16[192,768]{1,0:T(8,128)(2,1)}, u32[]{:S(2)}) copy-start(bf16[192,768]{1,0:T(8,128)(2,1)} %copy-done.14) | copy-start | bytes 884740
  60.6 7.7 %collective-permute-start.6 = (bf16[272,512]{1,0:T(8,128)(2,1)S(1)}, bf16[272,512]{1,0:T(8,128)(2,1)S(1)}, u32[]{:S(2)}, u32[]{:S(2)}) collective-permute-start(bf16[272,512]{1,0:T(8,128)(2,1)S(1)} %shard_map.123.patches.refs_0_), channel_id=1, source_target_pairs={{0,2},{1,3},{2,0},{3,1},{4,6},{5,7},{6,4},{7,5},{8,10},{9,11},{10,... | collective-permute-start | bytes 835592 | tf_op jit(solution)/shard_map/ppermute | solution.py:54
  67.4 16.5 %copy-start.7 = (bf16[256,1536]{1,0:T(8,128)(2,1)}, bf16[256,1536]{1,0:T(8,128)(2,1)S(1)}, u32[]{:S(2)}) copy-start(bf16[256,1536]{1,0:T(8,128)(2,1)S(1)} %collective-permute-done.7.refs_15_) | copy-start | bytes 2359300
  68.3 15.7 %collective-permute-start.10 = (bf16[256,1536]{1,0:T(8,128)(2,1)S(1)}, bf16[256,1536]{1,0:T(8,128)(2,1)S(1)}, u32[]{:S(2)}, u32[]{:S(2)}) collective-permute-start(bf16[256,1536]{1,0:T(8,128)(2,1)S(1)} %collective-permute-done.7.refs_15_), channel_id=1, source_target_pairs={{0,1},{1,0},{2,3},{3,2},{4,5},{5,4},{6,7},{7,6},{8,9},{9,8},{10,11... | collective-permute-start | bytes 2359304 | tf_op jit(solution)/shard_map/ppermute | solution.py:54
  68.3 2.7 %collective-permute-start.5 = (bf16[272,512]{1,0:T(8,128)(2,1)S(1)}, bf16[272,512]{1,0:T(8,128)(2,1)S(1)}, u32[]{:S(2)}, u32[]{:S(2)}) collective-permute-start(bf16[272,512]{1,0:T(8,128)(2,1)S(1)} %shard_map.123.patches.refs_0_), channel_id=1, source_target_pairs={{0,1},{1,0},{2,3},{3,2},{4,5},{5,4},{6,7},{7,6},{8,9},{9,8},{10,11... | collective-permute-start | bytes 835592 | tf_op jit(solution)/shard_map/ppermute | solution.py:54
  68.8 15.2 %collective-permute-start.11 = (bf16[192,768]{1,0:T(8,128)(2,1)S(1)}, bf16[192,768]{1,0:T(8,128)(2,1)S(1)}, u32[]{:S(2)}, u32[]{:S(2)}) collective-permute-start(bf16[192,768]{1,0:T(8,128)(2,1)S(1)} %copy-done.13), channel_id=1, source_target_pairs={{0,4},{4,0},{8,12},{12,8},{16,20},{20,16},{24,28},{28,24},{1,5},{5... | collective-permute-start | bytes 884744 | tf_op jit(solution)/shard_map/ppermute | solution.py:59
  70.2 13.9 %collective-permute-start.12 = (bf16[192,768]{1,0:T(8,128)(2,1)S(1)}, bf16[192,768]{1,0:T(8,128)(2,1)S(1)}, u32[]{:S(2)}, u32[]{:S(2)}) collective-permute-start(bf16[192,768]{1,0:T(8,128)(2,1)S(1)} %copy-done.15), channel_id=1, source_target_pairs={{0,4},{4,0},{8,12},{12,8},{16,20},{20,16},{24,28},{28,24},{1,5},{5... | collective-permute-start | bytes 884744 | tf_op jit(solution)/shard_map/ppermute | solution.py:59
  71.0 8.6 %collective-permute-start.8 = (bf16[272,512]{1,0:T(8,128)(2,1)S(1)}, bf16[272,512]{1,0:T(8,128)(2,1)S(1)}, u32[]{:S(2)}, u32[]{:S(2)}) collective-permute-start(bf16[272,512]{1,0:T(8,128)(2,1)S(1)} %collective-permute-done.6.patches.refs_2_), channel_id=1, source_target_pairs={{0,1},{1,0},{2,3},{3,2},{4,5},{5,4},{6,7},{7,6},{8,9},{9,8},{10,11... | collective-permute-start | bytes 835592 | tf_op jit(solution)/shard_map/ppermute | solution.py:54
  84.0 1.1 copy-start.6
  84.0 1.2 copy-start.16
  84.1 1.3 copy-start.17
  84.1 1.5 %copy-start.8 = (bf16[256,1536]{1,0:T(8,128)(2,1)}, bf16[256,1536]{1,0:T(8,128)(2,1)S(1)}, u32[]{:S(2)}) copy-start(bf16[256,1536]{1,0:T(8,128)(2,1)S(1)} %collective-permute-done.10.refs_16_) | copy-start | bytes 2359300
  97.6 13.8 %copy-start = (bf16[1024,768]{1,0:T(8,128)(2,1)}, bf16[1024,768]{1,0:T(8,128)(2,1)S(1)}, u32[]{:S(2)}) copy-start(bf16[1024,768]{1,0:T(8,128)(2,1)S(1)} %get-tuple-element.98.hidden) | copy-start | bytes 4718596
  97.6 14.9 %collective-permute-start.14 = (bf16[384,768]{1,0:T(8,128)(2,1)}, bf16[384,768]{1,0:T(8,128)(2,1)S(1)}, u32[]{:S(2)}, u32[]{:S(2)}) collective-permute-start(bf16[384,768]{1,0:T(8,128)(2,1)} %get-tuple-element.93), channel_id=1, source_target_pairs={{0,2},{1,3},{2,0},{3,1},{4,6},{5,7},{6,4},{7,5},{8,10},{9,11},{10,... | collective-permute-start | bytes 1769480 | tf_op jit(solution)/shard_map/ppermute | solution.py:54
  112.6 0.8 copy-start.9
  113.4 16.1 %all-to-all-start.2 = ((f32[32,1,1536]{2,1,0:T(1,128)}), f32[32,1,1536]{2,1,0:T(1,128)S(1)}, u32[]{:S(2)}, u32[]{:S(2)}) async-start(f32[32,1,1536]{2,1,0:T(1,128)} %shard_map.130), calls=%async_computation.2 | async-start | bytes 393216 | tf_op jit(solution)/shard_map/all_to_all | solution.py:608
  120.2 13.0 %collective-permute-start.13 = (bf16[384,768]{1,0:T(8,128)(2,1)}, bf16[384,768]{1,0:T(8,128)(2,1)}, u32[]{:S(2)}, u32[]{:S(2)}) collective-permute-start(bf16[384,768]{1,0:T(8,128)(2,1)} %get-tuple-element.80), channel_id=1, source_target_pairs={{0,1},{1,0},{2,3},{3,2},{4,5},{5,4},{6,7},{7,6},{8,9},{9,8},{10,11... | collective-permute-start | bytes 1769480 | tf_op jit(solution)/shard_map/ppermute | solution.py:54
  120.5 18.9 %collective-permute-start.15 = (bf16[384,768]{1,0:T(8,128)(2,1)}, bf16[384,768]{1,0:T(8,128)(2,1)}, u32[]{:S(2)}, u32[]{:S(2)}) collective-permute-start(bf16[384,768]{1,0:T(8,128)(2,1)} %get-tuple-element.96), channel_id=1, source_target_pairs={{0,3},{1,2},{2,1},{3,0},{4,7},{5,6},{6,5},{7,4},{8,11},{9,10},{10,... | collective-permute-start | bytes 1769480 | tf_op jit(solution)/shard_map/ppermute | solution.py:54
  122.1 1.4 copy-start.1
  130.5 11.9 %all-to-all-start.3 = ((f32[32,1,1536]{2,1,0:T(1,128)}), f32[32,1,1536]{2,1,0:T(1,128)S(1)}, u32[]{:S(2)}, u32[]{:S(2)}) async-start(f32[32,1,1536]{2,1,0:T(1,128)} %broadcast_in_dim.24), calls=%async_computation.3 | async-start | bytes 393216 | tf_op jit(solution)/shard_map/all_to_all | solution.py:622

commit v5 on v4

--- a/solution.py
+++ b/solution.py
@@ -196,72 +196,7 @@
     return tree(terms, low, middle) + tree(terms, middle, high)
 
 
-def forward(steps, blocks, patches, sub_ref, scales, work, mask, outs):
-    rows = steps * blocks
-    feat_ref, normed_ref, slope_ref, rstd_ref = outs
-    width, taps = scales.shape[1], scales.shape[0] - 1
-    span = (taps - 1) // 2
-    groups = range(len(patches))
-    for g in groups:
-        work[g * rows : (g + 1) * rows, :] = dot(patches[g][:rows, :], sub_ref[...], 1, 0)
-        counts = patches[g][rows:, :LANES].astype(jnp.float32)
-        for t in range(steps):
-            spot = g * rows + t * blocks
-            mask[spot : spot + blocks, :] = jnp.where(counts > t, 1.0, 0.0)
-
-    def column(c, _):
-        cols = pl.ds(pl.multiple_of(c * LANES, LANES), LANES)
-        weights = [
-            jnp.broadcast_to(scales[k : k + 1, cols], (blocks, LANES)).astype(jnp.bfloat16)
-            for k in range(taps)
-        ]
-        for g in groups:
-            spots = [
-                slice(g * rows + t * blocks, g * rows + (t + 1) * blocks) for t in range(steps)
-            ]
-            values = []
-            for t in range(steps):
-                rounded = (work[spots[t], cols] * mask[spots[t], :]).astype(jnp.bfloat16)
-                feat_ref[spots[t], cols] = rounded
-                values.append(rounded)
-            for t in range(steps):
-                terms = [
-                    (values[s], weights[s - t + span])
-                    for s in range(steps)
-                    if 0 <= s - t + span < taps
-                ]
-                conv = tree(terms, 0, len(terms)).astype(jnp.float32)
-                keep = mask[spots[t], :]
-                sigma = sigmoid(conv)
-                swish = conv * sigma
-                slope_ref[spots[t], cols] = (keep * (sigma + swish * (1.0 - sigma))).astype(
-                    jnp.bfloat16
-                )
-                work[spots[t], cols] = values[t].astype(jnp.float32) + keep * swish
-        return 0
-
-    lax.fori_loop(0, width // LANES, column, 0)
-
-    def norm(i, _):
-        at = pl.ds(pl.multiple_of(i * 32, 32), 32)
-        values = work[at, :]
-        centred = values - jnp.mean(values, axis=-1, keepdims=True)
-        rstd = lax.rsqrt(jnp.mean(centred * centred, axis=-1, keepdims=True) + EPSILON)
-        normed_ref[at, :] = (centred * rstd * scales[taps:, :]).astype(jnp.bfloat16)
-        rstd_ref[at, :] = jnp.broadcast_to(rstd, (32, LANES))
-        return 0
-
-    lax.fori_loop(0, len(patches) * rows // 32, norm, 0)
-
-
-def next_kernel(steps, blocks, patches, weight, scales, o0, o1, o2, o3, work, mask):
-    forward(steps, blocks, [patches], weight, scales, work, mask, (o0, o1, o2, o3))
-
-
-def first_kernel(
-    steps, blocks, patches, sub0, sub1, sub2, sub3, depth, gain,
-    o0, o1, o2, o3, weight, scales, work, mask, sems,
-):
+def order_kernel(sub0, sub1, sub2, sub3, depth, gain, weight, scales, sems):
     me = lax.axis_index("fsdp")
     deep = sub0.shape[0]
     copies = [
@@ -276,7 +211,56 @@
     scales[depth.shape[0] :, :] = gain[...]
     for copy in copies:
         copy.wait()
-    forward(steps, blocks, [patches], weight, scales, work, mask, (o0, o1, o2, o3))
+
+
+def forward_kernel(
+    steps, blocks, patches, weight, scales, feat_ref, normed_ref, slope_ref, rstd_ref, mixed, mask
+):
+    rows = steps * blocks
+    width, taps = scales.shape[1], scales.shape[0] - 1
+    span = (taps - 1) // 2
+    feat_ref[...] = dot(patches[:rows, :], weight[...], 1, 0).astype(jnp.bfloat16)
+    counts = patches[rows:, :LANES].astype(jnp.float32)
+    spots = [slice(t * blocks, (t + 1) * blocks) for t in range(steps)]
+    for t in range(steps):
+        mask[spots[t], :] = jnp.where(counts > t, 1.0, 0.0).astype(jnp.bfloat16)
+
+    def column(c, _):
+        cols = pl.ds(pl.multiple_of(c * LANES, LANES), LANES)
+        weights = [
+            jnp.broadcast_to(scales[k : k + 1, cols], (blocks, LANES)).astype(jnp.bfloat16)
+            for k in range(taps)
+        ]
+        values = []
+        for t in range(steps):
+            values.append(feat_ref[spots[t], cols] * mask[spots[t], :])
+            feat_ref[spots[t], cols] = values[t]
+        for t in range(steps):
+            terms = [
+                (values[s], weights[s - t + span])
+                for s in range(steps)
+                if 0 <= s - t + span < taps
+            ]
+            conv = tree(terms, 0, len(terms))
+            keep = mask[spots[t], :]
+            sigma = sigmoid(conv)
+            swish = conv * sigma
+            slope_ref[spots[t], cols] = keep * (sigma + swish * (1.0 - sigma))
+            mixed[spots[t], cols] = values[t] + keep * swish
+        return 0
+
+    lax.fori_loop(0, width // LANES, column, 0)
+
+    def norm(i, _):
+        at = pl.ds(pl.multiple_of(i * 32, 32), 32)
+        values = mixed[at, :].astype(jnp.float32)
+        centred = values - jnp.mean(values, axis=-1, keepdims=True)
+        rstd = lax.rsqrt(jnp.mean(centred * centred, axis=-1, keepdims=True) + EPSILON)
+        normed_ref[at, :] = (centred * rstd * scales[taps:, :]).astype(jnp.bfloat16)
+        rstd_ref[at, :] = jnp.broadcast_to(rstd, (32, LANES))
+        return 0
+
+    lax.fori_loop(0, rows // 32, norm, 0)
 
 
 def middle_kernel(steps, blocks, *refs):
@@ -459,6 +443,16 @@
 
     w_far, w_out, sub_weight, depth_kernel = far(w_in, w_out, sub_weight, depth_kernel)
     sub1, sub2 = across(sub_weight, 1), across(sub_weight, 2)
+    w2, w3 = pl.pallas_call(
+        functools.partial(cut_kernel, wide),
+        out_shape=(pltpu.HBM((deep // 2, wide), bf16),) * 2,
+        in_specs=[ANY],
+        out_specs=(ANY,) * 2,
+        scratch_shapes=[pltpu.VMEM((2, deep // 2, wide), bf16), dma((2, 2))],
+        compiler_params=params(),
+        cost_estimate=cost(1),
+    )(w_far)
+    w2 = across(w2, 2)
 
     block_shape = frames.shape[3:]
     held = frames[0, 0].reshape((cap, n) + block_shape) if split else frames[0, 0]
@@ -475,21 +469,11 @@
         cost_estimate=cost(2),
     )(order, infos, held)
     gain = norm_gain.reshape(1, width)
-    packed, sub1, sub2, gain, cot, w_late = lax.optimization_barrier(
-        (packed, sub1, sub2, gain, cotangent[0, 0], w_far)
-    )
+    packed, sub1, sub2, gain, cot, w2 = lax.optimization_barrier(
+        (packed, sub1, sub2, gain, cotangent[0, 0], w2)
+    )
+    w3 = across(w3, 3)
     got = lax.all_to_all(packed, "dp", split_axis=0, concat_axis=0, tiled=True)
-    w_late = far(w_late)[0]
-    w2, w3 = pl.pallas_call(
-        functools.partial(cut_kernel, wide),
-        out_shape=(pltpu.HBM((deep // 2, wide), bf16),) * 2,
-        in_specs=[ANY],
-        out_specs=(ANY,) * 2,
-        scratch_shapes=[pltpu.VMEM((2, deep // 2, wide), bf16), dma((2, 2))],
-        compiler_params=params(),
-        cost_estimate=cost(1),
-    )(w_late)
-    w2, w3 = across(w2, 2), across(w3, 3)
     sub_rows = sub_weight.shape[0]
     cot0, pair = pl.pallas_call(
         functools.partial(prepare_kernel, blocks, steps, wide),
@@ -507,11 +491,23 @@
         ],
         compiler_params=params(),
         cost_estimate=cost(2),
-    )(cot, w_late)
+    )(cot, w_far)
     sub3 = across(sub2, 1)
     cot2, pair = across(cot0, 2), across(pair, 1)
-    got, sub3, w2, w3 = lax.optimization_barrier((got, sub3, w2, w3))
-    w2b, w3b = across_dp(w2, 1), across_dp(w3, 1)
+    weight, scales = pl.pallas_call(
+        order_kernel,
+        out_shape=(
+            pltpu.VMEM((4 * sub_rows, width), bf16),
+            pltpu.VMEM((2 * steps, width), f32),
+        ),
+        in_specs=[ANY] * 4 + [VMEM] * 2,
+        out_specs=(VMEM,) * 2,
+        scratch_shapes=[dma((4,))],
+        compiler_params=params(),
+        cost_estimate=cost(1),
+    )(sub_weight, *far(sub1, sub2, sub3), depth_kernel, gain)
+    got, weight = lax.optimization_barrier((got, weight))
+    w2b = across_dp(w2, 1)
     patches0 = pl.pallas_call(
         functools.partial(unpack_kernel, n, cap, blocks, steps),
         out_shape=sds((rows + blocks, block_shape[0] // steps * LANES), bf16),
@@ -533,35 +529,24 @@
         pltpu.VMEM((rows, width), bf16),
         pltpu.VMEM((rows, LANES), f32),
     )
-    work = [pltpu.VMEM((rows, width), f32), pltpu.VMEM((rows, LANES), f32)]
-    *first, weight, scales = pl.pallas_call(
-        functools.partial(first_kernel, steps, blocks),
-        out_shape=(
-            *kept,
-            pltpu.VMEM((4 * sub_rows, width), bf16),
-            pltpu.VMEM((2 * steps, width), f32),
-        ),
-        in_specs=[VMEM] + [ANY] * 4 + [VMEM] * 2,
-        out_specs=(VMEM,) * 6,
-        scratch_shapes=[*work, dma((4,))],
-        compiler_params=params(),
-        cost_estimate=cost(4),
-    )(*near(patches0), sub_weight, *far(sub1, sub2, sub3), depth_kernel, gain)
-    first[0], cot_relay, patch_relay = lax.optimization_barrier((first[0], cot2, patches[2]))
-    cot3 = across(cot_relay, 1)
-    patches.append(across(patch_relay, 1))
-    following = pl.pallas_call(
-        functools.partial(next_kernel, steps, blocks),
+    forward = pl.pallas_call(
+        functools.partial(forward_kernel, steps, blocks),
         out_shape=kept,
         in_specs=[VMEM] * 3,
         out_specs=(VMEM,) * 4,
-        scratch_shapes=work,
+        scratch_shapes=[pltpu.VMEM((rows, width), bf16), pltpu.VMEM((rows, LANES), bf16)],
         compiler_params=params(),
         cost_estimate=cost(4),
     )
-    groups = [first]
+    groups = [list(forward(*near(patches0, weight, scales)))]
+    groups[0][0], cot_relay, patch_relay, w3, w2b = lax.optimization_barrier(
+        (groups[0][0], cot2, patches[2], w3, w2b)
+    )
+    w3b = across_dp(w3, 1)
+    cot3 = across(cot_relay, 1)
+    patches.append(across(patch_relay, 1))
     for k in (1, 2, 3):
-        groups.append(following(*near(patches[k], weight, scales)))
+        groups.append(forward(*near(patches[k], weight, scales)))
     feats, normeds, slopes, rstds = [near(*arrays) for arrays in zip(*groups)]
     g0, g1, g2, g3, scaled, hidden, masked, w_slice, means = pl.pallas_call(
         functools.partial(middle_kernel, steps, blocks),

time: 144 us -> 135 us (0.938)
  waiting for transfers between devices: 41.8 us -> 29.6 us
  starting transfers between devices: 31.8 us -> 35.8 us
  local copies, waits for them, and re-layouts: 9.08 us -> 6.11 us
  Pallas kernels: 58 us -> 60.9 us
    ppermute x14, waiting for transfers between devices: 34.7 us -> 13.5 us  [across(): return lax.ppermute(value, 'fsdp', [(i, i ^ k) for i in range(n)])]
    all_to_all x1, waiting for transfers between devices: 0.01 us -> 8.35 us  [on_device(): got = lax.all_to_all(packed, 'dp', split_axis=0, concat_axis=0, tiled=True)]
    pallas_call x4 -> x5, Pallas kernels: 19.4 us -> 22 us  [the longest x3 14.8 us: on_device(): groups.append(forward(*near(patches[k], weight, scales)))]
    unnamed x37 -> x27, local copies, waits for them, and re-layouts: 6.97 us -> 4.7 us
    all_to_all x1, starting transfers between devices: 3.56 us -> 5.55 us  [on_device(): got = lax.all_to_all(packed, 'dp', split_axis=0, concat_axis=0, tiled=True)]
    ppermute x2, starting transfers between devices: 1.47 us -> 3.19 us  [across_dp(): return lax.ppermute(value, 'dp', [(i, i ^ k) for i in range(n)])]
    ppermute x14, starting transfers between devices: 11.7 us -> 13.3 us  [across(): return lax.ppermute(value, 'fsdp', [(i, i ^ k) for i in range(n)])]
  transfers between devices with their start and end apart: 20 -> 20, of which waited for: 9 -> 8; matrix products, arithmetic and copies ran while one was open for 2% -> 1% of each run, Pallas kernels for 32% -> 36%
where the time goes in v5:
time: 135 us; the launch traced here: 134 us
  Pallas kernels  60.9 us (45%)
  starting transfers between devices  35.8 us (27%)
  waiting for transfers between devices  29.6 us (22%)
  local copies, waits for them, and re-layouts  6.11 us (5%)
  between operations  1.61 us (1%)
    pallas_call x3, Pallas kernels, on_device(): groups.append(forward(*near(patches[k], weight, scales)))  14.8 us
    ppermute x14, waiting for transfers between devices, across(): return lax.ppermute(value, 'fsdp', [(i, i ^ k) for i in range(n)])  13.5 us
    ppermute x14, starting transfers between devices, across(): return lax.ppermute(value, 'fsdp', [(i, i ^ k) for i in range(n)])  13.3 us
    pallas_call x1, Pallas kernels, on_device(): pl.pallas_call(functools.partial(backward_kernel, steps, blocks), out_sha...  12.3 us
    pallas_call x1, Pallas kernels, on_device(): pl.pallas_call(functools.partial(middle_kernel, steps, blocks), out_shape...  12.3 us
    all_to_all x1, waiting for transfers between devices, on_device(): got = lax.all_to_all(packed, 'dp', split_axis=0, concat_axis=0, tiled=True)  8.35 us
    all_to_all x1, starting transfers between devices, on_device(): lax.all_to_all(jnp.broadcast_to(info[None], (n, home + 1)), 'dp', split_a...  5.74 us
    all_to_all x1, starting transfers between devices, on_device(): got = lax.all_to_all(packed, 'dp', split_axis=0, concat_axis=0, tiled=True)  5.55 us
  transfers between devices with their start and end apart: 20, of which 8 were waited for; matrix products, arithmetic and copies ran while one was open for 1% of the time, Pallas kernels for 36%

profile of v5, /device:TPU:1, one launch (start us, length us, event | category | flops | bytes accessed | tf_op | source)
XLA Modules:
  0.0 134.3 jit_solution(11309320132652145134)
XLA Ops:
  0.7 0.1 collective-permute-start
  0.8 2.7 %collective-permute-start.1 = (bf16[128,1536]{1,0:T(8,128)(2,1)}, bf16[128,1536]{1,0:T(8,128)(2,1)S(1)}, u32[]{:S(2)}, u32[]{:S(2)}) collective-permute-start(bf16[128,1536]{1,0:T(8,128)(2,1)} %sub0.1), channel_id=1, source_target_pairs={{0,2},{1,3},{2,0},{3,1},{4,6},{5,7},{6,4},{7,5},{8,10},{9,11},{10,... | collective-permute-start | bytes 1179656 | tf_op jit(solution)/shard_map/ppermute | solution.py:54
  3.5 1.8 %shard_map.122 = (bf16[192,768]{1,0:T(8,128)(2,1)}, bf16[192,768]{1,0:T(8,128)(2,1)}) custom-call(bf16[384,3072]{1,0:T(8,128)(2,1)} %refs_17_.1), custom_call_target="tpu_custom_call" | custom-call | bytes 3600000 | tf_op jit(solution)/shard_map/pallas_call | solution.py:446
  6.1 0.6 broadcast_in_dim.20
  6.7 5.7 %all-to-all-start = ((s32[8,1,49]{2,1,0:T(1,128)}), s32[8,1,49]{2,1,0:T(1,128)S(1)}, u32[]{:S(2)}, u32[]{:S(2)}) async-start(s32[8,1,49]{2,1,0:T(1,128)} %broadcast_in_dim.20), calls=%async_computation | async-start | bytes 8192 | tf_op jit(solution)/shard_map/all_to_all | solution.py:440
  12.5 5.2 %all-to-all-done = s32[8,1,49]{2,1,0:T(1,128)S(1)} async-done(((s32[8,1,49]{2,1,0:T(1,128)}), s32[8,1,49]{2,1,0:T(1,128)S(1)}, u32[]{:S(2)}, u32[]{:S(2)}) %all-to-all-start) | async-done | bytes 1600 | tf_op jit(solution)/shard_map/all_to_all | solution.py:440
  17.7 1.8 %shard_map.121 = bf16[8,6,64,128]{3,2,1,0:T(8,128)(2,1)} custom-call(s32[1,8]{1,0:T(1,128)S(1)} %copy-done.4, s32[8,49]{1,0:T(8,128)S(1)} %bitcast.15, bf16[6,8,64,128]{3,2,1,0:T(8,128)(2,1)S(1)} %bitcast.13), custom_call_target="tpu_custom_call" | custom-call | bytes 7200000 | tf_op jit(solution)/shard_map/pallas_call | solution.py:459
  19.6 5.6 %all-to-all-start.1 = ((bf16[8,6,64,128]{3,2,1,0:T(8,128)(2,1)}), bf16[8,6,64,128]{3,2,1,0:T(8,128)(2,1)S(1)}, u32[]{:S(2)}, u32[]{:S(2)}) async-start(bf16[8,6,64,128]{3,2,1,0:T(8,128)(2,1)} %shard_map.121), calls=%async_computation.1 | async-start | bytes 1572864 | tf_op jit(solution)/shard_map/all_to_all | solution.py:476
  25.1 2.4 %shard_map.126 = (bf16[256,1536]{1,0:T(8,128)(2,1)}, bf16[448,1536]{1,0:T(8,128)(2,1)}) custom-call(bf16[16,16,1536]{2,1,0:T(8,128)(2,1)S(1)} %bitcast.14, bf16[384,3072]{1,0:T(8,128)(2,1)} %refs_17_.1), custom_call_target="tpu_custom_call" | custom-call | bytes 7200000 | tf_op jit(solution)/shard_map/pallas_call | solution.py:478
  27.6 1.3 collective-permute-start.6
  28.9 1.4 %collective-permute-start.3 = (bf16[128,1536]{1,0:T(8,128)(2,1)S(1)}, bf16[128,1536]{1,0:T(8,128)(2,1)S(1)}, u32[]{:S(2)}, u32[]{:S(2)}) collective-permute-start(bf16[128,1536]{1,0:T(8,128)(2,1)S(1)} %collective-permute-done.1.sub2), channel_id=1, source_target_pairs={{0,1},{1,0},{2,3},{3,2},{4,5},{5,4},{6,7},{7,6},{8,9},{9,8},{10,11... | collective-permute-start | bytes 1179656 | tf_op jit(solution)/shard_map/ppermute | solution.py:54
  30.3 0.6 collective-permute-start.7
  31.0 1.7 %collective-permute-start.8 = (bf16[192,768]{1,0:T(8,128)(2,1)}, bf16[192,768]{1,0:T(8,128)(2,1)}, u32[]{:S(2)}, u32[]{:S(2)}) collective-permute-start(bf16[192,768]{1,0:T(8,128)(2,1)} %collective-permute-done.2.refs_18_), channel_id=1, source_target_pairs={{0,4},{4,0},{8,12},{12,8},{16,20},{20,16},{24,28},{28,24},{1,5},{5... | collective-permute-start | bytes 884744 | tf_op jit(solution)/shard_map/ppermute | solution.py:59
  32.7 0.8 copy-done.9
  33.5 2.3 %shard_map.123 = (bf16[512,1536]{1,0:T(8,128)(2,1)S(1)}, f32[32,1536]{1,0:T(8,128)S(1)}) custom-call(bf16[128,1536]{1,0:T(8,128)(2,1)} %sub0.1, bf16[128,1536]{1,0:T(8,128)(2,1)} %copy-done.7, bf16[128,1536]{1,0:T(8,128)(2,1)} %copy-done.8, bf16[128,1536]{1,0:T(8,128)(2,1)} %copy-done.9, f32[31,1536]{1,0:T(8,128)} %depth.1, ...), custom_call_target="tpu_custom_call" | custom-call | bytes 3600000 | tf_op jit(solution)/shard_map/pallas_call | solution.py:497
  35.8 8.3 %all-to-all-done.1 = bf16[8,6,64,128]{3,2,1,0:T(8,128)(2,1)S(1)} async-done(((bf16[8,6,64,128]{3,2,1,0:T(8,128)(2,1)}), bf16[8,6,64,128]{3,2,1,0:T(8,128)(2,1)S(1)}, u32[]{:S(2)}, u32[]{:S(2)}) %all-to-all-start.1) | async-done | bytes 786464 | tf_op jit(solution)/shard_map/all_to_all | solution.py:476
  44.1 1.7 %shard_map.124.patches.refs_0_ = bf16[272,512]{1,0:T(8,128)(2,1)S(1)} custom-call(s32[1,8]{1,0:T(1,128)S(1)} %copy-done.4, s32[8,49]{1,0:T(8,128)S(1)} %bitcast.16, bf16[48,64,128]{2,1,0:T(8,128)(2,1)S(1)} %bitcast.12), custom_call_target="tpu_custom_call" | custom-call | bytes 7200000 | tf_op jit(solution)/shard_map/pallas_call | solution.py:511
  45.9 1.3 collective-permute-start.5
  47.2 4.9 %shard_map.125 = (bf16[256,1536]{1,0:T(8,128)(2,1)S(1)}, bf16[256,1536]{1,0:T(8,128)(2,1)S(1)}, bf16[256,1536]{1,0:T(8,128)(2,1)S(1)}, f32[256,128]{1,0:T(8,128)S(1)}) custom-call(bf16[272,512]{1,0:T(8,128)(2,1)S(1)} %shard_map.124.patches.refs_0_, bf16[512,1536]{1,0:T(8,128)(2,1)S(1)} %get-tuple-element.59.weight, f32[32,1536]{1,0:T(8,128)S(1)} %get-tuple-element.60.scales), custom_call_target="tpu_custom_call" | custom-call | bytes 14400000 | tf_op jit(solution)/shard_map/pallas_call | solution.py:541
  52.1 3.2 %collective-permute-done.7.refs_19_ = bf16[192,768]{1,0:T(8,128)(2,1)} collective-permute-done((bf16[192,768]{1,0:T(8,128)(2,1)}, bf16[192,768]{1,0:T(8,128)(2,1)}, u32[]{:S(2)}, u32[]{:S(2)}) %collective-permute-start.7) | collective-permute-done | bytes 294944 | tf_op jit(solution)/shard_map/ppermute | solution.py:54
  55.2 2.8 %collective-permute-done.5.patches.refs_2_ = bf16[272,512]{1,0:T(8,128)(2,1)S(1)} collective-permute-done((bf16[272,512]{1,0:T(8,128)(2,1)S(1)}, bf16[272,512]{1,0:T(8,128)(2,1)S(1)}, u32[]{:S(2)}, u32[]{:S(2)}) %collective-permute-start.5) | collective-permute-done | bytes 278560 | tf_op jit(solution)/shard_map/ppermute | solution.py:54
  58.1 2.1 %collective-permute-start.11 = (bf16[256,1536]{1,0:T(8,128)(2,1)}, bf16[256,1536]{1,0:T(8,128)(2,1)S(1)}, u32[]{:S(2)}, u32[]{:S(2)}) collective-permute-start(bf16[256,1536]{1,0:T(8,128)(2,1)} %collective-permute-done.6.refs_15_), channel_id=1, source_target_pairs={{0,1},{1,0},{2,3},{3,2},{4,5},{5,4},{6,7},{7,6},{8,9},{9,8},{10,11... | collective-permute-start | bytes 2359304 | tf_op jit(solution)/shard_map/ppermute | solution.py:54
  60.1 1.5 %collective-permute-start.12 = (bf16[192,768]{1,0:T(8,128)(2,1)}, bf16[192,768]{1,0:T(8,128)(2,1)S(1)}, u32[]{:S(2)}, u32[]{:S(2)}) collective-permute-start(bf16[192,768]{1,0:T(8,128)(2,1)} %collective-permute-done.7.refs_19_), channel_id=1, source_target_pairs={{0,4},{4,0},{8,12},{12,8},{16,20},{20,16},{24,28},{28,24},{1,5},{5... | collective-permute-start | bytes 884744 | tf_op jit(solution)/shard_map/ppermute | solution.py:59
  61.6 0.3 collective-permute-start.4
  61.9 0.2 collective-permute-start.9
  62.1 4.9 %shard_map.128 = (bf16[256,1536]{1,0:T(8,128)(2,1)S(1)}, bf16[256,1536]{1,0:T(8,128)(2,1)S(1)}, bf16[256,1536]{1,0:T(8,128)(2,1)S(1)}, f32[256,128]{1,0:T(8,128)S(1)}) custom-call(bf16[272,512]{1,0:T(8,128)(2,1)S(1)} %collective-permute-done.5.patches.refs_2_, bf16[512,1536]{1,0:T(8,128)(2,1)S(1)} %get-tuple-element.59.weight, ...), custom_call_target="tpu_custom_call" | custom-call | bytes 14400000 | tf_op jit(solution)/shard_map/pallas_call | solution.py:549
  67.0 4.9 %shard_map.127 = (bf16[256,1536]{1,0:T(8,128)(2,1)S(1)}, bf16[256,1536]{1,0:T(8,128)(2,1)S(1)}, bf16[256,1536]{1,0:T(8,128)(2,1)S(1)}, f32[256,128]{1,0:T(8,128)S(1)}) custom-call(bf16[272,512]{1,0:T(8,128)(2,1)S(1)} %collective-permute-done.4.patches.refs_1_, bf16[512,1536]{1,0:T(8,128)(2,1)S(1)} %get-tuple-element.59.weight, ...), custom_call_target="tpu_custom_call" | custom-call | bytes 14400000 | tf_op jit(solution)/shard_map/pallas_call | solution.py:549
  71.9 5.0 %shard_map.129 = (bf16[256,1536]{1,0:T(8,128)(2,1)S(1)}, bf16[256,1536]{1,0:T(8,128)(2,1)S(1)}, bf16[256,1536]{1,0:T(8,128)(2,1)S(1)}, f32[256,128]{1,0:T(8,128)S(1)}) custom-call(bf16[272,512]{1,0:T(8,128)(2,1)S(1)} %collective-permute-done.9.patches.refs_3_, bf16[512,1536]{1,0:T(8,128)(2,1)S(1)} %get-tuple-element.59.weight, ...), custom_call_target="tpu_custom_call" | custom-call | bytes 14400000 | tf_op jit(solution)/shard_map/pallas_call | solution.py:549
  77.0 0.7 copy-done.10
  77.7 0.3 copy-done.5
  77.9 12.3 %shard_map.130 = (bf16[384,768]{1,0:T(8,128)(2,1)}, bf16[384,768]{1,0:T(8,128)(2,1)}, bf16[384,768]{1,0:T(8,128)(2,1)}, bf16[384,768]{1,0:T(8,128)(2,1)}, bf16[1...) custom-call(bf16[272,512]{1,0:T(8,128)(2,1)S(1)} %shard_map.124.patc, ...), custom_call_target="tpu_custom_call" | custom-call | bytes 43200000 | tf_op jit(solution)/shard_map/pallas_call | solution.py:551
  90.2 1.3 collective-permute-start.14
  91.5 12.3 %shard_map.131 = f32[32,1,1536]{2,1,0:T(1,128)} custom-call(f32[1,1536]{1,0:T(1,128)S(1)} %reshape.35.gain.refs_12_.refs_0_, bf16[1024,768]{1,0:T(8,128)(2,1)S(1)} %get-tuple-element.81.refs_1_, bf16[1536,768]{1,0:T(8,128)(2,1)S(1)} %get-tuple-element.82.refs_2_, bf16[1024,1536]{1,0:T(8,128)(2,1)S(1)} %get-tuple-element.83.refs_3_.masked, ...), custom_call_target="tpu_custom_call" | custom-call | bytes 46800000 | tf_op jit(solution)/shard_map/pallas_call | solution.py:577
  103.9 1.3 collective-permute-done.14.refs_2_
  105.2 0.9 copy-done.6
  106.0 5.4 %all-to-all-start.2 = ((f32[32,1,1536]{2,1,0:T(1,128)}), f32[32,1,1536]{2,1,0:T(1,128)S(1)}, u32[]{:S(2)}, u32[]{:S(2)}) async-start(f32[32,1,1536]{2,1,0:T(1,128)} %shard_map.131), calls=%async_computation.2 | async-start | bytes 393216 | tf_op jit(solution)/shard_map/all_to_all | solution.py:593
  111.4 0.3 collective-permute-start.13
  111.7 1.5 %collective-permute-start.15 = (bf16[384,768]{1,0:T(8,128)(2,1)}, bf16[384,768]{1,0:T(8,128)(2,1)}, u32[]{:S(2)}, u32[]{:S(2)}) collective-permute-start(bf16[384,768]{1,0:T(8,128)(2,1)} %get-tuple-element.96), channel_id=1, source_target_pairs={{0,3},{1,2},{2,1},{3,0},{4,7},{5,6},{6,5},{7,4},{8,11},{9,10},{10,... | collective-permute-start | bytes 1769480 | tf_op jit(solution)/shard_map/ppermute | solution.py:54
  113.3 1.4 %copy-done.1 = bf16[1024,768]{1,0:T(8,128)(2,1)S(1)} copy-done((bf16[1024,768]{1,0:T(8,128)(2,1)S(1)}, bf16[1024,768]{1,0:T(8,128)(2,1)}, u32[]{:S(2)}) %copy-start.1) | copy-done | bytes 1572888
  114.7 4.0 %shard_map.133 = bf16[768,1536]{1,0:T(8,128)(2,1)} custom-call(bf16[1024,768]{1,0:T(8,128)(2,1)S(1)} %copy-done.1, bf16[1024,1536]{1,0:T(8,128)(2,1)S(1)} %get-tuple-element.83.refs_3_.masked), custom_call_target="tpu_custom_call" | custom-call | bytes 14400000 | tf_op jit(solution)/shard_map/pallas_call | solution.py:597
  118.7 2.0 %all-to-all-done.2 = f32[32,1,1536]{2,1,0:T(1,128)S(1)} async-done(((f32[32,1,1536]{2,1,0:T(1,128)}), f32[32,1,1536]{2,1,0:T(1,128)S(1)}, u32[]{:S(2)}, u32[]{:S(2)}) %all-to-all-start.2) | async-done | bytes 196640 | tf_op jit(solution)/shard_map/all_to_all | solution.py:593
  120.7 0.1 reduce_sum.9
  120.9 0.8 broadcast_in_dim.24
  121.7 2.7 %all-to-all-start.3 = ((f32[32,1,1536]{2,1,0:T(1,128)}), f32[32,1,1536]{2,1,0:T(1,128)S(1)}, u32[]{:S(2)}, u32[]{:S(2)}) async-start(f32[32,1,1536]{2,1,0:T(1,128)} %broadcast_in_dim.24), calls=%async_computation.3 | async-start | bytes 393216 | tf_op jit(solution)/shard_map/all_to_all | solution.py:607
  124.4 6.2 %collective-permute-done.15.refs_3_ = bf16[384,768]{1,0:T(8,128)(2,1)} collective-permute-done((bf16[384,768]{1,0:T(8,128)(2,1)}, bf16[384,768]{1,0:T(8,128)(2,1)}, u32[]{:S(2)}, u32[]{:S(2)}) %collective-permute-start.15) | collective-permute-done | bytes 589856 | tf_op jit(solution)/shard_map/ppermute | solution.py:54
  130.6 2.5 %shard_map.132 = bf16[384,3072]{1,0:T(8,128)(2,1)} custom-call(bf16[384,768]{1,0:T(8,128)(2,1)} %get-tuple-element.79.refs_0_, bf16[384,768]{1,0:T(8,128)(2,1)} %collective-permute-done.13.refs_1_, bf16[384,768]{1,0:T(8,128)(2,1)} %copy-done.6, bf16[384,768]{1,0:T(8,128)(2,1)} %collective-permute-done.15.refs_3_), custom_call_target="tpu_custom_call" | custom-call | bytes 7200000 | tf_op jit(solution)/shard_map/pallas_call | solution.py:612
  133.2 0.5 all-to-all-done.3
  133.7 0.7 copy.15
  (41 shorter events, 0.3 us)
Async XLA Ops:
  0.6 5.4 %copy-start.12 = (s32[1,1,48]{2,1,0:T(1,128)S(1)}, s32[1,1,48]{2,1,0:T(1,128)}, u32[]{:S(2)}) copy-start(s32[1,1,48]{2,1,0:T(1,128)} %param.12) | copy-start | bytes 580
  0.6 11.8 %copy-start.11 = (f32[1536]{0:T(1024)S(1)}, f32[1536]{0:T(1024)}, u32[]{:S(2)}) copy-start(f32[1536]{0:T(1024)} %param.17) | copy-start | bytes 18436
  0.7 17.1 %copy-start.4 = (s32[1,8]{1,0:T(1,128)S(1)}, s32[1,8]{1,0:T(1,128)}, u32[]{:S(2)}) copy-start(s32[1,8]{1,0:T(1,128)} %order_ref.3) | copy-start | bytes 100
  0.7 17.1 %copy-start.2 = (bf16[1,1,48,64,128]{4,3,2,1,0:T(8,128)(2,1)S(1)}, bf16[1,1,48,64,128]{4,3,2,1,0:T(8,128)(2,1)}, u32[]{:S(2)}) copy-start(bf16[1,1,48,64,128]{4,3,2,1,0:T(8,128)(2,1)} %param.10) | copy-start | bytes 2359300
  0.7 24.5 %copy-start.3 = (bf16[1,1,16,16,1536]{4,3,2,1,0:T(8,128)(2,1)S(1)}, bf16[1,1,16,16,1536]{4,3,2,1,0:T(8,128)(2,1)}, u32[]{:S(2)}) copy-start(bf16[1,1,16,16,1536]{4,3,2,1,0:T(8,128)(2,1)} %param.14) | copy-start | bytes 2359300
  0.7 18.9 %collective-permute-start = (bf16[128,1536]{1,0:T(8,128)(2,1)}, bf16[128,1536]{1,0:T(8,128)(2,1)S(1)}, u32[]{:S(2)}, u32[]{:S(2)}) collective-permute-start(bf16[128,1536]{1,0:T(8,128)(2,1)} %sub0.1), channel_id=1, source_target_pairs={{0,1},{1,0},{2,3},{3,2},{4,5},{5,4},{6,7},{7,6},{8,9},{9,8},{10,11... | collective-permute-start | bytes 1179656 | tf_op jit(solution)/shard_map/ppermute | solution.py:54
  0.8 18.8 %collective-permute-start.1 = (bf16[128,1536]{1,0:T(8,128)(2,1)}, bf16[128,1536]{1,0:T(8,128)(2,1)S(1)}, u32[]{:S(2)}, u32[]{:S(2)}) collective-permute-start(bf16[128,1536]{1,0:T(8,128)(2,1)} %sub0.1), channel_id=1, source_target_pairs={{0,2},{1,3},{2,0},{3,1},{4,6},{5,7},{6,4},{7,5},{8,10},{9,11},{10,... | collective-permute-start | bytes 1179656 | tf_op jit(solution)/shard_map/ppermute | solution.py:54
  5.3 14.2 %collective-permute-start.2 = (bf16[192,768]{1,0:T(8,128)(2,1)}, bf16[192,768]{1,0:T(8,128)(2,1)}, u32[]{:S(2)}, u32[]{:S(2)}) collective-permute-start(bf16[192,768]{1,0:T(8,128)(2,1)} %get-tuple-element.52), channel_id=1, source_target_pairs={{0,2},{1,3},{2,0},{3,1},{4,6},{5,7},{6,4},{7,5},{8,10},{9,11},{10,... | collective-permute-start | bytes 884744 | tf_op jit(solution)/shard_map/ppermute | solution.py:54
  6.7 11.0 %all-to-all-start = ((s32[8,1,49]{2,1,0:T(1,128)}), s32[8,1,49]{2,1,0:T(1,128)S(1)}, u32[]{:S(2)}, u32[]{:S(2)}) async-start(s32[8,1,49]{2,1,0:T(1,128)} %broadcast_in_dim.20), calls=%async_computation | async-start | bytes 8192 | tf_op jit(solution)/shard_map/all_to_all | solution.py:440
  19.6 8.0 %copy-start.7 = (bf16[128,1536]{1,0:T(8,128)(2,1)}, bf16[128,1536]{1,0:T(8,128)(2,1)S(1)}, u32[]{:S(2)}) copy-start(bf16[128,1536]{1,0:T(8,128)(2,1)S(1)} %collective-permute-done.sub1) | copy-start | bytes 1179652
  19.6 9.3 %copy-start.8 = (bf16[128,1536]{1,0:T(8,128)(2,1)}, bf16[128,1536]{1,0:T(8,128)(2,1)S(1)}, u32[]{:S(2)}) copy-start(bf16[128,1536]{1,0:T(8,128)(2,1)S(1)} %collective-permute-done.1.sub2) | copy-start | bytes 1179652
  19.6 24.5 %all-to-all-start.1 = ((bf16[8,6,64,128]{3,2,1,0:T(8,128)(2,1)}), bf16[8,6,64,128]{3,2,1,0:T(8,128)(2,1)S(1)}, u32[]{:S(2)}, u32[]{:S(2)}) async-start(bf16[8,6,64,128]{3,2,1,0:T(8,128)(2,1)} %shard_map.121), calls=%async_computation.1 | async-start | bytes 1572864 | tf_op jit(solution)/shard_map/all_to_all | solution.py:476
  27.6 27.6 %collective-permute-start.6 = (bf16[256,1536]{1,0:T(8,128)(2,1)}, bf16[256,1536]{1,0:T(8,128)(2,1)}, u32[]{:S(2)}, u32[]{:S(2)}) collective-permute-start(bf16[256,1536]{1,0:T(8,128)(2,1)} %get-tuple-element.63.refs_13_), channel_id=1, source_target_pairs={{0,2},{1,3},{2,0},{3,1},{4,6},{5,7},{6,4},{7,5},{8,10},{9,11},{10,... | collective-permute-start | bytes 2359304 | tf_op jit(solution)/shard_map/ppermute | solution.py:54
  28.9 3.8 %collective-permute-start.3 = (bf16[128,1536]{1,0:T(8,128)(2,1)S(1)}, bf16[128,1536]{1,0:T(8,128)(2,1)S(1)}, u32[]{:S(2)}, u32[]{:S(2)}) collective-permute-start(bf16[128,1536]{1,0:T(8,128)(2,1)S(1)} %collective-permute-done.1.sub2), channel_id=1, source_target_pairs={{0,1},{1,0},{2,3},{3,2},{4,5},{5,4},{6,7},{7,6},{8,9},{9,8},{10,11... | collective-permute-start | bytes 1179656 | tf_op jit(solution)/shard_map/ppermute | solution.py:54
  30.3 46.6 %collective-permute-start.10 = (bf16[448,1536]{1,0:T(8,128)(2,1)}, bf16[448,1536]{1,0:T(8,128)(2,1)}, u32[]{:S(2)}, u32[]{:S(2)}) collective-permute-start(bf16[448,1536]{1,0:T(8,128)(2,1)} %get-tuple-element.75), channel_id=1, source_target_pairs={{0,1},{1,0},{2,3},{3,2},{4,5},{5,4},{6,7},{7,6},{8,9},{9,8},{10,11... | collective-permute-start | bytes 4128776 | tf_op jit(solution)/shard_map/ppermute | solution.py:54
  30.3 24.9 %collective-permute-start.7 = (bf16[192,768]{1,0:T(8,128)(2,1)}, bf16[192,768]{1,0:T(8,128)(2,1)}, u32[]{:S(2)}, u32[]{:S(2)}) collective-permute-start(bf16[192,768]{1,0:T(8,128)(2,1)} %get-tuple-element.64), channel_id=1, source_target_pairs={{0,3},{1,2},{2,1},{3,0},{4,7},{5,6},{6,5},{7,4},{8,11},{9,10},{10,... | collective-permute-start | bytes 884744 | tf_op jit(solution)/shard_map/ppermute | solution.py:54
  31.0 24.3 %collective-permute-start.8 = (bf16[192,768]{1,0:T(8,128)(2,1)}, bf16[192,768]{1,0:T(8,128)(2,1)}, u32[]{:S(2)}, u32[]{:S(2)}) collective-permute-start(bf16[192,768]{1,0:T(8,128)(2,1)} %collective-permute-done.2.refs_18_), channel_id=1, source_target_pairs={{0,4},{4,0},{8,12},{12,8},{16,20},{20,16},{24,28},{28,24},{1,5},{5... | collective-permute-start | bytes 884744 | tf_op jit(solution)/shard_map/ppermute | solution.py:59
  32.7 0.8 copy-start.9
  45.9 12.2 %collective-permute-start.5 = (bf16[272,512]{1,0:T(8,128)(2,1)S(1)}, bf16[272,512]{1,0:T(8,128)(2,1)S(1)}, u32[]{:S(2)}, u32[]{:S(2)}) collective-permute-start(bf16[272,512]{1,0:T(8,128)(2,1)S(1)} %shard_map.124.patches.refs_0_), channel_id=1, source_target_pairs={{0,2},{1,3},{2,0},{3,1},{4,6},{5,7},{6,4},{7,5},{8,10},{9,11},{10,... | collective-permute-start | bytes 835592 | tf_op jit(solution)/shard_map/ppermute | solution.py:54
  58.1 18.9 %collective-permute-start.11 = (bf16[256,1536]{1,0:T(8,128)(2,1)}, bf16[256,1536]{1,0:T(8,128)(2,1)S(1)}, u32[]{:S(2)}, u32[]{:S(2)}) collective-permute-start(bf16[256,1536]{1,0:T(8,128)(2,1)} %collective-permute-done.6.refs_15_), channel_id=1, source_target_pairs={{0,1},{1,0},{2,3},{3,2},{4,5},{5,4},{6,7},{7,6},{8,9},{9,8},{10,11... | collective-permute-start | bytes 2359304 | tf_op jit(solution)/shard_map/ppermute | solution.py:54
  60.1 16.8 %collective-permute-start.12 = (bf16[192,768]{1,0:T(8,128)(2,1)}, bf16[192,768]{1,0:T(8,128)(2,1)S(1)}, u32[]{:S(2)}, u32[]{:S(2)}) collective-permute-start(bf16[192,768]{1,0:T(8,128)(2,1)} %collective-permute-done.7.refs_19_), channel_id=1, source_target_pairs={{0,4},{4,0},{8,12},{12,8},{16,20},{20,16},{24,28},{28,24},{1,5},{5... | collective-permute-start | bytes 884744 | tf_op jit(solution)/shard_map/ppermute | solution.py:59
  61.6 5.4 %collective-permute-start.4 = (bf16[272,512]{1,0:T(8,128)(2,1)S(1)}, bf16[272,512]{1,0:T(8,128)(2,1)S(1)}, u32[]{:S(2)}, u32[]{:S(2)}) collective-permute-start(bf16[272,512]{1,0:T(8,128)(2,1)S(1)} %shard_map.124.patches.refs_0_), channel_id=1, source_target_pairs={{0,1},{1,0},{2,3},{3,2},{4,5},{5,4},{6,7},{7,6},{8,9},{9,8},{10,11... | collective-permute-start | bytes 835592 | tf_op jit(solution)/shard_map/ppermute | solution.py:54
  61.9 10.0 %collective-permute-start.9 = (bf16[272,512]{1,0:T(8,128)(2,1)S(1)}, bf16[272,512]{1,0:T(8,128)(2,1)S(1)}, u32[]{:S(2)}, u32[]{:S(2)}) collective-permute-start(bf16[272,512]{1,0:T(8,128)(2,1)S(1)} %collective-permute-done.5.patches.refs_2_), channel_id=1, source_target_pairs={{0,1},{1,0},{2,3},{3,2},{4,5},{5,4},{6,7},{7,6},{8,9},{9,8},{10,11... | collective-permute-start | bytes 835592 | tf_op jit(solution)/shard_map/ppermute | solution.py:54
  77.0 0.7 copy-start.10
  77.0 1.0 copy-start.5
  90.2 13.7 %copy-start = (bf16[1024,768]{1,0:T(8,128)(2,1)}, bf16[1024,768]{1,0:T(8,128)(2,1)S(1)}, u32[]{:S(2)}) copy-start(bf16[1024,768]{1,0:T(8,128)(2,1)S(1)} %get-tuple-element.98.hidden) | copy-start | bytes 4718596
  90.2 14.9 %collective-permute-start.14 = (bf16[384,768]{1,0:T(8,128)(2,1)}, bf16[384,768]{1,0:T(8,128)(2,1)S(1)}, u32[]{:S(2)}, u32[]{:S(2)}) collective-permute-start(bf16[384,768]{1,0:T(8,128)(2,1)} %get-tuple-element.93), channel_id=1, source_target_pairs={{0,2},{1,3},{2,0},{3,1},{4,6},{5,7},{6,4},{7,5},{8,10},{9,11},{10,... | collective-permute-start | bytes 1769480 | tf_op jit(solution)/shard_map/ppermute | solution.py:54
  105.2 0.9 copy-start.6
  106.0 14.7 %all-to-all-start.2 = ((f32[32,1,1536]{2,1,0:T(1,128)}), f32[32,1,1536]{2,1,0:T(1,128)S(1)}, u32[]{:S(2)}, u32[]{:S(2)}) async-start(f32[32,1,1536]{2,1,0:T(1,128)} %shard_map.131), calls=%async_computation.2 | async-start | bytes 393216 | tf_op jit(solution)/shard_map/all_to_all | solution.py:593
  111.4 13.0 %collective-permute-start.13 = (bf16[384,768]{1,0:T(8,128)(2,1)}, bf16[384,768]{1,0:T(8,128)(2,1)}, u32[]{:S(2)}, u32[]{:S(2)}) collective-permute-start(bf16[384,768]{1,0:T(8,128)(2,1)} %get-tuple-element.80), channel_id=1, source_target_pairs={{0,1},{1,0},{2,3},{3,2},{4,5},{5,4},{6,7},{7,6},{8,9},{9,8},{10,11... | collective-permute-start | bytes 1769480 | tf_op jit(solution)/shard_map/ppermute | solution.py:54
  111.7 18.9 %collective-permute-start.15 = (bf16[384,768]{1,0:T(8,128)(2,1)}, bf16[384,768]{1,0:T(8,128)(2,1)}, u32[]{:S(2)}, u32[]{:S(2)}) collective-permute-start(bf16[384,768]{1,0:T(8,128)(2,1)} %get-tuple-element.96), channel_id=1, source_target_pairs={{0,3},{1,2},{2,1},{3,0},{4,7},{5,6},{6,5},{7,4},{8,11},{9,10},{10,... | collective-permute-start | bytes 1769480 | tf_op jit(solution)/shard_map/ppermute | solution.py:54
  113.3 1.4 %copy-start.1 = (bf16[1024,768]{1,0:T(8,128)(2,1)S(1)}, bf16[1024,768]{1,0:T(8,128)(2,1)}, u32[]{:S(2)}) copy-start(bf16[1024,768]{1,0:T(8,128)(2,1)} %copy-done) | copy-start | bytes 4718596
  121.7 11.9 %all-to-all-start.3 = ((f32[32,1,1536]{2,1,0:T(1,128)}), f32[32,1,1536]{2,1,0:T(1,128)S(1)}, u32[]{:S(2)}, u32[]{:S(2)}) async-start(f32[32,1,1536]{2,1,0:T(1,128)} %broadcast_in_dim.24), calls=%async_computation.3 | async-start | bytes 393216 | tf_op jit(solution)/shard_map/all_to_all | solution.py:607

commit v6 on v5

--- a/solution.py
+++ b/solution.py
@@ -214,16 +214,16 @@
 
 
 def forward_kernel(
-    steps, blocks, patches, weight, scales, feat_ref, normed_ref, slope_ref, rstd_ref, mixed, mask
+    steps, blocks, patches, weight, scales, feat_ref, normed_ref, slope_ref, rstd_ref, work, mask
 ):
     rows = steps * blocks
     width, taps = scales.shape[1], scales.shape[0] - 1
     span = (taps - 1) // 2
-    feat_ref[...] = dot(patches[:rows, :], weight[...], 1, 0).astype(jnp.bfloat16)
+    work[...] = dot(patches[:rows, :], weight[...], 1, 0)
     counts = patches[rows:, :LANES].astype(jnp.float32)
     spots = [slice(t * blocks, (t + 1) * blocks) for t in range(steps)]
     for t in range(steps):
-        mask[spots[t], :] = jnp.where(counts > t, 1.0, 0.0).astype(jnp.bfloat16)
+        mask[spots[t], :] = jnp.where(counts > t, 1.0, 0.0)
 
     def column(c, _):
         cols = pl.ds(pl.multiple_of(c * LANES, LANES), LANES)
@@ -233,7 +233,7 @@
         ]
         values = []
         for t in range(steps):
-            values.append(feat_ref[spots[t], cols] * mask[spots[t], :])
+            values.append((work[spots[t], cols] * mask[spots[t], :]).astype(jnp.bfloat16))
             feat_ref[spots[t], cols] = values[t]
         for t in range(steps):
             terms = [
@@ -241,19 +241,21 @@
                 for s in range(steps)
                 if 0 <= s - t + span < taps
             ]
-            conv = tree(terms, 0, len(terms))
+            conv = tree(terms, 0, len(terms)).astype(jnp.float32)
             keep = mask[spots[t], :]
             sigma = sigmoid(conv)
             swish = conv * sigma
-            slope_ref[spots[t], cols] = keep * (sigma + swish * (1.0 - sigma))
-            mixed[spots[t], cols] = values[t] + keep * swish
+            slope_ref[spots[t], cols] = (keep * (sigma + swish * (1.0 - sigma))).astype(
+                jnp.bfloat16
+            )
+            work[spots[t], cols] = values[t].astype(jnp.float32) + keep * swish
         return 0
 
     lax.fori_loop(0, width // LANES, column, 0)
 
     def norm(i, _):
         at = pl.ds(pl.multiple_of(i * 32, 32), 32)
-        values = mixed[at, :].astype(jnp.float32)
+        values = work[at, :]
         centred = values - jnp.mean(values, axis=-1, keepdims=True)
         rstd = lax.rsqrt(jnp.mean(centred * centred, axis=-1, keepdims=True) + EPSILON)
         normed_ref[at, :] = (centred * rstd * scales[taps:, :]).astype(jnp.bfloat16)
@@ -292,6 +294,8 @@
         move(w2b, w_in.at[rows_of(me ^ 2, 1 - parity, half), :]),
         move(w3b, w_in.at[rows_of(me ^ 3, 1 - parity, half), :]),
     ]
+    for copy in coming:
+        copy.wait()
     later = [
         move(w_out_in, w_out),
         move(cot0, masked.at[:rows, :]),
@@ -299,8 +303,6 @@
         move(cot2, masked.at[2 * rows : 3 * rows, :]),
         move(cot3, masked.at[3 * rows :, :]),
     ]
-    for copy in coming:
-        copy.wait()
     fine = jnp.broadcast_to(gain[...], (TILE, gain.shape[1]))
     coarse = fine.astype(jnp.bfloat16)
     small = (fine - coarse.astype(jnp.float32)).astype(jnp.bfloat16)
@@ -506,8 +508,9 @@
         compiler_params=params(),
         cost_estimate=cost(1),
     )(sub_weight, *far(sub1, sub2, sub3), depth_kernel, gain)
-    got, weight = lax.optimization_barrier((got, weight))
     w2b = across_dp(w2, 1)
+    got, weight, w3, w2b = lax.optimization_barrier((got, weight, w3, w2b))
+    w3b = across_dp(w3, 1)
     patches0 = pl.pallas_call(
         functools.partial(unpack_kernel, n, cap, blocks, steps),
         out_shape=sds((rows + blocks, block_shape[0] // steps * LANES), bf16),
@@ -534,18 +537,19 @@
         out_shape=kept,
         in_specs=[VMEM] * 3,
         out_specs=(VMEM,) * 4,
-        scratch_shapes=[pltpu.VMEM((rows, width), bf16), pltpu.VMEM((rows, LANES), bf16)],
+        scratch_shapes=[pltpu.VMEM((rows, width), f32), pltpu.VMEM((rows, LANES), f32)],
         compiler_params=params(),
         cost_estimate=cost(4),
     )
-    groups = [list(forward(*near(patches0, weight, scales)))]
-    groups[0][0], cot_relay, patch_relay, w3, w2b = lax.optimization_barrier(
-        (groups[0][0], cot2, patches[2], w3, w2b)
-    )
-    w3b = across_dp(w3, 1)
+    groups = [list(forward(*near(patches[0], weight, scales)))]
+    groups[0][0], patches[1] = lax.optimization_barrier((groups[0][0], patches[1]))
+    groups.append(list(forward(*near(patches[1], weight, scales))))
+    groups[1][0], cot_relay, patches[2] = lax.optimization_barrier(
+        (groups[1][0], cot2, patches[2])
+    )
     cot3 = across(cot_relay, 1)
-    patches.append(across(patch_relay, 1))
-    for k in (1, 2, 3):
+    patches.append(across(patches[2], 1))
+    for k in (2, 3):
         groups.append(forward(*near(patches[k], weight, scales)))
     feats, normeds, slopes, rstds = [near(*arrays) for arrays in zip(*groups)]
     g0, g1, g2, g3, scaled, hidden, masked, w_slice, means = pl.pallas_call(
@@ -617,7 +621,7 @@
         scratch_shapes=[pltpu.VMEM((4, deep, wide), bf16), dma((2, 4))],
         compiler_params=params(),
         cost_estimate=cost(2),
-    )(*far(g0, g1, g2, g3))
+    )(g0, g1, g2, g3)
     return (grad_in[None], grad_out[None], kernel_grad)
 
 

time: 135 us -> 137 us (1.015)
  waiting for transfers between devices: 29.6 us -> 33.6 us
  local copies, waits for them, and re-layouts: 6.11 us -> 9.62 us
  starting transfers between devices: 35.8 us -> 32.3 us
  Pallas kernels: 60.9 us -> 58.9 us
    ppermute x14, waiting for transfers between devices: 13.5 us -> 26.3 us  [across(): return lax.ppermute(value, 'fsdp', [(i, i ^ k) for i in range(n)])]
    all_to_all x1, waiting for transfers between devices: 8.35 us -> 0.01 us  [on_device(): got = lax.all_to_all(packed, 'dp', split_axis=0, concat_axis=0, tiled=True)]
    pallas_call x3 -> x2, Pallas kernels: 14.8 us -> 8.61 us  [on_device(): groups.append(forward(*near(patches[k], weight, scales)))]
    pallas_call x1 -> x2, Pallas kernels: 4.87 us -> 8.44 us  [the longest x1 4.22 us: on_device(): groups = [list(forward(*near(patches[0], weight, scales)))]]
    unnamed x27 -> x41, local copies, waits for them, and re-layouts: 4.7 us -> 8.2 us
    ppermute x14, starting transfers between devices: 13.3 us -> 10.9 us  [across(): return lax.ppermute(value, 'fsdp', [(i, i ^ k) for i in range(n)])]
  transfers between devices with their start and end apart: 20 -> 20, of which waited for: 8 -> 5; matrix products, arithmetic and copies ran while one was open for 1% -> 1% of each run, Pallas kernels for 36% -> 34%
where the time goes in v6:
time: 137 us; the launch traced here: 136 us
  Pallas kernels  58.9 us (43%)
  waiting for transfers between devices  33.6 us (25%)
  starting transfers between devices  32.3 us (24%)
  local copies, waits for them, and re-layouts  9.62 us (7%)
  between operations  1.67 us (1%)
    ppermute x14, waiting for transfers between devices, across(): return lax.ppermute(value, 'fsdp', [(i, i ^ k) for i in range(n)])  26.3 us
    pallas_call x1, Pallas kernels, on_device(): pl.pallas_call(functools.partial(middle_kernel, steps, blocks), out_shape...  12.8 us
    pallas_call x1, Pallas kernels, on_device(): pl.pallas_call(functools.partial(backward_kernel, steps, blocks), out_sha...  12.4 us
    ppermute x14, starting transfers between devices, across(): return lax.ppermute(value, 'fsdp', [(i, i ^ k) for i in range(n)])  10.9 us
    pallas_call x2, Pallas kernels, on_device(): groups.append(forward(*near(patches[k], weight, scales)))  8.61 us
    unnamed x41, local copies, waits for them, and re-layouts  8.2 us
    all_to_all x1, starting transfers between devices, on_device(): lax.all_to_all(jnp.broadcast_to(info[None], (n, home + 1)), 'dp', split_a...  5.74 us
    all_to_all x1, starting transfers between devices, on_device(): got = lax.all_to_all(packed, 'dp', split_axis=0, concat_axis=0, tiled=True)  5.44 us
  transfers between devices with their start and end apart: 20, of which 5 were waited for; matrix products, arithmetic and copies ran while one was open for 1% of the time, Pallas kernels for 34%

profile of v6, /device:TPU:1, one launch (start us, length us, event | category | flops | bytes accessed | tf_op | source)
XLA Modules:
  0.0 136.4 jit_solution(29882504248709875)
XLA Ops:
  0.7 0.1 collective-permute-start
  0.8 2.7 %collective-permute-start.1 = (bf16[128,1536]{1,0:T(8,128)(2,1)}, bf16[128,1536]{1,0:T(8,128)(2,1)S(1)}, u32[]{:S(2)}, u32[]{:S(2)}) collective-permute-start(bf16[128,1536]{1,0:T(8,128)(2,1)} %sub0.1), channel_id=1, source_target_pairs={{0,2},{1,3},{2,0},{3,1},{4,6},{5,7},{6,4},{7,5},{8,10},{9,11},{10,... | collective-permute-start | bytes 1179656 | tf_op jit(solution)/shard_map/ppermute | solution.py:54
  3.5 1.8 %shard_map.122 = (bf16[192,768]{1,0:T(8,128)(2,1)}, bf16[192,768]{1,0:T(8,128)(2,1)}) custom-call(bf16[384,3072]{1,0:T(8,128)(2,1)} %refs_17_.1), custom_call_target="tpu_custom_call" | custom-call | bytes 3600000 | tf_op jit(solution)/shard_map/pallas_call | solution.py:448
  6.2 0.6 broadcast_in_dim.20
  6.8 5.7 %all-to-all-start = ((s32[8,1,49]{2,1,0:T(1,128)}), s32[8,1,49]{2,1,0:T(1,128)S(1)}, u32[]{:S(2)}, u32[]{:S(2)}) async-start(s32[8,1,49]{2,1,0:T(1,128)} %broadcast_in_dim.20), calls=%async_computation | async-start | bytes 8192 | tf_op jit(solution)/shard_map/all_to_all | solution.py:442
  12.5 5.2 %all-to-all-done = s32[8,1,49]{2,1,0:T(1,128)S(1)} async-done(((s32[8,1,49]{2,1,0:T(1,128)}), s32[8,1,49]{2,1,0:T(1,128)S(1)}, u32[]{:S(2)}, u32[]{:S(2)}) %all-to-all-start) | async-done | bytes 1600 | tf_op jit(solution)/shard_map/all_to_all | solution.py:442
  17.7 1.8 %shard_map.121 = bf16[8,6,64,128]{3,2,1,0:T(8,128)(2,1)} custom-call(s32[1,8]{1,0:T(1,128)S(1)} %copy-done.7, s32[8,49]{1,0:T(8,128)S(1)} %bitcast.15, bf16[6,8,64,128]{3,2,1,0:T(8,128)(2,1)S(1)} %bitcast.13), custom_call_target="tpu_custom_call" | custom-call | bytes 7200000 | tf_op jit(solution)/shard_map/pallas_call | solution.py:461
  19.6 0.7 copy-done.12
  20.3 5.4 %all-to-all-start.1 = ((bf16[8,6,64,128]{3,2,1,0:T(8,128)(2,1)}), bf16[8,6,64,128]{3,2,1,0:T(8,128)(2,1)S(1)}, u32[]{:S(2)}, u32[]{:S(2)}) async-start(bf16[8,6,64,128]{3,2,1,0:T(8,128)(2,1)} %shard_map.121), calls=%async_computation.1 | async-start | bytes 1572864 | tf_op jit(solution)/shard_map/all_to_all | solution.py:478
  25.7 2.5 %shard_map.127 = (bf16[256,1536]{1,0:T(8,128)(2,1)}, bf16[448,1536]{1,0:T(8,128)(2,1)}) custom-call(bf16[16,16,1536]{2,1,0:T(8,128)(2,1)S(1)} %bitcast.14, bf16[384,3072]{1,0:T(8,128)(2,1)} %refs_17_.1), custom_call_target="tpu_custom_call" | custom-call | bytes 7200000 | tf_op jit(solution)/shard_map/pallas_call | solution.py:480
  28.2 1.3 collective-permute-start.7
  29.6 1.4 %collective-permute-start.3 = (bf16[128,1536]{1,0:T(8,128)(2,1)S(1)}, bf16[128,1536]{1,0:T(8,128)(2,1)S(1)}, u32[]{:S(2)}, u32[]{:S(2)}) collective-permute-start(bf16[128,1536]{1,0:T(8,128)(2,1)S(1)} %collective-permute-done.1.sub2), channel_id=1, source_target_pairs={{0,1},{1,0},{2,3},{3,2},{4,5},{5,4},{6,7},{7,6},{8,9},{9,8},{10,11... | collective-permute-start | bytes 1179656 | tf_op jit(solution)/shard_map/ppermute | solution.py:54
  31.0 0.6 collective-permute-start.4
  31.6 1.7 %collective-permute-start.5 = (bf16[192,768]{1,0:T(8,128)(2,1)S(1)}, bf16[192,768]{1,0:T(8,128)(2,1)}, u32[]{:S(2)}, u32[]{:S(2)}) collective-permute-start(bf16[192,768]{1,0:T(8,128)(2,1)S(1)} %copy-done.13), channel_id=1, source_target_pairs={{0,4},{4,0},{8,12},{12,8},{16,20},{20,16},{24,28},{28,24},{1,5},{5... | collective-permute-start | bytes 884744 | tf_op jit(solution)/shard_map/ppermute | solution.py:59
  33.3 0.8 copy-done.11
  34.1 2.3 %shard_map.123 = (bf16[512,1536]{1,0:T(8,128)(2,1)S(1)}, f32[32,1536]{1,0:T(8,128)S(1)}) custom-call(bf16[128,1536]{1,0:T(8,128)(2,1)} %sub0.1, bf16[128,1536]{1,0:T(8,128)(2,1)} %copy-done.9, bf16[128,1536]{1,0:T(8,128)(2,1)} %copy-done.10, bf16[128,1536]{1,0:T(8,128)(2,1)} %copy-done.11, f32[31,1536]{1,0:T(8,128)} %depth.1, ...), custom_call_target="tpu_custom_call" | custom-call | bytes 3600000 | tf_op jit(solution)/shard_map/pallas_call | solution.py:499
  36.4 17.7 %collective-permute-done.4.refs_19_ = bf16[192,768]{1,0:T(8,128)(2,1)S(1)} collective-permute-done((bf16[192,768]{1,0:T(8,128)(2,1)S(1)}, bf16[192,768]{1,0:T(8,128)(2,1)S(1)}, u32[]{:S(2)}, u32[]{:S(2)}) %collective-permute-start.4) | collective-permute-done | bytes 294944 | tf_op jit(solution)/shard_map/ppermute | solution.py:54
  54.1 0.7 copy-done.14
  54.8 1.7 %shard_map.124.patches.refs_0_ = bf16[272,512]{1,0:T(8,128)(2,1)S(1)} custom-call(s32[1,8]{1,0:T(1,128)S(1)} %copy-done.7, s32[8,49]{1,0:T(8,128)S(1)} %bitcast.16, bf16[48,64,128]{2,1,0:T(8,128)(2,1)S(1)} %bitcast.12), custom_call_target="tpu_custom_call" | custom-call | bytes 7200000 | tf_op jit(solution)/shard_map/pallas_call | solution.py:514
  56.7 1.3 collective-permute-start.8
  58.0 4.2 %shard_map.125 = (bf16[256,1536]{1,0:T(8,128)(2,1)S(1)}, bf16[256,1536]{1,0:T(8,128)(2,1)S(1)}, bf16[256,1536]{1,0:T(8,128)(2,1)S(1)}, f32[256,128]{1,0:T(8,128)S(1)}) custom-call(bf16[272,512]{1,0:T(8,128)(2,1)S(1)} %shard_map.124.patches.refs_0_, bf16[512,1536]{1,0:T(8,128)(2,1)S(1)} %get-tuple-element.63.weight, f32[32,1536]{1,0:T(8,128)S(1)} %get-tuple-element.64.scales), custom_call_target="tpu_custom_call" | custom-call | bytes 14400000 | tf_op jit(solution)/shard_map/pallas_call | solution.py:544
  62.2 4.2 %shard_map.126 = (bf16[256,1536]{1,0:T(8,128)(2,1)S(1)}, bf16[256,1536]{1,0:T(8,128)(2,1)S(1)}, bf16[256,1536]{1,0:T(8,128)(2,1)S(1)}, f32[256,128]{1,0:T(8,128)S(1)}) custom-call(bf16[272,512]{1,0:T(8,128)(2,1)S(1)} %collective-permute-done.6.patches.refs_1_, bf16[512,1536]{1,0:T(8,128)(2,1)S(1)} %get-tuple-element.63.weight, ...), custom_call_target="tpu_custom_call" | custom-call | bytes 14400000 | tf_op jit(solution)/shard_map/pallas_call | solution.py:546
  66.5 0.8 collective-permute-start.11
  67.2 1.5 %collective-permute-start.12 = (bf16[192,768]{1,0:T(8,128)(2,1)S(1)}, bf16[192,768]{1,0:T(8,128)(2,1)S(1)}, u32[]{:S(2)}, u32[]{:S(2)}) collective-permute-start(bf16[192,768]{1,0:T(8,128)(2,1)S(1)} %copy-done.15), channel_id=1, source_target_pairs={{0,4},{4,0},{8,12},{12,8},{16,20},{20,16},{24,28},{28,24},{1,5},{5... | collective-permute-start | bytes 884744 | tf_op jit(solution)/shard_map/ppermute | solution.py:59
  68.7 0.4 collective-permute-start.9
  69.1 4.2 %shard_map.128 = (bf16[256,1536]{1,0:T(8,128)(2,1)S(1)}, bf16[256,1536]{1,0:T(8,128)(2,1)S(1)}, bf16[256,1536]{1,0:T(8,128)(2,1)S(1)}, f32[256,128]{1,0:T(8,128)S(1)}) custom-call(bf16[272,512]{1,0:T(8,128)(2,1)S(1)} %collective-permute-done.8.patches.refs_2_, bf16[512,1536]{1,0:T(8,128)(2,1)S(1)} %get-tuple-element.63.weight, ...), custom_call_target="tpu_custom_call" | custom-call | bytes 14400000 | tf_op jit(solution)/shard_map/pallas_call | solution.py:553
  73.3 4.4 %shard_map.129 = (bf16[256,1536]{1,0:T(8,128)(2,1)S(1)}, bf16[256,1536]{1,0:T(8,128)(2,1)S(1)}, bf16[256,1536]{1,0:T(8,128)(2,1)S(1)}, f32[256,128]{1,0:T(8,128)S(1)}) custom-call(bf16[272,512]{1,0:T(8,128)(2,1)S(1)} %collective-permute-done.9.patches.refs_3_, bf16[512,1536]{1,0:T(8,128)(2,1)S(1)} %get-tuple-element.63.weight, ...), custom_call_target="tpu_custom_call" | custom-call | bytes 14400000 | tf_op jit(solution)/shard_map/pallas_call | solution.py:553
  77.7 0.7 copy-done.16
  78.4 0.3 copy-done.8
  78.7 12.8 %shard_map.130 = (bf16[384,768]{1,0:T(8,128)(2,1)}, bf16[384,768]{1,0:T(8,128)(2,1)}, bf16[384,768]{1,0:T(8,128)(2,1)}, bf16[384,768]{1,0:T(8,128)(2,1)}, bf16[1...) custom-call(bf16[272,512]{1,0:T(8,128)(2,1)S(1)} %shard_map.124.patc, ...), custom_call_target="tpu_custom_call" | custom-call | bytes 43200000 | tf_op jit(solution)/shard_map/pallas_call | solution.py:555
  91.5 0.3 collective-permute-start.14
  91.8 12.4 %shard_map.131 = f32[32,1,1536]{2,1,0:T(1,128)} custom-call(f32[1,1536]{1,0:T(1,128)S(1)} %reshape.35.gain.refs_12_.refs_0_, bf16[1024,768]{1,0:T(8,128)(2,1)S(1)} %get-tuple-element.85.refs_1_, bf16[1536,768]{1,0:T(8,128)(2,1)S(1)} %get-tuple-element.86.refs_2_, bf16[1024,1536]{1,0:T(8,128)(2,1)S(1)} %get-tuple-element.87.refs_3_.masked, ...), custom_call_target="tpu_custom_call" | custom-call | bytes 46800000 | tf_op jit(solution)/shard_map/pallas_call | solution.py:581
  104.1 2.4 %collective-permute-done.14.refs_2_ = bf16[384,768]{1,0:T(8,128)(2,1)S(1)} collective-permute-done((bf16[384,768]{1,0:T(8,128)(2,1)}, bf16[384,768]{1,0:T(8,128)(2,1)S(1)}, u32[]{:S(2)}, u32[]{:S(2)}) %collective-permute-start.14) | collective-permute-done | bytes 589856 | tf_op jit(solution)/shard_map/ppermute | solution.py:54
  106.5 0.8 copy-done.5
  107.4 4.3 %all-to-all-start.2 = ((f32[32,1,1536]{2,1,0:T(1,128)}), f32[32,1,1536]{2,1,0:T(1,128)S(1)}, u32[]{:S(2)}, u32[]{:S(2)}) async-start(f32[32,1,1536]{2,1,0:T(1,128)} %shard_map.131), calls=%async_computation.2 | async-start | bytes 393216 | tf_op jit(solution)/shard_map/all_to_all | solution.py:597
  111.7 0.5 collective-permute-start.13
  112.3 1.3 collective-permute-start.15
  113.6 1.4 %copy-done.1 = bf16[1024,768]{1,0:T(8,128)(2,1)S(1)} copy-done((bf16[1024,768]{1,0:T(8,128)(2,1)S(1)}, bf16[1024,768]{1,0:T(8,128)(2,1)}, u32[]{:S(2)}) %copy-start.1) | copy-done | bytes 1572888
  115.0 4.0 %shard_map.133 = bf16[768,1536]{1,0:T(8,128)(2,1)} custom-call(bf16[1024,768]{1,0:T(8,128)(2,1)S(1)} %copy-done.1, bf16[1024,1536]{1,0:T(8,128)(2,1)S(1)} %get-tuple-element.87.refs_3_.masked), custom_call_target="tpu_custom_call" | custom-call | bytes 14400000 | tf_op jit(solution)/shard_map/pallas_call | solution.py:601
  119.0 2.0 %all-to-all-done.2 = f32[32,1,1536]{2,1,0:T(1,128)S(1)} async-done(((f32[32,1,1536]{2,1,0:T(1,128)}), f32[32,1,1536]{2,1,0:T(1,128)S(1)}, u32[]{:S(2)}, u32[]{:S(2)}) %all-to-all-start.2) | async-done | bytes 196640 | tf_op jit(solution)/shard_map/all_to_all | solution.py:597
  121.1 0.1 reduce_sum.9
  121.2 0.8 broadcast_in_dim.24
  122.0 2.7 %all-to-all-start.3 = ((f32[32,1,1536]{2,1,0:T(1,128)}), f32[32,1,1536]{2,1,0:T(1,128)S(1)}, u32[]{:S(2)}, u32[]{:S(2)}) async-start(f32[32,1,1536]{2,1,0:T(1,128)} %broadcast_in_dim.24), calls=%async_computation.3 | async-start | bytes 393216 | tf_op jit(solution)/shard_map/all_to_all | solution.py:611
  124.7 6.2 %collective-permute-done.15.refs_3_ = bf16[384,768]{1,0:T(8,128)(2,1)} collective-permute-done((bf16[384,768]{1,0:T(8,128)(2,1)}, bf16[384,768]{1,0:T(8,128)(2,1)}, u32[]{:S(2)}, u32[]{:S(2)}) %collective-permute-start.15) | collective-permute-done | bytes 589856 | tf_op jit(solution)/shard_map/ppermute | solution.py:54
  130.9 1.1 copy-done.4
  132.0 1.1 copy-done.6
  133.1 2.5 %shard_map.132 = bf16[384,3072]{1,0:T(8,128)(2,1)} custom-call(bf16[384,768]{1,0:T(8,128)(2,1)S(1)} %copy-done.4, bf16[384,768]{1,0:T(8,128)(2,1)} %collective-permute-done.13.refs_1_, bf16[384,768]{1,0:T(8,128)(2,1)S(1)} %copy-done.6, bf16[384,768]{1,0:T(8,128)(2,1)} %collective-permute-done.15.refs_3_), custom_call_target="tpu_custom_call" | custom-call | bytes 7200000 | tf_op jit(solution)/shard_map/pallas_call | solution.py:616
  135.7 0.7 copy.15
  (55 shorter events, 0.4 us)
Async XLA Ops:
  0.6 5.4 %copy-start.19 = (s32[1,1,48]{2,1,0:T(1,128)S(1)}, s32[1,1,48]{2,1,0:T(1,128)}, u32[]{:S(2)}) copy-start(s32[1,1,48]{2,1,0:T(1,128)} %param.12) | copy-start | bytes 580
  0.6 11.9 %copy-start.17 = (f32[1536]{0:T(1024)S(1)}, f32[1536]{0:T(1024)}, u32[]{:S(2)}) copy-start(f32[1536]{0:T(1024)} %param.17) | copy-start | bytes 18436
  0.7 17.1 %copy-start.7 = (s32[1,8]{1,0:T(1,128)S(1)}, s32[1,8]{1,0:T(1,128)}, u32[]{:S(2)}) copy-start(s32[1,8]{1,0:T(1,128)} %order_ref.3) | copy-start | bytes 100
  0.7 17.1 %copy-start.2 = (bf16[1,1,48,64,128]{4,3,2,1,0:T(8,128)(2,1)S(1)}, bf16[1,1,48,64,128]{4,3,2,1,0:T(8,128)(2,1)}, u32[]{:S(2)}) copy-start(bf16[1,1,48,64,128]{4,3,2,1,0:T(8,128)(2,1)} %param.10) | copy-start | bytes 2359300
  0.7 25.1 %copy-start.3 = (bf16[1,1,16,16,1536]{4,3,2,1,0:T(8,128)(2,1)S(1)}, bf16[1,1,16,16,1536]{4,3,2,1,0:T(8,128)(2,1)}, u32[]{:S(2)}) copy-start(bf16[1,1,16,16,1536]{4,3,2,1,0:T(8,128)(2,1)} %param.14) | copy-start | bytes 2359300
  0.7 18.9 %collective-permute-start = (bf16[128,1536]{1,0:T(8,128)(2,1)}, bf16[128,1536]{1,0:T(8,128)(2,1)S(1)}, u32[]{:S(2)}, u32[]{:S(2)}) collective-permute-start(bf16[128,1536]{1,0:T(8,128)(2,1)} %sub0.1), channel_id=1, source_target_pairs={{0,1},{1,0},{2,3},{3,2},{4,5},{5,4},{6,7},{7,6},{8,9},{9,8},{10,11... | collective-permute-start | bytes 1179656 | tf_op jit(solution)/shard_map/ppermute | solution.py:54
  0.8 18.8 %collective-permute-start.1 = (bf16[128,1536]{1,0:T(8,128)(2,1)}, bf16[128,1536]{1,0:T(8,128)(2,1)S(1)}, u32[]{:S(2)}, u32[]{:S(2)}) collective-permute-start(bf16[128,1536]{1,0:T(8,128)(2,1)} %sub0.1), channel_id=1, source_target_pairs={{0,2},{1,3},{2,0},{3,1},{4,6},{5,7},{6,4},{7,5},{8,10},{9,11},{10,... | collective-permute-start | bytes 1179656 | tf_op jit(solution)/shard_map/ppermute | solution.py:54
  5.3 14.2 %collective-permute-start.2 = (bf16[192,768]{1,0:T(8,128)(2,1)}, bf16[192,768]{1,0:T(8,128)(2,1)S(1)}, u32[]{:S(2)}, u32[]{:S(2)}) collective-permute-start(bf16[192,768]{1,0:T(8,128)(2,1)} %get-tuple-element.54), channel_id=1, source_target_pairs={{0,2},{1,3},{2,0},{3,1},{4,6},{5,7},{6,4},{7,5},{8,10},{9,11},{10,... | collective-permute-start | bytes 884744 | tf_op jit(solution)/shard_map/ppermute | solution.py:54
  6.8 11.0 %all-to-all-start = ((s32[8,1,49]{2,1,0:T(1,128)}), s32[8,1,49]{2,1,0:T(1,128)S(1)}, u32[]{:S(2)}, u32[]{:S(2)}) async-start(s32[8,1,49]{2,1,0:T(1,128)} %broadcast_in_dim.20), calls=%async_computation | async-start | bytes 8192 | tf_op jit(solution)/shard_map/all_to_all | solution.py:442
  19.6 0.7 copy-start.12
  19.6 8.7 %copy-start.9 = (bf16[128,1536]{1,0:T(8,128)(2,1)}, bf16[128,1536]{1,0:T(8,128)(2,1)S(1)}, u32[]{:S(2)}) copy-start(bf16[128,1536]{1,0:T(8,128)(2,1)S(1)} %collective-permute-done.sub1) | copy-start | bytes 1179652
  19.6 10.0 %copy-start.10 = (bf16[128,1536]{1,0:T(8,128)(2,1)}, bf16[128,1536]{1,0:T(8,128)(2,1)S(1)}, u32[]{:S(2)}) copy-start(bf16[128,1536]{1,0:T(8,128)(2,1)S(1)} %collective-permute-done.1.sub2) | copy-start | bytes 1179652
  19.6 11.4 %copy-start.18 = (bf16[192,768]{1,0:T(8,128)(2,1)S(1)}, bf16[192,768]{1,0:T(8,128)(2,1)}, u32[]{:S(2)}) copy-start(bf16[192,768]{1,0:T(8,128)(2,1)} %get-tuple-element.60) | copy-start | bytes 884740
  20.3 34.5 %all-to-all-start.1 = ((bf16[8,6,64,128]{3,2,1,0:T(8,128)(2,1)}), bf16[8,6,64,128]{3,2,1,0:T(8,128)(2,1)S(1)}, u32[]{:S(2)}, u32[]{:S(2)}) async-start(bf16[8,6,64,128]{3,2,1,0:T(8,128)(2,1)} %shard_map.121), calls=%async_computation.1 | async-start | bytes 1572864 | tf_op jit(solution)/shard_map/all_to_all | solution.py:478
  25.7 5.9 %copy-start.13 = (bf16[192,768]{1,0:T(8,128)(2,1)S(1)}, bf16[192,768]{1,0:T(8,128)(2,1)}, u32[]{:S(2)}) copy-start(bf16[192,768]{1,0:T(8,128)(2,1)} %copy-done.12) | copy-start | bytes 884740
  28.2 38.2 %collective-permute-start.7 = (bf16[256,1536]{1,0:T(8,128)(2,1)}, bf16[256,1536]{1,0:T(8,128)(2,1)}, u32[]{:S(2)}, u32[]{:S(2)}) collective-permute-start(bf16[256,1536]{1,0:T(8,128)(2,1)} %get-tuple-element.69.refs_13_), channel_id=1, source_target_pairs={{0,2},{1,3},{2,0},{3,1},{4,6},{5,7},{6,4},{7,5},{8,10},{9,11},{10,... | collective-permute-start | bytes 2359304 | tf_op jit(solution)/shard_map/ppermute | solution.py:54
  29.6 3.8 %collective-permute-start.3 = (bf16[128,1536]{1,0:T(8,128)(2,1)S(1)}, bf16[128,1536]{1,0:T(8,128)(2,1)S(1)}, u32[]{:S(2)}, u32[]{:S(2)}) collective-permute-start(bf16[128,1536]{1,0:T(8,128)(2,1)S(1)} %collective-permute-done.1.sub2), channel_id=1, source_target_pairs={{0,1},{1,0},{2,3},{3,2},{4,5},{5,4},{6,7},{7,6},{8,9},{9,8},{10,11... | collective-permute-start | bytes 1179656 | tf_op jit(solution)/shard_map/ppermute | solution.py:54
  31.0 46.7 %collective-permute-start.10 = (bf16[448,1536]{1,0:T(8,128)(2,1)}, bf16[448,1536]{1,0:T(8,128)(2,1)}, u32[]{:S(2)}, u32[]{:S(2)}) collective-permute-start(bf16[448,1536]{1,0:T(8,128)(2,1)} %get-tuple-element.79), channel_id=1, source_target_pairs={{0,1},{1,0},{2,3},{3,2},{4,5},{5,4},{6,7},{7,6},{8,9},{9,8},{10,11... | collective-permute-start | bytes 4128776 | tf_op jit(solution)/shard_map/ppermute | solution.py:54
  31.0 23.1 %collective-permute-start.4 = (bf16[192,768]{1,0:T(8,128)(2,1)S(1)}, bf16[192,768]{1,0:T(8,128)(2,1)S(1)}, u32[]{:S(2)}, u32[]{:S(2)}) collective-permute-start(bf16[192,768]{1,0:T(8,128)(2,1)S(1)} %copy-done.18), channel_id=1, source_target_pairs={{0,3},{1,2},{2,1},{3,0},{4,7},{5,6},{6,5},{7,4},{8,11},{9,10},{10,... | collective-permute-start | bytes 884744 | tf_op jit(solution)/shard_map/ppermute | solution.py:54
  31.6 23.2 %collective-permute-start.5 = (bf16[192,768]{1,0:T(8,128)(2,1)S(1)}, bf16[192,768]{1,0:T(8,128)(2,1)}, u32[]{:S(2)}, u32[]{:S(2)}) collective-permute-start(bf16[192,768]{1,0:T(8,128)(2,1)S(1)} %copy-done.13), channel_id=1, source_target_pairs={{0,4},{4,0},{8,12},{12,8},{16,20},{20,16},{24,28},{28,24},{1,5},{5... | collective-permute-start | bytes 884744 | tf_op jit(solution)/shard_map/ppermute | solution.py:59
  33.3 0.8 copy-start.11
  54.1 0.7 copy-start.14
  54.8 12.4 %copy-start.15 = (bf16[192,768]{1,0:T(8,128)(2,1)S(1)}, bf16[192,768]{1,0:T(8,128)(2,1)}, u32[]{:S(2)}) copy-start(bf16[192,768]{1,0:T(8,128)(2,1)} %copy-done.14) | copy-start | bytes 884740
  56.6 5.6 %collective-permute-start.6 = (bf16[272,512]{1,0:T(8,128)(2,1)S(1)}, bf16[272,512]{1,0:T(8,128)(2,1)S(1)}, u32[]{:S(2)}, u32[]{:S(2)}) collective-permute-start(bf16[272,512]{1,0:T(8,128)(2,1)S(1)} %shard_map.124.patches.refs_0_), channel_id=1, source_target_pairs={{0,1},{1,0},{2,3},{3,2},{4,5},{5,4},{6,7},{7,6},{8,9},{9,8},{10,11... | collective-permute-start | bytes 835592 | tf_op jit(solution)/shard_map/ppermute | solution.py:54
  56.7 9.8 %collective-permute-start.8 = (bf16[272,512]{1,0:T(8,128)(2,1)S(1)}, bf16[272,512]{1,0:T(8,128)(2,1)S(1)}, u32[]{:S(2)}, u32[]{:S(2)}) collective-permute-start(bf16[272,512]{1,0:T(8,128)(2,1)S(1)} %shard_map.124.patches.refs_0_), channel_id=1, source_target_pairs={{0,2},{1,3},{2,0},{3,1},{4,6},{5,7},{6,4},{7,5},{8,10},{9,11},{10,... | collective-permute-start | bytes 835592 | tf_op jit(solution)/shard_map/ppermute | solution.py:54
  66.5 11.3 %collective-permute-start.11 = (bf16[256,1536]{1,0:T(8,128)(2,1)}, bf16[256,1536]{1,0:T(8,128)(2,1)S(1)}, u32[]{:S(2)}, u32[]{:S(2)}) collective-permute-start(bf16[256,1536]{1,0:T(8,128)(2,1)} %collective-permute-done.7.refs_15_), channel_id=1, source_target_pairs={{0,1},{1,0},{2,3},{3,2},{4,5},{5,4},{6,7},{7,6},{8,9},{9,8},{10,11... | collective-permute-start | bytes 2359304 | tf_op jit(solution)/shard_map/ppermute | solution.py:54
  67.2 10.5 %collective-permute-start.12 = (bf16[192,768]{1,0:T(8,128)(2,1)S(1)}, bf16[192,768]{1,0:T(8,128)(2,1)S(1)}, u32[]{:S(2)}, u32[]{:S(2)}) collective-permute-start(bf16[192,768]{1,0:T(8,128)(2,1)S(1)} %copy-done.15), channel_id=1, source_target_pairs={{0,4},{4,0},{8,12},{12,8},{16,20},{20,16},{24,28},{28,24},{1,5},{5... | collective-permute-start | bytes 884744 | tf_op jit(solution)/shard_map/ppermute | solution.py:59
  68.7 4.6 %collective-permute-start.9 = (bf16[272,512]{1,0:T(8,128)(2,1)S(1)}, bf16[272,512]{1,0:T(8,128)(2,1)S(1)}, u32[]{:S(2)}, u32[]{:S(2)}) collective-permute-start(bf16[272,512]{1,0:T(8,128)(2,1)S(1)} %collective-permute-done.8.patches.refs_2_), channel_id=1, source_target_pairs={{0,1},{1,0},{2,3},{3,2},{4,5},{5,4},{6,7},{7,6},{8,9},{9,8},{10,11... | collective-permute-start | bytes 835592 | tf_op jit(solution)/shard_map/ppermute | solution.py:54
  77.7 0.7 copy-start.16
  77.7 1.0 copy-start.8
  91.5 12.7 %copy-start = (bf16[1024,768]{1,0:T(8,128)(2,1)}, bf16[1024,768]{1,0:T(8,128)(2,1)S(1)}, u32[]{:S(2)}) copy-start(bf16[1024,768]{1,0:T(8,128)(2,1)S(1)} %get-tuple-element.102.hidden) | copy-start | bytes 4718596
  91.5 15.1 %collective-permute-start.14 = (bf16[384,768]{1,0:T(8,128)(2,1)}, bf16[384,768]{1,0:T(8,128)(2,1)S(1)}, u32[]{:S(2)}, u32[]{:S(2)}) collective-permute-start(bf16[384,768]{1,0:T(8,128)(2,1)} %get-tuple-element.97), channel_id=1, source_target_pairs={{0,2},{1,3},{2,0},{3,1},{4,6},{5,7},{6,4},{7,5},{8,10},{9,11},{10,... | collective-permute-start | bytes 1769480 | tf_op jit(solution)/shard_map/ppermute | solution.py:54
  106.5 0.8 copy-start.5
  107.4 13.7 %all-to-all-start.2 = ((f32[32,1,1536]{2,1,0:T(1,128)}), f32[32,1,1536]{2,1,0:T(1,128)S(1)}, u32[]{:S(2)}, u32[]{:S(2)}) async-start(f32[32,1,1536]{2,1,0:T(1,128)} %shard_map.131), calls=%async_computation.2 | async-start | bytes 393216 | tf_op jit(solution)/shard_map/all_to_all | solution.py:597
  111.7 13.0 %collective-permute-start.13 = (bf16[384,768]{1,0:T(8,128)(2,1)}, bf16[384,768]{1,0:T(8,128)(2,1)}, u32[]{:S(2)}, u32[]{:S(2)}) collective-permute-start(bf16[384,768]{1,0:T(8,128)(2,1)} %get-tuple-element.84), channel_id=1, source_target_pairs={{0,1},{1,0},{2,3},{3,2},{4,5},{5,4},{6,7},{7,6},{8,9},{9,8},{10,11... | collective-permute-start | bytes 1769480 | tf_op jit(solution)/shard_map/ppermute | solution.py:54
  112.3 18.7 %collective-permute-start.15 = (bf16[384,768]{1,0:T(8,128)(2,1)}, bf16[384,768]{1,0:T(8,128)(2,1)}, u32[]{:S(2)}, u32[]{:S(2)}) collective-permute-start(bf16[384,768]{1,0:T(8,128)(2,1)} %get-tuple-element.100), channel_id=1, source_target_pairs={{0,3},{1,2},{2,1},{3,0},{4,7},{5,6},{6,5},{7,4},{8,11},{9,10},{10,... | collective-permute-start | bytes 1769480 | tf_op jit(solution)/shard_map/ppermute | solution.py:54
  113.6 1.4 %copy-start.1 = (bf16[1024,768]{1,0:T(8,128)(2,1)S(1)}, bf16[1024,768]{1,0:T(8,128)(2,1)}, u32[]{:S(2)}) copy-start(bf16[1024,768]{1,0:T(8,128)(2,1)} %copy-done) | copy-start | bytes 4718596
  122.0 13.6 %all-to-all-start.3 = ((f32[32,1,1536]{2,1,0:T(1,128)}), f32[32,1,1536]{2,1,0:T(1,128)S(1)}, u32[]{:S(2)}, u32[]{:S(2)}) async-start(f32[32,1,1536]{2,1,0:T(1,128)} %broadcast_in_dim.24), calls=%async_computation.3 | async-start | bytes 393216 | tf_op jit(solution)/shard_map/all_to_all | solution.py:611
  130.9 1.1 copy-start.4
  132.0 1.1 copy-start.6

commit v7 on v6

--- a/solution.py
+++ b/solution.py
@@ -167,17 +167,17 @@
             ].astype(jnp.bfloat16)
 
 
-def cut_kernel(width, w_ref, p2, p3, held, sems):
+def cut_kernel(width, w_ref, p2, p3, half2, full3, sems):
     me = lax.axis_index("fsdp")
     half = p2.shape[0]
     part = pl.ds(pl.multiple_of(lax.rem(lax.axis_index("dp"), 2) * half, TILE), half)
     coming = [
-        pltpu.make_async_copy(w_ref.at[part, columns_of(me ^ k, width)], held.at[i], sems.at[0, i])
-        for i, k in enumerate((2, 3))
+        pltpu.make_async_copy(w_ref.at[part, columns_of(me ^ 2, width)], half2, sems.at[0]),
+        pltpu.make_async_copy(w_ref.at[:, columns_of(me ^ 3, width)], full3, sems.at[1]),
     ]
     leaving = [
-        pltpu.make_async_copy(held.at[i], target, sems.at[1, i])
-        for i, target in enumerate((p2, p3))
+        pltpu.make_async_copy(half2, p2, sems.at[2]),
+        pltpu.make_async_copy(full3, p3, sems.at[3]),
     ]
     for copy in coming:
         copy.start()
@@ -267,9 +267,9 @@
 
 def middle_kernel(steps, blocks, *refs):
     patches, normed, rstds, gain = refs[0:4], refs[4:8], refs[8:12], refs[12]
-    cot0, pair, cot2, cot3, w_own, w2, w3, w2b, w3b, w_out_in = refs[13:23]
-    grads, scaled, hidden, masked, w_in, means = refs[23:27], *refs[27:32]
-    pre_grad, w_out, held, sems = refs[32:36]
+    cot0, pair, cot2, cot3, w_own, w2, w3, w2b, w_out_in = refs[13:22]
+    grads, scaled, hidden, masked, w_in, means = refs[22:26], *refs[26:31]
+    pre_grad, w_out, held, sems = refs[31:35]
     me = lax.axis_index("fsdp")
     parity = lax.rem(lax.axis_index("dp"), 2)
     rows = steps * blocks
@@ -290,9 +290,8 @@
         move(pair.at[rows:, :wide], w_in.at[rows_of(me ^ 1, 0, half), :]),
         move(pair.at[rows:, wide:], w_in.at[rows_of(me ^ 1, 1, half), :]),
         move(w2, w_in.at[rows_of(me ^ 2, parity, half), :]),
-        move(w3, w_in.at[rows_of(me ^ 3, parity, half), :]),
+        move(w3, w_in.at[rows_of(me ^ 3), :]),
         move(w2b, w_in.at[rows_of(me ^ 2, 1 - parity, half), :]),
-        move(w3b, w_in.at[rows_of(me ^ 3, 1 - parity, half), :]),
     ]
     for copy in coming:
         copy.wait()
@@ -447,10 +446,14 @@
     sub1, sub2 = across(sub_weight, 1), across(sub_weight, 2)
     w2, w3 = pl.pallas_call(
         functools.partial(cut_kernel, wide),
-        out_shape=(pltpu.HBM((deep // 2, wide), bf16),) * 2,
+        out_shape=(pltpu.HBM((deep // 2, wide), bf16), pltpu.HBM((deep, wide), bf16)),
         in_specs=[ANY],
         out_specs=(ANY,) * 2,
-        scratch_shapes=[pltpu.VMEM((2, deep // 2, wide), bf16), dma((2, 2))],
+        scratch_shapes=[
+            pltpu.VMEM((deep // 2, wide), bf16),
+            pltpu.VMEM((deep, wide), bf16),
+            dma((4,)),
+        ],
         compiler_params=params(),
         cost_estimate=cost(1),
     )(w_far)
@@ -509,8 +512,7 @@
         cost_estimate=cost(1),
     )(sub_weight, *far(sub1, sub2, sub3), depth_kernel, gain)
     w2b = across_dp(w2, 1)
-    got, weight, w3, w2b = lax.optimization_barrier((got, weight, w3, w2b))
-    w3b = across_dp(w3, 1)
+    got, weight, w2b = lax.optimization_barrier((got, weight, w2b))
     patches0 = pl.pallas_call(
         functools.partial(unpack_kernel, n, cap, blocks, steps),
         out_shape=sds((rows + blocks, block_shape[0] // steps * LANES), bf16),
@@ -542,7 +544,7 @@
         cost_estimate=cost(4),
     )
     groups = [list(forward(*near(patches[0], weight, scales)))]
-    groups[0][0], patches[1] = lax.optimization_barrier((groups[0][0], patches[1]))
+    groups[0][0], patches[1], w3 = lax.optimization_barrier((groups[0][0], patches[1], w3))
     groups.append(list(forward(*near(patches[1], weight, scales))))
     groups[1][0], cot_relay, patches[2] = lax.optimization_barrier(
         (groups[1][0], cot2, patches[2])
@@ -562,7 +564,7 @@
             pltpu.VMEM((width, wide), bf16),
             pltpu.VMEM((2, 4 * rows, LANES), bf16),
         ),
-        in_specs=[VMEM] * 13 + [ANY] * 10,
+        in_specs=[VMEM] * 13 + [ANY] * 9,
         out_specs=(ANY,) * 4 + (VMEM,) * 5,
         scratch_shapes=[
             pltpu.VMEM((4 * rows, wide), bf16),
@@ -574,7 +576,7 @@
         cost_estimate=cost(12),
     )(
         *patches, *normeds, *rstds, gain,
-        *far(cot0, pair, cot2, cot3), w_far, *far(w2, w3, w2b, w3b), w_out,
+        *far(cot0, pair, cot2, cot3), w_far, *far(w2, w3, w2b), w_out,
     )
     g3, g2, g1 = across(g3, 3), across(g2, 2), across(g1, 1)
 
@@ -621,7 +623,7 @@
         scratch_shapes=[pltpu.VMEM((4, deep, wide), bf16), dma((2, 4))],
         compiler_params=params(),
         cost_estimate=cost(2),
-    )(g0, g1, g2, g3)
+    )(*far(g0, g1, g2, g3))
     return (grad_in[None], grad_out[None], kernel_grad)
 
 

time: 137 us -> 135 us (0.985)
  starting transfers between devices: 32.3 us -> 36 us
  local copies, waits for them, and re-layouts: 9.62 us -> 6.72 us
  waiting for transfers between devices: 33.6 us -> 31.2 us
    ppermute x14, waiting for transfers between devices: 26.3 us -> 15.2 us  [across(): return lax.ppermute(value, 'fsdp', [(i, i ^ k) for i in range(n)])]
    ppermute x2 -> x1, waiting for transfers between devices: 0.01 us -> 8.11 us  [across_dp(): return lax.ppermute(value, 'dp', [(i, i ^ k) for i in range(n)])]
    unnamed x41 -> x29, local copies, waits for them, and re-layouts: 8.2 us -> 5.31 us
    ppermute x14, starting transfers between devices: 10.9 us -> 13.6 us  [across(): return lax.ppermute(value, 'fsdp', [(i, i ^ k) for i in range(n)])]
    all_to_all x1, starting transfers between devices: 4.33 us -> 7.01 us  [on_device(): lax.all_to_all(taps.reshape(devices, 1, -1), every, split_axis=0, concat_...]
    ppermute x2 -> x1, starting transfers between devices: 3.2 us -> 1.73 us  [across_dp(): return lax.ppermute(value, 'dp', [(i, i ^ k) for i in range(n)])]
  transfers between devices with their start and end apart: 20 -> 19, of which waited for: 5 -> 8; matrix products, arithmetic and copies ran while one was open for 1% -> 1% of each run, Pallas kernels for 34% -> 34%
where the time goes in v7:
time: 135 us
  Pallas kernels  59.1 us (44%)
  starting transfers between devices  36 us (27%)
  waiting for transfers between devices  31.2 us (23%)
  local copies, waits for them, and re-layouts  6.72 us (5%)
  between operations  1.61 us (1%)
    ppermute x14, waiting for transfers between devices, across(): return lax.ppermute(value, 'fsdp', [(i, i ^ k) for i in range(n)])  15.2 us
    ppermute x14, starting transfers between devices, across(): return lax.ppermute(value, 'fsdp', [(i, i ^ k) for i in range(n)])  13.6 us
    pallas_call x1, Pallas kernels, on_device(): pl.pallas_call(functools.partial(middle_kernel, steps, blocks), out_shape...  12.8 us
    pallas_call x1, Pallas kernels, on_device(): pl.pallas_call(functools.partial(backward_kernel, steps, blocks), out_sha...  12.4 us
    pallas_call x2, Pallas kernels, on_device(): groups.append(forward(*near(patches[k], weight, scales)))  8.61 us
    ppermute x1, waiting for transfers between devices, across_dp(): return lax.ppermute(value, 'dp', [(i, i ^ k) for i in range(n)])  8.11 us
    all_to_all x1, starting transfers between devices, on_device(): lax.all_to_all(taps.reshape(devices, 1, -1), every, split_axis=0, concat_...  7.01 us
    all_to_all x1, starting transfers between devices, on_device(): lax.all_to_all(jnp.broadcast_to(info[None], (n, home + 1)), 'dp', split_a...  5.74 us
  transfers between devices with their start and end apart: 19, of which 8 were waited for; matrix products, arithmetic and copies ran while one was open for 1% of the time, Pallas kernels for 34%

profile of v7, /device:TPU:1, one launch (start us, length us, event | category | flops | bytes accessed | tf_op | source)
XLA Modules:
  0.0 135.0 jit_solution(17260671873280125167)
XLA Ops:
  0.7 0.1 collective-permute-start
  0.8 2.7 %collective-permute-start.1 = (bf16[128,1536]{1,0:T(8,128)(2,1)}, bf16[128,1536]{1,0:T(8,128)(2,1)S(1)}, u32[]{:S(2)}, u32[]{:S(2)}) collective-permute-start(bf16[128,1536]{1,0:T(8,128)(2,1)} %sub0.1), channel_id=1, source_target_pairs={{0,2},{1,3},{2,0},{3,1},{4,6},{5,7},{6,4},{7,5},{8,10},{9,11},{10,... | collective-permute-start | bytes 1179656 | tf_op jit(solution)/shard_map/ppermute | solution.py:54
  3.5 2.0 %shard_map.122 = (bf16[192,768]{1,0:T(8,128)(2,1)}, bf16[384,768]{1,0:T(8,128)(2,1)}) custom-call(bf16[384,3072]{1,0:T(8,128)(2,1)} %refs_17_.1), custom_call_target="tpu_custom_call" | custom-call | bytes 3600000 | tf_op jit(solution)/shard_map/pallas_call | solution.py:447
  6.3 0.1 pad_add_fusion
  6.3 0.6 broadcast_in_dim.20
  6.9 5.7 %all-to-all-start = ((s32[8,1,49]{2,1,0:T(1,128)}), s32[8,1,49]{2,1,0:T(1,128)S(1)}, u32[]{:S(2)}, u32[]{:S(2)}) async-start(s32[8,1,49]{2,1,0:T(1,128)} %broadcast_in_dim.20), calls=%async_computation | async-start | bytes 8192 | tf_op jit(solution)/shard_map/all_to_all | solution.py:441
  12.7 5.2 %all-to-all-done = s32[8,1,49]{2,1,0:T(1,128)S(1)} async-done(((s32[8,1,49]{2,1,0:T(1,128)}), s32[8,1,49]{2,1,0:T(1,128)S(1)}, u32[]{:S(2)}, u32[]{:S(2)}) %all-to-all-start) | async-done | bytes 1600 | tf_op jit(solution)/shard_map/all_to_all | solution.py:441
  17.9 1.8 %shard_map.121 = bf16[8,6,64,128]{3,2,1,0:T(8,128)(2,1)} custom-call(s32[1,8]{1,0:T(1,128)S(1)} %copy-done.4, s32[8,49]{1,0:T(8,128)S(1)} %bitcast.15, bf16[6,8,64,128]{3,2,1,0:T(8,128)(2,1)S(1)} %bitcast.13), custom_call_target="tpu_custom_call" | custom-call | bytes 7200000 | tf_op jit(solution)/shard_map/pallas_call | solution.py:464
  19.8 0.7 copy-done.10
  20.5 5.3 %all-to-all-start.1 = ((bf16[8,6,64,128]{3,2,1,0:T(8,128)(2,1)}), bf16[8,6,64,128]{3,2,1,0:T(8,128)(2,1)S(1)}, u32[]{:S(2)}, u32[]{:S(2)}) async-start(bf16[8,6,64,128]{3,2,1,0:T(8,128)(2,1)} %shard_map.121), calls=%async_computation.1 | async-start | bytes 1572864 | tf_op jit(solution)/shard_map/all_to_all | solution.py:481
  25.7 2.5 %shard_map.127 = (bf16[256,1536]{1,0:T(8,128)(2,1)}, bf16[448,1536]{1,0:T(8,128)(2,1)}) custom-call(bf16[16,16,1536]{2,1,0:T(8,128)(2,1)S(1)} %bitcast.14, bf16[384,3072]{1,0:T(8,128)(2,1)} %refs_17_.1), custom_call_target="tpu_custom_call" | custom-call | bytes 7200000 | tf_op jit(solution)/shard_map/pallas_call | solution.py:483
  28.3 1.3 collective-permute-start.7
  29.6 1.4 %collective-permute-start.3 = (bf16[128,1536]{1,0:T(8,128)(2,1)S(1)}, bf16[128,1536]{1,0:T(8,128)(2,1)S(1)}, u32[]{:S(2)}, u32[]{:S(2)}) collective-permute-start(bf16[128,1536]{1,0:T(8,128)(2,1)S(1)} %collective-permute-done.1.sub2), channel_id=1, source_target_pairs={{0,1},{1,0},{2,3},{3,2},{4,5},{5,4},{6,7},{7,6},{8,9},{9,8},{10,11... | collective-permute-start | bytes 1179656 | tf_op jit(solution)/shard_map/ppermute | solution.py:54
  31.0 0.1 collective-permute-start.6
  31.1 0.5 collective-permute-start.10
  31.6 1.7 %collective-permute-start.4 = (bf16[192,768]{1,0:T(8,128)(2,1)S(1)}, bf16[192,768]{1,0:T(8,128)(2,1)}, u32[]{:S(2)}, u32[]{:S(2)}) collective-permute-start(bf16[192,768]{1,0:T(8,128)(2,1)S(1)} %copy-done.11), channel_id=1, source_target_pairs={{0,4},{4,0},{8,12},{12,8},{16,20},{20,16},{24,28},{28,24},{1,5},{5... | collective-permute-start | bytes 884744 | tf_op jit(solution)/shard_map/ppermute | solution.py:59
  33.3 0.8 copy-done.9
  34.1 2.3 %shard_map.123 = (bf16[512,1536]{1,0:T(8,128)(2,1)S(1)}, f32[32,1536]{1,0:T(8,128)S(1)}) custom-call(bf16[128,1536]{1,0:T(8,128)(2,1)} %sub0.1, bf16[128,1536]{1,0:T(8,128)(2,1)} %copy-done.7, bf16[128,1536]{1,0:T(8,128)(2,1)} %copy-done.8, bf16[128,1536]{1,0:T(8,128)(2,1)} %copy-done.9, f32[31,1536]{1,0:T(8,128)} %depth.1, ...), custom_call_target="tpu_custom_call" | custom-call | bytes 3600000 | tf_op jit(solution)/shard_map/pallas_call | solution.py:502
  36.4 8.1 %collective-permute-done.4.refs_20_ = bf16[192,768]{1,0:T(8,128)(2,1)} collective-permute-done((bf16[192,768]{1,0:T(8,128)(2,1)S(1)}, bf16[192,768]{1,0:T(8,128)(2,1)}, u32[]{:S(2)}, u32[]{:S(2)}) %collective-permute-start.4) | collective-permute-done | bytes 294944 | tf_op jit(solution)/shard_map/ppermute | solution.py:59
  44.5 0.2 all-to-all-done.1
  44.7 1.7 %shard_map.124.patches.refs_0_ = bf16[272,512]{1,0:T(8,128)(2,1)S(1)} custom-call(s32[1,8]{1,0:T(1,128)S(1)} %copy-done.4, s32[8,49]{1,0:T(8,128)S(1)} %bitcast.16, bf16[48,64,128]{2,1,0:T(8,128)(2,1)S(1)} %bitcast.12), custom_call_target="tpu_custom_call" | custom-call | bytes 7200000 | tf_op jit(solution)/shard_map/pallas_call | solution.py:516
  46.5 2.3 %collective-permute-start.5 = (bf16[272,512]{1,0:T(8,128)(2,1)S(1)}, bf16[272,512]{1,0:T(8,128)(2,1)S(1)}, u32[]{:S(2)}, u32[]{:S(2)}) collective-permute-start(bf16[272,512]{1,0:T(8,128)(2,1)S(1)} %shard_map.124.patches.refs_0_), channel_id=1, source_target_pairs={{0,1},{1,0},{2,3},{3,2},{4,5},{5,4},{6,7},{7,6},{8,9},{9,8},{10,11... | collective-permute-start | bytes 835592 | tf_op jit(solution)/shard_map/ppermute | solution.py:54
  48.7 1.3 collective-permute-start.8
  50.0 4.2 %shard_map.125 = (bf16[256,1536]{1,0:T(8,128)(2,1)S(1)}, bf16[256,1536]{1,0:T(8,128)(2,1)S(1)}, bf16[256,1536]{1,0:T(8,128)(2,1)S(1)}, f32[256,128]{1,0:T(8,128)S(1)}) custom-call(bf16[272,512]{1,0:T(8,128)(2,1)S(1)} %shard_map.124.patches.refs_0_, bf16[512,1536]{1,0:T(8,128)(2,1)S(1)} %get-tuple-element.62.weight, f32[32,1536]{1,0:T(8,128)S(1)} %get-tuple-element.63.scales), custom_call_target="tpu_custom_call" | custom-call | bytes 14400000 | tf_op jit(solution)/shard_map/pallas_call | solution.py:546
  54.2 8.0 %collective-permute-done.6.refs_19_ = bf16[384,768]{1,0:T(8,128)(2,1)} collective-permute-done((bf16[384,768]{1,0:T(8,128)(2,1)}, bf16[384,768]{1,0:T(8,128)(2,1)}, u32[]{:S(2)}, u32[]{:S(2)}) %collective-permute-start.6) | collective-permute-done | bytes 589856 | tf_op jit(solution)/shard_map/ppermute | solution.py:54
  62.2 4.2 %shard_map.126 = (bf16[256,1536]{1,0:T(8,128)(2,1)S(1)}, bf16[256,1536]{1,0:T(8,128)(2,1)S(1)}, bf16[256,1536]{1,0:T(8,128)(2,1)S(1)}, f32[256,128]{1,0:T(8,128)S(1)}) custom-call(bf16[272,512]{1,0:T(8,128)(2,1)S(1)} %collective-permute-done.5.patches.refs_1_, bf16[512,1536]{1,0:T(8,128)(2,1)S(1)} %get-tuple-element.62.weight, ...), custom_call_target="tpu_custom_call" | custom-call | bytes 14400000 | tf_op jit(solution)/shard_map/pallas_call | solution.py:548
  66.4 0.7 collective-permute-start.11
  67.1 4.2 %shard_map.128 = (bf16[256,1536]{1,0:T(8,128)(2,1)S(1)}, bf16[256,1536]{1,0:T(8,128)(2,1)S(1)}, bf16[256,1536]{1,0:T(8,128)(2,1)S(1)}, f32[256,128]{1,0:T(8,128)S(1)}) custom-call(bf16[272,512]{1,0:T(8,128)(2,1)S(1)} %collective-permute-done.8.patches.refs_2_, bf16[512,1536]{1,0:T(8,128)(2,1)S(1)} %get-tuple-element.62.weight, ...), custom_call_target="tpu_custom_call" | custom-call | bytes 14400000 | tf_op jit(solution)/shard_map/pallas_call | solution.py:555
  71.3 4.4 %shard_map.129 = (bf16[256,1536]{1,0:T(8,128)(2,1)S(1)}, bf16[256,1536]{1,0:T(8,128)(2,1)S(1)}, bf16[256,1536]{1,0:T(8,128)(2,1)S(1)}, f32[256,128]{1,0:T(8,128)S(1)}) custom-call(bf16[272,512]{1,0:T(8,128)(2,1)S(1)} %collective-permute-done.9.patches.refs_3_, bf16[512,1536]{1,0:T(8,128)(2,1)S(1)} %get-tuple-element.62.weight, ...), custom_call_target="tpu_custom_call" | custom-call | bytes 14400000 | tf_op jit(solution)/shard_map/pallas_call | solution.py:555
  75.8 0.9 copy-done.5
  76.6 12.8 %shard_map.130 = (bf16[384,768]{1,0:T(8,128)(2,1)}, bf16[384,768]{1,0:T(8,128)(2,1)}, bf16[384,768]{1,0:T(8,128)(2,1)}, bf16[384,768]{1,0:T(8,128)(2,1)}, bf16[1...) custom-call(bf16[272,512]{1,0:T(8,128)(2,1)S(1)} %shard_map.124.patc, ...), custom_call_target="tpu_custom_call" | custom-call | bytes 43200000 | tf_op jit(solution)/shard_map/pallas_call | solution.py:557
  89.4 1.3 collective-permute-start.13
  90.7 12.4 %shard_map.131 = f32[32,1,1536]{2,1,0:T(1,128)} custom-call(f32[1,1536]{1,0:T(1,128)S(1)} %reshape.35.gain.refs_12_.refs_0_, bf16[1024,768]{1,0:T(8,128)(2,1)S(1)} %get-tuple-element.85.refs_1_, bf16[1536,768]{1,0:T(8,128)(2,1)S(1)} %get-tuple-element.86.refs_2_, bf16[1024,1536]{1,0:T(8,128)(2,1)S(1)} %get-tuple-element.87.refs_3_.masked, ...), custom_call_target="tpu_custom_call" | custom-call | bytes 46800000 | tf_op jit(solution)/shard_map/pallas_call | solution.py:583
  103.1 1.0 collective-permute-done.13.refs_2_
  104.1 0.9 copy-done.6
  105.0 7.0 %all-to-all-start.2 = ((f32[32,1,1536]{2,1,0:T(1,128)}), f32[32,1,1536]{2,1,0:T(1,128)S(1)}, u32[]{:S(2)}, u32[]{:S(2)}) async-start(f32[32,1,1536]{2,1,0:T(1,128)} %shard_map.131), calls=%async_computation.2 | async-start | bytes 393216 | tf_op jit(solution)/shard_map/all_to_all | solution.py:599
  112.0 0.3 collective-permute-start.12
  112.3 1.5 %collective-permute-start.14 = (bf16[384,768]{1,0:T(8,128)(2,1)}, bf16[384,768]{1,0:T(8,128)(2,1)}, u32[]{:S(2)}, u32[]{:S(2)}) collective-permute-start(bf16[384,768]{1,0:T(8,128)(2,1)} %get-tuple-element.100), channel_id=1, source_target_pairs={{0,3},{1,2},{2,1},{3,0},{4,7},{5,6},{6,5},{7,4},{8,11},{9,10},{10,... | collective-permute-start | bytes 1769480 | tf_op jit(solution)/shard_map/ppermute | solution.py:54
  113.9 1.4 %copy-done.1 = bf16[1024,768]{1,0:T(8,128)(2,1)S(1)} copy-done((bf16[1024,768]{1,0:T(8,128)(2,1)S(1)}, bf16[1024,768]{1,0:T(8,128)(2,1)}, u32[]{:S(2)}) %copy-start.1) | copy-done | bytes 1572888
  115.3 4.0 %shard_map.133 = bf16[768,1536]{1,0:T(8,128)(2,1)} custom-call(bf16[1024,768]{1,0:T(8,128)(2,1)S(1)} %copy-done.1, bf16[1024,1536]{1,0:T(8,128)(2,1)S(1)} %get-tuple-element.87.refs_3_.masked), custom_call_target="tpu_custom_call" | custom-call | bytes 14400000 | tf_op jit(solution)/shard_map/pallas_call | solution.py:603
  119.3 2.0 %all-to-all-done.2 = f32[32,1,1536]{2,1,0:T(1,128)S(1)} async-done(((f32[32,1,1536]{2,1,0:T(1,128)}), f32[32,1,1536]{2,1,0:T(1,128)S(1)}, u32[]{:S(2)}, u32[]{:S(2)}) %all-to-all-start.2) | async-done | bytes 196640 | tf_op jit(solution)/shard_map/all_to_all | solution.py:599
  121.3 0.1 reduce_sum.9
  121.5 0.8 broadcast_in_dim.24
  122.3 2.7 %all-to-all-start.3 = ((f32[32,1,1536]{2,1,0:T(1,128)}), f32[32,1,1536]{2,1,0:T(1,128)S(1)}, u32[]{:S(2)}, u32[]{:S(2)}) async-start(f32[32,1,1536]{2,1,0:T(1,128)} %broadcast_in_dim.24), calls=%async_computation.3 | async-start | bytes 393216 | tf_op jit(solution)/shard_map/all_to_all | solution.py:613
  125.0 6.2 %collective-permute-done.14.refs_3_ = bf16[384,768]{1,0:T(8,128)(2,1)} collective-permute-done((bf16[384,768]{1,0:T(8,128)(2,1)}, bf16[384,768]{1,0:T(8,128)(2,1)}, u32[]{:S(2)}, u32[]{:S(2)}) %collective-permute-start.14) | collective-permute-done | bytes 589856 | tf_op jit(solution)/shard_map/ppermute | solution.py:54
  131.2 2.5 %shard_map.132 = bf16[384,3072]{1,0:T(8,128)(2,1)} custom-call(bf16[384,768]{1,0:T(8,128)(2,1)} %get-tuple-element.83.refs_0_, bf16[384,768]{1,0:T(8,128)(2,1)} %collective-permute-done.12.refs_1_, bf16[384,768]{1,0:T(8,128)(2,1)} %copy-done.6, bf16[384,768]{1,0:T(8,128)(2,1)} %collective-permute-done.14.refs_3_), custom_call_target="tpu_custom_call" | custom-call | bytes 7200000 | tf_op jit(solution)/shard_map/pallas_call | solution.py:618
  133.8 0.5 all-to-all-done.3
  134.3 0.7 copy.15
  (41 shorter events, 0.2 us)
Async XLA Ops:
  0.6 5.6 %copy-start.13 = (s32[1,1,48]{2,1,0:T(1,128)S(1)}, s32[1,1,48]{2,1,0:T(1,128)}, u32[]{:S(2)}) copy-start(s32[1,1,48]{2,1,0:T(1,128)} %param.12) | copy-start | bytes 580
  0.6 12.0 %copy-start.12 = (f32[1536]{0:T(1024)S(1)}, f32[1536]{0:T(1024)}, u32[]{:S(2)}) copy-start(f32[1536]{0:T(1024)} %param.17) | copy-start | bytes 18436
  0.7 17.3 %copy-start.4 = (s32[1,8]{1,0:T(1,128)S(1)}, s32[1,8]{1,0:T(1,128)}, u32[]{:S(2)}) copy-start(s32[1,8]{1,0:T(1,128)} %order_ref.3) | copy-start | bytes 100
  0.7 17.3 %copy-start.2 = (bf16[1,1,48,64,128]{4,3,2,1,0:T(8,128)(2,1)S(1)}, bf16[1,1,48,64,128]{4,3,2,1,0:T(8,128)(2,1)}, u32[]{:S(2)}) copy-start(bf16[1,1,48,64,128]{4,3,2,1,0:T(8,128)(2,1)} %param.10) | copy-start | bytes 2359300
  0.7 25.1 %copy-start.3 = (bf16[1,1,16,16,1536]{4,3,2,1,0:T(8,128)(2,1)S(1)}, bf16[1,1,16,16,1536]{4,3,2,1,0:T(8,128)(2,1)}, u32[]{:S(2)}) copy-start(bf16[1,1,16,16,1536]{4,3,2,1,0:T(8,128)(2,1)} %param.14) | copy-start | bytes 2359300
  0.7 19.1 %collective-permute-start = (bf16[128,1536]{1,0:T(8,128)(2,1)}, bf16[128,1536]{1,0:T(8,128)(2,1)S(1)}, u32[]{:S(2)}, u32[]{:S(2)}) collective-permute-start(bf16[128,1536]{1,0:T(8,128)(2,1)} %sub0.1), channel_id=1, source_target_pairs={{0,1},{1,0},{2,3},{3,2},{4,5},{5,4},{6,7},{7,6},{8,9},{9,8},{10,11... | collective-permute-start | bytes 1179656 | tf_op jit(solution)/shard_map/ppermute | solution.py:54
  0.8 19.0 %collective-permute-start.1 = (bf16[128,1536]{1,0:T(8,128)(2,1)}, bf16[128,1536]{1,0:T(8,128)(2,1)S(1)}, u32[]{:S(2)}, u32[]{:S(2)}) collective-permute-start(bf16[128,1536]{1,0:T(8,128)(2,1)} %sub0.1), channel_id=1, source_target_pairs={{0,2},{1,3},{2,0},{3,1},{4,6},{5,7},{6,4},{7,5},{8,10},{9,11},{10,... | collective-permute-start | bytes 1179656 | tf_op jit(solution)/shard_map/ppermute | solution.py:54
  5.5 14.2 %collective-permute-start.2 = (bf16[192,768]{1,0:T(8,128)(2,1)}, bf16[192,768]{1,0:T(8,128)(2,1)S(1)}, u32[]{:S(2)}, u32[]{:S(2)}) collective-permute-start(bf16[192,768]{1,0:T(8,128)(2,1)} %get-tuple-element.54), channel_id=1, source_target_pairs={{0,2},{1,3},{2,0},{3,1},{4,6},{5,7},{6,4},{7,5},{8,10},{9,11},{10,... | collective-permute-start | bytes 884744 | tf_op jit(solution)/shard_map/ppermute | solution.py:54
  6.9 11.0 %all-to-all-start = ((s32[8,1,49]{2,1,0:T(1,128)}), s32[8,1,49]{2,1,0:T(1,128)S(1)}, u32[]{:S(2)}, u32[]{:S(2)}) async-start(s32[8,1,49]{2,1,0:T(1,128)} %broadcast_in_dim.20), calls=%async_computation | async-start | bytes 8192 | tf_op jit(solution)/shard_map/all_to_all | solution.py:441
  19.7 0.7 copy-start.10
  19.8 8.5 %copy-start.7 = (bf16[128,1536]{1,0:T(8,128)(2,1)}, bf16[128,1536]{1,0:T(8,128)(2,1)S(1)}, u32[]{:S(2)}) copy-start(bf16[128,1536]{1,0:T(8,128)(2,1)S(1)} %collective-permute-done.sub1) | copy-start | bytes 1179652
  19.8 9.8 %copy-start.8 = (bf16[128,1536]{1,0:T(8,128)(2,1)}, bf16[128,1536]{1,0:T(8,128)(2,1)S(1)}, u32[]{:S(2)}) copy-start(bf16[128,1536]{1,0:T(8,128)(2,1)S(1)} %collective-permute-done.1.sub2) | copy-start | bytes 1179652
  20.5 24.2 %all-to-all-start.1 = ((bf16[8,6,64,128]{3,2,1,0:T(8,128)(2,1)}), bf16[8,6,64,128]{3,2,1,0:T(8,128)(2,1)S(1)}, u32[]{:S(2)}, u32[]{:S(2)}) async-start(bf16[8,6,64,128]{3,2,1,0:T(8,128)(2,1)} %shard_map.121), calls=%async_computation.1 | async-start | bytes 1572864 | tf_op jit(solution)/shard_map/all_to_all | solution.py:481
  25.7 5.9 %copy-start.11 = (bf16[192,768]{1,0:T(8,128)(2,1)S(1)}, bf16[192,768]{1,0:T(8,128)(2,1)}, u32[]{:S(2)}) copy-start(bf16[192,768]{1,0:T(8,128)(2,1)} %copy-done.10) | copy-start | bytes 884740
  28.3 38.2 %collective-permute-start.7 = (bf16[256,1536]{1,0:T(8,128)(2,1)}, bf16[256,1536]{1,0:T(8,128)(2,1)}, u32[]{:S(2)}, u32[]{:S(2)}) collective-permute-start(bf16[256,1536]{1,0:T(8,128)(2,1)} %get-tuple-element.69.refs_13_), channel_id=1, source_target_pairs={{0,2},{1,3},{2,0},{3,1},{4,6},{5,7},{6,4},{7,5},{8,10},{9,11},{10,... | collective-permute-start | bytes 2359304 | tf_op jit(solution)/shard_map/ppermute | solution.py:54
  29.6 3.8 %collective-permute-start.3 = (bf16[128,1536]{1,0:T(8,128)(2,1)S(1)}, bf16[128,1536]{1,0:T(8,128)(2,1)S(1)}, u32[]{:S(2)}, u32[]{:S(2)}) collective-permute-start(bf16[128,1536]{1,0:T(8,128)(2,1)S(1)} %collective-permute-done.1.sub2), channel_id=1, source_target_pairs={{0,1},{1,0},{2,3},{3,2},{4,5},{5,4},{6,7},{7,6},{8,9},{9,8},{10,11... | collective-permute-start | bytes 1179656 | tf_op jit(solution)/shard_map/ppermute | solution.py:54
  31.0 31.2 %collective-permute-start.6 = (bf16[384,768]{1,0:T(8,128)(2,1)}, bf16[384,768]{1,0:T(8,128)(2,1)}, u32[]{:S(2)}, u32[]{:S(2)}) collective-permute-start(bf16[384,768]{1,0:T(8,128)(2,1)} %get-tuple-element.65), channel_id=1, source_target_pairs={{0,3},{1,2},{2,1},{3,0},{4,7},{5,6},{6,5},{7,4},{8,11},{9,10},{10,... | collective-permute-start | bytes 1769480 | tf_op jit(solution)/shard_map/ppermute | solution.py:54
  31.1 44.6 %collective-permute-start.10 = (bf16[448,1536]{1,0:T(8,128)(2,1)}, bf16[448,1536]{1,0:T(8,128)(2,1)}, u32[]{:S(2)}, u32[]{:S(2)}) collective-permute-start(bf16[448,1536]{1,0:T(8,128)(2,1)} %get-tuple-element.79), channel_id=1, source_target_pairs={{0,1},{1,0},{2,3},{3,2},{4,5},{5,4},{6,7},{7,6},{8,9},{9,8},{10,11... | collective-permute-start | bytes 4128776 | tf_op jit(solution)/shard_map/ppermute | solution.py:54
  31.6 12.9 %collective-permute-start.4 = (bf16[192,768]{1,0:T(8,128)(2,1)S(1)}, bf16[192,768]{1,0:T(8,128)(2,1)}, u32[]{:S(2)}, u32[]{:S(2)}) collective-permute-start(bf16[192,768]{1,0:T(8,128)(2,1)S(1)} %copy-done.11), channel_id=1, source_target_pairs={{0,4},{4,0},{8,12},{12,8},{16,20},{20,16},{24,28},{28,24},{1,5},{5... | collective-permute-start | bytes 884744 | tf_op jit(solution)/shard_map/ppermute | solution.py:59
  33.3 0.8 copy-start.9
  46.5 15.7 %collective-permute-start.5 = (bf16[272,512]{1,0:T(8,128)(2,1)S(1)}, bf16[272,512]{1,0:T(8,128)(2,1)S(1)}, u32[]{:S(2)}, u32[]{:S(2)}) collective-permute-start(bf16[272,512]{1,0:T(8,128)(2,1)S(1)} %shard_map.124.patches.refs_0_), channel_id=1, source_target_pairs={{0,1},{1,0},{2,3},{3,2},{4,5},{5,4},{6,7},{7,6},{8,9},{9,8},{10,11... | collective-permute-start | bytes 835592 | tf_op jit(solution)/shard_map/ppermute | solution.py:54
  48.7 17.7 %collective-permute-start.8 = (bf16[272,512]{1,0:T(8,128)(2,1)S(1)}, bf16[272,512]{1,0:T(8,128)(2,1)S(1)}, u32[]{:S(2)}, u32[]{:S(2)}) collective-permute-start(bf16[272,512]{1,0:T(8,128)(2,1)S(1)} %shard_map.124.patches.refs_0_), channel_id=1, source_target_pairs={{0,2},{1,3},{2,0},{3,1},{4,6},{5,7},{6,4},{7,5},{8,10},{9,11},{10,... | collective-permute-start | bytes 835592 | tf_op jit(solution)/shard_map/ppermute | solution.py:54
  66.4 9.3 %collective-permute-start.11 = (bf16[256,1536]{1,0:T(8,128)(2,1)}, bf16[256,1536]{1,0:T(8,128)(2,1)S(1)}, u32[]{:S(2)}, u32[]{:S(2)}) collective-permute-start(bf16[256,1536]{1,0:T(8,128)(2,1)} %collective-permute-done.7.refs_15_), channel_id=1, source_target_pairs={{0,1},{1,0},{2,3},{3,2},{4,5},{5,4},{6,7},{7,6},{8,9},{9,8},{10,11... | collective-permute-start | bytes 2359304 | tf_op jit(solution)/shard_map/ppermute | solution.py:54
  67.1 4.2 %collective-permute-start.9 = (bf16[272,512]{1,0:T(8,128)(2,1)S(1)}, bf16[272,512]{1,0:T(8,128)(2,1)S(1)}, u32[]{:S(2)}, u32[]{:S(2)}) collective-permute-start(bf16[272,512]{1,0:T(8,128)(2,1)S(1)} %collective-permute-done.8.patches.refs_2_), channel_id=1, source_target_pairs={{0,1},{1,0},{2,3},{3,2},{4,5},{5,4},{6,7},{7,6},{8,9},{9,8},{10,11... | collective-permute-start | bytes 835592 | tf_op jit(solution)/shard_map/ppermute | solution.py:54
  75.8 0.9 copy-start.5
  89.4 13.7 %copy-start = (bf16[1024,768]{1,0:T(8,128)(2,1)}, bf16[1024,768]{1,0:T(8,128)(2,1)S(1)}, u32[]{:S(2)}) copy-start(bf16[1024,768]{1,0:T(8,128)(2,1)S(1)} %get-tuple-element.102.hidden) | copy-start | bytes 4718596
  89.4 14.7 %collective-permute-start.13 = (bf16[384,768]{1,0:T(8,128)(2,1)}, bf16[384,768]{1,0:T(8,128)(2,1)S(1)}, u32[]{:S(2)}, u32[]{:S(2)}) collective-permute-start(bf16[384,768]{1,0:T(8,128)(2,1)} %get-tuple-element.97), channel_id=1, source_target_pairs={{0,2},{1,3},{2,0},{3,1},{4,6},{5,7},{6,4},{7,5},{8,10},{9,11},{10,... | collective-permute-start | bytes 1769480 | tf_op jit(solution)/shard_map/ppermute | solution.py:54
  104.1 0.9 copy-start.6
  105.0 16.4 %all-to-all-start.2 = ((f32[32,1,1536]{2,1,0:T(1,128)}), f32[32,1,1536]{2,1,0:T(1,128)S(1)}, u32[]{:S(2)}, u32[]{:S(2)}) async-start(f32[32,1,1536]{2,1,0:T(1,128)} %shard_map.131), calls=%async_computation.2 | async-start | bytes 393216 | tf_op jit(solution)/shard_map/all_to_all | solution.py:599
  112.0 13.0 %collective-permute-start.12 = (bf16[384,768]{1,0:T(8,128)(2,1)}, bf16[384,768]{1,0:T(8,128)(2,1)}, u32[]{:S(2)}, u32[]{:S(2)}) collective-permute-start(bf16[384,768]{1,0:T(8,128)(2,1)} %get-tuple-element.84), channel_id=1, source_target_pairs={{0,1},{1,0},{2,3},{3,2},{4,5},{5,4},{6,7},{7,6},{8,9},{9,8},{10,11... | collective-permute-start | bytes 1769480 | tf_op jit(solution)/shard_map/ppermute | solution.py:54
  112.3 18.9 %collective-permute-start.14 = (bf16[384,768]{1,0:T(8,128)(2,1)}, bf16[384,768]{1,0:T(8,128)(2,1)}, u32[]{:S(2)}, u32[]{:S(2)}) collective-permute-start(bf16[384,768]{1,0:T(8,128)(2,1)} %get-tuple-element.100), channel_id=1, source_target_pairs={{0,3},{1,2},{2,1},{3,0},{4,7},{5,6},{6,5},{7,4},{8,11},{9,10},{10,... | collective-permute-start | bytes 1769480 | tf_op jit(solution)/shard_map/ppermute | solution.py:54
  113.9 1.4 %copy-start.1 = (bf16[1024,768]{1,0:T(8,128)(2,1)S(1)}, bf16[1024,768]{1,0:T(8,128)(2,1)}, u32[]{:S(2)}) copy-start(bf16[1024,768]{1,0:T(8,128)(2,1)} %copy-done) | copy-start | bytes 4718596
  122.3 11.9 %all-to-all-start.3 = ((f32[32,1,1536]{2,1,0:T(1,128)}), f32[32,1,1536]{2,1,0:T(1,128)S(1)}, u32[]{:S(2)}, u32[]{:S(2)}) async-start(f32[32,1,1536]{2,1,0:T(1,128)} %broadcast_in_dim.24), calls=%async_computation.3 | async-start | bytes 393216 | tf_op jit(solution)/shard_map/all_to_all | solution.py:613

commit v8 on v7

--- a/solution.py
+++ b/solution.py
@@ -544,10 +544,10 @@
         cost_estimate=cost(4),
     )
     groups = [list(forward(*near(patches[0], weight, scales)))]
-    groups[0][0], patches[1], w3 = lax.optimization_barrier((groups[0][0], patches[1], w3))
+    groups[0][0], patches[1] = lax.optimization_barrier((groups[0][0], patches[1]))
     groups.append(list(forward(*near(patches[1], weight, scales))))
-    groups[1][0], cot_relay, patches[2] = lax.optimization_barrier(
-        (groups[1][0], cot2, patches[2])
+    groups[1][0], cot_relay, patches[2], w3 = lax.optimization_barrier(
+        (groups[1][0], cot2, patches[2], w3)
     )
     cot3 = across(cot_relay, 1)
     patches.append(across(patches[2], 1))

time: 135 us -> 135 us (level)
  waiting for transfers between devices: 31.2 us -> 29.8 us
    ppermute x14, starting transfers between devices: 13.6 us -> 15 us  [across(): return lax.ppermute(value, 'fsdp', [(i, i ^ k) for i in range(n)])]
    ppermute x14, waiting for transfers between devices: 15.2 us -> 13.8 us  [across(): return lax.ppermute(value, 'fsdp', [(i, i ^ k) for i in range(n)])]
  transfers between devices with their start and end apart: 19 -> 19, of which waited for: 8 -> 9; matrix products, arithmetic and copies ran while one was open for 1% -> 1% of each run, Pallas kernels for 34% -> 34%
where the time goes in v8:
time: 135 us
  Pallas kernels  59.1 us (44%)
  starting transfers between devices  37.2 us (28%)
  waiting for transfers between devices  29.8 us (22%)
  local copies, waits for them, and re-layouts  6.72 us (5%)
  between operations  1.6 us (1%)
    ppermute x14, starting transfers between devices, across(): return lax.ppermute(value, 'fsdp', [(i, i ^ k) for i in range(n)])  15 us
    ppermute x14, waiting for transfers between devices, across(): return lax.ppermute(value, 'fsdp', [(i, i ^ k) for i in range(n)])  13.8 us
    pallas_call x1, Pallas kernels, on_device(): pl.pallas_call(functools.partial(middle_kernel, steps, blocks), out_shape...  12.8 us
    pallas_call x1, Pallas kernels, on_device(): pl.pallas_call(functools.partial(backward_kernel, steps, blocks), out_sha...  12.4 us
    pallas_call x2, Pallas kernels, on_device(): groups.append(forward(*near(patches[k], weight, scales)))  8.61 us
    ppermute x1, waiting for transfers between devices, across_dp(): return lax.ppermute(value, 'dp', [(i, i ^ k) for i in range(n)])  8.11 us
    all_to_all x1, starting transfers between devices, on_device(): lax.all_to_all(taps.reshape(devices, 1, -1), every, split_axis=0, concat_...  6.82 us
    all_to_all x1, starting transfers between devices, on_device(): lax.all_to_all(jnp.broadcast_to(info[None], (n, home + 1)), 'dp', split_a...  5.74 us
  transfers between devices with their start and end apart: 19, of which 9 were waited for; matrix products, arithmetic and copies ran while one was open for 1% of the time, Pallas kernels for 34%

profile of v8, /device:TPU:1, one launch (start us, length us, event | category | flops | bytes accessed | tf_op | source)
XLA Modules:
  0.0 134.8 jit_solution(646281158224154065)
XLA Ops:
  0.7 0.1 collective-permute-start
  0.8 2.7 %collective-permute-start.1 = (bf16[128,1536]{1,0:T(8,128)(2,1)}, bf16[128,1536]{1,0:T(8,128)(2,1)S(1)}, u32[]{:S(2)}, u32[]{:S(2)}) collective-permute-start(bf16[128,1536]{1,0:T(8,128)(2,1)} %sub0.1), channel_id=1, source_target_pairs={{0,2},{1,3},{2,0},{3,1},{4,6},{5,7},{6,4},{7,5},{8,10},{9,11},{10,... | collective-permute-start | bytes 1179656 | tf_op jit(solution)/shard_map/ppermute | solution.py:54
  3.5 2.0 %shard_map.122 = (bf16[192,768]{1,0:T(8,128)(2,1)}, bf16[384,768]{1,0:T(8,128)(2,1)}) custom-call(bf16[384,3072]{1,0:T(8,128)(2,1)} %refs_17_.1), custom_call_target="tpu_custom_call" | custom-call | bytes 3600000 | tf_op jit(solution)/shard_map/pallas_call | solution.py:447
  6.3 0.6 broadcast_in_dim.20
  6.9 5.7 %all-to-all-start = ((s32[8,1,49]{2,1,0:T(1,128)}), s32[8,1,49]{2,1,0:T(1,128)S(1)}, u32[]{:S(2)}, u32[]{:S(2)}) async-start(s32[8,1,49]{2,1,0:T(1,128)} %broadcast_in_dim.20), calls=%async_computation | async-start | bytes 8192 | tf_op jit(solution)/shard_map/all_to_all | solution.py:441
  12.7 5.2 %all-to-all-done = s32[8,1,49]{2,1,0:T(1,128)S(1)} async-done(((s32[8,1,49]{2,1,0:T(1,128)}), s32[8,1,49]{2,1,0:T(1,128)S(1)}, u32[]{:S(2)}, u32[]{:S(2)}) %all-to-all-start) | async-done | bytes 1600 | tf_op jit(solution)/shard_map/all_to_all | solution.py:441
  17.9 1.8 %shard_map.121 = bf16[8,6,64,128]{3,2,1,0:T(8,128)(2,1)} custom-call(s32[1,8]{1,0:T(1,128)S(1)} %copy-done.4, s32[8,49]{1,0:T(8,128)S(1)} %bitcast.15, bf16[6,8,64,128]{3,2,1,0:T(8,128)(2,1)S(1)} %bitcast.13), custom_call_target="tpu_custom_call" | custom-call | bytes 7200000 | tf_op jit(solution)/shard_map/pallas_call | solution.py:464
  19.8 0.7 copy-done.10
  20.5 5.3 %all-to-all-start.1 = ((bf16[8,6,64,128]{3,2,1,0:T(8,128)(2,1)}), bf16[8,6,64,128]{3,2,1,0:T(8,128)(2,1)S(1)}, u32[]{:S(2)}, u32[]{:S(2)}) async-start(bf16[8,6,64,128]{3,2,1,0:T(8,128)(2,1)} %shard_map.121), calls=%async_computation.1 | async-start | bytes 1572864 | tf_op jit(solution)/shard_map/all_to_all | solution.py:481
  25.7 2.5 %shard_map.127 = (bf16[256,1536]{1,0:T(8,128)(2,1)}, bf16[448,1536]{1,0:T(8,128)(2,1)}) custom-call(bf16[16,16,1536]{2,1,0:T(8,128)(2,1)S(1)} %bitcast.14, bf16[384,3072]{1,0:T(8,128)(2,1)} %refs_17_.1), custom_call_target="tpu_custom_call" | custom-call | bytes 7200000 | tf_op jit(solution)/shard_map/pallas_call | solution.py:483
  28.3 1.3 collective-permute-start.6
  29.6 1.4 %collective-permute-start.3 = (bf16[128,1536]{1,0:T(8,128)(2,1)S(1)}, bf16[128,1536]{1,0:T(8,128)(2,1)S(1)}, u32[]{:S(2)}, u32[]{:S(2)}) collective-permute-start(bf16[128,1536]{1,0:T(8,128)(2,1)S(1)} %collective-permute-done.1.sub2), channel_id=1, source_target_pairs={{0,1},{1,0},{2,3},{3,2},{4,5},{5,4},{6,7},{7,6},{8,9},{9,8},{10,11... | collective-permute-start | bytes 1179656 | tf_op jit(solution)/shard_map/ppermute | solution.py:54
  31.0 0.1 collective-permute-start.8
  31.1 0.5 collective-permute-start.10
  31.6 1.7 %collective-permute-start.4 = (bf16[192,768]{1,0:T(8,128)(2,1)S(1)}, bf16[192,768]{1,0:T(8,128)(2,1)}, u32[]{:S(2)}, u32[]{:S(2)}) collective-permute-start(bf16[192,768]{1,0:T(8,128)(2,1)S(1)} %copy-done.11), channel_id=1, source_target_pairs={{0,4},{4,0},{8,12},{12,8},{16,20},{20,16},{24,28},{28,24},{1,5},{5... | collective-permute-start | bytes 884744 | tf_op jit(solution)/shard_map/ppermute | solution.py:59
  33.3 0.8 copy-done.9
  34.1 2.3 %shard_map.123 = (bf16[512,1536]{1,0:T(8,128)(2,1)S(1)}, f32[32,1536]{1,0:T(8,128)S(1)}) custom-call(bf16[128,1536]{1,0:T(8,128)(2,1)} %sub0.1, bf16[128,1536]{1,0:T(8,128)(2,1)} %copy-done.7, bf16[128,1536]{1,0:T(8,128)(2,1)} %copy-done.8, bf16[128,1536]{1,0:T(8,128)(2,1)} %copy-done.9, f32[31,1536]{1,0:T(8,128)} %depth.1, ...), custom_call_target="tpu_custom_call" | custom-call | bytes 3600000 | tf_op jit(solution)/shard_map/pallas_call | solution.py:502
  36.4 8.1 %collective-permute-done.4.refs_20_ = bf16[192,768]{1,0:T(8,128)(2,1)} collective-permute-done((bf16[192,768]{1,0:T(8,128)(2,1)S(1)}, bf16[192,768]{1,0:T(8,128)(2,1)}, u32[]{:S(2)}, u32[]{:S(2)}) %collective-permute-start.4) | collective-permute-done | bytes 294944 | tf_op jit(solution)/shard_map/ppermute | solution.py:59
  44.5 0.2 all-to-all-done.1
  44.7 1.7 %shard_map.124.patches.refs_0_ = bf16[272,512]{1,0:T(8,128)(2,1)S(1)} custom-call(s32[1,8]{1,0:T(1,128)S(1)} %copy-done.4, s32[8,49]{1,0:T(8,128)S(1)} %bitcast.16, bf16[48,64,128]{2,1,0:T(8,128)(2,1)S(1)} %bitcast.12), custom_call_target="tpu_custom_call" | custom-call | bytes 7200000 | tf_op jit(solution)/shard_map/pallas_call | solution.py:516
  46.5 2.3 %collective-permute-start.5 = (bf16[272,512]{1,0:T(8,128)(2,1)S(1)}, bf16[272,512]{1,0:T(8,128)(2,1)S(1)}, u32[]{:S(2)}, u32[]{:S(2)}) collective-permute-start(bf16[272,512]{1,0:T(8,128)(2,1)S(1)} %shard_map.124.patches.refs_0_), channel_id=1, source_target_pairs={{0,1},{1,0},{2,3},{3,2},{4,5},{5,4},{6,7},{7,6},{8,9},{9,8},{10,11... | collective-permute-start | bytes 835592 | tf_op jit(solution)/shard_map/ppermute | solution.py:54
  48.7 1.3 collective-permute-start.7
  50.0 4.2 %shard_map.125 = (bf16[256,1536]{1,0:T(8,128)(2,1)S(1)}, bf16[256,1536]{1,0:T(8,128)(2,1)S(1)}, bf16[256,1536]{1,0:T(8,128)(2,1)S(1)}, f32[256,128]{1,0:T(8,128)S(1)}) custom-call(bf16[272,512]{1,0:T(8,128)(2,1)S(1)} %shard_map.124.patches.refs_0_, bf16[512,1536]{1,0:T(8,128)(2,1)S(1)} %get-tuple-element.62.weight, f32[32,1536]{1,0:T(8,128)S(1)} %get-tuple-element.63.scales), custom_call_target="tpu_custom_call" | custom-call | bytes 14400000 | tf_op jit(solution)/shard_map/pallas_call | solution.py:546
  54.2 4.2 %shard_map.126 = (bf16[256,1536]{1,0:T(8,128)(2,1)S(1)}, bf16[256,1536]{1,0:T(8,128)(2,1)S(1)}, bf16[256,1536]{1,0:T(8,128)(2,1)S(1)}, f32[256,128]{1,0:T(8,128)S(1)}) custom-call(bf16[272,512]{1,0:T(8,128)(2,1)S(1)} %collective-permute-done.5.patches.refs_1_, bf16[512,1536]{1,0:T(8,128)(2,1)S(1)} %get-tuple-element.62.weight, ...), custom_call_target="tpu_custom_call" | custom-call | bytes 14400000 | tf_op jit(solution)/shard_map/pallas_call | solution.py:548
  58.5 3.7 %collective-permute-done.8.refs_19_ = bf16[384,768]{1,0:T(8,128)(2,1)} collective-permute-done((bf16[384,768]{1,0:T(8,128)(2,1)}, bf16[384,768]{1,0:T(8,128)(2,1)}, u32[]{:S(2)}, u32[]{:S(2)}) %collective-permute-start.8) | collective-permute-done | bytes 589856 | tf_op jit(solution)/shard_map/ppermute | solution.py:54
  62.2 2.8 %collective-permute-done.7.patches.refs_2_ = bf16[272,512]{1,0:T(8,128)(2,1)S(1)} collective-permute-done((bf16[272,512]{1,0:T(8,128)(2,1)S(1)}, bf16[272,512]{1,0:T(8,128)(2,1)S(1)}, u32[]{:S(2)}, u32[]{:S(2)}) %collective-permute-start.7) | collective-permute-done | bytes 278560 | tf_op jit(solution)/shard_map/ppermute | solution.py:54
  65.0 2.1 %collective-permute-start.11 = (bf16[256,1536]{1,0:T(8,128)(2,1)}, bf16[256,1536]{1,0:T(8,128)(2,1)S(1)}, u32[]{:S(2)}, u32[]{:S(2)}) collective-permute-start(bf16[256,1536]{1,0:T(8,128)(2,1)} %collective-permute-done.6.refs_15_), channel_id=1, source_target_pairs={{0,1},{1,0},{2,3},{3,2},{4,5},{5,4},{6,7},{7,6},{8,9},{9,8},{10,11... | collective-permute-start | bytes 2359304 | tf_op jit(solution)/shard_map/ppermute | solution.py:54
  67.1 4.2 %shard_map.128 = (bf16[256,1536]{1,0:T(8,128)(2,1)S(1)}, bf16[256,1536]{1,0:T(8,128)(2,1)S(1)}, bf16[256,1536]{1,0:T(8,128)(2,1)S(1)}, f32[256,128]{1,0:T(8,128)S(1)}) custom-call(bf16[272,512]{1,0:T(8,128)(2,1)S(1)} %collective-permute-done.7.patches.refs_2_, bf16[512,1536]{1,0:T(8,128)(2,1)S(1)} %get-tuple-element.62.weight, ...), custom_call_target="tpu_custom_call" | custom-call | bytes 14400000 | tf_op jit(solution)/shard_map/pallas_call | solution.py:555
  71.3 4.4 %shard_map.129 = (bf16[256,1536]{1,0:T(8,128)(2,1)S(1)}, bf16[256,1536]{1,0:T(8,128)(2,1)S(1)}, bf16[256,1536]{1,0:T(8,128)(2,1)S(1)}, f32[256,128]{1,0:T(8,128)S(1)}) custom-call(bf16[272,512]{1,0:T(8,128)(2,1)S(1)} %collective-permute-done.9.patches.refs_3_, bf16[512,1536]{1,0:T(8,128)(2,1)S(1)} %get-tuple-element.62.weight, ...), custom_call_target="tpu_custom_call" | custom-call | bytes 14400000 | tf_op jit(solution)/shard_map/pallas_call | solution.py:555
  75.8 0.9 copy-done.5
  76.6 12.8 %shard_map.130 = (bf16[384,768]{1,0:T(8,128)(2,1)}, bf16[384,768]{1,0:T(8,128)(2,1)}, bf16[384,768]{1,0:T(8,128)(2,1)}, bf16[384,768]{1,0:T(8,128)(2,1)}, bf16[1...) custom-call(bf16[272,512]{1,0:T(8,128)(2,1)S(1)} %shard_map.124.patc, ...), custom_call_target="tpu_custom_call" | custom-call | bytes 43200000 | tf_op jit(solution)/shard_map/pallas_call | solution.py:557
  89.4 1.3 collective-permute-start.13
  90.7 12.4 %shard_map.131 = f32[32,1,1536]{2,1,0:T(1,128)} custom-call(f32[1,1536]{1,0:T(1,128)S(1)} %reshape.35.gain.refs_12_.refs_0_, bf16[1024,768]{1,0:T(8,128)(2,1)S(1)} %get-tuple-element.85.refs_1_, bf16[1536,768]{1,0:T(8,128)(2,1)S(1)} %get-tuple-element.86.refs_2_, bf16[1024,1536]{1,0:T(8,128)(2,1)S(1)} %get-tuple-element.87.refs_3_.masked, ...), custom_call_target="tpu_custom_call" | custom-call | bytes 46800000 | tf_op jit(solution)/shard_map/pallas_call | solution.py:583
  103.1 1.0 collective-permute-done.13.refs_2_
  104.1 0.9 copy-done.6
  105.0 6.8 %all-to-all-start.2 = ((f32[32,1,1536]{2,1,0:T(1,128)}), f32[32,1,1536]{2,1,0:T(1,128)S(1)}, u32[]{:S(2)}, u32[]{:S(2)}) async-start(f32[32,1,1536]{2,1,0:T(1,128)} %shard_map.131), calls=%async_computation.2 | async-start | bytes 393216 | tf_op jit(solution)/shard_map/all_to_all | solution.py:599
  111.8 0.3 collective-permute-start.12
  112.1 1.5 %collective-permute-start.14 = (bf16[384,768]{1,0:T(8,128)(2,1)}, bf16[384,768]{1,0:T(8,128)(2,1)}, u32[]{:S(2)}, u32[]{:S(2)}) collective-permute-start(bf16[384,768]{1,0:T(8,128)(2,1)} %get-tuple-element.100), channel_id=1, source_target_pairs={{0,3},{1,2},{2,1},{3,0},{4,7},{5,6},{6,5},{7,4},{8,11},{9,10},{10,... | collective-permute-start | bytes 1769480 | tf_op jit(solution)/shard_map/ppermute | solution.py:54
  113.7 1.4 %copy-done.1 = bf16[1024,768]{1,0:T(8,128)(2,1)S(1)} copy-done((bf16[1024,768]{1,0:T(8,128)(2,1)S(1)}, bf16[1024,768]{1,0:T(8,128)(2,1)}, u32[]{:S(2)}) %copy-start.1) | copy-done | bytes 1572888
  115.1 4.0 %shard_map.133 = bf16[768,1536]{1,0:T(8,128)(2,1)} custom-call(bf16[1024,768]{1,0:T(8,128)(2,1)S(1)} %copy-done.1, bf16[1024,1536]{1,0:T(8,128)(2,1)S(1)} %get-tuple-element.87.refs_3_.masked), custom_call_target="tpu_custom_call" | custom-call | bytes 14400000 | tf_op jit(solution)/shard_map/pallas_call | solution.py:603
  119.1 2.0 %all-to-all-done.2 = f32[32,1,1536]{2,1,0:T(1,128)S(1)} async-done(((f32[32,1,1536]{2,1,0:T(1,128)}), f32[32,1,1536]{2,1,0:T(1,128)S(1)}, u32[]{:S(2)}, u32[]{:S(2)}) %all-to-all-start.2) | async-done | bytes 196640 | tf_op jit(solution)/shard_map/all_to_all | solution.py:599
  121.2 0.1 reduce_sum.9
  121.3 0.8 broadcast_in_dim.24
  122.1 2.7 %all-to-all-start.3 = ((f32[32,1,1536]{2,1,0:T(1,128)}), f32[32,1,1536]{2,1,0:T(1,128)S(1)}, u32[]{:S(2)}, u32[]{:S(2)}) async-start(f32[32,1,1536]{2,1,0:T(1,128)} %broadcast_in_dim.24), calls=%async_computation.3 | async-start | bytes 393216 | tf_op jit(solution)/shard_map/all_to_all | solution.py:613
  124.8 6.2 %collective-permute-done.14.refs_3_ = bf16[384,768]{1,0:T(8,128)(2,1)} collective-permute-done((bf16[384,768]{1,0:T(8,128)(2,1)}, bf16[384,768]{1,0:T(8,128)(2,1)}, u32[]{:S(2)}, u32[]{:S(2)}) %collective-permute-start.14) | collective-permute-done | bytes 589856 | tf_op jit(solution)/shard_map/ppermute | solution.py:54
  131.0 2.5 %shard_map.132 = bf16[384,3072]{1,0:T(8,128)(2,1)} custom-call(bf16[384,768]{1,0:T(8,128)(2,1)} %get-tuple-element.83.refs_0_, bf16[384,768]{1,0:T(8,128)(2,1)} %collective-permute-done.12.refs_1_, bf16[384,768]{1,0:T(8,128)(2,1)} %copy-done.6, bf16[384,768]{1,0:T(8,128)(2,1)} %collective-permute-done.14.refs_3_), custom_call_target="tpu_custom_call" | custom-call | bytes 7200000 | tf_op jit(solution)/shard_map/pallas_call | solution.py:618
  133.6 0.5 all-to-all-done.3
  134.1 0.7 copy.15
  (41 shorter events, 0.3 us)
Async XLA Ops:
  0.6 5.6 %copy-start.13 = (s32[1,1,48]{2,1,0:T(1,128)S(1)}, s32[1,1,48]{2,1,0:T(1,128)}, u32[]{:S(2)}) copy-start(s32[1,1,48]{2,1,0:T(1,128)} %param.12) | copy-start | bytes 580
  0.6 12.0 %copy-start.12 = (f32[1536]{0:T(1024)S(1)}, f32[1536]{0:T(1024)}, u32[]{:S(2)}) copy-start(f32[1536]{0:T(1024)} %param.17) | copy-start | bytes 18436
  0.7 17.3 %copy-start.4 = (s32[1,8]{1,0:T(1,128)S(1)}, s32[1,8]{1,0:T(1,128)}, u32[]{:S(2)}) copy-start(s32[1,8]{1,0:T(1,128)} %order_ref.3) | copy-start | bytes 100
  0.7 17.3 %copy-start.2 = (bf16[1,1,48,64,128]{4,3,2,1,0:T(8,128)(2,1)S(1)}, bf16[1,1,48,64,128]{4,3,2,1,0:T(8,128)(2,1)}, u32[]{:S(2)}) copy-start(bf16[1,1,48,64,128]{4,3,2,1,0:T(8,128)(2,1)} %param.10) | copy-start | bytes 2359300
  0.7 25.1 %copy-start.3 = (bf16[1,1,16,16,1536]{4,3,2,1,0:T(8,128)(2,1)S(1)}, bf16[1,1,16,16,1536]{4,3,2,1,0:T(8,128)(2,1)}, u32[]{:S(2)}) copy-start(bf16[1,1,16,16,1536]{4,3,2,1,0:T(8,128)(2,1)} %param.14) | copy-start | bytes 2359300
  0.7 19.1 %collective-permute-start = (bf16[128,1536]{1,0:T(8,128)(2,1)}, bf16[128,1536]{1,0:T(8,128)(2,1)S(1)}, u32[]{:S(2)}, u32[]{:S(2)}) collective-permute-start(bf16[128,1536]{1,0:T(8,128)(2,1)} %sub0.1), channel_id=1, source_target_pairs={{0,1},{1,0},{2,3},{3,2},{4,5},{5,4},{6,7},{7,6},{8,9},{9,8},{10,11... | collective-permute-start | bytes 1179656 | tf_op jit(solution)/shard_map/ppermute | solution.py:54
  0.8 19.0 %collective-permute-start.1 = (bf16[128,1536]{1,0:T(8,128)(2,1)}, bf16[128,1536]{1,0:T(8,128)(2,1)S(1)}, u32[]{:S(2)}, u32[]{:S(2)}) collective-permute-start(bf16[128,1536]{1,0:T(8,128)(2,1)} %sub0.1), channel_id=1, source_target_pairs={{0,2},{1,3},{2,0},{3,1},{4,6},{5,7},{6,4},{7,5},{8,10},{9,11},{10,... | collective-permute-start | bytes 1179656 | tf_op jit(solution)/shard_map/ppermute | solution.py:54
  5.5 14.2 %collective-permute-start.2 = (bf16[192,768]{1,0:T(8,128)(2,1)}, bf16[192,768]{1,0:T(8,128)(2,1)S(1)}, u32[]{:S(2)}, u32[]{:S(2)}) collective-permute-start(bf16[192,768]{1,0:T(8,128)(2,1)} %get-tuple-element.54), channel_id=1, source_target_pairs={{0,2},{1,3},{2,0},{3,1},{4,6},{5,7},{6,4},{7,5},{8,10},{9,11},{10,... | collective-permute-start | bytes 884744 | tf_op jit(solution)/shard_map/ppermute | solution.py:54
  6.9 11.0 %all-to-all-start = ((s32[8,1,49]{2,1,0:T(1,128)}), s32[8,1,49]{2,1,0:T(1,128)S(1)}, u32[]{:S(2)}, u32[]{:S(2)}) async-start(s32[8,1,49]{2,1,0:T(1,128)} %broadcast_in_dim.20), calls=%async_computation | async-start | bytes 8192 | tf_op jit(solution)/shard_map/all_to_all | solution.py:441
  19.7 0.7 copy-start.10
  19.8 8.5 %copy-start.7 = (bf16[128,1536]{1,0:T(8,128)(2,1)}, bf16[128,1536]{1,0:T(8,128)(2,1)S(1)}, u32[]{:S(2)}) copy-start(bf16[128,1536]{1,0:T(8,128)(2,1)S(1)} %collective-permute-done.sub1) | copy-start | bytes 1179652
  19.8 9.8 %copy-start.8 = (bf16[128,1536]{1,0:T(8,128)(2,1)}, bf16[128,1536]{1,0:T(8,128)(2,1)S(1)}, u32[]{:S(2)}) copy-start(bf16[128,1536]{1,0:T(8,128)(2,1)S(1)} %collective-permute-done.1.sub2) | copy-start | bytes 1179652
  20.5 24.2 %all-to-all-start.1 = ((bf16[8,6,64,128]{3,2,1,0:T(8,128)(2,1)}), bf16[8,6,64,128]{3,2,1,0:T(8,128)(2,1)S(1)}, u32[]{:S(2)}, u32[]{:S(2)}) async-start(bf16[8,6,64,128]{3,2,1,0:T(8,128)(2,1)} %shard_map.121), calls=%async_computation.1 | async-start | bytes 1572864 | tf_op jit(solution)/shard_map/all_to_all | solution.py:481
  25.7 5.9 %copy-start.11 = (bf16[192,768]{1,0:T(8,128)(2,1)S(1)}, bf16[192,768]{1,0:T(8,128)(2,1)}, u32[]{:S(2)}) copy-start(bf16[192,768]{1,0:T(8,128)(2,1)} %copy-done.10) | copy-start | bytes 884740
  28.3 33.9 %collective-permute-start.6 = (bf16[256,1536]{1,0:T(8,128)(2,1)}, bf16[256,1536]{1,0:T(8,128)(2,1)}, u32[]{:S(2)}, u32[]{:S(2)}) collective-permute-start(bf16[256,1536]{1,0:T(8,128)(2,1)} %get-tuple-element.68.refs_13_), channel_id=1, source_target_pairs={{0,2},{1,3},{2,0},{3,1},{4,6},{5,7},{6,4},{7,5},{8,10},{9,11},{10,... | collective-permute-start | bytes 2359304 | tf_op jit(solution)/shard_map/ppermute | solution.py:54
  29.6 3.8 %collective-permute-start.3 = (bf16[128,1536]{1,0:T(8,128)(2,1)S(1)}, bf16[128,1536]{1,0:T(8,128)(2,1)S(1)}, u32[]{:S(2)}, u32[]{:S(2)}) collective-permute-start(bf16[128,1536]{1,0:T(8,128)(2,1)S(1)} %collective-permute-done.1.sub2), channel_id=1, source_target_pairs={{0,1},{1,0},{2,3},{3,2},{4,5},{5,4},{6,7},{7,6},{8,9},{9,8},{10,11... | collective-permute-start | bytes 1179656 | tf_op jit(solution)/shard_map/ppermute | solution.py:54
  31.0 31.2 %collective-permute-start.8 = (bf16[384,768]{1,0:T(8,128)(2,1)}, bf16[384,768]{1,0:T(8,128)(2,1)}, u32[]{:S(2)}, u32[]{:S(2)}) collective-permute-start(bf16[384,768]{1,0:T(8,128)(2,1)} %get-tuple-element.69), channel_id=1, source_target_pairs={{0,3},{1,2},{2,1},{3,0},{4,7},{5,6},{6,5},{7,4},{8,11},{9,10},{10,... | collective-permute-start | bytes 1769480 | tf_op jit(solution)/shard_map/ppermute | solution.py:54
  31.1 44.6 %collective-permute-start.10 = (bf16[448,1536]{1,0:T(8,128)(2,1)}, bf16[448,1536]{1,0:T(8,128)(2,1)}, u32[]{:S(2)}, u32[]{:S(2)}) collective-permute-start(bf16[448,1536]{1,0:T(8,128)(2,1)} %get-tuple-element.79), channel_id=1, source_target_pairs={{0,1},{1,0},{2,3},{3,2},{4,5},{5,4},{6,7},{7,6},{8,9},{9,8},{10,11... | collective-permute-start | bytes 4128776 | tf_op jit(solution)/shard_map/ppermute | solution.py:54
  31.6 12.9 %collective-permute-start.4 = (bf16[192,768]{1,0:T(8,128)(2,1)S(1)}, bf16[192,768]{1,0:T(8,128)(2,1)}, u32[]{:S(2)}, u32[]{:S(2)}) collective-permute-start(bf16[192,768]{1,0:T(8,128)(2,1)S(1)} %copy-done.11), channel_id=1, source_target_pairs={{0,4},{4,0},{8,12},{12,8},{16,20},{20,16},{24,28},{28,24},{1,5},{5... | collective-permute-start | bytes 884744 | tf_op jit(solution)/shard_map/ppermute | solution.py:59
  33.3 0.8 copy-start.9
  46.5 7.8 %collective-permute-start.5 = (bf16[272,512]{1,0:T(8,128)(2,1)S(1)}, bf16[272,512]{1,0:T(8,128)(2,1)S(1)}, u32[]{:S(2)}, u32[]{:S(2)}) collective-permute-start(bf16[272,512]{1,0:T(8,128)(2,1)S(1)} %shard_map.124.patches.refs_0_), channel_id=1, source_target_pairs={{0,1},{1,0},{2,3},{3,2},{4,5},{5,4},{6,7},{7,6},{8,9},{9,8},{10,11... | collective-permute-start | bytes 835592 | tf_op jit(solution)/shard_map/ppermute | solution.py:54
  48.7 16.3 %collective-permute-start.7 = (bf16[272,512]{1,0:T(8,128)(2,1)S(1)}, bf16[272,512]{1,0:T(8,128)(2,1)S(1)}, u32[]{:S(2)}, u32[]{:S(2)}) collective-permute-start(bf16[272,512]{1,0:T(8,128)(2,1)S(1)} %shard_map.124.patches.refs_0_), channel_id=1, source_target_pairs={{0,2},{1,3},{2,0},{3,1},{4,6},{5,7},{6,4},{7,5},{8,10},{9,11},{10,... | collective-permute-start | bytes 835592 | tf_op jit(solution)/shard_map/ppermute | solution.py:54
  65.0 10.7 %collective-permute-start.11 = (bf16[256,1536]{1,0:T(8,128)(2,1)}, bf16[256,1536]{1,0:T(8,128)(2,1)S(1)}, u32[]{:S(2)}, u32[]{:S(2)}) collective-permute-start(bf16[256,1536]{1,0:T(8,128)(2,1)} %collective-permute-done.6.refs_15_), channel_id=1, source_target_pairs={{0,1},{1,0},{2,3},{3,2},{4,5},{5,4},{6,7},{7,6},{8,9},{9,8},{10,11... | collective-permute-start | bytes 2359304 | tf_op jit(solution)/shard_map/ppermute | solution.py:54
  67.1 4.2 %collective-permute-start.9 = (bf16[272,512]{1,0:T(8,128)(2,1)S(1)}, bf16[272,512]{1,0:T(8,128)(2,1)S(1)}, u32[]{:S(2)}, u32[]{:S(2)}) collective-permute-start(bf16[272,512]{1,0:T(8,128)(2,1)S(1)} %collective-permute-done.7.patches.refs_2_), channel_id=1, source_target_pairs={{0,1},{1,0},{2,3},{3,2},{4,5},{5,4},{6,7},{7,6},{8,9},{9,8},{10,11... | collective-permute-start | bytes 835592 | tf_op jit(solution)/shard_map/ppermute | solution.py:54
  75.8 0.9 copy-start.5
  89.4 13.7 %copy-start = (bf16[1024,768]{1,0:T(8,128)(2,1)}, bf16[1024,768]{1,0:T(8,128)(2,1)S(1)}, u32[]{:S(2)}) copy-start(bf16[1024,768]{1,0:T(8,128)(2,1)S(1)} %get-tuple-element.102.hidden) | copy-start | bytes 4718596
  89.4 14.7 %collective-permute-start.13 = (bf16[384,768]{1,0:T(8,128)(2,1)}, bf16[384,768]{1,0:T(8,128)(2,1)S(1)}, u32[]{:S(2)}, u32[]{:S(2)}) collective-permute-start(bf16[384,768]{1,0:T(8,128)(2,1)} %get-tuple-element.97), channel_id=1, source_target_pairs={{0,2},{1,3},{2,0},{3,1},{4,6},{5,7},{6,4},{7,5},{8,10},{9,11},{10,... | collective-permute-start | bytes 1769480 | tf_op jit(solution)/shard_map/ppermute | solution.py:54
  104.1 0.9 copy-start.6
  105.0 16.2 %all-to-all-start.2 = ((f32[32,1,1536]{2,1,0:T(1,128)}), f32[32,1,1536]{2,1,0:T(1,128)S(1)}, u32[]{:S(2)}, u32[]{:S(2)}) async-start(f32[32,1,1536]{2,1,0:T(1,128)} %shard_map.131), calls=%async_computation.2 | async-start | bytes 393216 | tf_op jit(solution)/shard_map/all_to_all | solution.py:599
  111.8 13.0 %collective-permute-start.12 = (bf16[384,768]{1,0:T(8,128)(2,1)}, bf16[384,768]{1,0:T(8,128)(2,1)}, u32[]{:S(2)}, u32[]{:S(2)}) collective-permute-start(bf16[384,768]{1,0:T(8,128)(2,1)} %get-tuple-element.84), channel_id=1, source_target_pairs={{0,1},{1,0},{2,3},{3,2},{4,5},{5,4},{6,7},{7,6},{8,9},{9,8},{10,11... | collective-permute-start | bytes 1769480 | tf_op jit(solution)/shard_map/ppermute | solution.py:54
  112.1 18.9 %collective-permute-start.14 = (bf16[384,768]{1,0:T(8,128)(2,1)}, bf16[384,768]{1,0:T(8,128)(2,1)}, u32[]{:S(2)}, u32[]{:S(2)}) collective-permute-start(bf16[384,768]{1,0:T(8,128)(2,1)} %get-tuple-element.100), channel_id=1, source_target_pairs={{0,3},{1,2},{2,1},{3,0},{4,7},{5,6},{6,5},{7,4},{8,11},{9,10},{10,... | collective-permute-start | bytes 1769480 | tf_op jit(solution)/shard_map/ppermute | solution.py:54
  113.7 1.4 %copy-start.1 = (bf16[1024,768]{1,0:T(8,128)(2,1)S(1)}, bf16[1024,768]{1,0:T(8,128)(2,1)}, u32[]{:S(2)}) copy-start(bf16[1024,768]{1,0:T(8,128)(2,1)} %copy-done) | copy-start | bytes 4718596
  122.1 11.9 %all-to-all-start.3 = ((f32[32,1,1536]{2,1,0:T(1,128)}), f32[32,1,1536]{2,1,0:T(1,128)S(1)}, u32[]{:S(2)}, u32[]{:S(2)}) async-start(f32[32,1,1536]{2,1,0:T(1,128)} %broadcast_in_dim.24), calls=%async_computation.3 | async-start | bytes 393216 | tf_op jit(solution)/shard_map/all_to_all | solution.py:613
